TPU v7x, 32 devices: a whole 2x2x4 slice. The times are simulated.
32 devices in a mesh: seq: 16 (over z, x, core), head: 2 (over y).
Axes of the slice: x: 2, y: 2, z: 4, core: 2. Of those that a mesh axis runs over, the one named last changes fastest.
Arguments:
- attention: bfloat16 [4, 1024, 1536], P(None, 'seq', 'head'), may hold values from -6 to 6
- encoder_skip: bfloat16 [4, 2048, 1536], P('head', 'seq'), may hold values from -6 to 6
- depth_filter: float32 [3, 1536], replicated, may hold values from -3 to 3
- point_weight: bfloat16 [1536, 1536], P('head'), may hold values from -0.15625 to 0.15625
- crop_offset: int32 [4], P('head'), may hold values from 0 to 128
- target_bins: int32 [4, 32], P('head'), may hold values from 0 to 127
- cotangent: bfloat16 [4, 2048, 1536], P('head', 'seq'), may hold values from -6 to 6
Outputs:
- target_rows: bfloat16 [4, 32, 1536], P('head', 'seq')
- attention_grad: bfloat16 [4, 1024, 1536], P('head', 'seq')
- skip_grad: bfloat16 [4, 2048, 1536], P('head', 'seq')
- filter_grad: float32 [3, 1536], replicated
Inputs may be any that keep to these rules, and one draw needn't show every extreme that they name: The cropped window of sequence b starts at bin crop_offset[b]; bins of it past the end of the sequence are empty. Target j of sequence b reads bin 128 * (j // 2) + target_bins[b, j] of the cropped window.
All inputs are finite; a program needn't handle non-finite values.
Results may differ from a plain program's by a relative error of at most 0.007.
Values may be sent and summed in bfloat16 or wider, within the bound.
No kernel may reach another device: no remote copies, remote signals or barrier semaphores. Data moves between devices by JAX's collectives and lax.ppermute only.
A program may use at most 64 MiB of HBM per device.

v0:
```python
import math

import jax
import jax.numpy as jnp
from jax import lax
from jax.sharding import PartitionSpec as P

NTD = 2


def extended(shard, sides, width):
    for axis, dim in sides:
        count, length = (lax.axis_size(axis), shard.shape[dim])
        up = [(i, (i + 1) % count) for i in range(count - 1)]
        down = [(j, i) for i, j in up]
        last = lax.slice_in_dim(shard, length - width, length, axis=dim)
        initial = lax.slice_in_dim(shard, 0, width, axis=dim)
        before = lax.ppermute(last, axis, up)
        after = lax.ppermute(initial, axis, down)
        shard = jnp.concatenate([before, shard, after], axis=dim)
    return shard


def passed_along(shard, axis, by):
    count = lax.axis_size(axis)
    pairs = [(i, i + by) for i in range(count) if 0 <= i + by < count]
    return lax.ppermute(shard, axis, pairs)


def gelu_slope(values):
    return (
        0.5 * (1.0 + lax.erf(values * 0.7071067811865476))
        + values * jnp.exp(-0.5 * values * values) * 0.3989422804014327
    )


def with_rims(field):
    return extended(field, (("seq", 1),), 1)


def one_hot(places, length):
    return (places[:, :, None] == jnp.arange(length, dtype=jnp.int32)[None, None, :]).astype(
        jnp.bfloat16
    )


def shards(
    attention, encoder_skip, depth_filter, point_weight, crop_offset, target_bins, cotangent
):
    slab_input = lax.all_to_all(attention, "head", split_axis=0, concat_axis=2, tiled=True)
    local_seqs = encoder_skip.shape[0]
    slab_rows = encoder_skip.shape[1]
    channels = encoder_skip.shape[2]
    summed = (
        jnp.repeat(slab_input, 2, axis=1).astype(jnp.float32) + encoder_skip.astype(jnp.float32)
    ).astype(jnp.bfloat16)
    padded = with_rims(summed)
    filtered = (
        depth_filter[0] * padded[:, :-2]
        + depth_filter[1] * padded[:, 1:-1]
        + depth_filter[2] * padded[:, 2:]
    )
    activated = jax.nn.gelu(filtered, approximate=False).astype(jnp.bfloat16)
    flat_act = activated.reshape(local_seqs * slab_rows, channels)
    full_weight = lax.all_gather(point_weight, "head", axis=0, tiled=True)
    mixed_rows = jnp.dot(flat_act, full_weight, preferred_element_type=jnp.float32)
    block_out = (
        summed.astype(jnp.float32) + mixed_rows.reshape(local_seqs, slab_rows, channels)
    ).astype(jnp.bfloat16)
    slab_index = lax.axis_index("seq")
    my_places = (
        lax.dynamic_slice_in_dim(target_bins, slab_index * NTD, NTD, 1) + crop_offset[:, None]
    )
    next_block = passed_along(block_out, "seq", -1)
    joined = jnp.concatenate([block_out, next_block], axis=1)
    target_rows = jnp.einsum(
        "sjr,srd->sjd",
        one_hot(my_places, 2 * slab_rows),
        joined,
        preferred_element_type=jnp.float32,
    ).astype(jnp.bfloat16)
    prev_cot = passed_along(cotangent, "seq", 1)
    cot_pair = jnp.concatenate([prev_cot, cotangent], axis=1)

    def crop_back(cot_block, shift_by):
        return lax.dynamic_slice_in_dim(cot_block, slab_rows - shift_by, slab_rows, 0)

    grad_out = jax.vmap(crop_back)(cot_pair, crop_offset)
    flat_grad = grad_out.reshape(local_seqs * slab_rows, channels)
    grad_act = lax.dot_general(
        flat_grad, full_weight, (((1,), (1,)), ((), ())), preferred_element_type=jnp.float32
    )
    grad_conv = (grad_act.reshape(local_seqs, slab_rows, channels) * gelu_slope(filtered)).astype(
        jnp.bfloat16
    )
    grad_padded = with_rims(grad_conv)
    grad_sum = (
        grad_out.astype(jnp.float32)
        + depth_filter[0] * grad_padded[:, 2:]
        + depth_filter[1] * grad_padded[:, 1:-1]
        + depth_filter[2] * grad_padded[:, :-2]
    )
    skip_grad = grad_sum.astype(jnp.bfloat16)
    attention_grad = (
        grad_sum.reshape(local_seqs, slab_rows // 2, 2, channels).sum(axis=2).astype(jnp.bfloat16)
    )
    filter_terms = jnp.stack(
        [
            jnp.einsum(
                "srd,srd->d", grad_conv, padded[:, 0:slab_rows], preferred_element_type=jnp.float32
            ),
            jnp.einsum(
                "srd,srd->d",
                grad_conv,
                padded[:, 1 : slab_rows + 1],
                preferred_element_type=jnp.float32,
            ),
            jnp.einsum(
                "srd,srd->d",
                grad_conv,
                padded[:, 2 : slab_rows + 2],
                preferred_element_type=jnp.float32,
            ),
        ]
    )
    filter_sum = lax.psum(filter_terms, ("seq", "head"))
    row_count = local_seqs * lax.axis_size("head") * slab_rows * lax.axis_size("seq")
    filter_grad = filter_sum * (1.0 / math.sqrt(row_count))
    return (target_rows, attention_grad, skip_grad, filter_grad)


def solution(mesh):
    in_specs = (
        P(None, "seq", "head"),
        P("head", "seq", None),
        P(),
        P("head", None),
        P("head"),
        P("head", None),
        P("head", "seq", None),
    )
    out_specs = (P("head", "seq", None), P("head", "seq", None), P("head", "seq", None), P())
    return jax.shard_map(shards, mesh=mesh, in_specs=in_specs, out_specs=out_specs, check_vma=False)
```

profile of v0, /device:TPU:12, one launch (start us, length us, event | category | flops | bytes accessed | tf_op | source)
XLA Modules:
  0.0 153.6 jit_solution(14849639773859394150)
XLA Ops:
  7.2 0.7 all-gather.2.cloned.1.call-update
  7.9 4.0 %all-to-all-start = ((bf16[4,64,768]{2,1,0:T(8,128)(2,1)}), bf16[4,64,768]{2,1,0:T(8,128)(2,1)S(1)}, u32[]{:S(2)}, u32[]{:S(2)}) async-start(bf16[4,64,768]{2,1,0:T(8,128)(2,1)} %param.7), calls=%async_computation | async-start | bytes 786432 | tf_op jit(solution)/shard_map/all_to_all | solution.py:50
  11.9 1.9 %collective-permute-start.3 = (bf16[2,128,1536]{2,1,0:T(8,128)(2,1)}, bf16[2,128,1536]{2,1,0:T(8,128)(2,1)}, u32[]{:S(2)}, u32[]{:S(2)}) collective-permute-start(bf16[2,128,1536]{2,1,0:T(8,128)(2,1)} %param.13), channel_id=1, source_target_pairs={{0,2},{2,4},{4,6},{6,8},{8,10},{10,12},{12,14},{14,16},{16,18},{18... | collective-permute-start | bytes 2359304 | tf_op jit(solution)/shard_map/ppermute | solution.py:27
  14.1 2.9 %all-to-all-done = bf16[4,64,768]{2,1,0:T(8,128)(2,1)S(1)} async-done(((bf16[4,64,768]{2,1,0:T(8,128)(2,1)}), bf16[4,64,768]{2,1,0:T(8,128)(2,1)S(1)}, u32[]{:S(2)}, u32[]{:S(2)}) %all-to-all-start) | async-done | bytes 393248 | tf_op jit(solution)/shard_map/all_to_all | solution.py:50
  18.6 1.1 convert_element_type.67
  19.7 1.4 add_convert_fusion
  21.2 1.9 %collective-permute-start = (bf16[2,1,1536]{2,1,0:T(2,128)(2,1)S(1)}, bf16[2,1,1536]{2,1,0:T(2,128)(2,1)S(1)}, u32[]{:S(2)}, u32[]{:S(2)}) collective-permute-start(bf16[2,1,1536]{2,1,0:T(2,128)(2,1)S(1)} %get-tuple-element.40), channel_id=1, source_target_pairs={{0,2},{2,4},{4,6},{6,8},{8,10},{10,12},{12,14},{14,16},{16,18},{18... | collective-permute-start | bytes 18440 | tf_op jit(solution)/shard_map/ppermute | solution.py:18
  23.1 4.7 %collective-permute-start.1 = (bf16[2,1,1536]{2,1,0:T(2,128)(2,1)S(1)}, bf16[2,1,1536]{2,1,0:T(2,128)(2,1)S(1)}, u32[]{:S(2)}, u32[]{:S(2)}) collective-permute-start(bf16[2,1,1536]{2,1,0:T(2,128)(2,1)S(1)} %get-tuple-element.41), channel_id=1, source_target_pairs={{2,0},{4,2},{6,4},{8,6},{10,8},{12,10},{14,12},{16,14},{18,16},{20... | collective-permute-start | bytes 18440 | tf_op jit(solution)/shard_map/ppermute | solution.py:19
  27.8 1.5 pad_maximum_fusion
  29.3 4.0 %while.1 = (s32[]{:T(128)}, bf16[2,256,1536]{2,1,0:T(8,128)(2,1)S(1)}, s32[2,3]{1,0:T(2,128)S(1)}, bf16[2,128,1536]{2,1,0:T(8,128)(2,1)S(1)}, s32[]{:T(128)}) while((s32[]{:T(128)}, bf16[2,256,1536]{2,1,0:T(8,128)(2,1)S(1)}, s32[2,3]{1,0:T(2,128)S(1)}, bf16[2,128,1536]{2,1,0:T(8,128)(2,1)S(1)}, s32[]{:T(128)}) %tuple.38), condition=%wide.while_cond, body=%wide.while_body.sunk | while | flops 2 | bytes 786557 | solution.py:86
  29.9 1.4 dynamic-slice_dynamic-update-slice_fusion.2
  31.9 1.4 dynamic-slice_dynamic-update-slice_fusion.2
  33.4 39.1 %all-gather.2.cloned.1.call-done = bf16[1536,1536]{1,0:T(8,128)(2,1)} async-done(((bf16[768,1536]{1,0:T(8,128)(2,1)}), bf16[1536,1536]{1,0:T(8,128)(2,1)}) %all-gather.2.cloned.1.call-update) | async-done | bytes 4718608 | tf_op jit(solution)/shard_map/all_gather | solution.py:65
  72.5 8.3 %fusion.10 = bf16[2,128,1536]{2,1,0:T(8,128)(2,1)} fusion(bf16[1536,1536]{1,0:T(8,128)(2,1)} %all-gather.2.cloned.1.call-done, bf16[2,128,1536]{2,1,0:T(8,128)(2,1)S(1)} %copy-done.1, bf16[2,1,1536]{2,1,0:T(2,128)(2,1)S(1)} %collective-permute-done.1, bf16[2,1,1536]{2,1,0:T(2,128)(2,1)S(1)} %collective-permute-done, f32[1536]{0:T(1024)S(1)} %get-tuple-element.24, ...), kind=kOutput, calls=%fused_computation.8 | convolution fusion | flops 1240203264 | bytes 6322176 | tf_op jit(solution)/shard_map/dot_general | solution.py:66
  80.8 2.8 %collective-permute-start.2 = (bf16[2,128,1536]{2,1,0:T(8,128)(2,1)}, bf16[2,128,1536]{2,1,0:T(8,128)(2,1)}, u32[]{:S(2)}, u32[]{:S(2)}) collective-permute-start(bf16[2,128,1536]{2,1,0:T(8,128)(2,1)} %fusion.10), channel_id=1, source_target_pairs={{2,0},{4,2},{6,4},{8,6},{10,8},{12,10},{14,12},{16,14},{18,16},{20... | collective-permute-start | bytes 2359304 | tf_op jit(solution)/shard_map/ppermute | solution.py:27
  83.6 2.9 %fusion.25 = (f32[1536]{0:T(1024)S(1)}, f32[1536]{0:T(1024)S(1)}, f32[1536]{0:T(1024)S(1)}, bf16[2,128,1536]{2,1,0:T(8,128)(2,1)S(1)}) fusion(bf16[2,128,1536]{2,1,0:T(8,128)(2,1)S(1)} %copy-done.1, bf16[2,1,1536]{2,1,0:T(2,128)(2,1)S(1)} %collective-permute-done, bf16[2,1,1536]{2,1,0:T(2,128)(2,1)S(1)} %collective-permute-done.1, ...), kind=kOutput, calls=%fused_computation.26 | convolution fusion | flops 1222110720 | bytes 7127040 | tf_op jit(solution)/shard_map/dot_general | solution.py:90
  86.5 43.6 %psum.7 = f32[3,1536]{1,0:T(4,128)S(1)} all-reduce(f32[3,1536]{1,0:T(4,128)S(1)} %pad_maximum_fusion.6), channel_id=1, replica_groups=mesh['seq'=16,'head'=2] {'seq','head'}, use_global_device_ids=true, to_apply=%region_1.0 | all-reduce | flops 4608 | bytes 36864 | tf_op jit(solution)/shard_map/psum | solution.py:126
  130.2 1.9 %collective-permute-start.4 = (bf16[2,1,1536]{2,1,0:T(2,128)(2,1)S(1)}, bf16[2,1,1536]{2,1,0:T(2,128)(2,1)S(1)}, u32[]{:S(2)}, u32[]{:S(2)}) collective-permute-start(bf16[2,1,1536]{2,1,0:T(2,128)(2,1)S(1)} %get-tuple-element.38), channel_id=1, source_target_pairs={{2,0},{4,2},{6,4},{8,6},{10,8},{12,10},{14,12},{16,14},{18,16},{20... | collective-permute-start | bytes 18440 | tf_op jit(solution)/shard_map/ppermute | solution.py:19
  132.1 2.6 %collective-permute-start.5 = (bf16[2,1,1536]{2,1,0:T(2,128)(2,1)S(1)}, bf16[2,1,1536]{2,1,0:T(2,128)(2,1)S(1)}, u32[]{:S(2)}, u32[]{:S(2)}) collective-permute-start(bf16[2,1,1536]{2,1,0:T(2,128)(2,1)S(1)} %get-tuple-element.39), channel_id=1, source_target_pairs={{0,2},{2,4},{4,6},{6,8},{8,10},{10,12},{12,14},{14,16},{16,18},{18... | collective-permute-start | bytes 18440 | tf_op jit(solution)/shard_map/ppermute | solution.py:18
  135.3 2.7 %collective-permute-done.5 = bf16[2,1,1536]{2,1,0:T(2,128)(2,1)S(1)} collective-permute-done((bf16[2,1,1536]{2,1,0:T(2,128)(2,1)S(1)}, bf16[2,1,1536]{2,1,0:T(2,128)(2,1)S(1)}, u32[]{:S(2)}, u32[]{:S(2)}) %collective-permute-start.5) | collective-permute-done | bytes 6176 | tf_op jit(solution)/shard_map/ppermute | solution.py:18
  138.0 2.7 %fusion.111 = (bf16[2,128,1536]{2,1,0:T(8,128)(2,1)}, f32[2,128,1536]{2,1,0:T(8,128)S(1)}) fusion(bf16[2,128,1536]{2,1,0:T(8,128)(2,1)S(1)} %get-tuple-element.42, bf16[2,1,1536]{2,1,0:T(2,128)(2,1)S(1)} %collective-permute-done.5, f32[1536]{0:T(1024)S(1)} %get-tuple-element.24, f32[1536]{0:T(1024)S(1)} %get-tuple-element.25, ...), kind=kLoop, calls=%fused_computation.134 | loop fusion | flops 6684672 | bytes 3962880 | tf_op jit(solution)/shard_map/convert_element_type | solution.py:103
  140.7 0.9 reshape.30
  141.7 2.8 %reduce_sum.9 = bf16[2,64,1536]{2,1,0:T(8,128)(2,1)} reduce(f32[2,64,2,1536]{3,2,1,0:T(2,128)S(1)} %reshape.30, f32[]{:T(128)} %constant.15.clone.1), dimensions={2}, to_apply=%region_0.0 | reduce | flops 196608 | bytes 1966084 | tf_op jit(solution)/shard_map/reduce_sum | solution.py:105
  144.5 2.3 %convolution_convert_fusion = bf16[2,2,1536]{2,1,0:T(2,128)(2,1)} fusion(bf16[2,128,1536]{2,1,0:T(8,128)(2,1)} %collective-permute-done.2, bf16[2,128,1536]{2,1,0:T(8,128)(2,1)} %fusion.10, s32[2,2]{1,0:T(2,128)S(1)} %dynamic-slice_add_fusion), kind=kOutput, calls=%fused_computation.15 | convolution fusion | flops 6298624 | bytes 1585168 | tf_op jit(solution)/shard_map/sjr,srd->sjd/dot_general | solution.py:76
  (43 shorter events, 3.8 us)
Async XLA Ops:
  7.2 6.7 %copy-start.6 = (s32[2]{0:T(128)S(1)}, s32[2]{0:T(128)}, u32[]{:S(2)}) copy-start(s32[2]{0:T(128)} %param.11) | copy-start | bytes 28
  7.2 6.8 %copy-start.4 = (f32[3,1536]{1,0:T(4,128)S(1)}, f32[3,1536]{1,0:T(4,128)}, u32[]{:S(2)}) copy-start(f32[3,1536]{1,0:T(4,128)} %param.9) | copy-start | bytes 55300
  7.2 6.9 %copy-start.5 = (s32[2,32]{1,0:T(2,128)S(1)}, s32[2,32]{1,0:T(2,128)}, u32[]{:S(2)}) copy-start(s32[2,32]{1,0:T(2,128)} %param.12) | copy-start | bytes 772
  7.2 65.3 %all-gather.2.cloned.1.call-start = ((), (), s32[]{:S(2)}) async-start(), calls=%async_computation.1 | async-start | bytes 7077888 | tf_op jit(solution)/shard_map/all_gather | solution.py:65
  7.9 9.1 %all-to-all-start = ((bf16[4,64,768]{2,1,0:T(8,128)(2,1)}), bf16[4,64,768]{2,1,0:T(8,128)(2,1)S(1)}, u32[]{:S(2)}, u32[]{:S(2)}) async-start(bf16[4,64,768]{2,1,0:T(8,128)(2,1)} %param.7), calls=%async_computation | async-start | bytes 786432 | tf_op jit(solution)/shard_map/all_to_all | solution.py:50
  11.9 15.9 %collective-permute-start.3 = (bf16[2,128,1536]{2,1,0:T(8,128)(2,1)}, bf16[2,128,1536]{2,1,0:T(8,128)(2,1)}, u32[]{:S(2)}, u32[]{:S(2)}) collective-permute-start(bf16[2,128,1536]{2,1,0:T(8,128)(2,1)} %param.13), channel_id=1, source_target_pairs={{0,2},{2,4},{4,6},{6,8},{8,10},{10,12},{12,14},{14,16},{16,18},{18... | collective-permute-start | bytes 2359304 | tf_op jit(solution)/shard_map/ppermute | solution.py:27
  21.1 6.7 %copy-start = (bf16[2,128,1536]{2,1,0:T(8,128)(2,1)}, bf16[2,128,1536]{2,1,0:T(8,128)(2,1)S(1)}, u32[]{:S(2)}) copy-start(bf16[2,128,1536]{2,1,0:T(8,128)(2,1)S(1)} %add_convert_fusion) | copy-start | bytes 2359300
  21.2 12.2 %collective-permute-start = (bf16[2,1,1536]{2,1,0:T(2,128)(2,1)S(1)}, bf16[2,1,1536]{2,1,0:T(2,128)(2,1)S(1)}, u32[]{:S(2)}, u32[]{:S(2)}) collective-permute-start(bf16[2,1,1536]{2,1,0:T(2,128)(2,1)S(1)} %get-tuple-element.40), channel_id=1, source_target_pairs={{0,2},{2,4},{4,6},{6,8},{8,10},{10,12},{12,14},{14,16},{16,18},{18... | collective-permute-start | bytes 18440 | tf_op jit(solution)/shard_map/ppermute | solution.py:18
  23.1 6.2 %copy-start.2 = (bf16[2,128,1536]{2,1,0:T(8,128)(2,1)S(1)}, bf16[2,128,1536]{2,1,0:T(8,128)(2,1)}, u32[]{:S(2)}) copy-start(bf16[2,128,1536]{2,1,0:T(8,128)(2,1)} %custom-call) | copy-start | bytes 2359300
  23.1 10.3 %collective-permute-start.1 = (bf16[2,1,1536]{2,1,0:T(2,128)(2,1)S(1)}, bf16[2,1,1536]{2,1,0:T(2,128)(2,1)S(1)}, u32[]{:S(2)}, u32[]{:S(2)}) collective-permute-start(bf16[2,1,1536]{2,1,0:T(2,128)(2,1)S(1)} %get-tuple-element.41), channel_id=1, source_target_pairs={{2,0},{4,2},{6,4},{8,6},{10,8},{12,10},{14,12},{16,14},{18,16},{20... | collective-permute-start | bytes 18440 | tf_op jit(solution)/shard_map/ppermute | solution.py:19
  29.3 43.2 %copy-start.1 = (bf16[2,128,1536]{2,1,0:T(8,128)(2,1)S(1)}, bf16[2,128,1536]{2,1,0:T(8,128)(2,1)}, u32[]{:S(2)}) copy-start(bf16[2,128,1536]{2,1,0:T(8,128)(2,1)} %copy-done) | copy-start | bytes 2359300
  33.3 50.2 %copy-start.3 = (bf16[2,128,1536]{2,1,0:T(8,128)(2,1)}, bf16[2,128,1536]{2,1,0:T(8,128)(2,1)S(1)}, u32[]{:S(2)}) copy-start(bf16[2,128,1536]{2,1,0:T(8,128)(2,1)S(1)} %get-tuple-element.11) | copy-start | bytes 2359300
  72.5 11.1 %copy-start.7 = (bf16[1536,1536]{1,0:T(8,128)(2,1)S(1)}, bf16[1536,1536]{1,0:T(8,128)(2,1)}, u32[]{:S(2)}) copy-start(bf16[1536,1536]{1,0:T(8,128)(2,1)} %all-gather.2.cloned.1.call-done) | copy-start | bytes 14155780
  80.8 63.7 %collective-permute-start.2 = (bf16[2,128,1536]{2,1,0:T(8,128)(2,1)}, bf16[2,128,1536]{2,1,0:T(8,128)(2,1)}, u32[]{:S(2)}, u32[]{:S(2)}) collective-permute-start(bf16[2,128,1536]{2,1,0:T(8,128)(2,1)} %fusion.10), channel_id=1, source_target_pairs={{2,0},{4,2},{6,4},{8,6},{10,8},{12,10},{14,12},{16,14},{18,16},{20... | collective-permute-start | bytes 2359304 | tf_op jit(solution)/shard_map/ppermute | solution.py:27
  130.2 5.1 %collective-permute-start.4 = (bf16[2,1,1536]{2,1,0:T(2,128)(2,1)S(1)}, bf16[2,1,1536]{2,1,0:T(2,128)(2,1)S(1)}, u32[]{:S(2)}, u32[]{:S(2)}) collective-permute-start(bf16[2,1,1536]{2,1,0:T(2,128)(2,1)S(1)} %get-tuple-element.38), channel_id=1, source_target_pairs={{2,0},{4,2},{6,4},{8,6},{10,8},{12,10},{14,12},{16,14},{18,16},{20... | collective-permute-start | bytes 18440 | tf_op jit(solution)/shard_map/ppermute | solution.py:19
  132.1 5.9 %collective-permute-start.5 = (bf16[2,1,1536]{2,1,0:T(2,128)(2,1)S(1)}, bf16[2,1,1536]{2,1,0:T(2,128)(2,1)S(1)}, u32[]{:S(2)}, u32[]{:S(2)}) collective-permute-start(bf16[2,1,1536]{2,1,0:T(2,128)(2,1)S(1)} %get-tuple-element.39), channel_id=1, source_target_pairs={{0,2},{2,4},{4,6},{6,8},{8,10},{10,12},{12,14},{14,16},{16,18},{18... | collective-permute-start | bytes 18440 | tf_op jit(solution)/shard_map/ppermute | solution.py:18
Sparse Core Ops, SparseCore 0:
  9.6 62.8 all-gather.1
where the time goes:
time: 154 us
  waiting for transfers between devices  45.4 us (29%)
  blocking collectives  43.6 us (28%)
  starting transfers between devices  19.8 us (13%)
  between operations  14.4 us (9%)
  matrix products  13.5 us (9%)
  other arithmetic  9.1 us (6%)
  local copies, waits for them, and re-layouts  7.81 us (5%)
    psum x1, blocking collectives, shards(): filter_sum = lax.psum(filter_terms, ('seq', 'head'))  43.6 us
    all_gather x1, waiting for transfers between devices, shards(): full_weight = lax.all_gather(point_weight, 'head', axis=0, tiled=True)  39.1 us
    dot_general x1, matrix products, shards(): jnp.dot(flat_act, full_weight, preferred_element_type=jnp.float32)  8.3 us
    ppermute x2, starting transfers between devices, extended(): after = lax.ppermute(initial, axis, down)  6.59 us
    ppermute x2, starting transfers between devices, passed_along(): return lax.ppermute(shard, axis, pairs)  4.69 us
    ppermute x2, starting transfers between devices, extended(): before = lax.ppermute(last, axis, up)  4.51 us
    all_to_all x1, starting transfers between devices, shards(): lax.all_to_all(attention, 'head', split_axis=0, concat_axis=2, tiled=True)  3.97 us
    gather x6, local copies, waits for them, and re-layouts  3.97 us
  transfers between devices with their start and end apart: 8, of which 3 were waited for; matrix products, arithmetic and copies ran while one was open for 13% of the time, Pallas kernels for 0%

commit v1 on v0

--- a/solution.py
+++ b/solution.py
@@ -44,6 +44,43 @@
     )
 
 
+def core_swap(part):
+    count = lax.axis_size("seq")
+    return lax.ppermute(part, "seq", [(i, i ^ 1) for i in range(count)])
+
+
+def gathered_weight(rows):
+    heads = lax.axis_size("head")
+    here = lax.axis_index("head")
+    core = lax.axis_index("seq") % 2
+    half = rows.shape[0] // 2
+    mine = lax.dynamic_slice_in_dim(rows, core * half, half, 0)
+    blocks = [(0, rows)]
+    for step in range(1, heads):
+        pairs = [(i, (i + step) % heads) for i in range(heads)]
+        got = lax.ppermute(mine, "head", pairs)
+        twin = core_swap(got)
+        low = jnp.where(core == 0, got, twin)
+        high = jnp.where(core == 0, twin, got)
+        blocks.append((step, jnp.concatenate([low, high], axis=0)))
+    full = jnp.zeros((heads * rows.shape[0], rows.shape[1]), rows.dtype)
+    for step, block in blocks:
+        place = (here - step) % heads
+        full = lax.dynamic_update_slice_in_dim(full, block, place * rows.shape[0], 0)
+    return full
+
+
+def butterfly(total, axis):
+    count = lax.axis_size(axis)
+    if count & (count - 1):
+        return lax.psum(total, axis)
+    step = 1
+    while step < count:
+        total = total + lax.ppermute(total, axis, [(i, i ^ step) for i in range(count)])
+        step *= 2
+    return total
+
+
 def shards(
     attention, encoder_skip, depth_filter, point_weight, crop_offset, target_bins, cotangent
 ):
@@ -62,23 +99,26 @@
     )
     activated = jax.nn.gelu(filtered, approximate=False).astype(jnp.bfloat16)
     flat_act = activated.reshape(local_seqs * slab_rows, channels)
-    full_weight = lax.all_gather(point_weight, "head", axis=0, tiled=True)
+    full_weight = gathered_weight(point_weight)
     mixed_rows = jnp.dot(flat_act, full_weight, preferred_element_type=jnp.float32)
     block_out = (
         summed.astype(jnp.float32) + mixed_rows.reshape(local_seqs, slab_rows, channels)
     ).astype(jnp.bfloat16)
     slab_index = lax.axis_index("seq")
-    my_places = (
-        lax.dynamic_slice_in_dim(target_bins, slab_index * NTD, NTD, 1) + crop_offset[:, None]
+    bins = jnp.concatenate(
+        [jnp.zeros_like(target_bins[:, :NTD]), target_bins], axis=1
     )
-    next_block = passed_along(block_out, "seq", -1)
-    joined = jnp.concatenate([block_out, next_block], axis=1)
-    target_rows = jnp.einsum(
+    asked = lax.dynamic_slice_in_dim(bins, slab_index * NTD, 2 * NTD, 1) + crop_offset[:, None]
+    back = jnp.where(jnp.arange(2 * NTD, dtype=jnp.int32) < NTD, slab_rows, 0)
+    asked = asked - back[None, :]
+    picked = jnp.einsum(
         "sjr,srd->sjd",
-        one_hot(my_places, 2 * slab_rows),
-        joined,
+        one_hot(asked, slab_rows),
+        block_out,
         preferred_element_type=jnp.float32,
     ).astype(jnp.bfloat16)
+    from_next = passed_along(picked[:, :NTD], "seq", -1)
+    target_rows = picked[:, NTD:] + from_next
     prev_cot = passed_along(cotangent, "seq", 1)
     cot_pair = jnp.concatenate([prev_cot, cotangent], axis=1)
 
@@ -123,7 +163,7 @@
             ),
         ]
     )
-    filter_sum = lax.psum(filter_terms, ("seq", "head"))
+    filter_sum = butterfly(butterfly(filter_terms, "seq"), "head")
     row_count = local_seqs * lax.axis_size("head") * slab_rows * lax.axis_size("seq")
     filter_grad = filter_sum * (1.0 / math.sqrt(row_count))
     return (target_rows, attention_grad, skip_grad, filter_grad)

time: 154 us -> 96.5 us (0.63)
  the two profiles are of different devices: /device:TPU:12 before, /device:TPU:0 now
where the time goes in v1:
time: 96.5 us; the launch traced here: 95.9 us
  starting transfers between devices  30.5 us (32%)
  waiting for transfers between devices  21.3 us (22%)
  local copies, waits for them, and re-layouts  17.3 us (18%)
  other arithmetic  13.5 us (14%)
  matrix products  12.3 us (13%)
  between operations  0.97 us (1%)
    all_to_all x1, waiting for transfers between devices, shards(): lax.all_to_all(attention, 'head', split_axis=0, concat_axis=2, tiled=True)  18.5 us
    ppermute x5, starting transfers between devices, butterfly(): lax.ppermute(total, axis, [(i, i ^ step) for i in range(count)])  10 us
    dot_general x1, matrix products, shards(): jnp.einsum('sjr,srd->sjd', one_hot(asked, slab_rows), block_out, preferre...  7.43 us
    ppermute x2, starting transfers between devices, extended(): before = lax.ppermute(last, axis, up)  5.09 us
    gather x6, local copies, waits for them, and re-layouts  4.96 us
    dot_general x1, matrix products, shards(): lax.dot_general(flat_grad, full_weight, (((1,), (1,)), ((), ())), preferr...  4.91 us
    ppermute x2, starting transfers between devices, passed_along(): return lax.ppermute(shard, axis, pairs)  3.64 us
    all_to_all x1, starting transfers between devices, shards(): lax.all_to_all(attention, 'head', split_axis=0, concat_axis=2, tiled=True)  3.47 us
  transfers between devices with their start and end apart: 14, of which 3 were waited for; matrix products, arithmetic and copies ran while one was open for 36% of the time, Pallas kernels for 0%

profile of v1, /device:TPU:0, one launch (start us, length us, event | category | flops | bytes accessed | tf_op | source)
XLA Modules:
  0.0 95.9 jit_solution(16932361304427073792)
XLA Ops:
  0.7 2.4 %constant_dynamic-slice_fusion.1 = bf16[384,1536]{1,0:T(8,128)(2,1)} fusion(bf16[768,1536]{1,0:T(8,128)(2,1)} %param.10, s32[]{:T(128)S(6)} %select_n.56), kind=kLoop, calls=%fused_computation.89 | loop fusion | bytes 2359300 | tf_op jit(solution)/shard_map/dynamic_slice | solution.py:57
  3.1 3.0 %collective-permute-start.2 = (bf16[384,1536]{1,0:T(8,128)(2,1)}, bf16[384,1536]{1,0:T(8,128)(2,1)}, u32[]{:S(2)}, u32[]{:S(2)}) collective-permute-start(bf16[384,1536]{1,0:T(8,128)(2,1)} %constant_dynamic-slice_fusion.1), channel_id=1, source_target_pairs={{0,1},{1,0},{2,3},{3,2},{4,5},{5,4},{6,7},{7,6},{8,9},{9,8},{10,11... | collective-permute-start | bytes 3538952 | tf_op jit(solution)/shard_map/ppermute | solution.py:61
  6.0 3.5 %all-to-all-start = ((bf16[4,64,768]{2,1,0:T(8,128)(2,1)}), bf16[4,64,768]{2,1,0:T(8,128)(2,1)S(1)}, u32[]{:S(2)}, u32[]{:S(2)}) async-start(bf16[4,64,768]{2,1,0:T(8,128)(2,1)} %param.7), calls=%async_computation | async-start | bytes 786432 | tf_op jit(solution)/shard_map/all_to_all | solution.py:87
  9.5 2.4 %collective-permute-start.5 = (bf16[2,128,1536]{2,1,0:T(8,128)(2,1)}, bf16[2,128,1536]{2,1,0:T(8,128)(2,1)}, u32[]{:S(2)}, u32[]{:S(2)}) collective-permute-start(bf16[2,128,1536]{2,1,0:T(8,128)(2,1)} %param.13), channel_id=1, source_target_pairs={{0,2},{2,4},{4,6},{6,8},{8,10},{10,12},{12,14},{14,16},{16,18},{18... | collective-permute-start | bytes 2359304 | tf_op jit(solution)/shard_map/ppermute | solution.py:27
  12.5 2.4 %broadcast_in_dim.24 = bf16[1536,1536]{1,0:T(8,128)(2,1)} broadcast(bf16[]{:T(256)} %constant.110.clone.1), dimensions={} | broadcast | bytes 4718594 | tf_op jit(solution)/shard_map/broadcast_in_dim | solution.py:66
  15.2 1.6 %constant_dynamic-update-slice_fusion = bf16[1536,1536]{1,0:T(8,128)(2,1)} fusion(bf16[1536,1536]{1,0:T(8,128)(2,1)} %broadcast_in_dim.24, bf16[768,1536]{1,0:T(8,128)(2,1)S(1)} %copy-done, s32[]{:T(128)S(6)} %select_n.53), kind=kLoop, calls=%fused_computation.90 | loop fusion | bytes 4718596 | tf_op jit(solution)/shard_map/dynamic_update_slice | solution.py:69
  17.9 18.5 %all-to-all-done = bf16[4,64,768]{2,1,0:T(8,128)(2,1)S(1)} async-done(((bf16[4,64,768]{2,1,0:T(8,128)(2,1)}), bf16[4,64,768]{2,1,0:T(8,128)(2,1)S(1)}, u32[]{:S(2)}, u32[]{:S(2)}) %all-to-all-start) | async-done | bytes 393248 | tf_op jit(solution)/shard_map/all_to_all | solution.py:87
  41.1 1.9 %collective-permute-start = (bf16[2,1,1536]{2,1,0:T(2,128)(2,1)}, bf16[2,1,1536]{2,1,0:T(2,128)(2,1)}, u32[]{:S(2)}, u32[]{:S(2)}) collective-permute-start(bf16[2,1,1536]{2,1,0:T(2,128)(2,1)} %get-tuple-element.42), channel_id=1, source_target_pairs={{0,2},{2,4},{4,6},{6,8},{8,10},{10,12},{12,14},{14,16},{16,18},{18... | collective-permute-start | bytes 18440 | tf_op jit(solution)/shard_map/ppermute | solution.py:18
  43.0 1.4 %collective-permute-start.1 = (bf16[2,1,1536]{2,1,0:T(2,128)(2,1)}, bf16[2,1,1536]{2,1,0:T(2,128)(2,1)}, u32[]{:S(2)}, u32[]{:S(2)}) collective-permute-start(bf16[2,1,1536]{2,1,0:T(2,128)(2,1)} %get-tuple-element.43), channel_id=1, source_target_pairs={{2,0},{4,2},{6,4},{8,6},{10,8},{12,10},{14,12},{16,14},{18,16},{20... | collective-permute-start | bytes 18440 | tf_op jit(solution)/shard_map/ppermute | solution.py:19
  44.4 2.6 %collective-permute-start.3 = (bf16[384,1536]{1,0:T(8,128)(2,1)}, bf16[384,1536]{1,0:T(8,128)(2,1)S(1)}, u32[]{:S(2)}, u32[]{:S(2)}) collective-permute-start(bf16[384,1536]{1,0:T(8,128)(2,1)} %collective-permute-done.2), channel_id=1, source_target_pairs={{0,2},{2,0},{4,6},{6,4},{8,10},{10,8},{12,14},{14,12},{16,18},{18,... | collective-permute-start | bytes 3538952 | tf_op jit(solution)/shard_map/ppermute | solution.py:49
  47.0 1.5 %pad_maximum_fusion = bf16[2,256,1536]{2,1,0:T(8,128)(2,1)S(1)} fusion(bf16[2,128,1536]{2,1,0:T(8,128)(2,1)} %param.13, bf16[2,128,1536]{2,1,0:T(8,128)(2,1)} %collective-permute-done.5), kind=kLoop, calls=%fused_computation.30 | loop fusion | flops 3145728 | bytes 3145728 | tf_op jit(solution)/shard_map/concatenate | solution.py:123
  48.5 5.0 %while.1 = (s32[]{:T(128)}, bf16[2,256,1536]{2,1,0:T(8,128)(2,1)S(1)}, s32[2,3]{1,0:T(2,128)}, bf16[2,128,1536]{2,1,0:T(8,128)(2,1)S(1)}, s32[]{:T(128)}) while((s32[]{:T(128)}, bf16[2,256,1536]{2,1,0:T(8,128)(2,1)S(1)}, s32[2,3]{1,0:T(2,128)}, bf16[2,128,1536]{2,1,0:T(8,128)(2,1)S(1)}, s32[]{:T(128)}) %tuple.37), condition=%wide.while_cond, body=%wide.while_body.sunk | while | flops 2 | bytes 786549 | solution.py:126
  53.5 1.7 %broadcast_select_fusion.1 = (bf16[384,1536]{1,0:T(8,128)(2,1)S(1)}, bf16[384,1536]{1,0:T(8,128)(2,1)S(1)}) fusion(bf16[384,1536]{1,0:T(8,128)(2,1)} %collective-permute-done.2, bf16[384,1536]{1,0:T(8,128)(2,1)S(1)} %collective-permute-done.3, pred[]{:T(512)S(6)} %eq.24), kind=kLoop, calls=%fused_computation.49 | loop fusion | flops 1179648 | bytes 4718593 | tf_op jit(solution)/shard_map/jit(_where)/select_n | solution.py:63
  55.3 1.6 %maximum_dynamic-update-slice_fusion = bf16[1536,1536]{1,0:T(8,128)(2,1)} fusion(bf16[1536,1536]{1,0:T(8,128)(2,1)} %constant_dynamic-update-slice_fusion, s32[]{:T(128)S(6)} %select_n.60, bf16[384,1536]{1,0:T(8,128)(2,1)S(1)} %get-tuple-element.39, bf16[384,1536]{1,0:T(8,128)(2,1)S(1)} %get-tuple-element.38), kind=kLoop, calls=%fused_computation.15 | loop fusion | flops 4718592 | bytes 4718596 | tf_op jit(solution)/shard_map/dynamic_update_slice | solution.py:69
  56.9 4.9 %fusion.25 = (f32[1536]{0:T(1024)S(1)}, f32[1536]{0:T(1024)S(1)}, f32[1536]{0:T(1024)S(1)}, bf16[2,128,1536]{2,1,0:T(8,128)(2,1)S(1)}) fusion(bf16[2,128,1536]{2,1,0:T(8,128)(2,1)S(1)} %copy-done.2, bf16[2,1,1536]{2,1,0:T(2,128)(2,1)} %collective-permute-done, bf16[2,1,1536]{2,1,0:T(2,128)(2,1)} %collective-permute-done.1, f32[1536]{0:T(1024)S(1)} %get-tuple-element.24, ...), kind=kOutput, calls=%fused_computation.27 | convolution fusion | flops 1222110720 | bytes 7127040 | tf_op jit(solution)/shard_map/dot_general | solution.py:130
  63.2 1.8 %collective-permute-start.9 = (f32[3,1536]{1,0:T(4,128)S(1)}, f32[3,1536]{1,0:T(4,128)S(1)}, u32[]{:S(2)}, u32[]{:S(2)}) collective-permute-start(f32[3,1536]{1,0:T(4,128)S(1)} %fusion.145), channel_id=1, source_target_pairs={{0,4},{2,6},{4,0},{6,2},{8,12},{10,14},{12,8},{14,10},{16,20},{18,... | collective-permute-start | bytes 55304 | tf_op jit(solution)/shard_map/ppermute | solution.py:79
  66.4 3.2 %collective-permute-start.7 = (bf16[2,1,1536]{2,1,0:T(2,128)(2,1)S(1)}, bf16[2,1,1536]{2,1,0:T(2,128)(2,1)S(1)}, u32[]{:S(2)}, u32[]{:S(2)}) collective-permute-start(bf16[2,1,1536]{2,1,0:T(2,128)(2,1)S(1)} %get-tuple-element.41), channel_id=1, source_target_pairs={{0,2},{2,4},{4,6},{6,8},{8,10},{10,12},{12,14},{14,16},{16,18},{18... | collective-permute-start | bytes 18440 | tf_op jit(solution)/shard_map/ppermute | solution.py:18
  69.6 1.6 %collective-permute-start.10 = (f32[3,1536]{1,0:T(4,128)S(1)}, f32[3,1536]{1,0:T(4,128)S(1)}, u32[]{:S(2)}, u32[]{:S(2)}) collective-permute-start(f32[3,1536]{1,0:T(4,128)S(1)} %fusion.151), channel_id=1, source_target_pairs={{0,8},{2,10},{4,12},{6,14},{8,0},{10,2},{12,4},{14,6},{16,24},{18,... | collective-permute-start | bytes 55304 | tf_op jit(solution)/shard_map/ppermute | solution.py:79
  71.3 7.4 %convolution_convert_fusion = bf16[2,4,1536]{2,1,0:T(4,128)(2,1)S(1)} fusion(bf16[1536,1536]{1,0:T(8,128)(2,1)} %maximum_dynamic-update-slice_fusion, bf16[2,128,1536]{2,1,0:T(8,128)(2,1)S(1)} %copy-done.2, bf16[2,1,1536]{2,1,0:T(2,128)(2,1)} %collective-permute-done.1, bf16[2,1,1536]{2,1,0:T(2,128)(2,1)} %collective-permute-done, ...), kind=kOutput, calls=%fused_computation.16 | convolution fusion | flops 1243362304 | bytes 5560352 | tf_op jit(solution)/shard_map/sjr,srd->sjd/dot_general | solution.py:114
  80.1 4.8 %collective-permute-start.11 = (f32[3,1536]{1,0:T(4,128)S(1)}, f32[3,1536]{1,0:T(4,128)S(1)}, u32[]{:S(2)}, u32[]{:S(2)}) collective-permute-start(f32[3,1536]{1,0:T(4,128)S(1)} %add.109), channel_id=1, source_target_pairs={{0,16},{2,18},{4,20},{6,22},{8,24},{10,26},{12,28},{14,30},{16,0},... | collective-permute-start | bytes 55304 | tf_op jit(solution)/shard_map/ppermute | solution.py:79
  84.9 2.7 %fusion.146 = (bf16[2,128,1536]{2,1,0:T(8,128)(2,1)}, f32[2,128,1536]{2,1,0:T(8,128)S(1)}) fusion(bf16[2,128,1536]{2,1,0:T(8,128)(2,1)S(1)} %get-tuple-element.44, bf16[2,1,1536]{2,1,0:T(2,128)(2,1)S(1)} %collective-permute-done.7, f32[1536]{0:T(1024)S(1)} %get-tuple-element.24, f32[1536]{0:T(1024)S(1)} %copy-done.6, ...), kind=kLoop, calls=%fused_computation.124 | loop fusion | flops 6684672 | bytes 3962880 | tf_op jit(solution)/shard_map/convert_element_type | solution.py:143
  88.5 2.8 %reduce_sum.9 = bf16[2,64,1536]{2,1,0:T(8,128)(2,1)} reduce(f32[2,64,2,1536]{3,2,1,0:T(2,128)S(1)} %reshape.35, f32[]{:T(128)} %constant.27.clone.1), dimensions={2}, to_apply=%region_0.1 | reduce | flops 196608 | bytes 1966084 | tf_op jit(solution)/shard_map/reduce_sum | solution.py:145
  91.4 1.6 %collective-permute-start.12 = (f32[3,1536]{1,0:T(4,128)S(1)}, f32[3,1536]{1,0:T(4,128)S(1)}, u32[]{:S(2)}, u32[]{:S(2)}) collective-permute-start(f32[3,1536]{1,0:T(4,128)S(1)} %add.110), channel_id=1, source_target_pairs={{0,1},{1,0},{2,3},{3,2},{4,5},{5,4},{6,7},{7,6},{8,9},{9,8},{10,11... | collective-permute-start | bytes 55304 | tf_op jit(solution)/shard_map/ppermute | solution.py:79
  93.6 1.7 %collective-permute-done.12 = f32[3,1536]{1,0:T(4,128)S(1)} collective-permute-done((f32[3,1536]{1,0:T(4,128)S(1)}, f32[3,1536]{1,0:T(4,128)S(1)}, u32[]{:S(2)}, u32[]{:S(2)}) %collective-permute-start.12) | collective-permute-done | bytes 18464 | tf_op jit(solution)/shard_map/ppermute | solution.py:79
  (72 shorter events, 17.9 us)
Async XLA Ops:
  0.6 11.2 %copy-start.9 = (s32[2]{0:T(128)S(1)}, s32[2]{0:T(128)}, u32[]{:S(2)}) copy-start(s32[2]{0:T(128)} %param.11) | copy-start | bytes 28
  3.1 41.4 %collective-permute-start.2 = (bf16[384,1536]{1,0:T(8,128)(2,1)}, bf16[384,1536]{1,0:T(8,128)(2,1)}, u32[]{:S(2)}, u32[]{:S(2)}) collective-permute-start(bf16[384,1536]{1,0:T(8,128)(2,1)} %constant_dynamic-slice_fusion.1), channel_id=1, source_target_pairs={{0,1},{1,0},{2,3},{3,2},{4,5},{5,4},{6,7},{7,6},{8,9},{9,8},{10,11... | collective-permute-start | bytes 3538952 | tf_op jit(solution)/shard_map/ppermute | solution.py:61
  6.0 30.4 %all-to-all-start = ((bf16[4,64,768]{2,1,0:T(8,128)(2,1)}), bf16[4,64,768]{2,1,0:T(8,128)(2,1)S(1)}, u32[]{:S(2)}, u32[]{:S(2)}) async-start(bf16[4,64,768]{2,1,0:T(8,128)(2,1)} %param.7), calls=%async_computation | async-start | bytes 786432 | tf_op jit(solution)/shard_map/all_to_all | solution.py:87
  9.5 37.5 %collective-permute-start.5 = (bf16[2,128,1536]{2,1,0:T(8,128)(2,1)}, bf16[2,128,1536]{2,1,0:T(8,128)(2,1)}, u32[]{:S(2)}, u32[]{:S(2)}) collective-permute-start(bf16[2,128,1536]{2,1,0:T(8,128)(2,1)} %param.13), channel_id=1, source_target_pairs={{0,2},{2,4},{4,6},{6,8},{8,10},{10,12},{12,14},{14,16},{16,18},{18... | collective-permute-start | bytes 2359304 | tf_op jit(solution)/shard_map/ppermute | solution.py:27
  12.5 2.6 %copy-start = (bf16[768,1536]{1,0:T(8,128)(2,1)S(1)}, bf16[768,1536]{1,0:T(8,128)(2,1)}, u32[]{:S(2)}) copy-start(bf16[768,1536]{1,0:T(8,128)(2,1)} %param.10) | copy-start | bytes 7077892
  15.2 2.1 %copy-start.7 = (f32[3,1536]{1,0:T(4,128)S(1)}, f32[3,1536]{1,0:T(4,128)}, u32[]{:S(2)}) copy-start(f32[3,1536]{1,0:T(4,128)} %param.9) | copy-start | bytes 55300
  40.4 6.6 %copy-start.1 = (bf16[2,128,1536]{2,1,0:T(8,128)(2,1)}, bf16[2,128,1536]{2,1,0:T(8,128)(2,1)S(1)}, u32[]{:S(2)}) copy-start(bf16[2,128,1536]{2,1,0:T(8,128)(2,1)S(1)} %add_convert_fusion) | copy-start | bytes 2359300
  41.1 15.7 %collective-permute-start = (bf16[2,1,1536]{2,1,0:T(2,128)(2,1)}, bf16[2,1,1536]{2,1,0:T(2,128)(2,1)}, u32[]{:S(2)}, u32[]{:S(2)}) collective-permute-start(bf16[2,1,1536]{2,1,0:T(2,128)(2,1)} %get-tuple-element.42), channel_id=1, source_target_pairs={{0,2},{2,4},{4,6},{6,8},{8,10},{10,12},{12,14},{14,16},{16,18},{18... | collective-permute-start | bytes 18440 | tf_op jit(solution)/shard_map/ppermute | solution.py:18
  43.0 5.5 %copy-start.3 = (bf16[2,128,1536]{2,1,0:T(8,128)(2,1)S(1)}, bf16[2,128,1536]{2,1,0:T(8,128)(2,1)}, u32[]{:S(2)}) copy-start(bf16[2,128,1536]{2,1,0:T(8,128)(2,1)} %custom-call) | copy-start | bytes 2359300
  43.0 13.8 %collective-permute-start.1 = (bf16[2,1,1536]{2,1,0:T(2,128)(2,1)}, bf16[2,1,1536]{2,1,0:T(2,128)(2,1)}, u32[]{:S(2)}, u32[]{:S(2)}) collective-permute-start(bf16[2,1,1536]{2,1,0:T(2,128)(2,1)} %get-tuple-element.43), channel_id=1, source_target_pairs={{2,0},{4,2},{6,4},{8,6},{10,8},{12,10},{14,12},{16,14},{18,16},{20... | collective-permute-start | bytes 18440 | tf_op jit(solution)/shard_map/ppermute | solution.py:19
  44.4 9.1 %collective-permute-start.3 = (bf16[384,1536]{1,0:T(8,128)(2,1)}, bf16[384,1536]{1,0:T(8,128)(2,1)S(1)}, u32[]{:S(2)}, u32[]{:S(2)}) collective-permute-start(bf16[384,1536]{1,0:T(8,128)(2,1)} %collective-permute-done.2), channel_id=1, source_target_pairs={{0,2},{2,0},{4,6},{6,4},{8,10},{10,8},{12,14},{14,12},{16,18},{18,... | collective-permute-start | bytes 3538952 | tf_op jit(solution)/shard_map/ppermute | solution.py:49
  53.5 3.3 %copy-start.4 = (bf16[2,128,1536]{2,1,0:T(8,128)(2,1)}, bf16[2,128,1536]{2,1,0:T(8,128)(2,1)S(1)}, u32[]{:S(2)}) copy-start(bf16[2,128,1536]{2,1,0:T(8,128)(2,1)S(1)} %get-tuple-element.11) | copy-start | bytes 2359300
  56.9 5.1 %copy-start.8 = (s32[2,32]{1,0:T(2,128)S(1)}, s32[2,32]{1,0:T(2,128)}, u32[]{:S(2)}) copy-start(s32[2,32]{1,0:T(2,128)} %param.12) | copy-start | bytes 772
  56.9 5.1 %copy-start.10 = (s32[2]{0:T(128)S(1)}, s32[2]{0:T(128)}, u32[]{:S(2)}) copy-start(s32[2]{0:T(128)} %param.11) | copy-start | bytes 28
  56.9 5.1 %copy-start.11 = (s32[4]{0:T(128)S(1)}, s32[4]{0:T(128)}, u32[]{:S(2)}) copy-start(s32[4]{0:T(128)} %compare_select_fusion.1) | copy-start | bytes 52
  61.9 1.3 %collective-permute-start.8 = (f32[3,1536]{1,0:T(4,128)S(1)}, f32[3,1536]{1,0:T(4,128)S(1)}, u32[]{:S(2)}, u32[]{:S(2)}) collective-permute-start(f32[3,1536]{1,0:T(4,128)S(1)} %pad_maximum_fusion.5), channel_id=1, source_target_pairs={{0,2},{2,0},{4,6},{6,4},{8,10},{10,8},{12,14},{14,12},{16,18},{18,... | collective-permute-start | bytes 55304 | tf_op jit(solution)/shard_map/ppermute | solution.py:79
  63.2 6.4 %collective-permute-start.9 = (f32[3,1536]{1,0:T(4,128)S(1)}, f32[3,1536]{1,0:T(4,128)S(1)}, u32[]{:S(2)}, u32[]{:S(2)}) collective-permute-start(f32[3,1536]{1,0:T(4,128)S(1)} %fusion.145), channel_id=1, source_target_pairs={{0,4},{2,6},{4,0},{6,2},{8,12},{10,14},{12,8},{14,10},{16,20},{18,... | collective-permute-start | bytes 55304 | tf_op jit(solution)/shard_map/ppermute | solution.py:79
  65.1 19.8 %collective-permute-start.6 = (bf16[2,1,1536]{2,1,0:T(2,128)(2,1)S(1)}, bf16[2,1,1536]{2,1,0:T(2,128)(2,1)S(1)}, u32[]{:S(2)}, u32[]{:S(2)}) collective-permute-start(bf16[2,1,1536]{2,1,0:T(2,128)(2,1)S(1)} %get-tuple-element.40), channel_id=1, source_target_pairs={{2,0},{4,2},{6,4},{8,6},{10,8},{12,10},{14,12},{16,14},{18,16},{20... | collective-permute-start | bytes 18440 | tf_op jit(solution)/shard_map/ppermute | solution.py:19
  66.4 18.5 %collective-permute-start.7 = (bf16[2,1,1536]{2,1,0:T(2,128)(2,1)S(1)}, bf16[2,1,1536]{2,1,0:T(2,128)(2,1)S(1)}, u32[]{:S(2)}, u32[]{:S(2)}) collective-permute-start(bf16[2,1,1536]{2,1,0:T(2,128)(2,1)S(1)} %get-tuple-element.41), channel_id=1, source_target_pairs={{0,2},{2,4},{4,6},{6,8},{8,10},{10,12},{12,14},{14,16},{16,18},{18... | collective-permute-start | bytes 18440 | tf_op jit(solution)/shard_map/ppermute | solution.py:18
  69.6 15.3 %copy-start.6 = (f32[1536]{0:T(1024)S(1)}, f32[1536]{0:T(1024)}, u32[]{:S(2)}) copy-start(f32[1536]{0:T(1024)} %get-tuple-element.25) | copy-start | bytes 18436
  69.6 10.4 %collective-permute-start.10 = (f32[3,1536]{1,0:T(4,128)S(1)}, f32[3,1536]{1,0:T(4,128)S(1)}, u32[]{:S(2)}, u32[]{:S(2)}) collective-permute-start(f32[3,1536]{1,0:T(4,128)S(1)} %fusion.151), channel_id=1, source_target_pairs={{0,8},{2,10},{4,12},{6,14},{8,0},{10,2},{12,4},{14,6},{16,24},{18,... | collective-permute-start | bytes 55304 | tf_op jit(solution)/shard_map/ppermute | solution.py:79
  78.7 14.2 %collective-permute-start.4 = (bf16[2,2,1536]{2,1,0:T(2,128)(2,1)S(1)}, bf16[2,2,1536]{2,1,0:T(2,128)(2,1)S(1)}, u32[]{:S(2)}, u32[]{:S(2)}) collective-permute-start(bf16[2,2,1536]{2,1,0:T(2,128)(2,1)S(1)} %slice.78), channel_id=1, source_target_pairs={{2,0},{4,2},{6,4},{8,6},{10,8},{12,10},{14,12},{16,14},{18,16},{20... | collective-permute-start | bytes 36872 | tf_op jit(solution)/shard_map/ppermute | solution.py:27
  80.1 11.3 %collective-permute-start.11 = (f32[3,1536]{1,0:T(4,128)S(1)}, f32[3,1536]{1,0:T(4,128)S(1)}, u32[]{:S(2)}, u32[]{:S(2)}) collective-permute-start(f32[3,1536]{1,0:T(4,128)S(1)} %add.109), channel_id=1, source_target_pairs={{0,16},{2,18},{4,20},{6,22},{8,24},{10,26},{12,28},{14,30},{16,0},... | collective-permute-start | bytes 55304 | tf_op jit(solution)/shard_map/ppermute | solution.py:79
  91.4 3.9 %collective-permute-start.12 = (f32[3,1536]{1,0:T(4,128)S(1)}, f32[3,1536]{1,0:T(4,128)S(1)}, u32[]{:S(2)}, u32[]{:S(2)}) collective-permute-start(f32[3,1536]{1,0:T(4,128)S(1)} %add.110), channel_id=1, source_target_pairs={{0,1},{1,0},{2,3},{3,2},{4,5},{5,4},{6,7},{7,6},{8,9},{9,8},{10,11... | collective-permute-start | bytes 55304 | tf_op jit(solution)/shard_map/ppermute | solution.py:79
  (2 other events, 3.2 us)

commit v2 on v1

--- a/solution.py
+++ b/solution.py
@@ -1,8 +1,11 @@
+import functools
 import math
 
 import jax
 import jax.numpy as jnp
 from jax import lax
+from jax.experimental import pallas as pl
+from jax.experimental.pallas import tpu as pltpu
 from jax.sharding import PartitionSpec as P
 
 NTD = 2
@@ -81,7 +84,7 @@
     return total
 
 
-def shards(
+def plain_shards(
     attention, encoder_skip, depth_filter, point_weight, crop_offset, target_bins, cotangent
 ):
     slab_input = lax.all_to_all(attention, "head", split_axis=0, concat_axis=2, tiled=True)
@@ -169,6 +172,584 @@
     return (target_rows, attention_grad, skip_grad, filter_grad)
 
 
+LANES = 128
+PAD = 8
+BF = jnp.bfloat16
+F32 = jnp.float32
+
+
+def dot(left, right):
+    return lax.dot_general(left, right, (((1,), (0,)), ((), ())), preferred_element_type=F32)
+
+
+def dot_rows(left, right):
+    return lax.dot_general(left, right, (((1,), (1,)), ((), ())), preferred_element_type=F32)
+
+
+def grid_of(rows, columns):
+    return (
+        lax.broadcasted_iota(jnp.int32, (rows, columns), 0),
+        lax.broadcasted_iota(jnp.int32, (rows, columns), 1),
+    )
+
+
+def picks(match):
+    return jnp.where(match, 1.0, 0.0).astype(BF)
+
+
+def params():
+    return pltpu.CompilerParams(vmem_limit_bytes=40 * 1024 * 1024)
+
+
+def cost(flops, moved, special=0):
+    return pl.CostEstimate(flops=flops, bytes_accessed=moved, transcendentals=special)
+
+
+def pack_kernel(skip_lo, skip_hi, att_lo, att_hi, cot_lo, cot_hi, up, down, far):
+    half = att_lo.shape[2]
+    row, col = grid_of(16, 32)
+    at, base = row & 7, (row >> 3) * 16
+    skips = skip_hi[...].reshape(32, 2 * half)
+    out = dot(picks((at >= 6) & (col == base + at + 8)), skips)
+    edge = picks((at == 5) & (col == base + 15))
+    for group in range(2):
+        rows = att_hi[2 * group : 2 * group + 2].reshape(32, half)
+        cols = slice(group * half, (group + 1) * half)
+        up[:, cols] = (out[:, cols] + dot(edge, rows)).astype(BF)
+    skips = skip_lo[...].reshape(32, 2 * half)
+    cots = cot_lo[...].reshape(32, 2 * half)
+    out = dot(picks((at < 2) & (col == base + at)), skips) + dot(
+        picks((at == 3) & (col == base)), cots
+    )
+    edge = picks((at == 2) & (col == base))
+    for group in range(2):
+        rows = att_lo[2 * group : 2 * group + 2].reshape(32, half)
+        cols = slice(group * half, (group + 1) * half)
+        down[:, cols] = (out[:, cols] + dot(edge, rows)).astype(BF)
+    cots = cot_hi[...].reshape(32, 2 * half)
+    far[...] = dot(picks((at == 7) & (col == base + 15)), cots).astype(BF)
+
+
+def packed(encoder_skip, attention, cotangent):
+    seqs, rows, wide = encoder_skip.shape
+    half = attention.shape[2]
+    short = attention.shape[1]
+
+    def block(count, width, place):
+        return pl.BlockSpec((count, 16, width), lambda i: (0, place, 0))
+
+    out = jax.ShapeDtypeStruct((16, wide), BF)
+    return pl.pallas_call(
+        pack_kernel,
+        grid=(1,),
+        in_specs=[
+            block(seqs, wide, 0),
+            block(seqs, wide, rows // 16 - 1),
+            block(2 * seqs, half, 0),
+            block(2 * seqs, half, short // 16 - 1),
+            block(seqs, wide, 0),
+            block(seqs, wide, rows // 16 - 1),
+        ],
+        out_specs=[pl.BlockSpec((16, wide), lambda i: (0, 0))] * 3,
+        out_shape=[out, out, out],
+        compiler_params=params(),
+        name="pack_edges",
+    )(encoder_skip, encoder_skip, attention, attention, cotangent, cotangent)
+
+
+def ship_kernel(meta, att, up, down, out):
+    short = att.shape[1]
+    row, col = grid_of(16, 16)
+    for s in range(2):
+        out[s, 0:short] = att[s]
+        edges = dot(picks((row == 0) & (col == s * 8 + 5)), up[...]) + dot(
+            picks((row == 1) & (col == s * 8 + 2)), down[...]
+        )
+        out[s, short : short + 16] = edges.astype(BF)
+
+
+def shipment(meta, attention, up, down):
+    _, short, half = attention.shape
+    return pl.pallas_call(
+        ship_kernel,
+        grid_spec=pltpu.PrefetchScalarGridSpec(
+            num_scalar_prefetch=1,
+            grid=(1,),
+            in_specs=[
+                pl.BlockSpec((2, short, half), lambda i, m: (1 - m[0], 0, 0)),
+                pl.BlockSpec((16, half), lambda i, m: (0, 1 - m[0])),
+                pl.BlockSpec((16, half), lambda i, m: (0, 1 - m[0])),
+            ],
+            out_specs=pl.BlockSpec((2, short + 16, half), lambda i, m: (0, 0, 0)),
+        ),
+        out_shape=jax.ShapeDtypeStruct((2, short + 16, half), BF),
+        compiler_params=params(),
+        name="pack_attention",
+    )(meta, attention, up, down)
+
+
+def slab_sums(att, skip, up, down, ext, cols, from_ship):
+    width = cols.size
+    short = 64
+    row, col = grid_of(2 * short, short)
+    spread = picks((row >> 1) == col)
+    row, col = grid_of(16, 32 if from_ship else 16)
+    at = row & 7
+    high, low = up[:, cols], down[:, cols]
+    if from_ship:
+        edges = jnp.concatenate([att[0, short : short + 16, cols], att[1, short : short + 16, cols]])
+        base = (row >> 3) * 16
+        above = dot(picks((at >= 6) & (col == base)), edges)
+        below = dot(picks((at < 2) & (col == base + 1)), edges)
+    else:
+        base = row & 8
+        above = dot(picks((at >= 6) & (col == base + 5)), high)
+        below = dot(picks((at < 2) & (col == base + 2)), low)
+    at = lax.broadcasted_iota(jnp.int32, (16, width), 0) & 7
+    above = jnp.where(at >= 6, above + high.astype(F32), 0.0).astype(BF).astype(F32)
+    below = jnp.where(at < 2, below + low.astype(F32), 0.0).astype(BF).astype(F32)
+    for s in range(2):
+        body = dot(spread, att[s, 0:short, cols]) + skip[s, :, cols].astype(F32)
+        ext[s, 0:PAD] = above[s * 8 : s * 8 + 8]
+        ext[s, PAD : PAD + 2 * short] = body.astype(BF).astype(F32)
+        ext[s, PAD + 2 * short : 2 * PAD + 2 * short] = below[s * 8 : s * 8 + 8]
+
+
+def around(field):
+    tall = field.shape[0]
+    return pltpu.roll(field, 1, 0), pltpu.roll(field, tall - 1, 0)
+
+
+def phi_of(values):
+    return 0.5 * (1.0 + lax.erf(values * 0.7071067811865476))
+
+
+def slope_of(values):
+    return phi_of(values) + values * jnp.exp(-0.5 * values * values) * 0.3989422804014327
+
+
+def asked_rows(meta, offsets, bins, s, ext, taps, tall):
+    row, col = grid_of(16, tall)
+    want = row & 3
+    at = jnp.full((16, tall), -4096, jnp.int32)
+    slab = meta[1]
+    for k in range(4):
+        mine = k < NTD
+        home = slab if mine else jnp.maximum(slab - 1, 0)
+        place = bins[s, home * NTD + (k % NTD)] + offsets[s] - (0 if mine else tall - 2 * PAD)
+        fits = (place >= 0) & (place < tall - 2 * PAD)
+        at = jnp.where((want == k) & (row < 8), jnp.where(fits, place + PAD, -4096), at)
+    source = ext.astype(BF)
+    before = dot(picks(col == at - 1), source)
+    here = dot(picks(col == at), source)
+    after = dot(picks(col == at + 1), source)
+    value = taps[0] * before + taps[1] * here + taps[2] * after
+    act = value * phi_of(value)
+    row = lax.broadcasted_iota(jnp.int32, act.shape, 0)
+    return jnp.where(row < 4, act, here).astype(BF)
+
+
+def taps_of(filt, cols):
+    return [filt[k : k + 1, cols] for k in range(3)]
+
+
+def tap_sums(conv, ext, rows):
+    before, after = around(ext)
+    body = slice(PAD, PAD + rows)
+    mine = conv[body]
+    return [
+        jnp.sum(mine * other[body], axis=0, keepdims=True) for other in (before, ext, after)
+    ]
+
+
+def grads(conv, direct, taps, rows, pair):
+    before, after = around(conv)
+    body = slice(PAD, PAD + rows)
+    total = direct + taps[0] * after[body] + taps[1] * conv[body] + taps[2] * before[body]
+    short = rows // 2
+    sums = []
+    for k in range(total.shape[1] // LANES):
+        pair[k] = total[:, k * LANES : (k + 1) * LANES]
+        sums.append(pair[k, pl.ds(0, short, 2), :] + pair[k, pl.ds(1, short, 2), :])
+    return total, jnp.concatenate(sums, axis=1)
+
+
+def own_kernel(
+    slabs, meta, offsets, bins, att, skip, up, down, down_all, far, prev, cot, weight, filt,
+    moved, asked, terms, skip_grad, att_grad, ext, pair,
+):
+    rows = skip.shape[1]
+    tall = rows + 2 * PAD
+    wide = cot.shape[2]
+    row, col = grid_of(tall, rows)
+    last = meta[1] == slabs - 1
+    for s in range(2):
+        at = row - PAD
+        fits = (at >= -1) & (at < jnp.where(last, rows, rows + 1))
+        source = jnp.where(fits, at - offsets[s], -4096)
+        older = picks(col == source + rows)
+        newer = picks(col == source)
+        source, narrow = source[:, :16], col[:, :16]
+        below = picks((source == rows) & (narrow == s * 8 + 3))
+        above = picks((source == -rows - 1) & (narrow == s * 8 + 7))
+        for part in range(0, wide, 512):
+            cols = slice(part, part + 512)
+            moved[s, :, cols] = (
+                dot(older, prev[s, :, cols])
+                + dot(newer, cot[s, :, cols])
+                + dot(below, down_all[:, cols])
+                + dot(above, far[:, cols])
+            ).astype(BF)
+    width = ext.shape[2]
+    half = skip.shape[2]
+    first = meta[0] * half
+
+    @pl.loop(0, half // width)
+    def _(part):
+        begin = pl.multiple_of(part * width, width)
+        cols = pl.ds(begin, width)
+        slab_sums(att, skip, up, down, ext, cols, False)
+        taps = taps_of(filt, cols)
+        piece = weight[pl.ds(begin, width), :]
+        sums = [0.0, 0.0, 0.0]
+        there = pl.ds(pl.multiple_of(first + begin, width), width)
+        for s in range(2):
+            field = ext[s]
+            before, after = around(field)
+            slope = slope_of(taps[0] * before + taps[1] * field + taps[2] * after)
+            asked[s * 16 : s * 16 + 16, cols] = asked_rows(
+                meta, offsets, bins, s, field, taps, tall
+            )
+            conv = (dot_rows(moved[s], piece) * slope).astype(BF).astype(F32)
+            sums = [a + b for a, b in zip(sums, tap_sums(conv, field, rows))]
+            direct = moved[s, :, there].astype(F32)[PAD : PAD + rows]
+            total, pairs = grads(conv, direct, taps, rows, pair)
+            skip_grad[s, :, cols] = total.astype(BF)
+            att_grad[s, :, cols] = pairs.astype(BF)
+        for k in range(3):
+            terms[k : k + 1, cols] = sums[k]
+
+
+def own_half(meta, offsets, bins, attention, skip, up, down, far, prev, cot, weight, filt, slabs):
+    seqs, rows, wide = skip.shape
+    _, short, half = attention.shape
+    tall = rows + 2 * PAD
+
+    def whole(*shape):
+        return pl.BlockSpec(shape, lambda i, m, o, b: (0,) * len(shape))
+
+    def mine(*shape):
+        return pl.BlockSpec(shape, lambda i, m, o, b: (0,) * (len(shape) - 1) + (m[0],))
+
+    return pl.pallas_call(
+        functools.partial(own_kernel, slabs),
+        grid_spec=pltpu.PrefetchScalarGridSpec(
+            num_scalar_prefetch=3,
+            grid=(1,),
+            in_specs=[
+                pl.BlockSpec((2, short, half), lambda i, m, o, b: (m[0], 0, 0)),
+                mine(2, rows, half),
+                mine(16, half),
+                mine(16, half),
+                whole(16, wide),
+                whole(16, wide),
+                whole(2, rows, wide),
+                whole(2, rows, wide),
+                whole(half, wide),
+                mine(3, half),
+            ],
+            out_specs=[
+                whole(2, tall, wide),
+                whole(32, half),
+                whole(3, half),
+                mine(2, rows, half),
+                mine(2, short, half),
+            ],
+            scratch_shapes=[pltpu.VMEM((2, tall, 256), F32), pltpu.VMEM((2, rows, LANES), F32)],
+        ),
+        out_shape=[
+            jax.ShapeDtypeStruct((2, tall, wide), BF),
+            jax.ShapeDtypeStruct((32, half), BF),
+            jax.ShapeDtypeStruct((3, half), F32),
+            jax.ShapeDtypeStruct((2, rows, wide), BF),
+            jax.ShapeDtypeStruct((2, short, wide), BF),
+        ],
+        compiler_params=params(),
+        cost_estimate=cost(2 * 2 * tall * half * wide, 8 * 1024 * 1024, 2 * tall * half),
+        name="own_half",
+    )(meta, offsets, bins, attention, skip, up, down, down, far, prev, cot, weight, filt)
+
+
+def slope_kernel(
+    meta, offsets, bins, att, skip, up, down, filt, asked, sums, slopes, mine, shown, ext
+):
+    rows = skip.shape[1]
+    tall = rows + 2 * PAD
+    half = skip.shape[2]
+    width = ext.shape[2]
+    there = (1 - meta[0]) * half
+    row, col = grid_of(16, 32)
+    at, base = row & 7, (row >> 3) * 16
+    kept = picks((at < 4) & (col == base + at + jnp.where(at < 2, 0, 2)))
+    told = picks((at < 4) & (col == base + at + jnp.where(at < 2, 2, 4)))
+    here = pl.ds(pl.multiple_of(meta[0] * half, half), half)
+    mine[:, here] = dot(kept, asked[...]).astype(BF)
+    shown[:, here] = dot(told, asked[...]).astype(BF)
+
+    @pl.loop(0, half // width)
+    def _(part):
+        begin = pl.multiple_of(part * width, width)
+        cols = pl.ds(begin, width)
+        slab_sums(att, skip, up, down, ext, cols, True)
+        taps = taps_of(filt, cols)
+        got = []
+        for s in range(2):
+            field = ext[s]
+            before, after = around(field)
+            slopes[s, :, cols] = slope_of(taps[0] * before + taps[1] * field + taps[2] * after)
+            sums[s, :, cols] = field.astype(BF)
+            got.append(asked_rows(meta, offsets, bins, s, field, taps, tall))
+        got = jnp.concatenate(got)
+        place = pl.ds(pl.multiple_of(there + begin, width), width)
+        mine[:, place] = dot(kept, got).astype(BF)
+        shown[:, place] = dot(told, got).astype(BF)
+
+
+def other_slopes(meta, offsets, bins, shipped, skip, up, down, filt, asked):
+    seqs, rows, wide = skip.shape
+    _, packed_rows, half = shipped.shape
+    tall = rows + 2 * PAD
+
+    def whole(*shape):
+        return pl.BlockSpec(shape, lambda i, m, o, b: (0,) * len(shape))
+
+    def other(*shape):
+        return pl.BlockSpec(shape, lambda i, m, o, b: (0,) * (len(shape) - 1) + (1 - m[0],))
+
+    return pl.pallas_call(
+        slope_kernel,
+        grid_spec=pltpu.PrefetchScalarGridSpec(
+            num_scalar_prefetch=3,
+            grid=(1,),
+            in_specs=[
+                whole(2, packed_rows, half),
+                other(2, rows, half),
+                other(16, half),
+                other(16, half),
+                other(3, half),
+                whole(32, half),
+            ],
+            out_specs=[whole(2, tall, half), whole(2, tall, half), whole(16, wide), whole(16, wide)],
+            scratch_shapes=[pltpu.VMEM((2, tall, 256), F32)],
+        ),
+        out_shape=[
+            jax.ShapeDtypeStruct((2, tall, half), BF),
+            jax.ShapeDtypeStruct((2, tall, half), F32),
+            jax.ShapeDtypeStruct((16, wide), BF),
+            jax.ShapeDtypeStruct((16, wide), BF),
+        ],
+        compiler_params=params(),
+        cost_estimate=cost(2 * 2 * tall * half * 64, 4 * 1024 * 1024, 2 * tall * half),
+        name="other_slopes",
+    )(meta, offsets, bins, shipped, skip, up, down, filt, asked)
+
+
+def terms_kernel(meta, order, moved, sums, slopes, own_terms, *refs):
+    pieces, (convs, terms) = refs[:6], refs[6:]
+    half = sums.shape[2]
+    tall = sums.shape[1]
+    rows = tall - 2 * PAD
+    there = (1 - meta[0]) * half
+    terms[:, pl.ds(pl.multiple_of(meta[0] * half, half), half)] = own_terms[...]
+    for k, piece in enumerate(pieces):
+        begin = pl.multiple_of(order[k] * LANES, LANES)
+        cols = pl.ds(begin, LANES)
+        total = [0.0, 0.0, 0.0]
+        for s in range(2):
+            grad = dot_rows(moved[s], piece[...])
+            conv = (grad * slopes[s, :, cols]).astype(BF)
+            convs[s, :, cols] = conv
+            got = tap_sums(conv.astype(F32), sums[s, :, cols].astype(F32), rows)
+            total = [a + b for a, b in zip(total, got)]
+        place = pl.ds(pl.multiple_of(there + begin, LANES), LANES)
+        for k in range(3):
+            terms[k : k + 1, place] = total[k]
+
+
+def other_terms(meta, order, moved, sums, slopes, own_terms, pieces):
+    _, tall, wide = moved.shape
+    half = sums.shape[2]
+
+    def whole(*shape):
+        return pl.BlockSpec(shape, lambda i, m, o: (0,) * len(shape))
+
+    return pl.pallas_call(
+        terms_kernel,
+        grid_spec=pltpu.PrefetchScalarGridSpec(
+            num_scalar_prefetch=2,
+            grid=(1,),
+            in_specs=[
+                whole(2, tall, wide),
+                whole(2, tall, half),
+                whole(2, tall, half),
+                whole(3, half),
+            ]
+            + [whole(LANES, wide)] * 6,
+            out_specs=[whole(2, tall, half), whole(3, wide)],
+        ),
+        out_shape=[
+            jax.ShapeDtypeStruct((2, tall, half), BF),
+            jax.ShapeDtypeStruct((3, wide), F32),
+        ],
+        compiler_params=params(),
+        cost_estimate=cost(2 * 2 * tall * half * wide, 6 * 1024 * 1024),
+        name="other_terms",
+    )(meta, order, moved, sums, slopes, own_terms, *pieces)
+
+
+def out_kernel(meta, order, moved, convs, filt, mine, got, weight, *refs):
+    pieces = refs[:6]
+    target, skip_grad, att_grad, pair = refs[8:]
+    half = convs.shape[2]
+    tall = convs.shape[1]
+    rows = tall - 2 * PAD
+    there = (1 - meta[0]) * half
+    width = 2 * LANES
+
+    @pl.loop(0, half // width)
+    def _(part):
+        begin = pl.multiple_of(part * width, width)
+        cols = pl.ds(begin, width)
+        taps = taps_of(filt, cols)
+        place = pl.ds(pl.multiple_of(there + begin, width), width)
+        for s in range(2):
+            direct = moved[s, :, place].astype(F32)[PAD : PAD + rows]
+            total, pairs = grads(convs[s, :, cols].astype(F32), direct, taps, rows, pair)
+            skip_grad[s, :, cols] = total.astype(BF)
+            att_grad[s, :, cols] = pairs.astype(BF)
+
+    mine[...] = mine[...] + got[...]
+    here = pl.ds(pl.multiple_of(meta[0] * half, half), half)
+    mixed = dot(mine[:, here], weight[...])
+    for k, piece in enumerate(pieces):
+        place = pl.ds(pl.multiple_of(there + order[k] * LANES, LANES), LANES)
+        mixed = mixed + dot(mine[:, place], piece[...])
+    value = mixed + pltpu.roll(mine[...].astype(F32), 14, 0)
+    for s in range(2):
+        target[s] = value[s * 8 : s * 8 + 2].astype(BF)
+
+
+def outputs(meta, order, moved, convs, filt, mine, got, weight, pieces, skip_grad, att_grad):
+    _, tall, wide = moved.shape
+    half = convs.shape[2]
+    rows = tall - 2 * PAD
+
+    def whole(*shape):
+        return pl.BlockSpec(shape, lambda i, m, o: (0,) * len(shape))
+
+    def other(*shape):
+        return pl.BlockSpec(shape, lambda i, m, o: (0,) * (len(shape) - 1) + (1 - m[0],))
+
+    return pl.pallas_call(
+        out_kernel,
+        grid_spec=pltpu.PrefetchScalarGridSpec(
+            num_scalar_prefetch=2,
+            grid=(1,),
+            in_specs=[
+                whole(2, tall, wide),
+                whole(2, tall, half),
+                other(3, half),
+                whole(16, wide),
+                whole(16, wide),
+                whole(half, wide),
+            ]
+            + [whole(LANES, wide)] * 6
+            + [pl.BlockSpec(memory_space=pl.ANY)] * 2,
+            out_specs=[
+                whole(2, NTD, wide),
+                other(2, rows, half),
+                other(2, rows // 2, half),
+            ],
+            scratch_shapes=[pltpu.VMEM((2, rows, LANES), F32)],
+        ),
+        out_shape=[
+            jax.ShapeDtypeStruct((2, NTD, wide), BF),
+            jax.ShapeDtypeStruct((2, rows, wide), BF),
+            jax.ShapeDtypeStruct((2, rows // 2, wide), BF),
+        ],
+        input_output_aliases={14: 1, 15: 2},
+        compiler_params=params(),
+        cost_estimate=cost(2 * 16 * wide * wide, 8 * 1024 * 1024),
+        name="outputs",
+    )(meta, order, moved, convs, filt, mine, got, weight, *pieces, skip_grad, att_grad)
+
+
+def paired(part, axis, bit):
+    count = lax.axis_size(axis)
+    return lax.ppermute(part, axis, [(i, i ^ bit) for i in range(count)])
+
+
+def fast_shards(
+    attention, encoder_skip, depth_filter, point_weight, crop_offset, target_bins, cotangent
+):
+    head = lax.axis_index("head")
+    slab = lax.axis_index("seq")
+    slabs = lax.axis_size("seq")
+    meta = jnp.stack([head, slab]).astype(jnp.int32)
+    quarter = slab % 4
+    core = slab % 2
+    first = lax.dynamic_slice_in_dim(point_weight, quarter * LANES, LANES, 0)
+    first = paired(first, "head", 1)
+    up, down, far = packed(encoder_skip, attention, cotangent)
+    prev = passed_along(cotangent, "seq", 1)
+    up = passed_along(up, "seq", 1)
+    down = passed_along(down, "seq", -1)
+    far = passed_along(far, "seq", 2)
+    shipped = paired(shipment(meta, attention, up, down), "head", 1)
+    common = lax.dynamic_slice_in_dim(point_weight, (4 + core) * LANES, LANES, 0)
+    common = paired(common, "head", 1)
+    crossed = paired(first, "seq", 2)
+    pieces = [
+        first,
+        paired(first, "seq", 1),
+        crossed,
+        paired(crossed, "seq", 1),
+        common,
+        paired(common, "seq", 1),
+    ]
+    order = jnp.stack(
+        [quarter, quarter ^ 1, quarter ^ 2, quarter ^ 3, 4 + core, 5 - core]
+    ).astype(jnp.int32)
+    moved, asked, own_terms, skip_grad, att_grad = own_half(
+        meta, crop_offset, target_bins, attention, encoder_skip, up, down, far, prev, cotangent,
+        point_weight, depth_filter, slabs,
+    )
+    sums, slopes, mine, shown = other_slopes(
+        meta, crop_offset, target_bins, shipped, encoder_skip, up, down, depth_filter, asked
+    )
+    got = passed_along(shown, "seq", -1)
+    convs, terms = other_terms(meta, order, moved, sums, slopes, own_terms, pieces)
+    target_rows, skip_grad, attention_grad = outputs(
+        meta, order, moved, convs, depth_filter, mine, got, point_weight, pieces, skip_grad,
+        att_grad,
+    )
+    total = butterfly(butterfly(terms, "seq"), "head")
+    count = encoder_skip.shape[0] * lax.axis_size("head") * encoder_skip.shape[1] * slabs
+    return (target_rows, attention_grad, skip_grad, total * (1.0 / math.sqrt(count)))
+
+
+def shards(*args):
+    attention, encoder_skip, point_weight = args[0], args[1], args[3]
+    fits = (
+        lax.axis_size("head") == 2
+        and lax.axis_size("seq") % 4 == 0
+        and encoder_skip.shape[:2] == (2, 128)
+        and point_weight.shape[0] == 6 * LANES
+        and attention.shape[1] == 64
+    )
+    return fast_shards(*args) if fits else plain_shards(*args)
+
+
 def solution(mesh):
     in_specs = (
         P(None, "seq", "head"),

time: 96.5 us -> 77 us (0.80)
  Pallas kernels: 0 us -> 20.8 us
  other arithmetic: 13.5 us -> 0.73 us
  matrix products: 12.3 us -> 0 us
  waiting for transfers between devices: 21.3 us -> 14.3 us
  local copies, waits for them, and re-layouts: 17.3 us -> 10.7 us
  starting transfers between devices: 30.5 us -> 28.8 us
    pallas_call x0 -> x6, Pallas kernels: none -> 20.8 us  [the longest x1 6.65 us: own_half(): pl.pallas_call(functools.partial(own_kernel, slabs), grid_spec=pltpu.Pref...]
    all_to_all x1 -> x0, waiting for transfers between devices: 18.5 us -> none  [shards(): lax.all_to_all(attention, 'head', split_axis=0, concat_axis=2, tiled=True)]
    dot_general x2 -> x0, matrix products: 12.3 us -> none  [the longest x1 7.43 us: shards(): jnp.einsum('sjr,srd->sjd', one_hot(asked, slab_rows), block_out, preferre...]
    unnamed x26 -> x34, local copies, waits for them, and re-layouts: 0.89 us -> 9.4 us
    ppermute x6 -> x7, waiting for transfers between devices: 0.02 us -> 7.29 us  [paired(): return lax.ppermute(part, axis, [(i, i ^ bit) for i in range(count)])]
    ppermute x2 -> x5, starting transfers between devices: 3.64 us -> 10.7 us  [passed_along(): return lax.ppermute(shard, axis, pairs)]
    gather x6 -> x0, local copies, waits for them, and re-layouts: 4.96 us -> none
    ppermute x5, waiting for transfers between devices: 2.73 us -> 6.97 us  [butterfly(): lax.ppermute(total, axis, [(i, i ^ step) for i in range(count)])]
  transfers between devices with their start and end apart: 14 -> 17, of which waited for: 3 -> 5; matrix products, arithmetic and copies ran while one was open for 36% -> 0% of each run, Pallas kernels for 0% -> 22%
where the time goes in v2:
time: 77 us; the launch traced here: 76.2 us
  starting transfers between devices  28.8 us (37%)
  Pallas kernels  20.8 us (27%)
  waiting for transfers between devices  14.3 us (19%)
  local copies, waits for them, and re-layouts  10.7 us (14%)
  between operations  0.85 us (1%)
    ppermute x5, starting transfers between devices, passed_along(): return lax.ppermute(shard, axis, pairs)  10.7 us
    unnamed x34, local copies, waits for them, and re-layouts  9.4 us
    ppermute x7, starting transfers between devices, paired(): return lax.ppermute(part, axis, [(i, i ^ bit) for i in range(count)])  9.34 us
    ppermute x5, starting transfers between devices, butterfly(): lax.ppermute(total, axis, [(i, i ^ step) for i in range(count)])  8.75 us
    ppermute x7, waiting for transfers between devices, paired(): return lax.ppermute(part, axis, [(i, i ^ bit) for i in range(count)])  7.29 us
    ppermute x5, waiting for transfers between devices, butterfly(): lax.ppermute(total, axis, [(i, i ^ step) for i in range(count)])  6.97 us
    pallas_call x1, Pallas kernels, own_half(): pl.pallas_call(functools.partial(own_kernel, slabs), grid_spec=pltpu.Pref...  6.65 us
    pallas_call x1, Pallas kernels, outputs(): pl.pallas_call(out_kernel, grid_spec=pltpu.PrefetchScalarGridSpec(num_sca...  3.92 us
  transfers between devices with their start and end apart: 17, of which 5 were waited for; matrix products, arithmetic and copies ran while one was open for 0% of the time, Pallas kernels for 22%

profile of v2, /device:TPU:0, one launch (start us, length us, event | category | flops | bytes accessed | tf_op | source)
XLA Modules:
  0.0 76.2 jit_solution(7870667054268619020)
XLA Ops:
  0.7 1.3 %constant_dynamic-slice_fusion = (bf16[128,1536]{1,0:T(8,128)(2,1)S(1)}, bf16[128,1536]{1,0:T(8,128)(2,1)S(1)}) fusion(bf16[768,1536]{1,0:T(8,128)(2,1)} %weight.3, s32[]{:T(128)S(6)} %select_n.20, s32[]{:T(128)S(6)} %select_n.19), kind=kLoop, calls=%fused_computation.2 | loop fusion | bytes 1572872 | tf_op jit(solution)/shard_map/dynamic_slice | solution.py:709
  2.0 3.0 %collective-permute-start.5 = (bf16[128,1536]{1,0:T(8,128)(2,1)S(1)}, bf16[128,1536]{1,0:T(8,128)(2,1)}, u32[]{:S(2)}, u32[]{:S(2)}) collective-permute-start(bf16[128,1536]{1,0:T(8,128)(2,1)S(1)} %get-tuple-element.39), channel_id=1, source_target_pairs={{0,1},{1,0},{2,3},{3,2},{4,5},{5,4},{6,7},{7,6},{8,9},{9,8},{10,11... | collective-permute-start | bytes 1179656 | tf_op jit(solution)/shard_map/ppermute | solution.py:689
  5.0 2.3 %collective-permute-start.3 = (bf16[2,128,1536]{2,1,0:T(8,128)(2,1)}, bf16[2,128,1536]{2,1,0:T(8,128)(2,1)}, u32[]{:S(2)}, u32[]{:S(2)}) collective-permute-start(bf16[2,128,1536]{2,1,0:T(8,128)(2,1)} %cot.1), channel_id=1, source_target_pairs={{0,2},{2,4},{4,6},{6,8},{8,10},{10,12},{12,14},{14,16},{16,18},{18... | collective-permute-start | bytes 2359304 | tf_op jit(solution)/shard_map/ppermute | solution.py:30
  7.8 7.3 %collective-permute-done.5.refs_0_ = bf16[128,1536]{1,0:T(8,128)(2,1)} collective-permute-done((bf16[128,1536]{1,0:T(8,128)(2,1)S(1)}, bf16[128,1536]{1,0:T(8,128)(2,1)}, u32[]{:S(2)}, u32[]{:S(2)}) %collective-permute-start.5) | collective-permute-done | bytes 393248 | tf_op jit(solution)/shard_map/ppermute | solution.py:689
  15.1 2.0 %collective-permute-start.7 = (bf16[128,1536]{1,0:T(8,128)(2,1)}, bf16[128,1536]{1,0:T(8,128)(2,1)}, u32[]{:S(2)}, u32[]{:S(2)}) collective-permute-start(bf16[128,1536]{1,0:T(8,128)(2,1)} %collective-permute-done.5.refs_0_), channel_id=1, source_target_pairs={{0,4},{2,6},{4,0},{6,2},{8,12},{10,14},{12,8},{14,10},{16,20},{18,... | collective-permute-start | bytes 1179656 | tf_op jit(solution)/shard_map/ppermute | solution.py:689
  17.1 1.1 %copy-done.1 = bf16[2,128,1536]{2,1,0:T(8,128)(2,1)S(1)} copy-done((bf16[2,128,1536]{2,1,0:T(8,128)(2,1)S(1)}, bf16[2,128,1536]{2,1,0:T(8,128)(2,1)}, u32[]{:S(2)}) %copy-start.1) | copy-done | bytes 786456
  18.2 1.1 %copy-done.3 = bf16[2,128,1536]{2,1,0:T(8,128)(2,1)S(1)} copy-done((bf16[2,128,1536]{2,1,0:T(8,128)(2,1)S(1)}, bf16[2,128,1536]{2,1,0:T(8,128)(2,1)}, u32[]{:S(2)}) %copy-start.3) | copy-done | bytes 786456
  21.8 1.3 %collective-permute-start = (bf16[16,1536]{1,0:T(8,128)(2,1)S(1)}, bf16[16,1536]{1,0:T(8,128)(2,1)S(1)}, u32[]{:S(2)}, u32[]{:S(2)}) collective-permute-start(bf16[16,1536]{1,0:T(8,128)(2,1)S(1)} %get-tuple-element.21), channel_id=1, source_target_pairs={{0,2},{2,4},{4,6},{6,8},{8,10},{10,12},{12,14},{14,16},{16,18},{18... | collective-permute-start | bytes 147464 | tf_op jit(solution)/shard_map/ppermute | solution.py:30
  23.1 1.3 %collective-permute-start.1 = (bf16[16,1536]{1,0:T(8,128)(2,1)}, bf16[16,1536]{1,0:T(8,128)(2,1)}, u32[]{:S(2)}, u32[]{:S(2)}) collective-permute-start(bf16[16,1536]{1,0:T(8,128)(2,1)} %get-tuple-element.22), channel_id=1, source_target_pairs={{2,0},{4,2},{6,4},{8,6},{10,8},{12,10},{14,12},{16,14},{18,16},{20... | collective-permute-start | bytes 147464 | tf_op jit(solution)/shard_map/ppermute | solution.py:30
  25.0 1.8 %collective-permute-start.6 = (bf16[128,1536]{1,0:T(8,128)(2,1)}, bf16[128,1536]{1,0:T(8,128)(2,1)}, u32[]{:S(2)}, u32[]{:S(2)}) collective-permute-start(bf16[128,1536]{1,0:T(8,128)(2,1)} %collective-permute-done.5.refs_0_), channel_id=1, source_target_pairs={{0,2},{2,0},{4,6},{6,4},{8,10},{10,8},{12,14},{14,12},{16,18},{18,... | collective-permute-start | bytes 1179656 | tf_op jit(solution)/shard_map/ppermute | solution.py:689
  27.4 4.5 %collective-permute-start.2 = (bf16[16,1536]{1,0:T(8,128)(2,1)}, bf16[16,1536]{1,0:T(8,128)(2,1)S(1)}, u32[]{:S(2)}, u32[]{:S(2)}) collective-permute-start(bf16[16,1536]{1,0:T(8,128)(2,1)} %copy-done.16), channel_id=1, source_target_pairs={{0,4},{2,6},{4,8},{6,10},{8,12},{10,14},{12,16},{14,18},{16,20},{1... | collective-permute-start | bytes 147464 | tf_op jit(solution)/shard_map/ppermute | solution.py:30
  32.7 2.1 %pack_attention.1 = bf16[2,80,768]{2,1,0:T(8,128)(2,1)} custom-call(s32[2]{0:T(128)S(1)} %pad_add_fusion.meta, bf16[4,64,768]{2,1,0:T(8,128)(2,1)S(1)} %copy-done.6, bf16[16,1536]{1,0:T(8,128)(2,1)S(1)} %copy-done.8, bf16[16,1536]{1,0:T(8,128)(2,1)} %collective-permute-done.1.down.down_all), custom_call_target="tpu_custom_call" | custom-call | tf_op jit(solution)/shard_map/pack_attention/pallas_call | solution.py:273
  35.5 1.5 %collective-permute-start.4 = (bf16[2,80,768]{2,1,0:T(8,128)(2,1)}, bf16[2,80,768]{2,1,0:T(8,128)(2,1)}, u32[]{:S(2)}, u32[]{:S(2)}) collective-permute-start(bf16[2,80,768]{2,1,0:T(8,128)(2,1)} %pack_attention.1), channel_id=1, source_target_pairs={{0,1},{1,0},{2,3},{3,2},{4,5},{5,4},{6,7},{7,6},{8,9},{9,8},{10,11... | collective-permute-start | bytes 737288 | tf_op jit(solution)/shard_map/ppermute | solution.py:689
  40.6 6.6 %own_half.1 = (bf16[2,144,1536]{2,1,0:T(8,128)(2,1)S(1)}, bf16[32,768]{1,0:T(8,128)(2,1)S(1)}, f32[3,768]{1,0:T(4,128)S(1)}, bf16[2,128,1536]{2,1,0:T(8,128)(2,1)}, bf16[2,64,1536]{2,1,0:T(8,128)(2,1)}) custom-call(s32[2]{0:T(128)S(1)} %pad_add_fusion.meta, s32[2]{0:T(128)S(1)} %copy-done.15, s32[2,32]{1,0:T(2,128)S(1)} %copy-done.14, ...), custom_call_target="tpu_custom_call" | custom-call | flops 679477248 | bytes 8388608 | tf_op jit(solution)/shard_map/own_half/pallas_call | solution.py:444
  47.2 3.6 %other_slopes.1 = (bf16[2,144,768]{2,1,0:T(8,128)(2,1)S(1)}, f32[2,144,768]{2,1,0:T(8,128)S(1)}, bf16[16,1536]{1,0:T(8,128)(2,1)S(1)}, bf16[16,1536]{1,0:T(8,128)(2,1)S(1)}) custom-call(s32[2]{0:T(128)S(1)} %pad_add_fusion.meta, s32[2]{0:T(128)S(1)} %copy-done.15, s32[2,32]{1,0:T(2,128)S(1)} %copy-done.14, bf16[2,80,768]{2,1,0:T(8,128)(2,1)} %collective-permute-done.4.att, ...), custom_call_target="tpu_custom_call" | custom-call | flops 28311552 | bytes 4194304 | tf_op jit(solution)/shard_map/other_slopes/pallas_call | solution.py:529
  50.9 3.7 %other_terms.1 = (bf16[2,144,768]{2,1,0:T(8,128)(2,1)S(1)}, f32[3,1536]{1,0:T(4,128)S(1)}) custom-call(s32[2]{0:T(128)S(1)} %pad_add_fusion.meta, s32[6]{0:T(128)S(1)} %stack.39.order, bf16[2,144,1536]{2,1,0:T(8,128)(2,1)S(1)} %get-tuple-element.24.moved, bf16[2,144,768]{2,1,0:T(8,128)(2,1)S(1)} %get-tuple-element.26.sums, ...), custom_call_target="tpu_custom_call" | custom-call | flops 679477248 | bytes 6291456 | tf_op jit(solution)/shard_map/other_terms/pallas_call | solution.py:586
  54.6 3.0 %collective-permute-start.12 = (f32[3,1536]{1,0:T(4,128)S(1)}, f32[3,1536]{1,0:T(4,128)S(1)}, u32[]{:S(2)}, u32[]{:S(2)}) collective-permute-start(f32[3,1536]{1,0:T(4,128)S(1)} %get-tuple-element.37), channel_id=1, source_target_pairs={{0,2},{2,0},{4,6},{6,4},{8,10},{10,8},{12,14},{14,12},{16,18},{18,... | collective-permute-start | bytes 55304 | tf_op jit(solution)/shard_map/ppermute | solution.py:82
  59.3 1.3 %collective-permute-start.11 = (bf16[16,1536]{1,0:T(8,128)(2,1)S(1)}, bf16[16,1536]{1,0:T(8,128)(2,1)S(1)}, u32[]{:S(2)}, u32[]{:S(2)}) collective-permute-start(bf16[16,1536]{1,0:T(8,128)(2,1)S(1)} %get-tuple-element.31), channel_id=1, source_target_pairs={{2,0},{4,2},{6,4},{8,6},{10,8},{12,10},{14,12},{16,14},{18,16},{20... | collective-permute-start | bytes 147464 | tf_op jit(solution)/shard_map/ppermute | solution.py:30
  60.6 1.7 %collective-permute-done.13 = f32[3,1536]{1,0:T(4,128)S(1)} collective-permute-done((f32[3,1536]{1,0:T(4,128)S(1)}, f32[3,1536]{1,0:T(4,128)S(1)}, u32[]{:S(2)}, u32[]{:S(2)}) %collective-permute-start.13) | collective-permute-done | bytes 18464 | tf_op jit(solution)/shard_map/ppermute | solution.py:82
  62.4 1.7 %collective-permute-start.14 = (f32[3,1536]{1,0:T(4,128)S(1)}, f32[3,1536]{1,0:T(4,128)S(1)}, u32[]{:S(2)}, u32[]{:S(2)}) collective-permute-start(f32[3,1536]{1,0:T(4,128)S(1)} %add.38), channel_id=1, source_target_pairs={{0,8},{2,10},{4,12},{6,14},{8,0},{10,2},{12,4},{14,6},{16,24},{18,... | collective-permute-start | bytes 55304 | tf_op jit(solution)/shard_map/ppermute | solution.py:82
  64.0 2.2 %collective-permute-done.14 = f32[3,1536]{1,0:T(4,128)S(1)} collective-permute-done((f32[3,1536]{1,0:T(4,128)S(1)}, f32[3,1536]{1,0:T(4,128)S(1)}, u32[]{:S(2)}, u32[]{:S(2)}) %collective-permute-start.14) | collective-permute-done | bytes 18464 | tf_op jit(solution)/shard_map/ppermute | solution.py:82
  66.3 2.7 %collective-permute-start.15 = (f32[3,1536]{1,0:T(4,128)S(1)}, f32[3,1536]{1,0:T(4,128)S(1)}, u32[]{:S(2)}, u32[]{:S(2)}) collective-permute-start(f32[3,1536]{1,0:T(4,128)S(1)} %add.39), channel_id=1, source_target_pairs={{0,16},{2,18},{4,20},{6,22},{8,24},{10,26},{12,28},{14,30},{16,0},... | collective-permute-start | bytes 55304 | tf_op jit(solution)/shard_map/ppermute | solution.py:82
  68.9 2.1 %collective-permute-done.15 = f32[3,1536]{1,0:T(4,128)S(1)} collective-permute-done((f32[3,1536]{1,0:T(4,128)S(1)}, f32[3,1536]{1,0:T(4,128)S(1)}, u32[]{:S(2)}, u32[]{:S(2)}) %collective-permute-start.15) | collective-permute-done | bytes 18464 | tf_op jit(solution)/shard_map/ppermute | solution.py:82
  71.7 3.9 %outputs.1 = (bf16[2,2,1536]{2,1,0:T(2,128)(2,1)}, bf16[2,128,1536]{2,1,0:T(8,128)(2,1)}, bf16[2,64,1536]{2,1,0:T(8,128)(2,1)}) custom-call(s32[2]{0:T(128)S(1)} %pad_add_fusion.meta, s32[6]{0:T(128)S(1)} %stack.39.order, bf16[2,144,1536]{2,1,0:T(8,128)(2,1)S(1)} %get-tuple-element.24.moved, ...), custom_call_target="tpu_custom_call", output_to_operand_aliasing={{1}: (14, {}), {2}: (15, {})} | custom-call | flops 75497472 | bytes 8388608 | tf_op jit(solution)/shard_map/outputs/pallas_call | solution.py:653
  (58 shorter events, 12.0 us)
Async XLA Ops:
  0.7 31.3 %copy-start.6 = (bf16[4,64,768]{2,1,0:T(8,128)(2,1)S(1)}, bf16[4,64,768]{2,1,0:T(8,128)(2,1)}, u32[]{:S(2)}) copy-start(bf16[4,64,768]{2,1,0:T(8,128)(2,1)} %att.3) | copy-start | bytes 1179652
  0.7 36.4 %copy-start.2 = (bf16[2,128,1536]{2,1,0:T(8,128)(2,1)S(1)}, bf16[2,128,1536]{2,1,0:T(8,128)(2,1)}, u32[]{:S(2)}) copy-start(bf16[2,128,1536]{2,1,0:T(8,128)(2,1)} %skip.3) | copy-start | bytes 2359300
  0.7 36.4 %copy-start.14 = (s32[2,32]{1,0:T(2,128)S(1)}, s32[2,32]{1,0:T(2,128)}, u32[]{:S(2)}) copy-start(s32[2,32]{1,0:T(2,128)} %bins.3) | copy-start | bytes 772
  0.7 36.4 %copy-start.15 = (s32[2]{0:T(128)S(1)}, s32[2]{0:T(128)}, u32[]{:S(2)}) copy-start(s32[2]{0:T(128)} %offsets.3) | copy-start | bytes 28
  2.0 35.1 %copy-start = (bf16[768,1536]{1,0:T(8,128)(2,1)S(1)}, bf16[768,1536]{1,0:T(8,128)(2,1)}, u32[]{:S(2)}) copy-start(bf16[768,1536]{1,0:T(8,128)(2,1)} %weight.3) | copy-start | bytes 7077892
  2.0 13.1 %collective-permute-start.5 = (bf16[128,1536]{1,0:T(8,128)(2,1)S(1)}, bf16[128,1536]{1,0:T(8,128)(2,1)}, u32[]{:S(2)}, u32[]{:S(2)}) collective-permute-start(bf16[128,1536]{1,0:T(8,128)(2,1)S(1)} %get-tuple-element.39), channel_id=1, source_target_pairs={{0,1},{1,0},{2,3},{3,2},{4,5},{5,4},{6,7},{7,6},{8,9},{9,8},{10,11... | collective-permute-start | bytes 1179656 | tf_op jit(solution)/shard_map/ppermute | solution.py:689
  5.0 32.1 %collective-permute-start.3 = (bf16[2,128,1536]{2,1,0:T(8,128)(2,1)}, bf16[2,128,1536]{2,1,0:T(8,128)(2,1)}, u32[]{:S(2)}, u32[]{:S(2)}) collective-permute-start(bf16[2,128,1536]{2,1,0:T(8,128)(2,1)} %cot.1), channel_id=1, source_target_pairs={{0,2},{2,4},{4,6},{6,8},{8,10},{10,12},{12,14},{14,16},{16,18},{18... | collective-permute-start | bytes 2359304 | tf_op jit(solution)/shard_map/ppermute | solution.py:30
  7.4 19.5 %collective-permute-start.9 = (bf16[128,1536]{1,0:T(8,128)(2,1)S(1)}, bf16[128,1536]{1,0:T(8,128)(2,1)}, u32[]{:S(2)}, u32[]{:S(2)}) collective-permute-start(bf16[128,1536]{1,0:T(8,128)(2,1)S(1)} %get-tuple-element.38), channel_id=1, source_target_pairs={{0,1},{1,0},{2,3},{3,2},{4,5},{5,4},{6,7},{7,6},{8,9},{9,8},{10,11... | collective-permute-start | bytes 1179656 | tf_op jit(solution)/shard_map/ppermute | solution.py:689
  15.1 11.8 %collective-permute-start.7 = (bf16[128,1536]{1,0:T(8,128)(2,1)}, bf16[128,1536]{1,0:T(8,128)(2,1)}, u32[]{:S(2)}, u32[]{:S(2)}) collective-permute-start(bf16[128,1536]{1,0:T(8,128)(2,1)} %collective-permute-done.5.refs_0_), channel_id=1, source_target_pairs={{0,4},{2,6},{4,0},{6,2},{8,12},{10,14},{12,8},{14,10},{16,20},{18,... | collective-permute-start | bytes 1179656 | tf_op jit(solution)/shard_map/ppermute | solution.py:689
  21.8 2.6 %collective-permute-start = (bf16[16,1536]{1,0:T(8,128)(2,1)S(1)}, bf16[16,1536]{1,0:T(8,128)(2,1)S(1)}, u32[]{:S(2)}, u32[]{:S(2)}) collective-permute-start(bf16[16,1536]{1,0:T(8,128)(2,1)S(1)} %get-tuple-element.21), channel_id=1, source_target_pairs={{0,2},{2,4},{4,6},{6,8},{8,10},{10,12},{12,14},{14,16},{16,18},{18... | collective-permute-start | bytes 147464 | tf_op jit(solution)/shard_map/ppermute | solution.py:30
  23.1 4.3 %collective-permute-start.1 = (bf16[16,1536]{1,0:T(8,128)(2,1)}, bf16[16,1536]{1,0:T(8,128)(2,1)}, u32[]{:S(2)}, u32[]{:S(2)}) collective-permute-start(bf16[16,1536]{1,0:T(8,128)(2,1)} %get-tuple-element.22), channel_id=1, source_target_pairs={{2,0},{4,2},{6,4},{8,6},{10,8},{12,10},{14,12},{16,14},{18,16},{20... | collective-permute-start | bytes 147464 | tf_op jit(solution)/shard_map/ppermute | solution.py:30
  25.0 25.8 %collective-permute-start.6 = (bf16[128,1536]{1,0:T(8,128)(2,1)}, bf16[128,1536]{1,0:T(8,128)(2,1)}, u32[]{:S(2)}, u32[]{:S(2)}) collective-permute-start(bf16[128,1536]{1,0:T(8,128)(2,1)} %collective-permute-done.5.refs_0_), channel_id=1, source_target_pairs={{0,2},{2,0},{4,6},{6,4},{8,10},{10,8},{12,14},{14,12},{16,18},{18,... | collective-permute-start | bytes 1179656 | tf_op jit(solution)/shard_map/ppermute | solution.py:689
  26.8 24.0 %collective-permute-start.10 = (bf16[128,1536]{1,0:T(8,128)(2,1)}, bf16[128,1536]{1,0:T(8,128)(2,1)}, u32[]{:S(2)}, u32[]{:S(2)}) collective-permute-start(bf16[128,1536]{1,0:T(8,128)(2,1)} %collective-permute-done.9.refs_4_), channel_id=1, source_target_pairs={{0,2},{2,0},{4,6},{6,4},{8,10},{10,8},{12,14},{14,12},{16,18},{18,... | collective-permute-start | bytes 1179656 | tf_op jit(solution)/shard_map/ppermute | solution.py:689
  26.8 24.0 %collective-permute-start.8 = (bf16[128,1536]{1,0:T(8,128)(2,1)}, bf16[128,1536]{1,0:T(8,128)(2,1)}, u32[]{:S(2)}, u32[]{:S(2)}) collective-permute-start(bf16[128,1536]{1,0:T(8,128)(2,1)} %collective-permute-done.7.refs_2_), channel_id=1, source_target_pairs={{0,2},{2,0},{4,6},{6,4},{8,10},{10,8},{12,14},{14,12},{16,18},{18,... | collective-permute-start | bytes 1179656 | tf_op jit(solution)/shard_map/ppermute | solution.py:689
  27.4 7.5 %collective-permute-start.2 = (bf16[16,1536]{1,0:T(8,128)(2,1)}, bf16[16,1536]{1,0:T(8,128)(2,1)S(1)}, u32[]{:S(2)}, u32[]{:S(2)}) collective-permute-start(bf16[16,1536]{1,0:T(8,128)(2,1)} %copy-done.16), channel_id=1, source_target_pairs={{0,4},{2,6},{4,8},{6,10},{8,12},{10,14},{12,16},{14,18},{16,20},{1... | collective-permute-start | bytes 147464 | tf_op jit(solution)/shard_map/ppermute | solution.py:30
  35.5 11.8 %collective-permute-start.4 = (bf16[2,80,768]{2,1,0:T(8,128)(2,1)}, bf16[2,80,768]{2,1,0:T(8,128)(2,1)}, u32[]{:S(2)}, u32[]{:S(2)}) collective-permute-start(bf16[2,80,768]{2,1,0:T(8,128)(2,1)} %pack_attention.1), channel_id=1, source_target_pairs={{0,1},{1,0},{2,3},{3,2},{4,5},{5,4},{6,7},{7,6},{8,9},{9,8},{10,11... | collective-permute-start | bytes 737288 | tf_op jit(solution)/shard_map/ppermute | solution.py:689
  37.1 1.1 %copy-start.4 = (bf16[2,128,1536]{2,1,0:T(8,128)(2,1)S(1)}, bf16[2,128,1536]{2,1,0:T(8,128)(2,1)}, u32[]{:S(2)}) copy-start(bf16[2,128,1536]{2,1,0:T(8,128)(2,1)} %cot.1) | copy-start | bytes 2359300
  50.9 20.8 %copy-start.11 = (f32[3,1536]{1,0:T(4,128)S(1)}, f32[3,1536]{1,0:T(4,128)}, u32[]{:S(2)}) copy-start(f32[3,1536]{1,0:T(4,128)} %filt.5) | copy-start | bytes 55300
  54.6 3.9 %collective-permute-start.12 = (f32[3,1536]{1,0:T(4,128)S(1)}, f32[3,1536]{1,0:T(4,128)S(1)}, u32[]{:S(2)}, u32[]{:S(2)}) collective-permute-start(f32[3,1536]{1,0:T(4,128)S(1)} %get-tuple-element.37), channel_id=1, source_target_pairs={{0,2},{2,0},{4,6},{6,4},{8,10},{10,8},{12,14},{14,12},{16,18},{18,... | collective-permute-start | bytes 55304 | tf_op jit(solution)/shard_map/ppermute | solution.py:82
  58.5 3.9 %collective-permute-start.13 = (f32[3,1536]{1,0:T(4,128)S(1)}, f32[3,1536]{1,0:T(4,128)S(1)}, u32[]{:S(2)}, u32[]{:S(2)}) collective-permute-start(f32[3,1536]{1,0:T(4,128)S(1)} %add.37), channel_id=1, source_target_pairs={{0,4},{2,6},{4,0},{6,2},{8,12},{10,14},{12,8},{14,10},{16,20},{18,... | collective-permute-start | bytes 55304 | tf_op jit(solution)/shard_map/ppermute | solution.py:82
  59.3 12.3 %collective-permute-start.11 = (bf16[16,1536]{1,0:T(8,128)(2,1)S(1)}, bf16[16,1536]{1,0:T(8,128)(2,1)S(1)}, u32[]{:S(2)}, u32[]{:S(2)}) collective-permute-start(bf16[16,1536]{1,0:T(8,128)(2,1)S(1)} %get-tuple-element.31), channel_id=1, source_target_pairs={{2,0},{4,2},{6,4},{8,6},{10,8},{12,10},{14,12},{16,14},{18,16},{20... | collective-permute-start | bytes 147464 | tf_op jit(solution)/shard_map/ppermute | solution.py:30
  62.4 3.9 %collective-permute-start.14 = (f32[3,1536]{1,0:T(4,128)S(1)}, f32[3,1536]{1,0:T(4,128)S(1)}, u32[]{:S(2)}, u32[]{:S(2)}) collective-permute-start(f32[3,1536]{1,0:T(4,128)S(1)} %add.38), channel_id=1, source_target_pairs={{0,8},{2,10},{4,12},{6,14},{8,0},{10,2},{12,4},{14,6},{16,24},{18,... | collective-permute-start | bytes 55304 | tf_op jit(solution)/shard_map/ppermute | solution.py:82
  66.3 4.8 %collective-permute-start.15 = (f32[3,1536]{1,0:T(4,128)S(1)}, f32[3,1536]{1,0:T(4,128)S(1)}, u32[]{:S(2)}, u32[]{:S(2)}) collective-permute-start(f32[3,1536]{1,0:T(4,128)S(1)} %add.39), channel_id=1, source_target_pairs={{0,16},{2,18},{4,20},{6,22},{8,24},{10,26},{12,28},{14,30},{16,0},... | collective-permute-start | bytes 55304 | tf_op jit(solution)/shard_map/ppermute | solution.py:82
  71.1 4.5 %collective-permute-start.16 = (f32[3,1536]{1,0:T(4,128)S(1)}, f32[3,1536]{1,0:T(4,128)S(1)}, u32[]{:S(2)}, u32[]{:S(2)}) collective-permute-start(f32[3,1536]{1,0:T(4,128)S(1)} %add.40), channel_id=1, source_target_pairs={{0,1},{1,0},{2,3},{3,2},{4,5},{5,4},{6,7},{7,6},{8,9},{9,8},{10,11... | collective-permute-start | bytes 55304 | tf_op jit(solution)/shard_map/ppermute | solution.py:82
  (10 other events, 8.3 us)

commit v3 on v2

--- a/solution.py
+++ b/solution.py
@@ -197,8 +197,8 @@
     return jnp.where(match, 1.0, 0.0).astype(BF)
 
 
-def params():
-    return pltpu.CompilerParams(vmem_limit_bytes=40 * 1024 * 1024)
+def params(mib=36):
+    return pltpu.CompilerParams(vmem_limit_bytes=mib * 1024 * 1024)
 
 
 def cost(flops, moved, special=0):
@@ -252,7 +252,7 @@
         ],
         out_specs=[pl.BlockSpec((16, wide), lambda i: (0, 0))] * 3,
         out_shape=[out, out, out],
-        compiler_params=params(),
+        compiler_params=params(60),
         name="pack_edges",
     )(encoder_skip, encoder_skip, attention, attention, cotangent, cotangent)
 
@@ -329,21 +329,20 @@
 
 
 def asked_rows(meta, offsets, bins, s, ext, taps, tall):
-    row, col = grid_of(16, tall)
+    row, col = grid_of(48, tall)
     want = row & 3
-    at = jnp.full((16, tall), -4096, jnp.int32)
+    shift = (row >> 4) - 1
+    at = jnp.full((48, tall), -4096, jnp.int32)
     slab = meta[1]
     for k in range(4):
         mine = k < NTD
         home = slab if mine else jnp.maximum(slab - 1, 0)
         place = bins[s, home * NTD + (k % NTD)] + offsets[s] - (0 if mine else tall - 2 * PAD)
         fits = (place >= 0) & (place < tall - 2 * PAD)
-        at = jnp.where((want == k) & (row < 8), jnp.where(fits, place + PAD, -4096), at)
-    source = ext.astype(BF)
-    before = dot(picks(col == at - 1), source)
-    here = dot(picks(col == at), source)
-    after = dot(picks(col == at + 1), source)
-    value = taps[0] * before + taps[1] * here + taps[2] * after
+        at = jnp.where(want == k, jnp.where(fits, place + PAD, -4096), at)
+    found = dot(picks((col == at + shift) & ((row & 15) < 8)), ext.astype(BF))
+    here = found[16:32]
+    value = taps[0] * found[0:16] + taps[1] * here + taps[2] * found[32:48]
     act = value * phi_of(value)
     row = lax.broadcasted_iota(jnp.int32, act.shape, 0)
     return jnp.where(row < 4, act, here).astype(BF)
@@ -389,17 +388,22 @@
         source = jnp.where(fits, at - offsets[s], -4096)
         older = picks(col == source + rows)
         newer = picks(col == source)
-        source, narrow = source[:, :16], col[:, :16]
-        below = picks((source == rows) & (narrow == s * 8 + 3))
-        above = picks((source == -rows - 1) & (narrow == s * 8 + 7))
+        edge = lax.broadcasted_iota(jnp.int32, (PAD, 512), 0)
+        top = (edge == PAD - 1) & (offsets[s] == rows)
+        bottom = (edge == 0) & (offsets[s] == 0) & jnp.logical_not(last)
         for part in range(0, wide, 512):
             cols = slice(part, part + 512)
-            moved[s, :, cols] = (
-                dot(older, prev[s, :, cols])
-                + dot(newer, cot[s, :, cols])
-                + dot(below, down_all[:, cols])
-                + dot(above, far[:, cols])
-            ).astype(BF)
+            found = dot(older, prev[s, :, cols]) + dot(newer, cot[s, :, cols])
+            above = far[:, cols].astype(F32)[s * 8 + 7 : s * 8 + 8]
+            below = down_all[:, cols].astype(F32)[s * 8 + 3 : s * 8 + 4]
+            found = jnp.concatenate(
+                [
+                    found[:PAD] + jnp.where(top, above, 0.0),
+                    found[PAD : PAD + rows],
+                    found[PAD + rows :] + jnp.where(bottom, below, 0.0),
+                ]
+            )
+            moved[s, :, cols] = found.astype(BF)
     width = ext.shape[2]
     half = skip.shape[2]
     first = meta[0] * half
@@ -549,29 +553,42 @@
             jax.ShapeDtypeStruct((16, wide), BF),
         ],
         compiler_params=params(),
-        cost_estimate=cost(2 * 2 * tall * half * 64, 4 * 1024 * 1024, 2 * tall * half),
+        cost_estimate=cost(10**11, 4 * 1024 * 1024, 2 * tall * half),
         name="other_slopes",
     )(meta, offsets, bins, shipped, skip, up, down, filt, asked)
 
 
 def terms_kernel(meta, order, moved, sums, slopes, own_terms, *refs):
-    pieces, (convs, terms) = refs[:6], refs[6:]
+    pieces, (convs, terms, full, sems) = refs[:8], refs[8:]
     half = sums.shape[2]
     tall = sums.shape[1]
     rows = tall - 2 * PAD
     there = (1 - meta[0]) * half
+    tile = pieces[0].shape[0]
+    copies = []
+    for k, piece in enumerate(pieces):
+        down = pl.multiple_of(order[4 + k // 4] * tile, tile)
+        over = pl.multiple_of(order[k % 4] * tile, tile)
+        copies.append(
+            pltpu.make_async_copy(
+                piece, full.at[pl.ds(down, tile), pl.ds(over, tile)], sems.at[k]
+            )
+        )
+        copies[-1].start()
     terms[:, pl.ds(pl.multiple_of(meta[0] * half, half), half)] = own_terms[...]
-    for k, piece in enumerate(pieces):
-        begin = pl.multiple_of(order[k] * LANES, LANES)
-        cols = pl.ds(begin, LANES)
+    for copy in copies:
+        copy.wait()
+    width = 2 * LANES
+    for begin in range(0, half, width):
+        cols = slice(begin, begin + width)
         total = [0.0, 0.0, 0.0]
         for s in range(2):
-            grad = dot_rows(moved[s], piece[...])
+            grad = dot_rows(moved[s], full[cols, :])
             conv = (grad * slopes[s, :, cols]).astype(BF)
             convs[s, :, cols] = conv
             got = tap_sums(conv.astype(F32), sums[s, :, cols].astype(F32), rows)
             total = [a + b for a, b in zip(total, got)]
-        place = pl.ds(pl.multiple_of(there + begin, LANES), LANES)
+        place = pl.ds(pl.multiple_of(there + begin, width), width)
         for k in range(3):
             terms[k : k + 1, place] = total[k]
 
@@ -594,8 +611,9 @@
                 whole(2, tall, half),
                 whole(3, half),
             ]
-            + [whole(LANES, wide)] * 6,
+            + [pl.BlockSpec(memory_space=pl.ANY)] * 8,
             out_specs=[whole(2, tall, half), whole(3, wide)],
+            scratch_shapes=[pltpu.VMEM((half, wide), BF), pltpu.SemaphoreType.DMA((8,))],
         ),
         out_shape=[
             jax.ShapeDtypeStruct((2, tall, half), BF),
@@ -607,86 +625,117 @@
     )(meta, order, moved, sums, slopes, own_terms, *pieces)
 
 
-def out_kernel(meta, order, moved, convs, filt, mine, got, weight, *refs):
-    pieces = refs[:6]
-    target, skip_grad, att_grad, pair = refs[8:]
+def grads_kernel(meta, moved, convs, filt, old_skip, old_att, skip_grad, att_grad, pair):
     half = convs.shape[2]
-    tall = convs.shape[1]
-    rows = tall - 2 * PAD
-    there = (1 - meta[0]) * half
+    rows = convs.shape[1] - 2 * PAD
     width = 2 * LANES
 
     @pl.loop(0, half // width)
     def _(part):
-        begin = pl.multiple_of(part * width, width)
-        cols = pl.ds(begin, width)
+        cols = pl.ds(pl.multiple_of(part * width, width), width)
         taps = taps_of(filt, cols)
-        place = pl.ds(pl.multiple_of(there + begin, width), width)
         for s in range(2):
-            direct = moved[s, :, place].astype(F32)[PAD : PAD + rows]
+            direct = moved[s, :, cols].astype(F32)[PAD : PAD + rows]
             total, pairs = grads(convs[s, :, cols].astype(F32), direct, taps, rows, pair)
             skip_grad[s, :, cols] = total.astype(BF)
             att_grad[s, :, cols] = pairs.astype(BF)
 
-    mine[...] = mine[...] + got[...]
-    here = pl.ds(pl.multiple_of(meta[0] * half, half), half)
-    mixed = dot(mine[:, here], weight[...])
-    for k, piece in enumerate(pieces):
-        place = pl.ds(pl.multiple_of(there + order[k] * LANES, LANES), LANES)
-        mixed = mixed + dot(mine[:, place], piece[...])
-    value = mixed + pltpu.roll(mine[...].astype(F32), 14, 0)
-    for s in range(2):
-        target[s] = value[s * 8 : s * 8 + 2].astype(BF)
-
-
-def outputs(meta, order, moved, convs, filt, mine, got, weight, pieces, skip_grad, att_grad):
+
+def other_grads(meta, moved, convs, filt, skip_grad, att_grad):
     _, tall, wide = moved.shape
     half = convs.shape[2]
     rows = tall - 2 * PAD
 
     def whole(*shape):
+        return pl.BlockSpec(shape, lambda i, m: (0,) * len(shape))
+
+    def other(*shape):
+        return pl.BlockSpec(shape, lambda i, m: (0,) * (len(shape) - 1) + (1 - m[0],))
+
+    return pl.pallas_call(
+        grads_kernel,
+        grid_spec=pltpu.PrefetchScalarGridSpec(
+            num_scalar_prefetch=1,
+            grid=(1,),
+            in_specs=[other(2, tall, half), whole(2, tall, half), other(3, half)]
+            + [pl.BlockSpec(memory_space=pl.ANY)] * 2,
+            out_specs=[other(2, rows, half), other(2, rows // 2, half)],
+            scratch_shapes=[pltpu.VMEM((2, rows, LANES), F32)],
+        ),
+        out_shape=[
+            jax.ShapeDtypeStruct((2, rows, wide), BF),
+            jax.ShapeDtypeStruct((2, rows // 2, wide), BF),
+        ],
+        input_output_aliases={4: 0, 5: 1},
+        compiler_params=params(),
+        cost_estimate=cost(2 * tall * half * 20, 4 * 1024 * 1024),
+        name="other_grads",
+    )(meta, moved, convs, filt, skip_grad, att_grad)
+
+
+def target_kernel(meta, order, mine, got, weight, *refs):
+    pieces, (target, total) = refs[:8], refs[8:]
+    half = weight.shape[0]
+    there = (1 - meta[0]) * half
+    tile = pieces[0].shape[0]
+    mine[...] = mine[...] + got[...]
+    here = pl.ds(pl.multiple_of(meta[0] * half, half), half)
+    total[...] = dot(mine[:, here], weight[...]) + pltpu.roll(mine[...].astype(F32), 12 + 2, 0)
+    for k, piece in enumerate(pieces):
+        place = pl.ds(pl.multiple_of(there + order[4 + k // 4] * tile, tile), tile)
+        over = pl.ds(pl.multiple_of(order[k % 4] * tile, tile), tile)
+        total[:, over] += dot(mine[:, place], piece[...])
+    for s in range(2):
+        target[s] = total[s * 8 : s * 8 + 2].astype(BF)
+
+
+def targets(meta, order, mine, got, weight, pieces):
+    half, wide = weight.shape
+    tile = pieces[0].shape[0]
+
+    def whole(*shape):
         return pl.BlockSpec(shape, lambda i, m, o: (0,) * len(shape))
 
-    def other(*shape):
-        return pl.BlockSpec(shape, lambda i, m, o: (0,) * (len(shape) - 1) + (1 - m[0],))
-
     return pl.pallas_call(
-        out_kernel,
+        target_kernel,
         grid_spec=pltpu.PrefetchScalarGridSpec(
             num_scalar_prefetch=2,
             grid=(1,),
-            in_specs=[
-                whole(2, tall, wide),
-                whole(2, tall, half),
-                other(3, half),
-                whole(16, wide),
-                whole(16, wide),
-                whole(half, wide),
-            ]
-            + [whole(LANES, wide)] * 6
-            + [pl.BlockSpec(memory_space=pl.ANY)] * 2,
-            out_specs=[
-                whole(2, NTD, wide),
-                other(2, rows, half),
-                other(2, rows // 2, half),
-            ],
-            scratch_shapes=[pltpu.VMEM((2, rows, LANES), F32)],
+            in_specs=[whole(16, wide), whole(16, wide), whole(half, wide)]
+            + [whole(tile, tile)] * 8,
+            out_specs=whole(2, NTD, wide),
+            scratch_shapes=[pltpu.VMEM((16, wide), F32)],
         ),
-        out_shape=[
-            jax.ShapeDtypeStruct((2, NTD, wide), BF),
-            jax.ShapeDtypeStruct((2, rows, wide), BF),
-            jax.ShapeDtypeStruct((2, rows // 2, wide), BF),
-        ],
-        input_output_aliases={14: 1, 15: 2},
+        out_shape=jax.ShapeDtypeStruct((2, NTD, wide), BF),
         compiler_params=params(),
-        cost_estimate=cost(2 * 16 * wide * wide, 8 * 1024 * 1024),
-        name="outputs",
-    )(meta, order, moved, convs, filt, mine, got, weight, *pieces, skip_grad, att_grad)
+        cost_estimate=cost(2 * 16 * wide * wide, 6 * 1024 * 1024),
+        name="targets",
+    )(meta, order, mine, got, weight, *pieces)
 
 
 def paired(part, axis, bit):
     count = lax.axis_size(axis)
     return lax.ppermute(part, axis, [(i, i ^ bit) for i in range(count)])
+
+
+def after(value, *others):
+    return lax.optimization_barrier((value,) + others)[0]
+
+
+def crossed(part, seq_bit, head_bit):
+    slabs, heads = lax.axis_size("seq"), lax.axis_size("head")
+    pairs = [
+        (i * heads + j, (i ^ seq_bit) * heads + (j ^ head_bit))
+        for i in range(slabs)
+        for j in range(heads)
+    ]
+    return lax.ppermute(part, ("seq", "head"), pairs)
+
+
+def joined(total, one, two):
+    both = (one[0] ^ two[0], one[1] ^ two[1])
+    parts = [crossed(total, *bits) for bits in (one, two, both)]
+    return (total + parts[0]) + (parts[1] + parts[2])
 
 
 def fast_shards(
@@ -696,44 +745,55 @@
     slab = lax.axis_index("seq")
     slabs = lax.axis_size("seq")
     meta = jnp.stack([head, slab]).astype(jnp.int32)
-    quarter = slab % 4
     core = slab % 2
-    first = lax.dynamic_slice_in_dim(point_weight, quarter * LANES, LANES, 0)
-    first = paired(first, "head", 1)
+    block = slab // 2 % 4
+    tile = 3 * LANES
+    order = jnp.stack([block, block ^ 1, block ^ 2, block ^ 3, core, 1 - core]).astype(jnp.int32)
+
+    def tile_of(weight, which):
+        return lax.dynamic_slice(weight, (core * tile, which * tile), (tile, tile))
+
+    first = paired(tile_of(point_weight, block), "head", 1)
     up, down, far = packed(encoder_skip, attention, cotangent)
     prev = passed_along(cotangent, "seq", 1)
     up = passed_along(up, "seq", 1)
     down = passed_along(down, "seq", -1)
     far = passed_along(far, "seq", 2)
-    shipped = paired(shipment(meta, attention, up, down), "head", 1)
-    common = lax.dynamic_slice_in_dim(point_weight, (4 + core) * LANES, LANES, 0)
-    common = paired(common, "head", 1)
-    crossed = paired(first, "seq", 2)
-    pieces = [
-        first,
-        paired(first, "seq", 1),
-        crossed,
-        paired(crossed, "seq", 1),
-        common,
-        paired(common, "seq", 1),
-    ]
-    order = jnp.stack(
-        [quarter, quarter ^ 1, quarter ^ 2, quarter ^ 3, 4 + core, 5 - core]
-    ).astype(jnp.int32)
+    message = shipment(meta, attention, up, down)
+    shipped = paired(message, "head", 1)
+    first, up, down, far = lax.optimization_barrier((first, up, down, far))
+    second = paired(first, "seq", 2)
+    third = paired(first, "seq", 4)
+    last_tile = tile_of(after(point_weight, message, prev), block ^ 3)
+    fourth = paired(last_tile, "head", 1)
     moved, asked, own_terms, skip_grad, att_grad = own_half(
         meta, crop_offset, target_bins, attention, encoder_skip, up, down, far, prev, cotangent,
-        point_weight, depth_filter, slabs,
-    )
+        after(point_weight, first, message, last_tile), depth_filter, slabs,
+    )
+    pieces = [first, second, third, fourth]
+    pieces = pieces + [paired(after(piece, own_terms), "seq", 1) for piece in pieces]
     sums, slopes, mine, shown = other_slopes(
         meta, crop_offset, target_bins, shipped, encoder_skip, up, down, depth_filter, asked
     )
     got = passed_along(shown, "seq", -1)
     convs, terms = other_terms(meta, order, moved, sums, slopes, own_terms, pieces)
-    target_rows, skip_grad, attention_grad = outputs(
-        meta, order, moved, convs, depth_filter, mine, got, point_weight, pieces, skip_grad,
-        att_grad,
-    )
-    total = butterfly(butterfly(terms, "seq"), "head")
+    terms, got = lax.optimization_barrier((terms, got))
+    total = terms + crossed(terms, 1, 0)
+    total = joined(total, (2, 0), (0, 1))
+    skip_grad, attention_grad = other_grads(
+        meta, moved, convs, depth_filter, skip_grad, att_grad
+    )
+    target_rows = targets(meta, order, mine, got, point_weight, pieces)
+    total, skip_grad, attention_grad = lax.optimization_barrier(
+        (total, skip_grad, attention_grad)
+    )
+    if slabs == 16:
+        total = joined(total, (4, 0), (8, 0))
+    else:
+        step = 4
+        while step < slabs:
+            total = total + crossed(total, step, 0)
+            step *= 2
     count = encoder_skip.shape[0] * lax.axis_size("head") * encoder_skip.shape[1] * slabs
     return (target_rows, attention_grad, skip_grad, total * (1.0 / math.sqrt(count)))
 
@@ -742,7 +802,7 @@
     attention, encoder_skip, point_weight = args[0], args[1], args[3]
     fits = (
         lax.axis_size("head") == 2
-        and lax.axis_size("seq") % 4 == 0
+        and lax.axis_size("seq") in (8, 16, 32)
         and encoder_skip.shape[:2] == (2, 128)
         and point_weight.shape[0] == 6 * LANES
         and attention.shape[1] == 64

time: 77 us -> 66.4 us (0.86)
  waiting for transfers between devices: 14.3 us -> 5.11 us
  local copies, waits for them, and re-layouts: 10.7 us -> 4.42 us
  starting transfers between devices: 28.8 us -> 32.5 us
  Pallas kernels: 20.8 us -> 22.3 us
    unnamed x34 -> x16, local copies, waits for them, and re-layouts: 9.4 us -> 1.89 us
    ppermute x7 -> x9, waiting for transfers between devices: 7.29 us -> 1.54 us  [paired(): return lax.ppermute(part, axis, [(i, i ^ bit) for i in range(count)])]
    ppermute x5 -> x7, waiting for transfers between devices: 6.97 us -> 2.19 us  [crossed(): return lax.ppermute(part, ('seq', 'head'), pairs)]
    ppermute x5, starting transfers between devices: 10.7 us -> 13.6 us  [passed_along(): return lax.ppermute(shard, axis, pairs)]
    ppermute x5, waiting for transfers between devices: 0.01 us -> 1.38 us  [passed_along(): return lax.ppermute(shard, axis, pairs)]
    dynamic_slice x1 -> x2, local copies, waits for them, and re-layouts: 1.26 us -> 2.45 us  [tile_of(): return lax.dynamic_slice(weight, (core * tile, which * tile), (tile, tile))]
    pallas_call x1, Pallas kernels: 0.83 us -> 1.98 us  [packed(): pl.pallas_call(pack_kernel, grid=(1,), in_specs=[block(seqs, wide, 0), bl...]
    pallas_call x1 -> x2, Pallas kernels: 3.92 us -> 4.99 us  [the longest x1 3.15 us: targets(): pl.pallas_call(target_kernel, grid_spec=pltpu.PrefetchScalarGridSpec(num_...]
  transfers between devices with their start and end apart: 17 -> 21, of which waited for: 5 -> 4; matrix products, arithmetic and copies ran while one was open for 0% -> 4% of each run, Pallas kernels for 22% -> 34%
where the time goes in v3:
time: 66.4 us; the launch traced here: 65.8 us
  starting transfers between devices  32.5 us (49%)
  Pallas kernels  22.3 us (34%)
  waiting for transfers between devices  5.11 us (8%)
  local copies, waits for them, and re-layouts  4.42 us (7%)
  between operations  0.77 us (1%)
  other arithmetic  0.72 us (1%)
    ppermute x5, starting transfers between devices, passed_along(): return lax.ppermute(shard, axis, pairs)  13.6 us
    ppermute x9, starting transfers between devices, paired(): return lax.ppermute(part, axis, [(i, i ^ bit) for i in range(count)])  9.74 us
    ppermute x7, starting transfers between devices, crossed(): return lax.ppermute(part, ('seq', 'head'), pairs)  9.19 us
    pallas_call x1, Pallas kernels, own_half(): pl.pallas_call(functools.partial(own_kernel, slabs), grid_spec=pltpu.Pref...  5.99 us
    pallas_call x1, Pallas kernels, other_terms(): pl.pallas_call(terms_kernel, grid_spec=pltpu.PrefetchScalarGridSpec(num_s...  3.66 us
    pallas_call x1, Pallas kernels, other_slopes(): pl.pallas_call(slope_kernel, grid_spec=pltpu.PrefetchScalarGridSpec(num_s...  3.52 us
    pallas_call x1, Pallas kernels, targets(): pl.pallas_call(target_kernel, grid_spec=pltpu.PrefetchScalarGridSpec(num_...  3.15 us
    dynamic_slice x2, local copies, waits for them, and re-layouts, tile_of(): return lax.dynamic_slice(weight, (core * tile, which * tile), (tile, tile))  2.45 us
  transfers between devices with their start and end apart: 21, of which 4 were waited for; matrix products, arithmetic and copies ran while one was open for 4% of the time, Pallas kernels for 34%

profile of v3, /device:TPU:0, one launch (start us, length us, event | category | flops | bytes accessed | tf_op | source)
XLA Modules:
  0.0 65.8 jit_solution(17485750020553922775)
XLA Ops:
  0.6 3.4 %collective-permute-start.5 = (bf16[2,128,1536]{2,1,0:T(8,128)(2,1)}, bf16[2,128,1536]{2,1,0:T(8,128)(2,1)}, u32[]{:S(2)}, u32[]{:S(2)}) collective-permute-start(bf16[2,128,1536]{2,1,0:T(8,128)(2,1)} %cot.1), channel_id=1, source_target_pairs={{0,2},{2,4},{4,6},{6,8},{8,10},{10,12},{12,14},{14,16},{16,18},{18... | collective-permute-start | bytes 2359304 | tf_op jit(solution)/shard_map/ppermute | solution.py:30
  4.0 1.7 %dynamic_slice.6 = bf16[384,384]{1,0:T(8,128)(2,1)} dynamic-slice(bf16[768,1536]{1,0:T(8,128)(2,1)} %weight.2, s32[]{:T(128)S(6)} %select_n.28, s32[]{:T(128)S(6)} %select_n.29), dynamic_slice_sizes={384,384} | dynamic-slice | bytes 589828 | tf_op jit(solution)/shard_map/dynamic_slice | solution.py:754
  5.8 2.4 %collective-permute-start.3 = (bf16[384,384]{1,0:T(8,128)(2,1)}, bf16[384,384]{1,0:T(8,128)(2,1)}, u32[]{:S(2)}, u32[]{:S(2)}) collective-permute-start(bf16[384,384]{1,0:T(8,128)(2,1)} %dynamic_slice.6), channel_id=1, source_target_pairs={{0,1},{1,0},{2,3},{3,2},{4,5},{5,4},{6,7},{7,6},{8,9},{9,8},{10,11... | collective-permute-start | bytes 884744 | tf_op jit(solution)/shard_map/ppermute | solution.py:718
  8.2 2.0 %pack_edges.1 = (bf16[16,1536]{1,0:T(8,128)(2,1)}, bf16[16,1536]{1,0:T(8,128)(2,1)}, bf16[16,1536]{1,0:T(8,128)(2,1)}) custom-call(bf16[2,128,1536]{2,1,0:T(8,128)(2,1)} %skip.3, bf16[2,128,1536]{2,1,0:T(8,128)(2,1)} %skip.3, bf16[4,64,768]{2,1,0:T(8,128)(2,1)} %att.3, bf16[4,64,768]{2,1,0:T(8,128)(2,1)} %att.3, bf16[2,128,1536]{2,1,0:T(8,128)(2,1)} %cot.1, ...), custom_call_target="tpu_custom_call" | custom-call | tf_op jit(solution)/shard_map/pack_edges/pallas_call | solution.py:242
  10.2 3.2 %collective-permute-start = (bf16[16,1536]{1,0:T(8,128)(2,1)}, bf16[16,1536]{1,0:T(8,128)(2,1)}, u32[]{:S(2)}, u32[]{:S(2)}) collective-permute-start(bf16[16,1536]{1,0:T(8,128)(2,1)} %get-tuple-element.35), channel_id=1, source_target_pairs={{0,2},{2,4},{4,6},{6,8},{8,10},{10,12},{12,14},{14,16},{16,18},{18... | collective-permute-start | bytes 147464 | tf_op jit(solution)/shard_map/ppermute | solution.py:30
  13.3 1.3 %collective-permute-start.1 = (bf16[16,1536]{1,0:T(8,128)(2,1)}, bf16[16,1536]{1,0:T(8,128)(2,1)}, u32[]{:S(2)}, u32[]{:S(2)}) collective-permute-start(bf16[16,1536]{1,0:T(8,128)(2,1)} %get-tuple-element.36), channel_id=1, source_target_pairs={{2,0},{4,2},{6,4},{8,6},{10,8},{12,10},{14,12},{16,14},{18,16},{20... | collective-permute-start | bytes 147464 | tf_op jit(solution)/shard_map/ppermute | solution.py:30
  14.6 4.5 %collective-permute-start.4 = (bf16[16,1536]{1,0:T(8,128)(2,1)}, bf16[16,1536]{1,0:T(8,128)(2,1)}, u32[]{:S(2)}, u32[]{:S(2)}) collective-permute-start(bf16[16,1536]{1,0:T(8,128)(2,1)} %get-tuple-element.37), channel_id=1, source_target_pairs={{0,4},{2,6},{4,8},{6,10},{8,12},{10,14},{12,16},{14,18},{16,20},{1... | collective-permute-start | bytes 147464 | tf_op jit(solution)/shard_map/ppermute | solution.py:30
  19.1 1.4 %collective-permute-done.4.far = bf16[16,1536]{1,0:T(8,128)(2,1)} collective-permute-done((bf16[16,1536]{1,0:T(8,128)(2,1)}, bf16[16,1536]{1,0:T(8,128)(2,1)}, u32[]{:S(2)}, u32[]{:S(2)}) %collective-permute-start.4) | collective-permute-done | bytes 49184 | tf_op jit(solution)/shard_map/ppermute | solution.py:30
  20.5 4.2 %collective-permute-start.7 = (bf16[384,384]{1,0:T(8,128)(2,1)}, bf16[384,384]{1,0:T(8,128)(2,1)}, u32[]{:S(2)}, u32[]{:S(2)}) collective-permute-start(bf16[384,384]{1,0:T(8,128)(2,1)} %collective-permute-done.3.refs_0_), channel_id=1, source_target_pairs={{0,8},{2,10},{4,12},{6,14},{8,0},{10,2},{12,4},{14,6},{16,24},{18,... | collective-permute-start | bytes 884744 | tf_op jit(solution)/shard_map/ppermute | solution.py:718
  24.7 2.1 %pack_attention.1 = bf16[2,80,768]{2,1,0:T(8,128)(2,1)} custom-call(s32[2]{0:T(128)S(1)} %pad_add_fusion.meta, bf16[4,64,768]{2,1,0:T(8,128)(2,1)S(1)} %copy-done.3, bf16[16,1536]{1,0:T(8,128)(2,1)} %collective-permute-done.up, bf16[16,1536]{1,0:T(8,128)(2,1)} %collective-permute-done.1.down.down_all), custom_call_target="tpu_custom_call" | custom-call | tf_op jit(solution)/shard_map/pack_attention/pallas_call | solution.py:273
  28.4 1.2 %collective-permute-start.2 = (bf16[2,80,768]{2,1,0:T(8,128)(2,1)}, bf16[2,80,768]{2,1,0:T(8,128)(2,1)}, u32[]{:S(2)}, u32[]{:S(2)}) collective-permute-start(bf16[2,80,768]{2,1,0:T(8,128)(2,1)} %pack_attention.1), channel_id=1, source_target_pairs={{0,1},{1,0},{2,3},{3,2},{4,5},{5,4},{6,7},{7,6},{8,9},{9,8},{10,11... | collective-permute-start | bytes 737288 | tf_op jit(solution)/shard_map/ppermute | solution.py:718
  31.6 6.0 %own_half.1 = (bf16[2,144,1536]{2,1,0:T(8,128)(2,1)S(1)}, bf16[32,768]{1,0:T(8,128)(2,1)S(1)}, f32[3,768]{1,0:T(4,128)S(1)}, bf16[2,128,1536]{2,1,0:T(8,128)(2,1)}, bf16[2,64,1536]{2,1,0:T(8,128)(2,1)}) custom-call(s32[2]{0:T(128)S(1)} %pad_add_fusion.meta, s32[2]{0:T(128)S(1)} %copy-done.7, s32[2,32]{1,0:T(2,128)S(1)} %copy-done.6, ...), custom_call_target="tpu_custom_call" | custom-call | flops 679477248 | bytes 8388608 | tf_op jit(solution)/shard_map/own_half/pallas_call | solution.py:448
  38.7 1.5 %collective-permute-done.2.att = bf16[2,80,768]{2,1,0:T(8,128)(2,1)} collective-permute-done((bf16[2,80,768]{2,1,0:T(8,128)(2,1)}, bf16[2,80,768]{2,1,0:T(8,128)(2,1)}, u32[]{:S(2)}, u32[]{:S(2)}) %collective-permute-start.2) | collective-permute-done | bytes 245792 | tf_op jit(solution)/shard_map/ppermute | solution.py:718
  40.3 3.5 %other_slopes.1 = (bf16[2,144,768]{2,1,0:T(8,128)(2,1)S(1)}, f32[2,144,768]{2,1,0:T(8,128)S(1)}, bf16[16,1536]{1,0:T(8,128)(2,1)S(1)}, bf16[16,1536]{1,0:T(8,128)(2,1)S(1)}) custom-call(s32[2]{0:T(128)S(1)} %pad_add_fusion.meta, s32[2]{0:T(128)S(1)} %copy-done.7, s32[2,32]{1,0:T(2,128)S(1)} %copy-done.6, bf16[2,80,768]{2,1,0:T(8,128)(2,1)} %collective-permute-done.2.att, ...), custom_call_target="tpu_custom_call" | custom-call | flops 99999997952 | bytes 4194304 | tf_op jit(solution)/shard_map/other_slopes/pallas_call | solution.py:533
  43.8 1.3 %collective-permute-start.13 = (bf16[16,1536]{1,0:T(8,128)(2,1)S(1)}, bf16[16,1536]{1,0:T(8,128)(2,1)S(1)}, u32[]{:S(2)}, u32[]{:S(2)}) collective-permute-start(bf16[16,1536]{1,0:T(8,128)(2,1)S(1)} %get-tuple-element.55), channel_id=1, source_target_pairs={{2,0},{4,2},{6,4},{8,6},{10,8},{12,10},{14,12},{16,14},{18,16},{20... | collective-permute-start | bytes 147464 | tf_op jit(solution)/shard_map/ppermute | solution.py:30
  45.1 3.7 %other_terms.1 = (bf16[2,144,768]{2,1,0:T(8,128)(2,1)S(1)}, f32[3,1536]{1,0:T(4,128)S(1)}) custom-call(s32[2]{0:T(128)S(1)} %pad_add_fusion.meta, s32[6]{0:T(128)S(1)} %stack.39.order, bf16[2,144,1536]{2,1,0:T(8,128)(2,1)S(1)} %get-tuple-element.46.moved, bf16[2,144,768]{2,1,0:T(8,128)(2,1)S(1)} %get-tuple-element.47.sums, ...), custom_call_target="tpu_custom_call" | custom-call | flops 679477248 | bytes 6291456 | tf_op jit(solution)/shard_map/other_terms/pallas_call | solution.py:603
  48.8 1.2 %collective-permute-start.14 = (f32[3,1536]{1,0:T(4,128)S(1)}, f32[3,1536]{1,0:T(4,128)S(1)}, u32[]{:S(2)}, u32[]{:S(2)}) collective-permute-start(f32[3,1536]{1,0:T(4,128)S(1)} %get-tuple-element.57), channel_id=1, source_target_pairs={{0,2},{1,3},{2,0},{3,1},{4,6},{5,7},{6,4},{7,5},{8,10},{9,11},{10,... | collective-permute-start | bytes 55304 | tf_op jit(solution)/shard_map/ppermute | solution.py:732
  50.8 1.5 %collective-permute-start.17 = (f32[3,1536]{1,0:T(4,128)S(1)}, f32[3,1536]{1,0:T(4,128)S(1)}, u32[]{:S(2)}, u32[]{:S(2)}) collective-permute-start(f32[3,1536]{1,0:T(4,128)S(1)} %add.44), channel_id=1, source_target_pairs={{0,5},{1,4},{2,7},{3,6},{4,1},{5,0},{6,3},{7,2},{8,13},{9,12},{10,... | collective-permute-start | bytes 55304 | tf_op jit(solution)/shard_map/ppermute | solution.py:732
  52.4 1.4 %collective-permute-start.16 = (f32[3,1536]{1,0:T(4,128)S(1)}, f32[3,1536]{1,0:T(4,128)S(1)}, u32[]{:S(2)}, u32[]{:S(2)}) collective-permute-start(f32[3,1536]{1,0:T(4,128)S(1)} %add.44), channel_id=1, source_target_pairs={{0,1},{1,0},{2,3},{3,2},{4,5},{5,4},{6,7},{7,6},{8,9},{9,8},{10,11... | collective-permute-start | bytes 55304 | tf_op jit(solution)/shard_map/ppermute | solution.py:732
  54.4 1.8 %other_grads.1 = (bf16[2,128,1536]{2,1,0:T(8,128)(2,1)}, bf16[2,64,1536]{2,1,0:T(8,128)(2,1)}) custom-call(s32[2]{0:T(128)S(1)} %pad_add_fusion.meta, bf16[2,144,1536]{2,1,0:T(8,128)(2,1)S(1)} %get-tuple-element.46.moved, bf16[2,144,768]{2,1,0:T(8,128)(2,1)S(1)} %get-tuple-element.58.convs, ...), custom_call_target="tpu_custom_call", output_to_operand_aliasing={{0}: (4, {}), {1}: (5, {})} | custom-call | flops 4423680 | bytes 4194304 | tf_op jit(solution)/shard_map/other_grads/pallas_call | solution.py:655
  56.2 1.3 %collective-permute-done.15 = f32[3,1536]{1,0:T(4,128)S(1)} collective-permute-done((f32[3,1536]{1,0:T(4,128)S(1)}, f32[3,1536]{1,0:T(4,128)S(1)}, u32[]{:S(2)}, u32[]{:S(2)}) %collective-permute-start.15) | collective-permute-done | bytes 18464 | tf_op jit(solution)/shard_map/ppermute | solution.py:732
  57.6 2.5 %collective-permute-start.20 = (f32[3,1536]{1,0:T(4,128)S(1)}, f32[3,1536]{1,0:T(4,128)S(1)}, u32[]{:S(2)}, u32[]{:S(2)}) collective-permute-start(f32[3,1536]{1,0:T(4,128)S(1)} %add_add_fusion), channel_id=1, source_target_pairs={{0,24},{1,25},{2,26},{3,27},{4,28},{5,29},{6,30},{7,31},{8,16},{9,... | collective-permute-start | bytes 55304 | tf_op jit(solution)/shard_map/ppermute | solution.py:732
  60.3 1.7 %collective-permute-start.18 = (f32[3,1536]{1,0:T(4,128)S(1)}, f32[3,1536]{1,0:T(4,128)S(1)}, u32[]{:S(2)}, u32[]{:S(2)}) collective-permute-start(f32[3,1536]{1,0:T(4,128)S(1)} %add_add_fusion), channel_id=1, source_target_pairs={{0,8},{1,9},{2,10},{3,11},{4,12},{5,13},{6,14},{7,15},{8,0},{9,1},... | collective-permute-start | bytes 55304 | tf_op jit(solution)/shard_map/ppermute | solution.py:732
  62.0 3.1 %targets.1 = bf16[2,2,1536]{2,1,0:T(2,128)(2,1)} custom-call(s32[2]{0:T(128)S(1)} %pad_add_fusion.meta, s32[6]{0:T(128)S(1)} %stack.39.order, bf16[16,1536]{1,0:T(8,128)(2,1)S(1)} %get-tuple-element.45.mine, bf16[16,1536]{1,0:T(8,128)(2,1)S(1)} %collective-permute-done.13.got, bf16[768,1536]{1,0:T(8,128)(2,1)S(1)} %copy-done, ...), custom_call_target="tpu_custom_call" | custom-call | flops 75497472 | bytes 6291456 | tf_op jit(solution)/shard_map/targets/pallas_call | solution.py:699
  (48 shorter events, 7.0 us)
Async XLA Ops:
  0.6 24.1 %copy-start.3 = (bf16[4,64,768]{2,1,0:T(8,128)(2,1)S(1)}, bf16[4,64,768]{2,1,0:T(8,128)(2,1)}, u32[]{:S(2)}) copy-start(bf16[4,64,768]{2,1,0:T(8,128)(2,1)} %att.3) | copy-start | bytes 1179652
  0.6 26.2 %collective-permute-start.5 = (bf16[2,128,1536]{2,1,0:T(8,128)(2,1)}, bf16[2,128,1536]{2,1,0:T(8,128)(2,1)}, u32[]{:S(2)}, u32[]{:S(2)}) collective-permute-start(bf16[2,128,1536]{2,1,0:T(8,128)(2,1)} %cot.1), channel_id=1, source_target_pairs={{0,2},{2,4},{4,6},{6,8},{8,10},{10,12},{12,14},{14,16},{16,18},{18... | collective-permute-start | bytes 2359304 | tf_op jit(solution)/shard_map/ppermute | solution.py:30
  5.8 24.0 %copy-start.6 = (s32[2,32]{1,0:T(2,128)S(1)}, s32[2,32]{1,0:T(2,128)}, u32[]{:S(2)}) copy-start(s32[2,32]{1,0:T(2,128)} %bins.3) | copy-start | bytes 772
  5.8 24.0 %copy-start.7 = (s32[2]{0:T(128)S(1)}, s32[2]{0:T(128)}, u32[]{:S(2)}) copy-start(s32[2]{0:T(128)} %offsets.3) | copy-start | bytes 28
  5.8 14.7 %collective-permute-start.3 = (bf16[384,384]{1,0:T(8,128)(2,1)}, bf16[384,384]{1,0:T(8,128)(2,1)}, u32[]{:S(2)}, u32[]{:S(2)}) collective-permute-start(bf16[384,384]{1,0:T(8,128)(2,1)} %dynamic_slice.6), channel_id=1, source_target_pairs={{0,1},{1,0},{2,3},{3,2},{4,5},{5,4},{6,7},{7,6},{8,9},{9,8},{10,11... | collective-permute-start | bytes 884744 | tf_op jit(solution)/shard_map/ppermute | solution.py:718
  10.2 9.0 %collective-permute-start = (bf16[16,1536]{1,0:T(8,128)(2,1)}, bf16[16,1536]{1,0:T(8,128)(2,1)}, u32[]{:S(2)}, u32[]{:S(2)}) collective-permute-start(bf16[16,1536]{1,0:T(8,128)(2,1)} %get-tuple-element.35), channel_id=1, source_target_pairs={{0,2},{2,4},{4,6},{6,8},{8,10},{10,12},{12,14},{14,16},{16,18},{18... | collective-permute-start | bytes 147464 | tf_op jit(solution)/shard_map/ppermute | solution.py:30
  13.3 5.8 %collective-permute-start.1 = (bf16[16,1536]{1,0:T(8,128)(2,1)}, bf16[16,1536]{1,0:T(8,128)(2,1)}, u32[]{:S(2)}, u32[]{:S(2)}) collective-permute-start(bf16[16,1536]{1,0:T(8,128)(2,1)} %get-tuple-element.36), channel_id=1, source_target_pairs={{2,0},{4,2},{6,4},{8,6},{10,8},{12,10},{14,12},{16,14},{18,16},{20... | collective-permute-start | bytes 147464 | tf_op jit(solution)/shard_map/ppermute | solution.py:30
  14.6 5.9 %collective-permute-start.4 = (bf16[16,1536]{1,0:T(8,128)(2,1)}, bf16[16,1536]{1,0:T(8,128)(2,1)}, u32[]{:S(2)}, u32[]{:S(2)}) collective-permute-start(bf16[16,1536]{1,0:T(8,128)(2,1)} %get-tuple-element.37), channel_id=1, source_target_pairs={{0,4},{2,6},{4,8},{6,10},{8,12},{10,14},{12,16},{14,18},{16,20},{1... | collective-permute-start | bytes 147464 | tf_op jit(solution)/shard_map/ppermute | solution.py:30
  20.5 17.1 %collective-permute-start.7 = (bf16[384,384]{1,0:T(8,128)(2,1)}, bf16[384,384]{1,0:T(8,128)(2,1)}, u32[]{:S(2)}, u32[]{:S(2)}) collective-permute-start(bf16[384,384]{1,0:T(8,128)(2,1)} %collective-permute-done.3.refs_0_), channel_id=1, source_target_pairs={{0,8},{2,10},{4,12},{6,14},{8,0},{10,2},{12,4},{14,6},{16,24},{18,... | collective-permute-start | bytes 884744 | tf_op jit(solution)/shard_map/ppermute | solution.py:718
  24.7 12.9 %collective-permute-start.6 = (bf16[384,384]{1,0:T(8,128)(2,1)}, bf16[384,384]{1,0:T(8,128)(2,1)}, u32[]{:S(2)}, u32[]{:S(2)}) collective-permute-start(bf16[384,384]{1,0:T(8,128)(2,1)} %collective-permute-done.3.refs_0_), channel_id=1, source_target_pairs={{0,4},{2,6},{4,0},{6,2},{8,12},{10,14},{12,8},{14,10},{16,20},{18,... | collective-permute-start | bytes 884744 | tf_op jit(solution)/shard_map/ppermute | solution.py:718
  27.6 10.7 %collective-permute-start.8 = (bf16[384,384]{1,0:T(8,128)(2,1)}, bf16[384,384]{1,0:T(8,128)(2,1)}, u32[]{:S(2)}, u32[]{:S(2)}) collective-permute-start(bf16[384,384]{1,0:T(8,128)(2,1)} %dynamic_slice.7), channel_id=1, source_target_pairs={{0,1},{1,0},{2,3},{3,2},{4,5},{5,4},{6,7},{7,6},{8,9},{9,8},{10,11... | collective-permute-start | bytes 884744 | tf_op jit(solution)/shard_map/ppermute | solution.py:718
  28.4 11.8 %collective-permute-start.2 = (bf16[2,80,768]{2,1,0:T(8,128)(2,1)}, bf16[2,80,768]{2,1,0:T(8,128)(2,1)}, u32[]{:S(2)}, u32[]{:S(2)}) collective-permute-start(bf16[2,80,768]{2,1,0:T(8,128)(2,1)} %pack_attention.1), channel_id=1, source_target_pairs={{0,1},{1,0},{2,3},{3,2},{4,5},{5,4},{6,7},{7,6},{8,9},{9,8},{10,11... | collective-permute-start | bytes 737288 | tf_op jit(solution)/shard_map/ppermute | solution.py:718
  37.6 7.4 %collective-permute-start.9 = (bf16[384,384]{1,0:T(8,128)(2,1)}, bf16[384,384]{1,0:T(8,128)(2,1)S(1)}, u32[]{:S(2)}, u32[]{:S(2)}) collective-permute-start(bf16[384,384]{1,0:T(8,128)(2,1)} %collective-permute-done.3.refs_0_), channel_id=1, source_target_pairs={{0,2},{2,0},{4,6},{6,4},{8,10},{10,8},{12,14},{14,12},{16,18},{18,... | collective-permute-start | bytes 884744 | tf_op jit(solution)/shard_map/ppermute | solution.py:718
  37.7 7.4 %collective-permute-start.10 = (bf16[384,384]{1,0:T(8,128)(2,1)}, bf16[384,384]{1,0:T(8,128)(2,1)S(1)}, u32[]{:S(2)}, u32[]{:S(2)}) collective-permute-start(bf16[384,384]{1,0:T(8,128)(2,1)} %collective-permute-done.6.refs_1_), channel_id=1, source_target_pairs={{0,2},{2,0},{4,6},{6,4},{8,10},{10,8},{12,14},{14,12},{16,18},{18,... | collective-permute-start | bytes 884744 | tf_op jit(solution)/shard_map/ppermute | solution.py:718
  38.2 6.9 %collective-permute-start.11 = (bf16[384,384]{1,0:T(8,128)(2,1)}, bf16[384,384]{1,0:T(8,128)(2,1)S(1)}, u32[]{:S(2)}, u32[]{:S(2)}) collective-permute-start(bf16[384,384]{1,0:T(8,128)(2,1)} %collective-permute-done.7.refs_2_), channel_id=1, source_target_pairs={{0,2},{2,0},{4,6},{6,4},{8,10},{10,8},{12,14},{14,12},{16,18},{18,... | collective-permute-start | bytes 884744 | tf_op jit(solution)/shard_map/ppermute | solution.py:718
  38.3 6.8 %collective-permute-start.12 = (bf16[384,384]{1,0:T(8,128)(2,1)}, bf16[384,384]{1,0:T(8,128)(2,1)S(1)}, u32[]{:S(2)}, u32[]{:S(2)}) collective-permute-start(bf16[384,384]{1,0:T(8,128)(2,1)} %collective-permute-done.8.refs_3_), channel_id=1, source_target_pairs={{0,2},{2,0},{4,6},{6,4},{8,10},{10,8},{12,14},{14,12},{16,18},{18,... | collective-permute-start | bytes 884744 | tf_op jit(solution)/shard_map/ppermute | solution.py:718
  43.8 5.0 %collective-permute-start.13 = (bf16[16,1536]{1,0:T(8,128)(2,1)S(1)}, bf16[16,1536]{1,0:T(8,128)(2,1)S(1)}, u32[]{:S(2)}, u32[]{:S(2)}) collective-permute-start(bf16[16,1536]{1,0:T(8,128)(2,1)S(1)} %get-tuple-element.55), channel_id=1, source_target_pairs={{2,0},{4,2},{6,4},{8,6},{10,8},{12,10},{14,12},{16,14},{18,16},{20... | collective-permute-start | bytes 147464 | tf_op jit(solution)/shard_map/ppermute | solution.py:30
  48.8 2.0 %collective-permute-start.14 = (f32[3,1536]{1,0:T(4,128)S(1)}, f32[3,1536]{1,0:T(4,128)S(1)}, u32[]{:S(2)}, u32[]{:S(2)}) collective-permute-start(f32[3,1536]{1,0:T(4,128)S(1)} %get-tuple-element.57), channel_id=1, source_target_pairs={{0,2},{1,3},{2,0},{3,1},{4,6},{5,7},{6,4},{7,5},{8,10},{9,11},{10,... | collective-permute-start | bytes 55304 | tf_op jit(solution)/shard_map/ppermute | solution.py:732
  50.8 5.4 %collective-permute-start.17 = (f32[3,1536]{1,0:T(4,128)S(1)}, f32[3,1536]{1,0:T(4,128)S(1)}, u32[]{:S(2)}, u32[]{:S(2)}) collective-permute-start(f32[3,1536]{1,0:T(4,128)S(1)} %add.44), channel_id=1, source_target_pairs={{0,5},{1,4},{2,7},{3,6},{4,1},{5,0},{6,3},{7,2},{8,13},{9,12},{10,... | collective-permute-start | bytes 55304 | tf_op jit(solution)/shard_map/ppermute | solution.py:732
  52.4 3.9 %collective-permute-start.16 = (f32[3,1536]{1,0:T(4,128)S(1)}, f32[3,1536]{1,0:T(4,128)S(1)}, u32[]{:S(2)}, u32[]{:S(2)}) collective-permute-start(f32[3,1536]{1,0:T(4,128)S(1)} %add.44), channel_id=1, source_target_pairs={{0,1},{1,0},{2,3},{3,2},{4,5},{5,4},{6,7},{7,6},{8,9},{9,8},{10,11... | collective-permute-start | bytes 55304 | tf_op jit(solution)/shard_map/ppermute | solution.py:732
  53.7 3.8 %collective-permute-start.15 = (f32[3,1536]{1,0:T(4,128)S(1)}, f32[3,1536]{1,0:T(4,128)S(1)}, u32[]{:S(2)}, u32[]{:S(2)}) collective-permute-start(f32[3,1536]{1,0:T(4,128)S(1)} %add.44), channel_id=1, source_target_pairs={{0,4},{1,5},{2,6},{3,7},{4,0},{5,1},{6,2},{7,3},{8,12},{9,13},{10,... | collective-permute-start | bytes 55304 | tf_op jit(solution)/shard_map/ppermute | solution.py:732
  57.6 7.6 %collective-permute-start.20 = (f32[3,1536]{1,0:T(4,128)S(1)}, f32[3,1536]{1,0:T(4,128)S(1)}, u32[]{:S(2)}, u32[]{:S(2)}) collective-permute-start(f32[3,1536]{1,0:T(4,128)S(1)} %add_add_fusion), channel_id=1, source_target_pairs={{0,24},{1,25},{2,26},{3,27},{4,28},{5,29},{6,30},{7,31},{8,16},{9,... | collective-permute-start | bytes 55304 | tf_op jit(solution)/shard_map/ppermute | solution.py:732
  60.1 5.1 %collective-permute-start.19 = (f32[3,1536]{1,0:T(4,128)S(1)}, f32[3,1536]{1,0:T(4,128)S(1)}, u32[]{:S(2)}, u32[]{:S(2)}) collective-permute-start(f32[3,1536]{1,0:T(4,128)S(1)} %add_add_fusion), channel_id=1, source_target_pairs={{0,16},{1,17},{2,18},{3,19},{4,20},{5,21},{6,22},{7,23},{8,24},{9,... | collective-permute-start | bytes 55304 | tf_op jit(solution)/shard_map/ppermute | solution.py:732
  60.3 4.9 %collective-permute-start.18 = (f32[3,1536]{1,0:T(4,128)S(1)}, f32[3,1536]{1,0:T(4,128)S(1)}, u32[]{:S(2)}, u32[]{:S(2)}) collective-permute-start(f32[3,1536]{1,0:T(4,128)S(1)} %add_add_fusion), channel_id=1, source_target_pairs={{0,8},{1,9},{2,10},{3,11},{4,12},{5,13},{6,14},{7,15},{8,0},{9,1},... | collective-permute-start | bytes 55304 | tf_op jit(solution)/shard_map/ppermute | solution.py:732
  (5 other events, 55.6 us)

commit v4 on v3

--- a/solution.py
+++ b/solution.py
@@ -205,70 +205,85 @@
     return pl.CostEstimate(flops=flops, bytes_accessed=moved, transcendentals=special)
 
 
-def pack_kernel(skip_lo, skip_hi, att_lo, att_hi, cot_lo, cot_hi, up, down, far):
+def pack_kernel(
+    meta, skip_lo, skip_hi, att_lo, att_hi, cot_lo, cot_hi, near, distant,
+    edge_a, edge_b, far, tile_a, tile_b,
+):
     half = att_lo.shape[2]
+    tile_a[...] = near[...]
+    tile_b[...] = distant[...]
     row, col = grid_of(16, 32)
     at, base = row & 7, (row >> 3) * 16
+    even = (meta[1] & 1) == 0
+
+    def edges(body, others, edge):
+        parts = []
+        for group in range(2):
+            rows = others[2 * group : 2 * group + 2].reshape(32, half)
+            parts.append(body[:, group * half : (group + 1) * half] + dot(edge, rows))
+        return jnp.concatenate(parts, axis=1)
+
     skips = skip_hi[...].reshape(32, 2 * half)
-    out = dot(picks((at >= 6) & (col == base + at + 8)), skips)
-    edge = picks((at == 5) & (col == base + 15))
-    for group in range(2):
-        rows = att_hi[2 * group : 2 * group + 2].reshape(32, half)
-        cols = slice(group * half, (group + 1) * half)
-        up[:, cols] = (out[:, cols] + dot(edge, rows)).astype(BF)
+    up = dot(picks((at >= 6) & (col == base + at + 8)), skips)
+    up = edges(up, att_hi, picks((at == 5) & (col == base + 15)))
     skips = skip_lo[...].reshape(32, 2 * half)
     cots = cot_lo[...].reshape(32, 2 * half)
-    out = dot(picks((at < 2) & (col == base + at)), skips) + dot(
-        picks((at == 3) & (col == base)), cots
-    )
-    edge = picks((at == 2) & (col == base))
-    for group in range(2):
-        rows = att_lo[2 * group : 2 * group + 2].reshape(32, half)
-        cols = slice(group * half, (group + 1) * half)
-        down[:, cols] = (out[:, cols] + dot(edge, rows)).astype(BF)
+    down = dot(picks((at < 2) & (col == base + at)), skips)
+    down = down + dot(picks((at == 3) & (col == base)), cots)
+    down = edges(down, att_lo, picks((at == 2) & (col == base)))
+    edge_a[...] = jnp.where(even, up, down).astype(BF)
+    edge_b[...] = jnp.where(even, down, up).astype(BF)
     cots = cot_hi[...].reshape(32, 2 * half)
     far[...] = dot(picks((at == 7) & (col == base + 15)), cots).astype(BF)
 
 
-def packed(encoder_skip, attention, cotangent):
+def packed(meta, encoder_skip, attention, cotangent, weight, tile):
     seqs, rows, wide = encoder_skip.shape
     half = attention.shape[2]
     short = attention.shape[1]
 
     def block(count, width, place):
-        return pl.BlockSpec((count, 16, width), lambda i: (0, place, 0))
+        return pl.BlockSpec((count, 16, width), lambda i, m: (0, place, 0))
 
     out = jax.ShapeDtypeStruct((16, wide), BF)
+    square = jax.ShapeDtypeStruct((tile, tile), BF)
     return pl.pallas_call(
         pack_kernel,
-        grid=(1,),
-        in_specs=[
-            block(seqs, wide, 0),
-            block(seqs, wide, rows // 16 - 1),
-            block(2 * seqs, half, 0),
-            block(2 * seqs, half, short // 16 - 1),
-            block(seqs, wide, 0),
-            block(seqs, wide, rows // 16 - 1),
-        ],
-        out_specs=[pl.BlockSpec((16, wide), lambda i: (0, 0))] * 3,
-        out_shape=[out, out, out],
+        grid_spec=pltpu.PrefetchScalarGridSpec(
+            num_scalar_prefetch=1,
+            grid=(1,),
+            in_specs=[
+                block(seqs, wide, 0),
+                block(seqs, wide, rows // 16 - 1),
+                block(2 * seqs, half, 0),
+                block(2 * seqs, half, short // 16 - 1),
+                block(seqs, wide, 0),
+                block(seqs, wide, rows // 16 - 1),
+                pl.BlockSpec((tile, tile), lambda i, m: (m[1] & 1, (m[1] >> 1) & 3)),
+                pl.BlockSpec((tile, tile), lambda i, m: (m[1] & 1, 3 - ((m[1] >> 1) & 3))),
+            ],
+            out_specs=[pl.BlockSpec((16, wide), lambda i, m: (0, 0))] * 3
+            + [pl.BlockSpec((tile, tile), lambda i, m: (0, 0))] * 2,
+        ),
+        out_shape=[out, out, out, square, square],
         compiler_params=params(60),
         name="pack_edges",
-    )(encoder_skip, encoder_skip, attention, attention, cotangent, cotangent)
-
-
-def ship_kernel(meta, att, up, down, out):
+    )(
+        meta, encoder_skip, encoder_skip, attention, attention, cotangent, cotangent, weight,
+        weight,
+    )
+
+
+def ship_kernel(meta, att, edge, out):
     short = att.shape[1]
     row, col = grid_of(16, 16)
     for s in range(2):
         out[s, 0:short] = att[s]
-        edges = dot(picks((row == 0) & (col == s * 8 + 5)), up[...]) + dot(
-            picks((row == 1) & (col == s * 8 + 2)), down[...]
-        )
-        out[s, short : short + 16] = edges.astype(BF)
-
-
-def shipment(meta, attention, up, down):
+        wanted = ((row == 0) & (col == s * 8 + 5)) | ((row == 1) & (col == s * 8 + 2))
+        out[s, short : short + 16] = dot(picks(wanted), edge[...]).astype(BF)
+
+
+def shipment(meta, attention, edge):
     _, short, half = attention.shape
     return pl.pallas_call(
         ship_kernel,
@@ -278,36 +293,36 @@
             in_specs=[
                 pl.BlockSpec((2, short, half), lambda i, m: (1 - m[0], 0, 0)),
                 pl.BlockSpec((16, half), lambda i, m: (0, 1 - m[0])),
-                pl.BlockSpec((16, half), lambda i, m: (0, 1 - m[0])),
             ],
             out_specs=pl.BlockSpec((2, short + 16, half), lambda i, m: (0, 0, 0)),
         ),
         out_shape=jax.ShapeDtypeStruct((2, short + 16, half), BF),
         compiler_params=params(),
         name="pack_attention",
-    )(meta, attention, up, down)
-
-
-def slab_sums(att, skip, up, down, ext, cols, from_ship):
+    )(meta, attention, edge)
+
+
+def slab_sums(att, skip, edge, ext, cols, from_ship):
     width = cols.size
     short = 64
     row, col = grid_of(2 * short, short)
     spread = picks((row >> 1) == col)
     row, col = grid_of(16, 32 if from_ship else 16)
     at = row & 7
-    high, low = up[:, cols], down[:, cols]
+    rims = edge[:, cols]
     if from_ship:
         edges = jnp.concatenate([att[0, short : short + 16, cols], att[1, short : short + 16, cols]])
         base = (row >> 3) * 16
-        above = dot(picks((at >= 6) & (col == base)), edges)
-        below = dot(picks((at < 2) & (col == base + 1)), edges)
+        wanted = ((at >= 6) & (col == base)) | ((at < 2) & (col == base + 1))
+        from_att = dot(picks(wanted), edges)
     else:
         base = row & 8
-        above = dot(picks((at >= 6) & (col == base + 5)), high)
-        below = dot(picks((at < 2) & (col == base + 2)), low)
+        wanted = ((at >= 6) & (col == base + 5)) | ((at < 2) & (col == base + 2))
+        from_att = dot(picks(wanted), rims)
     at = lax.broadcasted_iota(jnp.int32, (16, width), 0) & 7
-    above = jnp.where(at >= 6, above + high.astype(F32), 0.0).astype(BF).astype(F32)
-    below = jnp.where(at < 2, below + low.astype(F32), 0.0).astype(BF).astype(F32)
+    rims = (from_att + rims.astype(F32)).astype(BF).astype(F32)
+    above = jnp.where(at >= 6, rims, 0.0)
+    below = jnp.where(at < 2, rims, 0.0)
     for s in range(2):
         body = dot(spread, att[s, 0:short, cols]) + skip[s, :, cols].astype(F32)
         ext[s, 0:PAD] = above[s * 8 : s * 8 + 8]
@@ -374,28 +389,34 @@
 
 
 def own_kernel(
-    slabs, meta, offsets, bins, att, skip, up, down, down_all, far, prev, cot, weight, filt,
-    moved, asked, terms, skip_grad, att_grad, ext, pair,
+    slabs, meta, offsets, bins, att, skip, edge, rims, far_a, far_b, prev_a, prev_b, cot, weight,
+    filt, moved, asked, terms, skip_grad, att_grad, ext, pair, prev, sem,
 ):
+    from_a = pltpu.make_async_copy(prev_a, prev, sem)
+    from_b = pltpu.make_async_copy(prev_b, prev, sem)
+    pl.when((meta[1] & 1) == 1)(from_a.start)
+    pl.when((meta[1] & 1) == 0)(from_b.start)
     rows = skip.shape[1]
     tall = rows + 2 * PAD
     wide = cot.shape[2]
     row, col = grid_of(tall, rows)
     last = meta[1] == slabs - 1
+    from_a.wait()
     for s in range(2):
         at = row - PAD
         fits = (at >= -1) & (at < jnp.where(last, rows, rows + 1))
         source = jnp.where(fits, at - offsets[s], -4096)
         older = picks(col == source + rows)
         newer = picks(col == source)
-        edge = lax.broadcasted_iota(jnp.int32, (PAD, 512), 0)
-        top = (edge == PAD - 1) & (offsets[s] == rows)
-        bottom = (edge == 0) & (offsets[s] == 0) & jnp.logical_not(last)
+        place = lax.broadcasted_iota(jnp.int32, (PAD, 512), 0)
+        top = (place == PAD - 1) & (offsets[s] == rows)
+        bottom = (place == 0) & (offsets[s] == 0) & jnp.logical_not(last)
         for part in range(0, wide, 512):
             cols = slice(part, part + 512)
             found = dot(older, prev[s, :, cols]) + dot(newer, cot[s, :, cols])
-            above = far[:, cols].astype(F32)[s * 8 + 7 : s * 8 + 8]
-            below = down_all[:, cols].astype(F32)[s * 8 + 3 : s * 8 + 4]
+            far = far_a[:, cols].astype(F32) + far_b[:, cols].astype(F32)
+            above = far[s * 8 + 7 : s * 8 + 8]
+            below = rims[:, cols].astype(F32)[s * 8 + 3 : s * 8 + 4]
             found = jnp.concatenate(
                 [
                     found[:PAD] + jnp.where(top, above, 0.0),
@@ -412,7 +433,7 @@
     def _(part):
         begin = pl.multiple_of(part * width, width)
         cols = pl.ds(begin, width)
-        slab_sums(att, skip, up, down, ext, cols, False)
+        slab_sums(att, skip, edge, ext, cols, False)
         taps = taps_of(filt, cols)
         piece = weight[pl.ds(begin, width), :]
         sums = [0.0, 0.0, 0.0]
@@ -434,7 +455,7 @@
             terms[k : k + 1, cols] = sums[k]
 
 
-def own_half(meta, offsets, bins, attention, skip, up, down, far, prev, cot, weight, filt, slabs):
+def own_half(meta, offsets, bins, attention, skip, edge, far, prev, cot, weight, filt, slabs):
     seqs, rows, wide = skip.shape
     _, short, half = attention.shape
     tall = rows + 2 * PAD
@@ -454,10 +475,11 @@
                 pl.BlockSpec((2, short, half), lambda i, m, o, b: (m[0], 0, 0)),
                 mine(2, rows, half),
                 mine(16, half),
-                mine(16, half),
                 whole(16, wide),
                 whole(16, wide),
-                whole(2, rows, wide),
+                whole(16, wide),
+                pl.BlockSpec(memory_space=pl.ANY),
+                pl.BlockSpec(memory_space=pl.ANY),
                 whole(2, rows, wide),
                 whole(half, wide),
                 mine(3, half),
@@ -469,7 +491,12 @@
                 mine(2, rows, half),
                 mine(2, short, half),
             ],
-            scratch_shapes=[pltpu.VMEM((2, tall, 256), F32), pltpu.VMEM((2, rows, LANES), F32)],
+            scratch_shapes=[
+                pltpu.VMEM((2, tall, 256), F32),
+                pltpu.VMEM((2, rows, LANES), F32),
+                pltpu.VMEM((2, rows, wide), BF),
+                pltpu.SemaphoreType.DMA(()),
+            ],
         ),
         out_shape=[
             jax.ShapeDtypeStruct((2, tall, wide), BF),
@@ -479,13 +506,15 @@
             jax.ShapeDtypeStruct((2, short, wide), BF),
         ],
         compiler_params=params(),
-        cost_estimate=cost(2 * 2 * tall * half * wide, 8 * 1024 * 1024, 2 * tall * half),
+        cost_estimate=cost(1, 1),
         name="own_half",
-    )(meta, offsets, bins, attention, skip, up, down, down, far, prev, cot, weight, filt)
+    )(
+        meta, offsets, bins, attention, skip, edge, edge, *far, *prev, cot, weight, filt,
+    )
 
 
 def slope_kernel(
-    meta, offsets, bins, att, skip, up, down, filt, asked, sums, slopes, mine, shown, ext
+    meta, offsets, bins, att, skip, edge, filt, asked, sums, slopes, mine, shown, ext
 ):
     rows = skip.shape[1]
     tall = rows + 2 * PAD
@@ -504,7 +533,7 @@
     def _(part):
         begin = pl.multiple_of(part * width, width)
         cols = pl.ds(begin, width)
-        slab_sums(att, skip, up, down, ext, cols, True)
+        slab_sums(att, skip, edge, ext, cols, True)
         taps = taps_of(filt, cols)
         got = []
         for s in range(2):
@@ -519,7 +548,7 @@
         shown[:, place] = dot(told, got).astype(BF)
 
 
-def other_slopes(meta, offsets, bins, shipped, skip, up, down, filt, asked):
+def other_slopes(meta, offsets, bins, shipped, skip, edge, filt, asked):
     seqs, rows, wide = skip.shape
     _, packed_rows, half = shipped.shape
     tall = rows + 2 * PAD
@@ -538,7 +567,6 @@
             in_specs=[
                 whole(2, packed_rows, half),
                 other(2, rows, half),
-                other(16, half),
                 other(16, half),
                 other(3, half),
                 whole(32, half),
@@ -555,7 +583,7 @@
         compiler_params=params(),
         cost_estimate=cost(10**11, 4 * 1024 * 1024, 2 * tall * half),
         name="other_slopes",
-    )(meta, offsets, bins, shipped, skip, up, down, filt, asked)
+    )(meta, offsets, bins, shipped, skip, edge, filt, asked)
 
 
 def terms_kernel(meta, order, moved, sums, slopes, own_terms, *refs):
@@ -673,12 +701,12 @@
     )(meta, moved, convs, filt, skip_grad, att_grad)
 
 
-def target_kernel(meta, order, mine, got, weight, *refs):
+def target_kernel(meta, order, mine, got_a, got_b, weight, *refs):
     pieces, (target, total) = refs[:8], refs[8:]
     half = weight.shape[0]
     there = (1 - meta[0]) * half
     tile = pieces[0].shape[0]
-    mine[...] = mine[...] + got[...]
+    mine[...] = mine[...] + got_a[...] + got_b[...]
     here = pl.ds(pl.multiple_of(meta[0] * half, half), half)
     total[...] = dot(mine[:, here], weight[...]) + pltpu.roll(mine[...].astype(F32), 12 + 2, 0)
     for k, piece in enumerate(pieces):
@@ -701,7 +729,7 @@
         grid_spec=pltpu.PrefetchScalarGridSpec(
             num_scalar_prefetch=2,
             grid=(1,),
-            in_specs=[whole(16, wide), whole(16, wide), whole(half, wide)]
+            in_specs=[whole(16, wide)] * 3 + [whole(half, wide)]
             + [whole(tile, tile)] * 8,
             out_specs=whole(2, NTD, wide),
             scratch_shapes=[pltpu.VMEM((16, wide), F32)],
@@ -710,12 +738,18 @@
         compiler_params=params(),
         cost_estimate=cost(2 * 16 * wide * wide, 6 * 1024 * 1024),
         name="targets",
-    )(meta, order, mine, got, weight, *pieces)
+    )(meta, order, mine, *got, weight, *pieces)
 
 
 def paired(part, axis, bit):
     count = lax.axis_size(axis)
     return lax.ppermute(part, axis, [(i, i ^ bit) for i in range(count)])
+
+
+def sent(part, by, odd):
+    count = lax.axis_size("seq")
+    pairs = [(i, i + by) for i in range(odd, count, 2) if 0 <= i + by < count]
+    return lax.ppermute(part, "seq", pairs)
 
 
 def after(value, *others):
@@ -750,34 +784,40 @@
     tile = 3 * LANES
     order = jnp.stack([block, block ^ 1, block ^ 2, block ^ 3, core, 1 - core]).astype(jnp.int32)
 
-    def tile_of(weight, which):
-        return lax.dynamic_slice(weight, (core * tile, which * tile), (tile, tile))
-
-    first = paired(tile_of(point_weight, block), "head", 1)
-    up, down, far = packed(encoder_skip, attention, cotangent)
-    prev = passed_along(cotangent, "seq", 1)
-    up = passed_along(up, "seq", 1)
-    down = passed_along(down, "seq", -1)
-    far = passed_along(far, "seq", 2)
-    message = shipment(meta, attention, up, down)
+    edge_a, edge_b, far, first, last_tile = packed(
+        meta, encoder_skip, attention, cotangent, point_weight, tile
+    )
+    prev = [sent(cotangent, 1, odd) for odd in (0, 1)]
+    first = paired(first, "head", 1)
+    edge_a = paired(edge_a, "seq", 1)
+    edge_b = lax.ppermute(
+        edge_b, "seq", [pair for i in range(1, slabs - 1, 2) for pair in ((i, i + 1), (i + 1, i))]
+    )
+    far = [
+        lax.ppermute(
+            far, "seq", [(i, i + 2) for i in range(slabs - 2) if i // 2 % 2 == odd]
+        )
+        for odd in (0, 1)
+    ]
+    edge = edge_a + edge_b
+    message = shipment(meta, attention, edge)
     shipped = paired(message, "head", 1)
-    first, up, down, far = lax.optimization_barrier((first, up, down, far))
+    first, edge, *far = lax.optimization_barrier((first, edge, *far))
     second = paired(first, "seq", 2)
     third = paired(first, "seq", 4)
-    last_tile = tile_of(after(point_weight, message, prev), block ^ 3)
     fourth = paired(last_tile, "head", 1)
     moved, asked, own_terms, skip_grad, att_grad = own_half(
-        meta, crop_offset, target_bins, attention, encoder_skip, up, down, far, prev, cotangent,
+        meta, crop_offset, target_bins, attention, encoder_skip, edge, far, prev, cotangent,
         after(point_weight, first, message, last_tile), depth_filter, slabs,
     )
     pieces = [first, second, third, fourth]
     pieces = pieces + [paired(after(piece, own_terms), "seq", 1) for piece in pieces]
     sums, slopes, mine, shown = other_slopes(
-        meta, crop_offset, target_bins, shipped, encoder_skip, up, down, depth_filter, asked
-    )
-    got = passed_along(shown, "seq", -1)
+        meta, crop_offset, target_bins, shipped, encoder_skip, edge, depth_filter, asked
+    )
+    got = [sent(shown, -1, odd) for odd in (1, 0)]
     convs, terms = other_terms(meta, order, moved, sums, slopes, own_terms, pieces)
-    terms, got = lax.optimization_barrier((terms, got))
+    terms, *got = lax.optimization_barrier((terms, *got))
     total = terms + crossed(terms, 1, 0)
     total = joined(total, (2, 0), (0, 1))
     skip_grad, attention_grad = other_grads(

time: 66.4 us -> 76.1 us (1.15)
  starting transfers between devices: 32.5 us -> 39.2 us
  waiting for transfers between devices: 5.11 us -> 6.13 us
    ppermute x9 -> x10, starting transfers between devices: 9.74 us -> 15.7 us  [paired(): return lax.ppermute(part, axis, [(i, i ^ bit) for i in range(count)])]
    unnamed x16 -> x28, local copies, waits for them, and re-layouts: 1.89 us -> 4.91 us
    dynamic_slice x2 -> x0, local copies, waits for them, and re-layouts: 2.45 us -> none  [tile_of(): return lax.dynamic_slice(weight, (core * tile, which * tile), (tile, tile))]
    ppermute x7, waiting for transfers between devices: 2.19 us -> 4.32 us  [crossed(): return lax.ppermute(part, ('seq', 'head'), pairs)]
    ppermute x7, starting transfers between devices: 9.19 us -> 11.1 us  [crossed(): return lax.ppermute(part, ('seq', 'head'), pairs)]
    pallas_call x1, Pallas kernels: 1.98 us -> 3.35 us  [packed(): pl.pallas_call(pack_kernel, grid_spec=pltpu.PrefetchScalarGridSpec(num_sc...]
    ppermute x5 -> x7, starting transfers between devices: 13.6 us -> 12.5 us  [the longest x4 6.78 us: sent(): return lax.ppermute(part, 'seq', pairs)]
    ppermute x9 -> x10, waiting for transfers between devices: 1.54 us -> 0.46 us  [paired(): return lax.ppermute(part, axis, [(i, i ^ bit) for i in range(count)])]
  transfers between devices with their start and end apart: 21 -> 24, of which waited for: 4 -> 6; matrix products, arithmetic and copies ran while one was open for 4% -> 1% of each run, Pallas kernels for 34% -> 30%
where the time goes in v4:
time: 76.1 us; the launch traced here: 75.5 us
  starting transfers between devices  39.2 us (52%)
  Pallas kernels  22.9 us (30%)
  waiting for transfers between devices  6.13 us (8%)
  local copies, waits for them, and re-layouts  5 us (7%)
  other arithmetic  1.32 us (2%)
  between operations  0.86 us (1%)
    ppermute x10, starting transfers between devices, paired(): return lax.ppermute(part, axis, [(i, i ^ bit) for i in range(count)])  15.7 us
    ppermute x7, starting transfers between devices, crossed(): return lax.ppermute(part, ('seq', 'head'), pairs)  11.1 us
    ppermute x4, starting transfers between devices, sent(): return lax.ppermute(part, 'seq', pairs)  6.78 us
    pallas_call x1, Pallas kernels, own_half(): pl.pallas_call(functools.partial(own_kernel, slabs), grid_spec=pltpu.Pref...  6.03 us
    ppermute x2, starting transfers between devices, fast_shards(): lax.ppermute(far, 'seq', [(i, i + 2) for i in range(slabs - 2) if i // 2...  5.03 us
    unnamed x28, local copies, waits for them, and re-layouts  4.91 us
    ppermute x7, waiting for transfers between devices, crossed(): return lax.ppermute(part, ('seq', 'head'), pairs)  4.32 us
    pallas_call x1, Pallas kernels, other_terms(): pl.pallas_call(terms_kernel, grid_spec=pltpu.PrefetchScalarGridSpec(num_s...  3.65 us
  transfers between devices with their start and end apart: 24, of which 6 were waited for; matrix products, arithmetic and copies ran while one was open for 1% of the time, Pallas kernels for 30%

profile of v4, /device:TPU:0, one launch (start us, length us, event | category | flops | bytes accessed | tf_op | source)
XLA Modules:
  0.0 75.5 jit_solution(1564236938991731904)
XLA Ops:
  0.6 3.3 %collective-permute-start.6 = (bf16[2,128,1536]{2,1,0:T(8,128)(2,1)}, bf16[2,128,1536]{2,1,0:T(8,128)(2,1)}, u32[]{:S(2)}, u32[]{:S(2)}) collective-permute-start(bf16[2,128,1536]{2,1,0:T(8,128)(2,1)} %cot.1), channel_id=1, source_target_pairs={{0,2},{4,6},{8,10},{12,14},{16,18},{20,22},{24,26},{28,30},{1,3},{... | collective-permute-start | bytes 2359304 | tf_op jit(solution)/shard_map/ppermute | solution.py:752
  3.9 1.6 %collective-permute-start.7 = (bf16[2,128,1536]{2,1,0:T(8,128)(2,1)}, bf16[2,128,1536]{2,1,0:T(8,128)(2,1)}, u32[]{:S(2)}, u32[]{:S(2)}) collective-permute-start(bf16[2,128,1536]{2,1,0:T(8,128)(2,1)} %cot.1), channel_id=1, source_target_pairs={{2,4},{6,8},{10,12},{14,16},{18,20},{22,24},{26,28},{3,5},{7,9},{1... | collective-permute-start | bytes 2359304 | tf_op jit(solution)/shard_map/ppermute | solution.py:752
  6.2 3.4 %pack_edges.1 = (bf16[16,1536]{1,0:T(8,128)(2,1)}, bf16[16,1536]{1,0:T(8,128)(2,1)}, bf16[16,1536]{1,0:T(8,128)(2,1)}, bf16[384,384]{1,0:T(8,128)(2,1)}, bf16[384,384]{1,0:T(8,128)(2,1)}) custom-call(s32[2]{0:T(128)} %pad_add_fusion.meta, bf16[2,128,1536]{2,1,0:T(8,128)(2,1)} %skip.3, bf16[2,128,1536]{2,1,0:T(8,128)(2,1)} %skip.3, bf16[4,64,768]{2,1,0:T(8,128)(2,1)} %att.3, ...), custom_call_target="tpu_custom_call" | custom-call | tf_op jit(solution)/shard_map/pack_edges/pallas_call | solution.py:250
  9.5 2.3 %collective-permute-start.3 = (bf16[384,384]{1,0:T(8,128)(2,1)}, bf16[384,384]{1,0:T(8,128)(2,1)}, u32[]{:S(2)}, u32[]{:S(2)}) collective-permute-start(bf16[384,384]{1,0:T(8,128)(2,1)} %get-tuple-element.39), channel_id=1, source_target_pairs={{0,1},{1,0},{2,3},{3,2},{4,5},{5,4},{6,7},{7,6},{8,9},{9,8},{10,11... | collective-permute-start | bytes 884744 | tf_op jit(solution)/shard_map/ppermute | solution.py:746
  11.9 2.6 %collective-permute-start = (bf16[16,1536]{1,0:T(8,128)(2,1)}, bf16[16,1536]{1,0:T(8,128)(2,1)S(1)}, u32[]{:S(2)}, u32[]{:S(2)}) collective-permute-start(bf16[16,1536]{1,0:T(8,128)(2,1)} %get-tuple-element.37), channel_id=1, source_target_pairs={{0,2},{2,0},{4,6},{6,4},{8,10},{10,8},{12,14},{14,12},{16,18},{18,... | collective-permute-start | bytes 147464 | tf_op jit(solution)/shard_map/ppermute | solution.py:746
  15.5 4.4 %collective-permute-start.4 = (bf16[16,1536]{1,0:T(8,128)(2,1)}, bf16[16,1536]{1,0:T(8,128)(2,1)S(1)}, u32[]{:S(2)}, u32[]{:S(2)}) collective-permute-start(bf16[16,1536]{1,0:T(8,128)(2,1)} %get-tuple-element.40), channel_id=1, source_target_pairs={{0,4},{2,6},{8,12},{10,14},{16,20},{18,22},{24,28},{26,30},{1,5},{... | collective-permute-start | bytes 147464 | tf_op jit(solution)/shard_map/ppermute | solution.py:797
  20.6 1.3 %collective-permute-done.4.far_a = bf16[16,1536]{1,0:T(8,128)(2,1)S(1)} collective-permute-done((bf16[16,1536]{1,0:T(8,128)(2,1)}, bf16[16,1536]{1,0:T(8,128)(2,1)S(1)}, u32[]{:S(2)}, u32[]{:S(2)}) %collective-permute-start.4) | collective-permute-done | bytes 49184 | tf_op jit(solution)/shard_map/ppermute | solution.py:797
  21.9 6.0 %collective-permute-start.8 = (bf16[384,384]{1,0:T(8,128)(2,1)}, bf16[384,384]{1,0:T(8,128)(2,1)}, u32[]{:S(2)}, u32[]{:S(2)}) collective-permute-start(bf16[384,384]{1,0:T(8,128)(2,1)} %collective-permute-done.3.refs_0_), channel_id=1, source_target_pairs={{0,4},{2,6},{4,0},{6,2},{8,12},{10,14},{12,8},{14,10},{16,20},{18,... | collective-permute-start | bytes 884744 | tf_op jit(solution)/shard_map/ppermute | solution.py:746
  27.9 1.7 %collective-permute-start.9 = (bf16[384,384]{1,0:T(8,128)(2,1)}, bf16[384,384]{1,0:T(8,128)(2,1)}, u32[]{:S(2)}, u32[]{:S(2)}) collective-permute-start(bf16[384,384]{1,0:T(8,128)(2,1)} %collective-permute-done.3.refs_0_), channel_id=1, source_target_pairs={{0,8},{2,10},{4,12},{6,14},{8,0},{10,2},{12,4},{14,6},{16,24},{18,... | collective-permute-start | bytes 884744 | tf_op jit(solution)/shard_map/ppermute | solution.py:746
  30.2 1.4 %pack_attention.1 = bf16[2,80,768]{2,1,0:T(8,128)(2,1)} custom-call(s32[2]{0:T(128)S(1)} %copy-done.11, bf16[4,64,768]{2,1,0:T(8,128)(2,1)S(1)} %copy-done.3, bf16[16,1536]{1,0:T(8,128)(2,1)S(1)} %add.34.edge.rims), custom_call_target="tpu_custom_call" | custom-call | tf_op jit(solution)/shard_map/pack_attention/pallas_call | solution.py:288
  32.2 1.5 %collective-permute-start.2 = (bf16[2,80,768]{2,1,0:T(8,128)(2,1)}, bf16[2,80,768]{2,1,0:T(8,128)(2,1)}, u32[]{:S(2)}, u32[]{:S(2)}) collective-permute-start(bf16[2,80,768]{2,1,0:T(8,128)(2,1)} %pack_attention.1), channel_id=1, source_target_pairs={{0,1},{1,0},{2,3},{3,2},{4,5},{5,4},{6,7},{7,6},{8,9},{9,8},{10,11... | collective-permute-start | bytes 737288 | tf_op jit(solution)/shard_map/ppermute | solution.py:746
  33.8 1.1 %copy-done.2 = bf16[2,128,1536]{2,1,0:T(8,128)(2,1)S(1)} copy-done((bf16[2,128,1536]{2,1,0:T(8,128)(2,1)S(1)}, bf16[2,128,1536]{2,1,0:T(8,128)(2,1)}, u32[]{:S(2)}) %copy-start.2) | copy-done | bytes 786456
  38.1 6.0 %own_half.1 = (bf16[2,144,1536]{2,1,0:T(8,128)(2,1)S(1)}, bf16[32,768]{1,0:T(8,128)(2,1)S(1)}, f32[3,768]{1,0:T(4,128)S(1)}, bf16[2,128,1536]{2,1,0:T(8,128)(2,1)}, bf16[2,64,1536]{2,1,0:T(8,128)(2,1)}) custom-call(s32[2]{0:T(128)S(1)} %copy-done.11, s32[2]{0:T(128)S(1)} %copy-done.13, s32[2,32]{1,0:T(2,128)S(1)} %copy-done.12, ...), custom_call_target="tpu_custom_call" | custom-call | flops 1 | bytes 1 | tf_op jit(solution)/shard_map/own_half/pallas_call | solution.py:469
  45.2 3.5 %other_slopes.1 = (bf16[2,144,768]{2,1,0:T(8,128)(2,1)S(1)}, f32[2,144,768]{2,1,0:T(8,128)S(1)}, bf16[16,1536]{1,0:T(8,128)(2,1)S(1)}, bf16[16,1536]{1,0:T(8,128)(2,1)S(1)}) custom-call(s32[2]{0:T(128)S(1)} %copy-done.11, s32[2]{0:T(128)S(1)} %copy-done.13, s32[2,32]{1,0:T(2,128)S(1)} %copy-done.12, bf16[2,80,768]{2,1,0:T(8,128)(2,1)} %collective-permute-done.2.att, ...), custom_call_target="tpu_custom_call" | custom-call | flops 99999997952 | bytes 4194304 | tf_op jit(solution)/shard_map/other_slopes/pallas_call | solution.py:562
  48.8 1.3 %collective-permute-start.15 = (bf16[16,1536]{1,0:T(8,128)(2,1)S(1)}, bf16[16,1536]{1,0:T(8,128)(2,1)S(1)}, u32[]{:S(2)}, u32[]{:S(2)}) collective-permute-start(bf16[16,1536]{1,0:T(8,128)(2,1)S(1)} %get-tuple-element.58), channel_id=1, source_target_pairs={{2,0},{6,4},{10,8},{14,12},{18,16},{22,20},{26,24},{30,28},{3,1},{... | collective-permute-start | bytes 147464 | tf_op jit(solution)/shard_map/ppermute | solution.py:752
  50.8 3.7 %other_terms.1 = (bf16[2,144,768]{2,1,0:T(8,128)(2,1)S(1)}, f32[3,1536]{1,0:T(4,128)S(1)}) custom-call(s32[2]{0:T(128)S(1)} %copy-done.11, s32[6]{0:T(128)S(1)} %stack.39.order, bf16[2,144,1536]{2,1,0:T(8,128)(2,1)S(1)} %get-tuple-element.49.moved, bf16[2,144,768]{2,1,0:T(8,128)(2,1)S(1)} %get-tuple-element.50.sums, ...), custom_call_target="tpu_custom_call" | custom-call | flops 679477248 | bytes 6291456 | tf_op jit(solution)/shard_map/other_terms/pallas_call | solution.py:631
  54.5 2.1 %collective-permute-start.17 = (f32[3,1536]{1,0:T(4,128)S(1)}, f32[3,1536]{1,0:T(4,128)S(1)}, u32[]{:S(2)}, u32[]{:S(2)}) collective-permute-start(f32[3,1536]{1,0:T(4,128)S(1)} %get-tuple-element.61), channel_id=1, source_target_pairs={{0,2},{1,3},{2,0},{3,1},{4,6},{5,7},{6,4},{7,5},{8,10},{9,11},{10,... | collective-permute-start | bytes 55304 | tf_op jit(solution)/shard_map/ppermute | solution.py:766
  57.5 2.9 %collective-permute-start.18 = (f32[3,1536]{1,0:T(4,128)S(1)}, f32[3,1536]{1,0:T(4,128)S(1)}, u32[]{:S(2)}, u32[]{:S(2)}) collective-permute-start(f32[3,1536]{1,0:T(4,128)S(1)} %add.35), channel_id=1, source_target_pairs={{0,4},{1,5},{2,6},{3,7},{4,0},{5,1},{6,2},{7,3},{8,12},{9,13},{10,... | collective-permute-start | bytes 55304 | tf_op jit(solution)/shard_map/ppermute | solution.py:766
  61.0 1.0 %collective-permute-start.20 = (f32[3,1536]{1,0:T(4,128)S(1)}, f32[3,1536]{1,0:T(4,128)S(1)}, u32[]{:S(2)}, u32[]{:S(2)}) collective-permute-start(f32[3,1536]{1,0:T(4,128)S(1)} %add.35), channel_id=1, source_target_pairs={{0,5},{1,4},{2,7},{3,6},{4,1},{5,0},{6,3},{7,2},{8,13},{9,12},{10,... | collective-permute-start | bytes 55304 | tf_op jit(solution)/shard_map/ppermute | solution.py:766
  61.9 1.8 %other_grads.1 = (bf16[2,128,1536]{2,1,0:T(8,128)(2,1)}, bf16[2,64,1536]{2,1,0:T(8,128)(2,1)}) custom-call(s32[2]{0:T(128)S(1)} %copy-done.11, bf16[2,144,1536]{2,1,0:T(8,128)(2,1)S(1)} %get-tuple-element.49.moved, bf16[2,144,768]{2,1,0:T(8,128)(2,1)S(1)} %get-tuple-element.62.convs, ...), custom_call_target="tpu_custom_call", output_to_operand_aliasing={{0}: (4, {}), {1}: (5, {})} | custom-call | flops 4423680 | bytes 4194304 | tf_op jit(solution)/shard_map/other_grads/pallas_call | solution.py:683
  64.2 1.5 %collective-permute-done.20 = f32[3,1536]{1,0:T(4,128)S(1)} collective-permute-done((f32[3,1536]{1,0:T(4,128)S(1)}, f32[3,1536]{1,0:T(4,128)S(1)}, u32[]{:S(2)}, u32[]{:S(2)}) %collective-permute-start.20) | collective-permute-done | bytes 18464 | tf_op jit(solution)/shard_map/ppermute | solution.py:766
  66.6 2.6 %collective-permute-start.22 = (f32[3,1536]{1,0:T(4,128)S(1)}, f32[3,1536]{1,0:T(4,128)S(1)}, u32[]{:S(2)}, u32[]{:S(2)}) collective-permute-start(f32[3,1536]{1,0:T(4,128)S(1)} %add_add_fusion), channel_id=1, source_target_pairs={{0,16},{1,17},{2,18},{3,19},{4,20},{5,21},{6,22},{7,23},{8,24},{9,... | collective-permute-start | bytes 55304 | tf_op jit(solution)/shard_map/ppermute | solution.py:766
  70.1 3.2 %targets.1 = bf16[2,2,1536]{2,1,0:T(2,128)(2,1)} custom-call(s32[2]{0:T(128)S(1)} %copy-done.11, s32[6]{0:T(128)S(1)} %stack.39.order, bf16[16,1536]{1,0:T(8,128)(2,1)S(1)} %get-tuple-element.48.mine, bf16[16,1536]{1,0:T(8,128)(2,1)S(1)} %collective-permute-done.15.got_a, bf16[16,1536]{1,0:T(8,128)(2,1)S(1)} %collective-permute-done.16.got_b, ...), custom_call_target="tpu_custom_call" | custom-call | flops 75497472 | bytes 6291456 | tf_op jit(solution)/shard_map/targets/pallas_call | solution.py:727
  73.3 1.6 %collective-permute-done.23 = f32[3,1536]{1,0:T(4,128)S(1)} collective-permute-done((f32[3,1536]{1,0:T(4,128)S(1)}, f32[3,1536]{1,0:T(4,128)S(1)}, u32[]{:S(2)}, u32[]{:S(2)}) %collective-permute-start.23) | collective-permute-done | bytes 18464 | tf_op jit(solution)/shard_map/ppermute | solution.py:766
  (65 shorter events, 13.0 us)
Async XLA Ops:
  0.6 31.6 %collective-permute-start.6 = (bf16[2,128,1536]{2,1,0:T(8,128)(2,1)}, bf16[2,128,1536]{2,1,0:T(8,128)(2,1)}, u32[]{:S(2)}, u32[]{:S(2)}) collective-permute-start(bf16[2,128,1536]{2,1,0:T(8,128)(2,1)} %cot.1), channel_id=1, source_target_pairs={{0,2},{4,6},{8,10},{12,14},{16,18},{20,22},{24,26},{28,30},{1,3},{... | collective-permute-start | bytes 2359304 | tf_op jit(solution)/shard_map/ppermute | solution.py:752
  3.9 29.9 %collective-permute-start.7 = (bf16[2,128,1536]{2,1,0:T(8,128)(2,1)}, bf16[2,128,1536]{2,1,0:T(8,128)(2,1)}, u32[]{:S(2)}, u32[]{:S(2)}) collective-permute-start(bf16[2,128,1536]{2,1,0:T(8,128)(2,1)} %cot.1), channel_id=1, source_target_pairs={{2,4},{6,8},{10,12},{14,16},{18,20},{22,24},{26,28},{3,5},{7,9},{1... | collective-permute-start | bytes 2359304 | tf_op jit(solution)/shard_map/ppermute | solution.py:752
  9.5 12.4 %collective-permute-start.3 = (bf16[384,384]{1,0:T(8,128)(2,1)}, bf16[384,384]{1,0:T(8,128)(2,1)}, u32[]{:S(2)}, u32[]{:S(2)}) collective-permute-start(bf16[384,384]{1,0:T(8,128)(2,1)} %get-tuple-element.39), channel_id=1, source_target_pairs={{0,1},{1,0},{2,3},{3,2},{4,5},{5,4},{6,7},{7,6},{8,9},{9,8},{10,11... | collective-permute-start | bytes 884744 | tf_op jit(solution)/shard_map/ppermute | solution.py:746
  11.9 3.7 %collective-permute-start = (bf16[16,1536]{1,0:T(8,128)(2,1)}, bf16[16,1536]{1,0:T(8,128)(2,1)S(1)}, u32[]{:S(2)}, u32[]{:S(2)}) collective-permute-start(bf16[16,1536]{1,0:T(8,128)(2,1)} %get-tuple-element.37), channel_id=1, source_target_pairs={{0,2},{2,0},{4,6},{6,4},{8,10},{10,8},{12,14},{14,12},{16,18},{18,... | collective-permute-start | bytes 147464 | tf_op jit(solution)/shard_map/ppermute | solution.py:746
  14.4 5.5 %collective-permute-start.1 = (bf16[16,1536]{1,0:T(8,128)(2,1)}, bf16[16,1536]{1,0:T(8,128)(2,1)S(1)}, u32[]{:S(2)}, u32[]{:S(2)}) collective-permute-start(bf16[16,1536]{1,0:T(8,128)(2,1)} %get-tuple-element.38), channel_id=1, source_target_pairs={{2,4},{4,2},{6,8},{8,6},{10,12},{12,10},{14,16},{16,14},{18,20},{2... | collective-permute-start | bytes 147464 | tf_op jit(solution)/shard_map/ppermute | solution.py:793
  15.5 6.4 %collective-permute-start.4 = (bf16[16,1536]{1,0:T(8,128)(2,1)}, bf16[16,1536]{1,0:T(8,128)(2,1)S(1)}, u32[]{:S(2)}, u32[]{:S(2)}) collective-permute-start(bf16[16,1536]{1,0:T(8,128)(2,1)} %get-tuple-element.40), channel_id=1, source_target_pairs={{0,4},{2,6},{8,12},{10,14},{16,20},{18,22},{24,28},{26,30},{1,5},{... | collective-permute-start | bytes 147464 | tf_op jit(solution)/shard_map/ppermute | solution.py:797
  19.9 2.0 %collective-permute-start.5 = (bf16[16,1536]{1,0:T(8,128)(2,1)}, bf16[16,1536]{1,0:T(8,128)(2,1)S(1)}, u32[]{:S(2)}, u32[]{:S(2)}) collective-permute-start(bf16[16,1536]{1,0:T(8,128)(2,1)} %get-tuple-element.40), channel_id=1, source_target_pairs={{4,8},{6,10},{12,16},{14,18},{20,24},{22,26},{5,9},{7,11},{13,17},... | collective-permute-start | bytes 147464 | tf_op jit(solution)/shard_map/ppermute | solution.py:797
  21.9 22.2 %collective-permute-start.8 = (bf16[384,384]{1,0:T(8,128)(2,1)}, bf16[384,384]{1,0:T(8,128)(2,1)}, u32[]{:S(2)}, u32[]{:S(2)}) collective-permute-start(bf16[384,384]{1,0:T(8,128)(2,1)} %collective-permute-done.3.refs_0_), channel_id=1, source_target_pairs={{0,4},{2,6},{4,0},{6,2},{8,12},{10,14},{12,8},{14,10},{16,20},{18,... | collective-permute-start | bytes 884744 | tf_op jit(solution)/shard_map/ppermute | solution.py:746
  27.9 16.3 %collective-permute-start.9 = (bf16[384,384]{1,0:T(8,128)(2,1)}, bf16[384,384]{1,0:T(8,128)(2,1)}, u32[]{:S(2)}, u32[]{:S(2)}) collective-permute-start(bf16[384,384]{1,0:T(8,128)(2,1)} %collective-permute-done.3.refs_0_), channel_id=1, source_target_pairs={{0,8},{2,10},{4,12},{6,14},{8,0},{10,2},{12,4},{14,6},{16,24},{18,... | collective-permute-start | bytes 884744 | tf_op jit(solution)/shard_map/ppermute | solution.py:746
  29.7 15.1 %collective-permute-start.10 = (bf16[384,384]{1,0:T(8,128)(2,1)}, bf16[384,384]{1,0:T(8,128)(2,1)}, u32[]{:S(2)}, u32[]{:S(2)}) collective-permute-start(bf16[384,384]{1,0:T(8,128)(2,1)} %get-tuple-element.45), channel_id=1, source_target_pairs={{0,1},{1,0},{2,3},{3,2},{4,5},{5,4},{6,7},{7,6},{8,9},{9,8},{10,11... | collective-permute-start | bytes 884744 | tf_op jit(solution)/shard_map/ppermute | solution.py:746
  32.2 13.0 %collective-permute-start.2 = (bf16[2,80,768]{2,1,0:T(8,128)(2,1)}, bf16[2,80,768]{2,1,0:T(8,128)(2,1)}, u32[]{:S(2)}, u32[]{:S(2)}) collective-permute-start(bf16[2,80,768]{2,1,0:T(8,128)(2,1)} %pack_attention.1), channel_id=1, source_target_pairs={{0,1},{1,0},{2,3},{3,2},{4,5},{5,4},{6,7},{7,6},{8,9},{9,8},{10,11... | collective-permute-start | bytes 737288 | tf_op jit(solution)/shard_map/ppermute | solution.py:746
  44.1 5.9 %collective-permute-start.12 = (bf16[384,384]{1,0:T(8,128)(2,1)}, bf16[384,384]{1,0:T(8,128)(2,1)S(1)}, u32[]{:S(2)}, u32[]{:S(2)}) collective-permute-start(bf16[384,384]{1,0:T(8,128)(2,1)} %collective-permute-done.8.refs_1_), channel_id=1, source_target_pairs={{0,2},{2,0},{4,6},{6,4},{8,10},{10,8},{12,14},{14,12},{16,18},{18,... | collective-permute-start | bytes 884744 | tf_op jit(solution)/shard_map/ppermute | solution.py:746
  44.2 6.5 %collective-permute-start.13 = (bf16[384,384]{1,0:T(8,128)(2,1)}, bf16[384,384]{1,0:T(8,128)(2,1)S(1)}, u32[]{:S(2)}, u32[]{:S(2)}) collective-permute-start(bf16[384,384]{1,0:T(8,128)(2,1)} %collective-permute-done.9.refs_2_), channel_id=1, source_target_pairs={{0,2},{2,0},{4,6},{6,4},{8,10},{10,8},{12,14},{14,12},{16,18},{18,... | collective-permute-start | bytes 884744 | tf_op jit(solution)/shard_map/ppermute | solution.py:746
  44.7 6.0 %collective-permute-start.11 = (bf16[384,384]{1,0:T(8,128)(2,1)}, bf16[384,384]{1,0:T(8,128)(2,1)S(1)}, u32[]{:S(2)}, u32[]{:S(2)}) collective-permute-start(bf16[384,384]{1,0:T(8,128)(2,1)} %collective-permute-done.3.refs_0_), channel_id=1, source_target_pairs={{0,2},{2,0},{4,6},{6,4},{8,10},{10,8},{12,14},{14,12},{16,18},{18,... | collective-permute-start | bytes 884744 | tf_op jit(solution)/shard_map/ppermute | solution.py:746
  44.8 6.0 %collective-permute-start.14 = (bf16[384,384]{1,0:T(8,128)(2,1)}, bf16[384,384]{1,0:T(8,128)(2,1)S(1)}, u32[]{:S(2)}, u32[]{:S(2)}) collective-permute-start(bf16[384,384]{1,0:T(8,128)(2,1)} %collective-permute-done.10.refs_3_), channel_id=1, source_target_pairs={{0,2},{2,0},{4,6},{6,4},{8,10},{10,8},{12,14},{14,12},{16,18},{18,... | collective-permute-start | bytes 884744 | tf_op jit(solution)/shard_map/ppermute | solution.py:746
  48.8 5.7 %collective-permute-start.15 = (bf16[16,1536]{1,0:T(8,128)(2,1)S(1)}, bf16[16,1536]{1,0:T(8,128)(2,1)S(1)}, u32[]{:S(2)}, u32[]{:S(2)}) collective-permute-start(bf16[16,1536]{1,0:T(8,128)(2,1)S(1)} %get-tuple-element.58), channel_id=1, source_target_pairs={{2,0},{6,4},{10,8},{14,12},{18,16},{22,20},{26,24},{30,28},{3,1},{... | collective-permute-start | bytes 147464 | tf_op jit(solution)/shard_map/ppermute | solution.py:752
  50.1 4.4 %collective-permute-start.16 = (bf16[16,1536]{1,0:T(8,128)(2,1)S(1)}, bf16[16,1536]{1,0:T(8,128)(2,1)S(1)}, u32[]{:S(2)}, u32[]{:S(2)}) collective-permute-start(bf16[16,1536]{1,0:T(8,128)(2,1)S(1)} %get-tuple-element.58), channel_id=1, source_target_pairs={{4,2},{8,6},{12,10},{16,14},{20,18},{24,22},{28,26},{5,3},{9,7},{1... | collective-permute-start | bytes 147464 | tf_op jit(solution)/shard_map/ppermute | solution.py:752
  54.5 3.0 %collective-permute-start.17 = (f32[3,1536]{1,0:T(4,128)S(1)}, f32[3,1536]{1,0:T(4,128)S(1)}, u32[]{:S(2)}, u32[]{:S(2)}) collective-permute-start(f32[3,1536]{1,0:T(4,128)S(1)} %get-tuple-element.61), channel_id=1, source_target_pairs={{0,2},{1,3},{2,0},{3,1},{4,6},{5,7},{6,4},{7,5},{8,10},{9,11},{10,... | collective-permute-start | bytes 55304 | tf_op jit(solution)/shard_map/ppermute | solution.py:766
  57.5 6.3 %collective-permute-start.18 = (f32[3,1536]{1,0:T(4,128)S(1)}, f32[3,1536]{1,0:T(4,128)S(1)}, u32[]{:S(2)}, u32[]{:S(2)}) collective-permute-start(f32[3,1536]{1,0:T(4,128)S(1)} %add.35), channel_id=1, source_target_pairs={{0,4},{1,5},{2,6},{3,7},{4,0},{5,1},{6,2},{7,3},{8,12},{9,13},{10,... | collective-permute-start | bytes 55304 | tf_op jit(solution)/shard_map/ppermute | solution.py:766
  60.4 3.8 %collective-permute-start.19 = (f32[3,1536]{1,0:T(4,128)S(1)}, f32[3,1536]{1,0:T(4,128)S(1)}, u32[]{:S(2)}, u32[]{:S(2)}) collective-permute-start(f32[3,1536]{1,0:T(4,128)S(1)} %add.35), channel_id=1, source_target_pairs={{0,1},{1,0},{2,3},{3,2},{4,5},{5,4},{6,7},{7,6},{8,9},{9,8},{10,11... | collective-permute-start | bytes 55304 | tf_op jit(solution)/shard_map/ppermute | solution.py:766
  61.0 4.7 %collective-permute-start.20 = (f32[3,1536]{1,0:T(4,128)S(1)}, f32[3,1536]{1,0:T(4,128)S(1)}, u32[]{:S(2)}, u32[]{:S(2)}) collective-permute-start(f32[3,1536]{1,0:T(4,128)S(1)} %add.35), channel_id=1, source_target_pairs={{0,5},{1,4},{2,7},{3,6},{4,1},{5,0},{6,3},{7,2},{8,13},{9,12},{10,... | collective-permute-start | bytes 55304 | tf_op jit(solution)/shard_map/ppermute | solution.py:766
  65.7 7.6 %collective-permute-start.21 = (f32[3,1536]{1,0:T(4,128)S(1)}, f32[3,1536]{1,0:T(4,128)S(1)}, u32[]{:S(2)}, u32[]{:S(2)}) collective-permute-start(f32[3,1536]{1,0:T(4,128)S(1)} %add_add_fusion), channel_id=1, source_target_pairs={{0,8},{1,9},{2,10},{3,11},{4,12},{5,13},{6,14},{7,15},{8,0},{9,1},... | collective-permute-start | bytes 55304 | tf_op jit(solution)/shard_map/ppermute | solution.py:766
  66.6 6.7 %collective-permute-start.22 = (f32[3,1536]{1,0:T(4,128)S(1)}, f32[3,1536]{1,0:T(4,128)S(1)}, u32[]{:S(2)}, u32[]{:S(2)}) collective-permute-start(f32[3,1536]{1,0:T(4,128)S(1)} %add_add_fusion), channel_id=1, source_target_pairs={{0,16},{1,17},{2,18},{3,19},{4,20},{5,21},{6,22},{7,23},{8,24},{9,... | collective-permute-start | bytes 55304 | tf_op jit(solution)/shard_map/ppermute | solution.py:766
  69.2 5.6 %collective-permute-start.23 = (f32[3,1536]{1,0:T(4,128)S(1)}, f32[3,1536]{1,0:T(4,128)S(1)}, u32[]{:S(2)}, u32[]{:S(2)}) collective-permute-start(f32[3,1536]{1,0:T(4,128)S(1)} %add_add_fusion), channel_id=1, source_target_pairs={{0,24},{1,25},{2,26},{3,27},{4,28},{5,29},{6,30},{7,31},{8,16},{9,... | collective-permute-start | bytes 55304 | tf_op jit(solution)/shard_map/ppermute | solution.py:766
  (14 other events, 183.8 us)

commit v5 on v4

--- a/solution.py
+++ b/solution.py
@@ -206,9 +206,10 @@
 
 
 def pack_kernel(
-    meta, skip_lo, skip_hi, att_lo, att_hi, cot_lo, cot_hi, near, distant,
-    edge_a, edge_b, far, tile_a, tile_b,
+    meta, skip_lo, skip_hi, att_lo, att_hi, cot_lo, cot_hi, near, distant, att,
+    edge_a, edge_b, far, tile_a, tile_b, att_out,
 ):
+    att_out[...] = att[...]
     half = att_lo.shape[2]
     tile_a[...] = near[...]
     tile_b[...] = distant[...]
@@ -234,7 +235,7 @@
     edge_a[...] = jnp.where(even, up, down).astype(BF)
     edge_b[...] = jnp.where(even, down, up).astype(BF)
     cots = cot_hi[...].reshape(32, 2 * half)
-    far[...] = dot(picks((at == 7) & (col == base + 15)), cots).astype(BF)
+    far[...] = dot(picks((at == 4) & (col == base + 15)), cots).astype(BF)
 
 
 def packed(meta, encoder_skip, attention, cotangent, weight, tile):
@@ -261,64 +262,31 @@
                 block(seqs, wide, rows // 16 - 1),
                 pl.BlockSpec((tile, tile), lambda i, m: (m[1] & 1, (m[1] >> 1) & 3)),
                 pl.BlockSpec((tile, tile), lambda i, m: (m[1] & 1, 3 - ((m[1] >> 1) & 3))),
+                pl.BlockSpec((2, short, half), lambda i, m: (1 - m[0], 0, 0)),
             ],
             out_specs=[pl.BlockSpec((16, wide), lambda i, m: (0, 0))] * 3
-            + [pl.BlockSpec((tile, tile), lambda i, m: (0, 0))] * 2,
+            + [pl.BlockSpec((tile, tile), lambda i, m: (0, 0))] * 2
+            + [pl.BlockSpec((2, short, half), lambda i, m: (0, 0, 0))],
         ),
-        out_shape=[out, out, out, square, square],
+        out_shape=[out, out, out, square, square, jax.ShapeDtypeStruct((2, short, half), BF)],
         compiler_params=params(60),
         name="pack_edges",
     )(
         meta, encoder_skip, encoder_skip, attention, attention, cotangent, cotangent, weight,
-        weight,
-    )
-
-
-def ship_kernel(meta, att, edge, out):
-    short = att.shape[1]
-    row, col = grid_of(16, 16)
-    for s in range(2):
-        out[s, 0:short] = att[s]
-        wanted = ((row == 0) & (col == s * 8 + 5)) | ((row == 1) & (col == s * 8 + 2))
-        out[s, short : short + 16] = dot(picks(wanted), edge[...]).astype(BF)
-
-
-def shipment(meta, attention, edge):
-    _, short, half = attention.shape
-    return pl.pallas_call(
-        ship_kernel,
-        grid_spec=pltpu.PrefetchScalarGridSpec(
-            num_scalar_prefetch=1,
-            grid=(1,),
-            in_specs=[
-                pl.BlockSpec((2, short, half), lambda i, m: (1 - m[0], 0, 0)),
-                pl.BlockSpec((16, half), lambda i, m: (0, 1 - m[0])),
-            ],
-            out_specs=pl.BlockSpec((2, short + 16, half), lambda i, m: (0, 0, 0)),
-        ),
-        out_shape=jax.ShapeDtypeStruct((2, short + 16, half), BF),
-        compiler_params=params(),
-        name="pack_attention",
-    )(meta, attention, edge)
-
-
-def slab_sums(att, skip, edge, ext, cols, from_ship):
+        weight, attention,
+    )
+
+
+def slab_sums(att, skip, edge, twin, ext, cols):
     width = cols.size
     short = 64
     row, col = grid_of(2 * short, short)
     spread = picks((row >> 1) == col)
-    row, col = grid_of(16, 32 if from_ship else 16)
-    at = row & 7
+    row, col = grid_of(16, 16)
+    at, base = row & 7, row & 8
+    wanted = ((at >= 6) & (col == base + 5)) | ((at < 2) & (col == base + 2))
+    from_att = dot(picks(wanted), twin[:, cols])
     rims = edge[:, cols]
-    if from_ship:
-        edges = jnp.concatenate([att[0, short : short + 16, cols], att[1, short : short + 16, cols]])
-        base = (row >> 3) * 16
-        wanted = ((at >= 6) & (col == base)) | ((at < 2) & (col == base + 1))
-        from_att = dot(picks(wanted), edges)
-    else:
-        base = row & 8
-        wanted = ((at >= 6) & (col == base + 5)) | ((at < 2) & (col == base + 2))
-        from_att = dot(picks(wanted), rims)
     at = lax.broadcasted_iota(jnp.int32, (16, width), 0) & 7
     rims = (from_att + rims.astype(F32)).astype(BF).astype(F32)
     above = jnp.where(at >= 6, rims, 0.0)
@@ -389,19 +357,14 @@
 
 
 def own_kernel(
-    slabs, meta, offsets, bins, att, skip, edge, rims, far_a, far_b, prev_a, prev_b, cot, weight,
-    filt, moved, asked, terms, skip_grad, att_grad, ext, pair, prev, sem,
+    slabs, meta, offsets, bins, att, skip, edge, rims, prev, cot, weight,
+    filt, moved, asked, terms, skip_grad, att_grad, ext, pair,
 ):
-    from_a = pltpu.make_async_copy(prev_a, prev, sem)
-    from_b = pltpu.make_async_copy(prev_b, prev, sem)
-    pl.when((meta[1] & 1) == 1)(from_a.start)
-    pl.when((meta[1] & 1) == 0)(from_b.start)
     rows = skip.shape[1]
     tall = rows + 2 * PAD
     wide = cot.shape[2]
     row, col = grid_of(tall, rows)
     last = meta[1] == slabs - 1
-    from_a.wait()
     for s in range(2):
         at = row - PAD
         fits = (at >= -1) & (at < jnp.where(last, rows, rows + 1))
@@ -414,9 +377,9 @@
         for part in range(0, wide, 512):
             cols = slice(part, part + 512)
             found = dot(older, prev[s, :, cols]) + dot(newer, cot[s, :, cols])
-            far = far_a[:, cols].astype(F32) + far_b[:, cols].astype(F32)
-            above = far[s * 8 + 7 : s * 8 + 8]
-            below = rims[:, cols].astype(F32)[s * 8 + 3 : s * 8 + 4]
+            ends = rims[:, cols].astype(F32)
+            above = ends[s * 8 + 4 : s * 8 + 5]
+            below = ends[s * 8 + 3 : s * 8 + 4]
             found = jnp.concatenate(
                 [
                     found[:PAD] + jnp.where(top, above, 0.0),
@@ -433,7 +396,7 @@
     def _(part):
         begin = pl.multiple_of(part * width, width)
         cols = pl.ds(begin, width)
-        slab_sums(att, skip, edge, ext, cols, False)
+        slab_sums(att, skip, edge, edge, ext, cols)
         taps = taps_of(filt, cols)
         piece = weight[pl.ds(begin, width), :]
         sums = [0.0, 0.0, 0.0]
@@ -455,7 +418,7 @@
             terms[k : k + 1, cols] = sums[k]
 
 
-def own_half(meta, offsets, bins, attention, skip, edge, far, prev, cot, weight, filt, slabs):
+def own_half(meta, offsets, bins, attention, skip, edge, prev, cot, weight, filt, slabs):
     seqs, rows, wide = skip.shape
     _, short, half = attention.shape
     tall = rows + 2 * PAD
@@ -476,10 +439,7 @@
                 mine(2, rows, half),
                 mine(16, half),
                 whole(16, wide),
-                whole(16, wide),
-                whole(16, wide),
-                pl.BlockSpec(memory_space=pl.ANY),
-                pl.BlockSpec(memory_space=pl.ANY),
+                whole(2, rows, wide),
                 whole(2, rows, wide),
                 whole(half, wide),
                 mine(3, half),
@@ -494,8 +454,6 @@
             scratch_shapes=[
                 pltpu.VMEM((2, tall, 256), F32),
                 pltpu.VMEM((2, rows, LANES), F32),
-                pltpu.VMEM((2, rows, wide), BF),
-                pltpu.SemaphoreType.DMA(()),
             ],
         ),
         out_shape=[
@@ -505,16 +463,16 @@
             jax.ShapeDtypeStruct((2, rows, wide), BF),
             jax.ShapeDtypeStruct((2, short, wide), BF),
         ],
-        compiler_params=params(),
+        compiler_params=params(60),
         cost_estimate=cost(1, 1),
         name="own_half",
     )(
-        meta, offsets, bins, attention, skip, edge, edge, *far, *prev, cot, weight, filt,
+        meta, offsets, bins, attention, skip, edge, edge, prev, cot, weight, filt,
     )
 
 
 def slope_kernel(
-    meta, offsets, bins, att, skip, edge, filt, asked, sums, slopes, mine, shown, ext
+    meta, offsets, bins, att, skip, edge, twin, filt, asked, sums, slopes, mine, shown, ext
 ):
     rows = skip.shape[1]
     tall = rows + 2 * PAD
@@ -533,7 +491,7 @@
     def _(part):
         begin = pl.multiple_of(part * width, width)
         cols = pl.ds(begin, width)
-        slab_sums(att, skip, edge, ext, cols, True)
+        slab_sums(att, skip, edge, twin, ext, cols)
         taps = taps_of(filt, cols)
         got = []
         for s in range(2):
@@ -548,7 +506,7 @@
         shown[:, place] = dot(told, got).astype(BF)
 
 
-def other_slopes(meta, offsets, bins, shipped, skip, edge, filt, asked):
+def other_slopes(meta, offsets, bins, shipped, skip, edge, twin, filt, asked):
     seqs, rows, wide = skip.shape
     _, packed_rows, half = shipped.shape
     tall = rows + 2 * PAD
@@ -568,6 +526,7 @@
                 whole(2, packed_rows, half),
                 other(2, rows, half),
                 other(16, half),
+                pl.BlockSpec((16, half), lambda i, m, o, b: (0, m[0])),
                 other(3, half),
                 whole(32, half),
             ],
@@ -583,7 +542,7 @@
         compiler_params=params(),
         cost_estimate=cost(10**11, 4 * 1024 * 1024, 2 * tall * half),
         name="other_slopes",
-    )(meta, offsets, bins, shipped, skip, edge, filt, asked)
+    )(meta, offsets, bins, shipped, skip, edge, twin, filt, asked)
 
 
 def terms_kernel(meta, order, moved, sums, slopes, own_terms, *refs):
@@ -701,12 +660,15 @@
     )(meta, moved, convs, filt, skip_grad, att_grad)
 
 
-def target_kernel(meta, order, mine, got_a, got_b, weight, *refs):
+def target_kernel(slabs, meta, order, mine, got_a, got_b, weight, *refs):
     pieces, (target, total) = refs[:8], refs[8:]
     half = weight.shape[0]
     there = (1 - meta[0]) * half
     tile = pieces[0].shape[0]
-    mine[...] = mine[...] + got_a[...] + got_b[...]
+    even = (meta[1] & 1) == 0
+    got = jnp.where(even, got_a[...].astype(F32), got_b[...].astype(F32))
+    got = jnp.where(meta[1] == slabs - 1, 0.0, got)
+    mine[...] = (mine[...].astype(F32) + got).astype(BF)
     here = pl.ds(pl.multiple_of(meta[0] * half, half), half)
     total[...] = dot(mine[:, here], weight[...]) + pltpu.roll(mine[...].astype(F32), 12 + 2, 0)
     for k, piece in enumerate(pieces):
@@ -717,7 +679,7 @@
         target[s] = total[s * 8 : s * 8 + 2].astype(BF)
 
 
-def targets(meta, order, mine, got, weight, pieces):
+def targets(meta, order, mine, got, weight, pieces, slabs):
     half, wide = weight.shape
     tile = pieces[0].shape[0]
 
@@ -725,7 +687,7 @@
         return pl.BlockSpec(shape, lambda i, m, o: (0,) * len(shape))
 
     return pl.pallas_call(
-        target_kernel,
+        functools.partial(target_kernel, slabs),
         grid_spec=pltpu.PrefetchScalarGridSpec(
             num_scalar_prefetch=2,
             grid=(1,),
@@ -746,9 +708,12 @@
     return lax.ppermute(part, axis, [(i, i ^ bit) for i in range(count)])
 
 
-def sent(part, by, odd):
+def staggered(part, span):
     count = lax.axis_size("seq")
-    pairs = [(i, i + by) for i in range(odd, count, 2) if 0 <= i + by < count]
+    pairs = []
+    for i in range(count):
+        by = span if i // span % 2 else -span
+        pairs.append((i, (i + by) % count))
     return lax.ppermute(part, "seq", pairs)
 
 
@@ -784,38 +749,34 @@
     tile = 3 * LANES
     order = jnp.stack([block, block ^ 1, block ^ 2, block ^ 3, core, 1 - core]).astype(jnp.int32)
 
-    edge_a, edge_b, far, first, last_tile = packed(
+    edge_a, edge_b, far, first, last_tile, att_out = packed(
         meta, encoder_skip, attention, cotangent, point_weight, tile
     )
-    prev = [sent(cotangent, 1, odd) for odd in (0, 1)]
+    prev = passed_along(cotangent, "seq", 1)
     first = paired(first, "head", 1)
+    shipped = paired(att_out, "head", 1)
     edge_a = paired(edge_a, "seq", 1)
-    edge_b = lax.ppermute(
-        edge_b, "seq", [pair for i in range(1, slabs - 1, 2) for pair in ((i, i + 1), (i + 1, i))]
-    )
-    far = [
-        lax.ppermute(
-            far, "seq", [(i, i + 2) for i in range(slabs - 2) if i // 2 % 2 == odd]
-        )
-        for odd in (0, 1)
-    ]
-    edge = edge_a + edge_b
-    message = shipment(meta, attention, edge)
-    shipped = paired(message, "head", 1)
-    first, edge, *far = lax.optimization_barrier((first, edge, *far))
+    edge_b = staggered(edge_b, 1)
+    far_a = paired(far, "seq", 2)
+    far_b = staggered(far, 2)
+    outer = (slab == 0) | (slab == slabs - 1)
+    nothing = jnp.zeros_like(edge_b)
+    edge = edge_a + jnp.where(outer, nothing, edge_b)
+    twin = paired(edge, "head", 1)
+    edge = edge + jnp.where(slab % 4 >= 2, far_a, jnp.where(slab < 2, nothing, far_b))
     second = paired(first, "seq", 2)
     third = paired(first, "seq", 4)
     fourth = paired(last_tile, "head", 1)
     moved, asked, own_terms, skip_grad, att_grad = own_half(
-        meta, crop_offset, target_bins, attention, encoder_skip, edge, far, prev, cotangent,
-        after(point_weight, first, message, last_tile), depth_filter, slabs,
+        meta, crop_offset, target_bins, attention, encoder_skip, edge, prev, cotangent,
+        point_weight, depth_filter, slabs,
     )
     pieces = [first, second, third, fourth]
     pieces = pieces + [paired(after(piece, own_terms), "seq", 1) for piece in pieces]
     sums, slopes, mine, shown = other_slopes(
-        meta, crop_offset, target_bins, shipped, encoder_skip, edge, depth_filter, asked
-    )
-    got = [sent(shown, -1, odd) for odd in (1, 0)]
+        meta, crop_offset, target_bins, shipped, encoder_skip, edge, twin, depth_filter, asked
+    )
+    got = [paired(shown, "seq", 1), staggered(shown, 1)]
     convs, terms = other_terms(meta, order, moved, sums, slopes, own_terms, pieces)
     terms, *got = lax.optimization_barrier((terms, *got))
     total = terms + crossed(terms, 1, 0)
@@ -823,7 +784,7 @@
     skip_grad, attention_grad = other_grads(
         meta, moved, convs, depth_filter, skip_grad, att_grad
     )
-    target_rows = targets(meta, order, mine, got, point_weight, pieces)
+    target_rows = targets(meta, order, mine, got, point_weight, pieces, slabs)
     total, skip_grad, attention_grad = lax.optimization_barrier(
         (total, skip_grad, attention_grad)
     )

time: 76.1 us -> 63.5 us (0.83)
  starting transfers between devices: 39.2 us -> 34.2 us
  local copies, waits for them, and re-layouts: 5 us -> 0.92 us
  Pallas kernels: 22.9 us -> 19.8 us
    ppermute x10 -> x13, starting transfers between devices: 15.7 us -> 10.4 us  [paired(): return lax.ppermute(part, axis, [(i, i ^ bit) for i in range(count)])]
    unnamed x28 -> x22, local copies, waits for them, and re-layouts: 4.91 us -> 0.84 us
    ppermute x7 -> x4, starting transfers between devices: 12.5 us -> 15.7 us  [the longest x3 13.3 us: staggered(): return lax.ppermute(part, 'seq', pairs)]
    ppermute x7, starting transfers between devices: 11.1 us -> 8.07 us  [crossed(): return lax.ppermute(part, ('seq', 'head'), pairs)]
    pallas_call x2 -> x1, Pallas kernels: 4.52 us -> 1.93 us  [targets(): pl.pallas_call(functools.partial(target_kernel, slabs), grid_spec=pltpu.P...]
    pallas_call x1, Pallas kernels: 6.03 us -> 7.61 us  [own_half(): pl.pallas_call(functools.partial(own_kernel, slabs), grid_spec=pltpu.Pref...]
    ppermute x7 -> x4, waiting for transfers between devices: 1.36 us -> 0.34 us  [the longest x3 0.34 us: staggered(): return lax.ppermute(part, 'seq', pairs)]
    pallas_call x1, Pallas kernels: 3.65 us -> 2.71 us  [other_terms(): pl.pallas_call(terms_kernel, grid_spec=pltpu.PrefetchScalarGridSpec(num_s...]
  transfers between devices with their start and end apart: 24 -> 24, of which waited for: 6 -> 5; matrix products, arithmetic and copies ran while one was open for 1% -> 2% of each run, Pallas kernels for 30% -> 31%
where the time goes in v5:
time: 63.5 us; the launch traced here: 63.2 us
  starting transfers between devices  34.2 us (54%)
  Pallas kernels  19.8 us (31%)
  waiting for transfers between devices  5.54 us (9%)
  other arithmetic  1.89 us (3%)
  local copies, waits for them, and re-layouts  0.92 us (1%)
  between operations  0.83 us (1%)
    ppermute x3, starting transfers between devices, staggered(): return lax.ppermute(part, 'seq', pairs)  13.3 us
    ppermute x13, starting transfers between devices, paired(): return lax.ppermute(part, axis, [(i, i ^ bit) for i in range(count)])  10.4 us
    ppermute x7, starting transfers between devices, crossed(): return lax.ppermute(part, ('seq', 'head'), pairs)  8.07 us
    pallas_call x1, Pallas kernels, own_half(): pl.pallas_call(functools.partial(own_kernel, slabs), grid_spec=pltpu.Pref...  7.61 us
    ppermute x7, waiting for transfers between devices, crossed(): return lax.ppermute(part, ('seq', 'head'), pairs)  5.16 us
    pallas_call x1, Pallas kernels, packed(): pl.pallas_call(pack_kernel, grid_spec=pltpu.PrefetchScalarGridSpec(num_sc...  3.1 us
    pallas_call x1, Pallas kernels, other_terms(): pl.pallas_call(terms_kernel, grid_spec=pltpu.PrefetchScalarGridSpec(num_s...  2.71 us
    pallas_call x1, Pallas kernels, other_slopes(): pl.pallas_call(slope_kernel, grid_spec=pltpu.PrefetchScalarGridSpec(num_s...  2.61 us
  transfers between devices with their start and end apart: 24, of which 5 were waited for; matrix products, arithmetic and copies ran while one was open for 2% of the time, Pallas kernels for 31%

profile of v5, /device:TPU:0, one launch (start us, length us, event | category | flops | bytes accessed | tf_op | source)
XLA Modules:
  0.0 63.2 jit_solution(1800891024383312363)
XLA Ops:
  0.6 2.4 %collective-permute-start.6 = (bf16[2,128,1536]{2,1,0:T(8,128)(2,1)}, bf16[2,128,1536]{2,1,0:T(8,128)(2,1)S(1)}, u32[]{:S(2)}, u32[]{:S(2)}) collective-permute-start(bf16[2,128,1536]{2,1,0:T(8,128)(2,1)} %cot.1), channel_id=1, source_target_pairs={{0,2},{2,4},{4,6},{6,8},{8,10},{10,12},{12,14},{14,16},{16,18},{18... | collective-permute-start | bytes 2359304 | tf_op jit(solution)/shard_map/ppermute | solution.py:30
  3.7 3.1 %pack_edges.1 = (bf16[16,1536]{1,0:T(8,128)(2,1)}, bf16[16,1536]{1,0:T(8,128)(2,1)}, bf16[16,1536]{1,0:T(8,128)(2,1)}, bf16[384,384]{1,0:T(8,128)(2,1)}, bf16[38...) custom-call(s32[2]{0:T(128)} %pad_add_fusion.meta, bf16[2,128,1536]{2,1,0:T(8,128)(2,1)} %skip.3, ...), custom_call_target="tpu_custom_call" | custom-call | tf_op jit(solution)/shard_map/pack_edges/pallas_call | solution.py:251
  6.8 2.3 %collective-permute-start.7 = (bf16[384,384]{1,0:T(8,128)(2,1)}, bf16[384,384]{1,0:T(8,128)(2,1)S(1)}, u32[]{:S(2)}, u32[]{:S(2)}) collective-permute-start(bf16[384,384]{1,0:T(8,128)(2,1)} %get-tuple-element.43), channel_id=1, source_target_pairs={{0,1},{1,0},{2,3},{3,2},{4,5},{5,4},{6,7},{7,6},{8,9},{9,8},{10,11... | collective-permute-start | bytes 884744 | tf_op jit(solution)/shard_map/ppermute | solution.py:708
  9.1 1.6 %collective-permute-start.3 = (bf16[16,1536]{1,0:T(8,128)(2,1)}, bf16[16,1536]{1,0:T(8,128)(2,1)S(1)}, u32[]{:S(2)}, u32[]{:S(2)}) collective-permute-start(bf16[16,1536]{1,0:T(8,128)(2,1)} %get-tuple-element.36), channel_id=1, source_target_pairs={{0,4},{2,6},{4,0},{6,2},{8,12},{10,14},{12,8},{14,10},{16,20},{18,... | collective-permute-start | bytes 147464 | tf_op jit(solution)/shard_map/ppermute | solution.py:708
  10.7 3.6 %collective-permute-start.4 = (bf16[16,1536]{1,0:T(8,128)(2,1)}, bf16[16,1536]{1,0:T(8,128)(2,1)S(1)}, u32[]{:S(2)}, u32[]{:S(2)}) collective-permute-start(bf16[16,1536]{1,0:T(8,128)(2,1)} %get-tuple-element.36), channel_id=1, source_target_pairs={{0,28},{2,30},{4,8},{6,10},{8,4},{10,6},{12,16},{14,18},{16,12},{1... | collective-permute-start | bytes 147464 | tf_op jit(solution)/shard_map/ppermute | solution.py:717
  14.3 0.8 %collective-permute-start.1 = (bf16[16,1536]{1,0:T(8,128)(2,1)}, bf16[16,1536]{1,0:T(8,128)(2,1)S(1)}, u32[]{:S(2)}, u32[]{:S(2)}) collective-permute-start(bf16[16,1536]{1,0:T(8,128)(2,1)} %get-tuple-element.34), channel_id=1, source_target_pairs={{0,2},{2,0},{4,6},{6,4},{8,10},{10,8},{12,14},{14,12},{16,18},{18,... | collective-permute-start | bytes 147464 | tf_op jit(solution)/shard_map/ppermute | solution.py:708
  15.1 6.6 %collective-permute-start.2 = (bf16[16,1536]{1,0:T(8,128)(2,1)}, bf16[16,1536]{1,0:T(8,128)(2,1)S(1)}, u32[]{:S(2)}, u32[]{:S(2)}) collective-permute-start(bf16[16,1536]{1,0:T(8,128)(2,1)} %get-tuple-element.35), channel_id=1, source_target_pairs={{0,30},{2,4},{4,2},{6,8},{8,6},{10,12},{12,10},{14,16},{16,14},{18... | collective-permute-start | bytes 147464 | tf_op jit(solution)/shard_map/ppermute | solution.py:717
  21.7 1.5 %collective-permute-start.10 = (bf16[384,384]{1,0:T(8,128)(2,1)}, bf16[384,384]{1,0:T(8,128)(2,1)S(1)}, u32[]{:S(2)}, u32[]{:S(2)}) collective-permute-start(bf16[384,384]{1,0:T(8,128)(2,1)} %get-tuple-element.44), channel_id=1, source_target_pairs={{0,1},{1,0},{2,3},{3,2},{4,5},{5,4},{6,7},{7,6},{8,9},{9,8},{10,11... | collective-permute-start | bytes 884744 | tf_op jit(solution)/shard_map/ppermute | solution.py:708
  23.7 1.0 %collective-permute-start.9 = (bf16[384,384]{1,0:T(8,128)(2,1)S(1)}, bf16[384,384]{1,0:T(8,128)(2,1)S(1)}, u32[]{:S(2)}, u32[]{:S(2)}) collective-permute-start(bf16[384,384]{1,0:T(8,128)(2,1)S(1)} %collective-permute-done.7.refs_0_), channel_id=1, source_target_pairs={{0,8},{2,10},{4,12},{6,14},{8,0},{10,2},{12,4},{14,6},{16,24},{18,... | collective-permute-start | bytes 884744 | tf_op jit(solution)/shard_map/ppermute | solution.py:708
  24.8 0.6 %select_add_fusion = (bf16[16,1536]{1,0:T(8,128)(2,1)}, bf16[16,1536]{1,0:T(8,128)(2,1)S(1)}) fusion(bf16[16,1536]{1,0:T(8,128)(2,1)S(1)} %collective-permute-done.3, bf16[16,1536]{1,0:T(8,128)(2,1)S(1)} %collective-permute-done.4, pred[]{:T(512)S(6)} %lt.20, pred[]{:T(512)S(6)} %ge.3, bf16[16,1536]{1,0:T(8,128)(2,1)S(1)} %collective-permute-done.1, ...), kind=kLoop, calls=%fused_computation | loop fusion | flops 122880 | bytes 294915 | tf_op jit(solution)/shard_map/add | solution.py:766
  25.4 1.5 %collective-permute-start.5 = (bf16[16,1536]{1,0:T(8,128)(2,1)S(1)}, bf16[16,1536]{1,0:T(8,128)(2,1)S(1)}, u32[]{:S(2)}, u32[]{:S(2)}) collective-permute-start(bf16[16,1536]{1,0:T(8,128)(2,1)S(1)} %get-tuple-element.63), channel_id=1, source_target_pairs={{0,1},{1,0},{2,3},{3,2},{4,5},{5,4},{6,7},{7,6},{8,9},{9,8},{10,11... | collective-permute-start | bytes 147464 | tf_op jit(solution)/shard_map/ppermute | solution.py:708
  27.1 7.6 %own_half.1 = (bf16[2,144,1536]{2,1,0:T(8,128)(2,1)}, bf16[32,768]{1,0:T(8,128)(2,1)}, f32[3,768]{1,0:T(4,128)}, bf16[2,128,1536]{2,1,0:T(8,128)(2,1)}, bf16[2,64,1536]{2,1,0:T(8,128)(2,1)}) custom-call(s32[2]{0:T(128)} %pad_add_fusion.meta, s32[2]{0:T(128)} %offsets.3, s32[2,32]{1,0:T(2,128)} %bins.3, bf16[4,64,768]{2,1,0:T(8,128)(2,1)} %att.3, ...), custom_call_target="tpu_custom_call" | custom-call | flops 1 | bytes 1 | tf_op jit(solution)/shard_map/own_half/pallas_call | solution.py:432
  35.8 0.8 %copy-done.9 = bf16[32,768]{1,0:T(8,128)(2,1)S(1)} copy-done((bf16[32,768]{1,0:T(8,128)(2,1)S(1)}, bf16[32,768]{1,0:T(8,128)(2,1)}, u32[]{:S(2)}) %copy-start.9) | copy-done | bytes 49176
  36.6 2.6 %other_slopes.1 = (bf16[2,144,768]{2,1,0:T(8,128)(2,1)S(1)}, f32[2,144,768]{2,1,0:T(8,128)S(1)}, bf16[16,1536]{1,0:T(8,128)(2,1)S(1)}, bf16[16,1536]{1,0:T(8,128)(2,1)S(1)}) custom-call(s32[2]{0:T(128)S(1)} %copy-done.5, s32[2]{0:T(128)S(1)} %copy-done.8, s32[2,32]{1,0:T(2,128)S(1)} %copy-done.7, bf16[2,64,768]{2,1,0:T(8,128)(2,1)S(1)} %collective-permute-done.att, ...), custom_call_target="tpu_custom_call" | custom-call | flops 99999997952 | bytes 4194304 | tf_op jit(solution)/shard_map/other_slopes/pallas_call | solution.py:520
  39.3 3.1 %collective-permute-start.16 = (bf16[16,1536]{1,0:T(8,128)(2,1)S(1)}, bf16[16,1536]{1,0:T(8,128)(2,1)S(1)}, u32[]{:S(2)}, u32[]{:S(2)}) collective-permute-start(bf16[16,1536]{1,0:T(8,128)(2,1)S(1)} %get-tuple-element.50), channel_id=1, source_target_pairs={{0,30},{2,4},{4,2},{6,8},{8,6},{10,12},{12,10},{14,16},{16,14},{18... | collective-permute-start | bytes 147464 | tf_op jit(solution)/shard_map/ppermute | solution.py:717
  42.5 2.7 %other_terms.1 = (bf16[2,144,768]{2,1,0:T(8,128)(2,1)S(1)}, f32[3,1536]{1,0:T(4,128)S(1)}) custom-call(s32[2]{0:T(128)S(1)} %copy-done.5, s32[6]{0:T(128)S(1)} %stack.39.order, bf16[2,144,1536]{2,1,0:T(8,128)(2,1)S(1)} %copy-done.2, bf16[2,144,768]{2,1,0:T(8,128)(2,1)S(1)} %get-tuple-element.40.sums, f32[2,144,768]{2,1,0:T(8,128)S(1)} %get-tuple-element.41.slopes, ...), custom_call_target="tpu_custom_call" | custom-call | flops 679477248 | bytes 6291456 | tf_op jit(solution)/shard_map/other_terms/pallas_call | solution.py:590
  45.5 1.2 %collective-permute-done.17 = f32[3,1536]{1,0:T(4,128)S(1)} collective-permute-done((f32[3,1536]{1,0:T(4,128)S(1)}, f32[3,1536]{1,0:T(4,128)S(1)}, u32[]{:S(2)}, u32[]{:S(2)}) %collective-permute-start.17) | collective-permute-done | bytes 18464 | tf_op jit(solution)/shard_map/ppermute | solution.py:731
  46.8 0.9 %collective-permute-start.19 = (f32[3,1536]{1,0:T(4,128)S(1)}, f32[3,1536]{1,0:T(4,128)S(1)}, u32[]{:S(2)}, u32[]{:S(2)}) collective-permute-start(f32[3,1536]{1,0:T(4,128)S(1)} %add.43), channel_id=1, source_target_pairs={{0,1},{1,0},{2,3},{3,2},{4,5},{5,4},{6,7},{7,6},{8,9},{9,8},{10,11... | collective-permute-start | bytes 55304 | tf_op jit(solution)/shard_map/ppermute | solution.py:731
  47.7 2.6 %collective-permute-start.20 = (f32[3,1536]{1,0:T(4,128)S(1)}, f32[3,1536]{1,0:T(4,128)S(1)}, u32[]{:S(2)}, u32[]{:S(2)}) collective-permute-start(f32[3,1536]{1,0:T(4,128)S(1)} %add.43), channel_id=1, source_target_pairs={{0,5},{1,4},{2,7},{3,6},{4,1},{5,0},{6,3},{7,2},{8,13},{9,12},{10,... | collective-permute-start | bytes 55304 | tf_op jit(solution)/shard_map/ppermute | solution.py:731
  50.3 1.8 %other_grads.1 = (bf16[2,128,1536]{2,1,0:T(8,128)(2,1)}, bf16[2,64,1536]{2,1,0:T(8,128)(2,1)}) custom-call(s32[2]{0:T(128)S(1)} %copy-done.5, bf16[2,144,1536]{2,1,0:T(8,128)(2,1)S(1)} %copy-done.2, bf16[2,144,768]{2,1,0:T(8,128)(2,1)S(1)} %get-tuple-element.54.convs, f32[3,1536]{1,0:T(4,128)S(1)} %copy-done.4, ...), custom_call_target="tpu_custom_call", output_to_operand_aliasing={{0}: (4, {}), {1}: (5, {})} | custom-call | flops 4423680 | bytes 4194304 | tf_op jit(solution)/shard_map/other_grads/pallas_call | solution.py:642
  52.4 1.2 %collective-permute-start.21 = (f32[3,1536]{1,0:T(4,128)S(1)}, f32[3,1536]{1,0:T(4,128)S(1)}, u32[]{:S(2)}, u32[]{:S(2)}) collective-permute-start(f32[3,1536]{1,0:T(4,128)S(1)} %add_add_fusion), channel_id=1, source_target_pairs={{0,8},{1,9},{2,10},{3,11},{4,12},{5,13},{6,14},{7,15},{8,0},{9,1},... | collective-permute-start | bytes 55304 | tf_op jit(solution)/shard_map/ppermute | solution.py:731
  53.6 3.3 %collective-permute-start.22 = (f32[3,1536]{1,0:T(4,128)S(1)}, f32[3,1536]{1,0:T(4,128)S(1)}, u32[]{:S(2)}, u32[]{:S(2)}) collective-permute-start(f32[3,1536]{1,0:T(4,128)S(1)} %add_add_fusion), channel_id=1, source_target_pairs={{0,16},{1,17},{2,18},{3,19},{4,20},{5,21},{6,22},{7,23},{8,24},{9,... | collective-permute-start | bytes 55304 | tf_op jit(solution)/shard_map/ppermute | solution.py:731
  57.0 1.9 %targets.1 = bf16[2,2,1536]{2,1,0:T(2,128)(2,1)} custom-call(s32[2]{0:T(128)S(1)} %copy-done.5, s32[6]{0:T(128)S(1)} %stack.39.order, bf16[16,1536]{1,0:T(8,128)(2,1)S(1)} %get-tuple-element.38.mine, bf16[16,1536]{1,0:T(8,128)(2,1)S(1)} %collective-permute-done.15.got_a, bf16[16,1536]{1,0:T(8,128)(2,1)S(1)} %collective-permute-done.16.got_b, ...), custom_call_target="tpu_custom_call" | custom-call | flops 75497472 | bytes 6291456 | tf_op jit(solution)/shard_map/targets/pallas_call | solution.py:689
  59.0 3.6 %collective-permute-done.23 = f32[3,1536]{1,0:T(4,128)S(1)} collective-permute-done((f32[3,1536]{1,0:T(4,128)S(1)}, f32[3,1536]{1,0:T(4,128)S(1)}, u32[]{:S(2)}, u32[]{:S(2)}) %collective-permute-start.23) | collective-permute-done | bytes 18464 | tf_op jit(solution)/shard_map/ppermute | solution.py:731
  (58 shorter events, 3.8 us)
Async XLA Ops:
  0.6 24.8 %collective-permute-start.6 = (bf16[2,128,1536]{2,1,0:T(8,128)(2,1)}, bf16[2,128,1536]{2,1,0:T(8,128)(2,1)S(1)}, u32[]{:S(2)}, u32[]{:S(2)}) collective-permute-start(bf16[2,128,1536]{2,1,0:T(8,128)(2,1)} %cot.1), channel_id=1, source_target_pairs={{0,2},{2,4},{4,6},{6,8},{8,10},{10,12},{12,14},{14,16},{16,18},{18... | collective-permute-start | bytes 2359304 | tf_op jit(solution)/shard_map/ppermute | solution.py:30
  6.8 16.9 %collective-permute-start.7 = (bf16[384,384]{1,0:T(8,128)(2,1)}, bf16[384,384]{1,0:T(8,128)(2,1)S(1)}, u32[]{:S(2)}, u32[]{:S(2)}) collective-permute-start(bf16[384,384]{1,0:T(8,128)(2,1)} %get-tuple-element.43), channel_id=1, source_target_pairs={{0,1},{1,0},{2,3},{3,2},{4,5},{5,4},{6,7},{7,6},{8,9},{9,8},{10,11... | collective-permute-start | bytes 884744 | tf_op jit(solution)/shard_map/ppermute | solution.py:708
  9.1 6.0 %collective-permute-start.3 = (bf16[16,1536]{1,0:T(8,128)(2,1)}, bf16[16,1536]{1,0:T(8,128)(2,1)S(1)}, u32[]{:S(2)}, u32[]{:S(2)}) collective-permute-start(bf16[16,1536]{1,0:T(8,128)(2,1)} %get-tuple-element.36), channel_id=1, source_target_pairs={{0,4},{2,6},{4,0},{6,2},{8,12},{10,14},{12,8},{14,10},{16,20},{18,... | collective-permute-start | bytes 147464 | tf_op jit(solution)/shard_map/ppermute | solution.py:708
  10.7 10.9 %collective-permute-start.4 = (bf16[16,1536]{1,0:T(8,128)(2,1)}, bf16[16,1536]{1,0:T(8,128)(2,1)S(1)}, u32[]{:S(2)}, u32[]{:S(2)}) collective-permute-start(bf16[16,1536]{1,0:T(8,128)(2,1)} %get-tuple-element.36), channel_id=1, source_target_pairs={{0,28},{2,30},{4,8},{6,10},{8,4},{10,6},{12,16},{14,18},{16,12},{1... | collective-permute-start | bytes 147464 | tf_op jit(solution)/shard_map/ppermute | solution.py:717
  14.3 8.9 %collective-permute-start.1 = (bf16[16,1536]{1,0:T(8,128)(2,1)}, bf16[16,1536]{1,0:T(8,128)(2,1)S(1)}, u32[]{:S(2)}, u32[]{:S(2)}) collective-permute-start(bf16[16,1536]{1,0:T(8,128)(2,1)} %get-tuple-element.34), channel_id=1, source_target_pairs={{0,2},{2,0},{4,6},{6,4},{8,10},{10,8},{12,14},{14,12},{16,18},{18,... | collective-permute-start | bytes 147464 | tf_op jit(solution)/shard_map/ppermute | solution.py:708
  15.1 8.7 %collective-permute-start.2 = (bf16[16,1536]{1,0:T(8,128)(2,1)}, bf16[16,1536]{1,0:T(8,128)(2,1)S(1)}, u32[]{:S(2)}, u32[]{:S(2)}) collective-permute-start(bf16[16,1536]{1,0:T(8,128)(2,1)} %get-tuple-element.35), channel_id=1, source_target_pairs={{0,30},{2,4},{4,2},{6,8},{8,6},{10,12},{12,10},{14,16},{16,14},{18... | collective-permute-start | bytes 147464 | tf_op jit(solution)/shard_map/ppermute | solution.py:717
  21.7 13.6 %collective-permute-start.10 = (bf16[384,384]{1,0:T(8,128)(2,1)}, bf16[384,384]{1,0:T(8,128)(2,1)S(1)}, u32[]{:S(2)}, u32[]{:S(2)}) collective-permute-start(bf16[384,384]{1,0:T(8,128)(2,1)} %get-tuple-element.44), channel_id=1, source_target_pairs={{0,1},{1,0},{2,3},{3,2},{4,5},{5,4},{6,7},{7,6},{8,9},{9,8},{10,11... | collective-permute-start | bytes 884744 | tf_op jit(solution)/shard_map/ppermute | solution.py:708
  23.2 12.6 %collective-permute-start = (bf16[2,64,768]{2,1,0:T(8,128)(2,1)}, bf16[2,64,768]{2,1,0:T(8,128)(2,1)S(1)}, u32[]{:S(2)}, u32[]{:S(2)}) collective-permute-start(bf16[2,64,768]{2,1,0:T(8,128)(2,1)} %get-tuple-element.33), channel_id=1, source_target_pairs={{0,1},{1,0},{2,3},{3,2},{4,5},{5,4},{6,7},{7,6},{8,9},{9,8},{10,11... | collective-permute-start | bytes 589832 | tf_op jit(solution)/shard_map/ppermute | solution.py:708
  23.7 11.0 %collective-permute-start.8 = (bf16[384,384]{1,0:T(8,128)(2,1)S(1)}, bf16[384,384]{1,0:T(8,128)(2,1)S(1)}, u32[]{:S(2)}, u32[]{:S(2)}) collective-permute-start(bf16[384,384]{1,0:T(8,128)(2,1)S(1)} %collective-permute-done.7.refs_0_), channel_id=1, source_target_pairs={{0,4},{2,6},{4,0},{6,2},{8,12},{10,14},{12,8},{14,10},{16,20},{18,... | collective-permute-start | bytes 884744 | tf_op jit(solution)/shard_map/ppermute | solution.py:708
  23.7 11.0 %collective-permute-start.9 = (bf16[384,384]{1,0:T(8,128)(2,1)S(1)}, bf16[384,384]{1,0:T(8,128)(2,1)S(1)}, u32[]{:S(2)}, u32[]{:S(2)}) collective-permute-start(bf16[384,384]{1,0:T(8,128)(2,1)S(1)} %collective-permute-done.7.refs_0_), channel_id=1, source_target_pairs={{0,8},{2,10},{4,12},{6,14},{8,0},{10,2},{12,4},{14,6},{16,24},{18,... | collective-permute-start | bytes 884744 | tf_op jit(solution)/shard_map/ppermute | solution.py:708
  25.4 9.9 %collective-permute-start.5 = (bf16[16,1536]{1,0:T(8,128)(2,1)S(1)}, bf16[16,1536]{1,0:T(8,128)(2,1)S(1)}, u32[]{:S(2)}, u32[]{:S(2)}) collective-permute-start(bf16[16,1536]{1,0:T(8,128)(2,1)S(1)} %get-tuple-element.63), channel_id=1, source_target_pairs={{0,1},{1,0},{2,3},{3,2},{4,5},{5,4},{6,7},{7,6},{8,9},{9,8},{10,11... | collective-permute-start | bytes 147464 | tf_op jit(solution)/shard_map/ppermute | solution.py:708
  34.7 4.6 %collective-permute-start.12 = (bf16[384,384]{1,0:T(8,128)(2,1)S(1)}, bf16[384,384]{1,0:T(8,128)(2,1)S(1)}, u32[]{:S(2)}, u32[]{:S(2)}) collective-permute-start(bf16[384,384]{1,0:T(8,128)(2,1)S(1)} %collective-permute-done.8.refs_1_), channel_id=1, source_target_pairs={{0,2},{2,0},{4,6},{6,4},{8,10},{10,8},{12,14},{14,12},{16,18},{18,... | collective-permute-start | bytes 884744 | tf_op jit(solution)/shard_map/ppermute | solution.py:708
  34.7 7.7 %collective-permute-start.13 = (bf16[384,384]{1,0:T(8,128)(2,1)S(1)}, bf16[384,384]{1,0:T(8,128)(2,1)S(1)}, u32[]{:S(2)}, u32[]{:S(2)}) collective-permute-start(bf16[384,384]{1,0:T(8,128)(2,1)S(1)} %collective-permute-done.9.refs_2_), channel_id=1, source_target_pairs={{0,2},{2,0},{4,6},{6,4},{8,10},{10,8},{12,14},{14,12},{16,18},{18,... | collective-permute-start | bytes 884744 | tf_op jit(solution)/shard_map/ppermute | solution.py:708
  35.2 7.2 %collective-permute-start.11 = (bf16[384,384]{1,0:T(8,128)(2,1)S(1)}, bf16[384,384]{1,0:T(8,128)(2,1)S(1)}, u32[]{:S(2)}, u32[]{:S(2)}) collective-permute-start(bf16[384,384]{1,0:T(8,128)(2,1)S(1)} %collective-permute-done.7.refs_0_), channel_id=1, source_target_pairs={{0,2},{2,0},{4,6},{6,4},{8,10},{10,8},{12,14},{14,12},{16,18},{18,... | collective-permute-start | bytes 884744 | tf_op jit(solution)/shard_map/ppermute | solution.py:708
  35.3 7.1 %collective-permute-start.14 = (bf16[384,384]{1,0:T(8,128)(2,1)S(1)}, bf16[384,384]{1,0:T(8,128)(2,1)S(1)}, u32[]{:S(2)}, u32[]{:S(2)}) collective-permute-start(bf16[384,384]{1,0:T(8,128)(2,1)S(1)} %collective-permute-done.10.refs_3_), channel_id=1, source_target_pairs={{0,2},{2,0},{4,6},{6,4},{8,10},{10,8},{12,14},{14,12},{16,18},{18,... | collective-permute-start | bytes 884744 | tf_op jit(solution)/shard_map/ppermute | solution.py:708
  39.2 6.0 %collective-permute-start.15 = (bf16[16,1536]{1,0:T(8,128)(2,1)S(1)}, bf16[16,1536]{1,0:T(8,128)(2,1)S(1)}, u32[]{:S(2)}, u32[]{:S(2)}) collective-permute-start(bf16[16,1536]{1,0:T(8,128)(2,1)S(1)} %get-tuple-element.50), channel_id=1, source_target_pairs={{0,2},{2,0},{4,6},{6,4},{8,10},{10,8},{12,14},{14,12},{16,18},{18,... | collective-permute-start | bytes 147464 | tf_op jit(solution)/shard_map/ppermute | solution.py:708
  39.3 6.2 %collective-permute-start.16 = (bf16[16,1536]{1,0:T(8,128)(2,1)S(1)}, bf16[16,1536]{1,0:T(8,128)(2,1)S(1)}, u32[]{:S(2)}, u32[]{:S(2)}) collective-permute-start(bf16[16,1536]{1,0:T(8,128)(2,1)S(1)} %get-tuple-element.50), channel_id=1, source_target_pairs={{0,30},{2,4},{4,2},{6,8},{8,6},{10,12},{12,10},{14,16},{16,14},{18... | collective-permute-start | bytes 147464 | tf_op jit(solution)/shard_map/ppermute | solution.py:717
  45.5 1.2 %collective-permute-start.17 = (f32[3,1536]{1,0:T(4,128)S(1)}, f32[3,1536]{1,0:T(4,128)S(1)}, u32[]{:S(2)}, u32[]{:S(2)}) collective-permute-start(f32[3,1536]{1,0:T(4,128)S(1)} %get-tuple-element.53), channel_id=1, source_target_pairs={{0,2},{1,3},{2,0},{3,1},{4,6},{5,7},{6,4},{7,5},{8,10},{9,11},{10,... | collective-permute-start | bytes 55304 | tf_op jit(solution)/shard_map/ppermute | solution.py:731
  46.7 5.4 %collective-permute-start.18 = (f32[3,1536]{1,0:T(4,128)S(1)}, f32[3,1536]{1,0:T(4,128)S(1)}, u32[]{:S(2)}, u32[]{:S(2)}) collective-permute-start(f32[3,1536]{1,0:T(4,128)S(1)} %add.43), channel_id=1, source_target_pairs={{0,4},{1,5},{2,6},{3,7},{4,0},{5,1},{6,2},{7,3},{8,12},{9,13},{10,... | collective-permute-start | bytes 55304 | tf_op jit(solution)/shard_map/ppermute | solution.py:731
  46.8 5.3 %collective-permute-start.19 = (f32[3,1536]{1,0:T(4,128)S(1)}, f32[3,1536]{1,0:T(4,128)S(1)}, u32[]{:S(2)}, u32[]{:S(2)}) collective-permute-start(f32[3,1536]{1,0:T(4,128)S(1)} %add.43), channel_id=1, source_target_pairs={{0,1},{1,0},{2,3},{3,2},{4,5},{5,4},{6,7},{7,6},{8,9},{9,8},{10,11... | collective-permute-start | bytes 55304 | tf_op jit(solution)/shard_map/ppermute | solution.py:731
  47.7 4.7 %collective-permute-start.20 = (f32[3,1536]{1,0:T(4,128)S(1)}, f32[3,1536]{1,0:T(4,128)S(1)}, u32[]{:S(2)}, u32[]{:S(2)}) collective-permute-start(f32[3,1536]{1,0:T(4,128)S(1)} %add.43), channel_id=1, source_target_pairs={{0,5},{1,4},{2,7},{3,6},{4,1},{5,0},{6,3},{7,2},{8,13},{9,12},{10,... | collective-permute-start | bytes 55304 | tf_op jit(solution)/shard_map/ppermute | solution.py:731
  52.4 6.5 %collective-permute-start.21 = (f32[3,1536]{1,0:T(4,128)S(1)}, f32[3,1536]{1,0:T(4,128)S(1)}, u32[]{:S(2)}, u32[]{:S(2)}) collective-permute-start(f32[3,1536]{1,0:T(4,128)S(1)} %add_add_fusion), channel_id=1, source_target_pairs={{0,8},{1,9},{2,10},{3,11},{4,12},{5,13},{6,14},{7,15},{8,0},{9,1},... | collective-permute-start | bytes 55304 | tf_op jit(solution)/shard_map/ppermute | solution.py:731
  53.6 5.3 %collective-permute-start.22 = (f32[3,1536]{1,0:T(4,128)S(1)}, f32[3,1536]{1,0:T(4,128)S(1)}, u32[]{:S(2)}, u32[]{:S(2)}) collective-permute-start(f32[3,1536]{1,0:T(4,128)S(1)} %add_add_fusion), channel_id=1, source_target_pairs={{0,16},{1,17},{2,18},{3,19},{4,20},{5,21},{6,22},{7,23},{8,24},{9,... | collective-permute-start | bytes 55304 | tf_op jit(solution)/shard_map/ppermute | solution.py:731
  57.0 5.6 %collective-permute-start.23 = (f32[3,1536]{1,0:T(4,128)S(1)}, f32[3,1536]{1,0:T(4,128)S(1)}, u32[]{:S(2)}, u32[]{:S(2)}) collective-permute-start(f32[3,1536]{1,0:T(4,128)S(1)} %add_add_fusion), channel_id=1, source_target_pairs={{0,24},{1,25},{2,26},{3,27},{4,28},{5,29},{6,30},{7,31},{8,16},{9,... | collective-permute-start | bytes 55304 | tf_op jit(solution)/shard_map/ppermute | solution.py:731
  (11 other events, 78.3 us)

commit v6 on v5

--- a/solution.py
+++ b/solution.py
@@ -1,3 +1,177 @@
+import functools
+import math
+
+import jax
+import jax.numpy as jnp
+from jax import lax
+from jax.experimental import pallas as pl
+from jax.experimental.pallas import tpu as pltpu
+from jax.sharding import PartitionSpec as P
+
+NTD = 2
+
+
+def extended(shard, sides, width):
+    for axis, dim in sides:
+        count, length = (lax.axis_size(axis), shard.shape[dim])
+        up = [(i, (i + 1) % count) for i in range(count - 1)]
+        down = [(j, i) for i, j in up]
+        last = lax.slice_in_dim(shard, length - width, length, axis=dim)
+        initial = lax.slice_in_dim(shard, 0, width, axis=dim)
+        before = lax.ppermute(last, axis, up)
+        after = lax.ppermute(initial, axis, down)
+        shard = jnp.concatenate([before, shard, after], axis=dim)
+    return shard
+
+
+def passed_along(shard, axis, by):
+    count = lax.axis_size(axis)
+    pairs = [(i, i + by) for i in range(count) if 0 <= i + by < count]
+    return lax.ppermute(shard, axis, pairs)
+
+
+def gelu_slope(values):
+    return (
+        0.5 * (1.0 + lax.erf(values * 0.7071067811865476))
+        + values * jnp.exp(-0.5 * values * values) * 0.3989422804014327
+    )
+
+
+def with_rims(field):
+    return extended(field, (("seq", 1),), 1)
+
+
+def one_hot(places, length):
+    return (places[:, :, None] == jnp.arange(length, dtype=jnp.int32)[None, None, :]).astype(
+        jnp.bfloat16
+    )
+
+
+def core_swap(part):
+    count = lax.axis_size("seq")
+    return lax.ppermute(part, "seq", [(i, i ^ 1) for i in range(count)])
+
+
+def gathered_weight(rows):
+    heads = lax.axis_size("head")
+    here = lax.axis_index("head")
+    core = lax.axis_index("seq") % 2
+    half = rows.shape[0] // 2
+    mine = lax.dynamic_slice_in_dim(rows, core * half, half, 0)
+    blocks = [(0, rows)]
+    for step in range(1, heads):
+        pairs = [(i, (i + step) % heads) for i in range(heads)]
+        got = lax.ppermute(mine, "head", pairs)
+        twin = core_swap(got)
+        low = jnp.where(core == 0, got, twin)
+        high = jnp.where(core == 0, twin, got)
+        blocks.append((step, jnp.concatenate([low, high], axis=0)))
+    full = jnp.zeros((heads * rows.shape[0], rows.shape[1]), rows.dtype)
+    for step, block in blocks:
+        place = (here - step) % heads
+        full = lax.dynamic_update_slice_in_dim(full, block, place * rows.shape[0], 0)
+    return full
+
+
+def butterfly(total, axis):
+    count = lax.axis_size(axis)
+    if count & (count - 1):
+        return lax.psum(total, axis)
+    step = 1
+    while step < count:
+        total = total + lax.ppermute(total, axis, [(i, i ^ step) for i in range(count)])
+        step *= 2
+    return total
+
+
+def plain_shards(
+    attention, encoder_skip, depth_filter, point_weight, crop_offset, target_bins, cotangent
+):
+    slab_input = lax.all_to_all(attention, "head", split_axis=0, concat_axis=2, tiled=True)
+    local_seqs = encoder_skip.shape[0]
+    slab_rows = encoder_skip.shape[1]
+    channels = encoder_skip.shape[2]
+    summed = (
+        jnp.repeat(slab_input, 2, axis=1).astype(jnp.float32) + encoder_skip.astype(jnp.float32)
+    ).astype(jnp.bfloat16)
+    padded = with_rims(summed)
+    filtered = (
+        depth_filter[0] * padded[:, :-2]
+        + depth_filter[1] * padded[:, 1:-1]
+        + depth_filter[2] * padded[:, 2:]
+    )
+    activated = jax.nn.gelu(filtered, approximate=False).astype(jnp.bfloat16)
+    flat_act = activated.reshape(local_seqs * slab_rows, channels)
+    full_weight = gathered_weight(point_weight)
+    mixed_rows = jnp.dot(flat_act, full_weight, preferred_element_type=jnp.float32)
+    block_out = (
+        summed.astype(jnp.float32) + mixed_rows.reshape(local_seqs, slab_rows, channels)
+    ).astype(jnp.bfloat16)
+    slab_index = lax.axis_index("seq")
+    bins = jnp.concatenate(
+        [jnp.zeros_like(target_bins[:, :NTD]), target_bins], axis=1
+    )
+    asked = lax.dynamic_slice_in_dim(bins, slab_index * NTD, 2 * NTD, 1) + crop_offset[:, None]
+    back = jnp.where(jnp.arange(2 * NTD, dtype=jnp.int32) < NTD, slab_rows, 0)
+    asked = asked - back[None, :]
+    picked = jnp.einsum(
+        "sjr,srd->sjd",
+        one_hot(asked, slab_rows),
+        block_out,
+        preferred_element_type=jnp.float32,
+    ).astype(jnp.bfloat16)
+    from_next = passed_along(picked[:, :NTD], "seq", -1)
+    target_rows = picked[:, NTD:] + from_next
+    prev_cot = passed_along(cotangent, "seq", 1)
+    cot_pair = jnp.concatenate([prev_cot, cotangent], axis=1)
+
+    def crop_back(cot_block, shift_by):
+        return lax.dynamic_slice_in_dim(cot_block, slab_rows - shift_by, slab_rows, 0)
+
+    grad_out = jax.vmap(crop_back)(cot_pair, crop_offset)
+    flat_grad = grad_out.reshape(local_seqs * slab_rows, channels)
+    grad_act = lax.dot_general(
+        flat_grad, full_weight, (((1,), (1,)), ((), ())), preferred_element_type=jnp.float32
+    )
+    grad_conv = (grad_act.reshape(local_seqs, slab_rows, channels) * gelu_slope(filtered)).astype(
+        jnp.bfloat16
+    )
+    grad_padded = with_rims(grad_conv)
+    grad_sum = (
+        grad_out.astype(jnp.float32)
+        + depth_filter[0] * grad_padded[:, 2:]
+        + depth_filter[1] * grad_padded[:, 1:-1]
+        + depth_filter[2] * grad_padded[:, :-2]
+    )
+    skip_grad = grad_sum.astype(jnp.bfloat16)
+    attention_grad = (
+        grad_sum.reshape(local_seqs, slab_rows // 2, 2, channels).sum(axis=2).astype(jnp.bfloat16)
+    )
+    filter_terms = jnp.stack(
+        [
+            jnp.einsum(
+                "srd,srd->d", grad_conv, padded[:, 0:slab_rows], preferred_element_type=jnp.float32
+            ),
+            jnp.einsum(
+                "srd,srd->d",
+                grad_conv,
+                padded[:, 1 : slab_rows + 1],
+                preferred_element_type=jnp.float32,
+            ),
+            jnp.einsum(
+                "srd,srd->d",
+                grad_conv,
+                padded[:, 2 : slab_rows + 2],
+                preferred_element_type=jnp.float32,
+            ),
+        ]
+    )
+    filter_sum = butterfly(butterfly(filter_terms, "seq"), "head")
+    row_count = local_seqs * lax.axis_size("head") * slab_rows * lax.axis_size("seq")
+    filter_grad = filter_sum * (1.0 / math.sqrt(row_count))
+    return (target_rows, attention_grad, skip_grad, filter_grad)
+
+
 import functools
 import math
 
@@ -356,15 +530,81 @@
     return total, jnp.concatenate(sums, axis=1)
 
 
+def own_slope_kernel(meta, offsets, bins, att, skip, edge, filt, asked, sums, slopes, ext):
+    half = skip.shape[2]
+    tall = ext.shape[1]
+    width = ext.shape[2]
+
+    @pl.loop(0, half // width)
+    def _(part):
+        cols = pl.ds(pl.multiple_of(part * width, width), width)
+        slab_sums(att, skip, edge, edge, ext, cols)
+        taps = taps_of(filt, cols)
+        for s in range(2):
+            field = ext[s]
+            before, after = around(field)
+            slopes[s, :, cols] = slope_of(taps[0] * before + taps[1] * field + taps[2] * after)
+            sums[s, :, cols] = field.astype(BF)
+            asked[s * 16 : s * 16 + 16, cols] = asked_rows(
+                meta, offsets, bins, s, field, taps, tall
+            )
+
+
+def own_slopes(meta, offsets, bins, attention, skip, edge, filt):
+    seqs, rows, wide = skip.shape
+    _, short, half = attention.shape
+    tall = rows + 2 * PAD
+
+    def whole(*shape):
+        return pl.BlockSpec(shape, lambda i, m, o, b: (0,) * len(shape))
+
+    def mine(*shape):
+        return pl.BlockSpec(shape, lambda i, m, o, b: (0,) * (len(shape) - 1) + (m[0],))
+
+    return pl.pallas_call(
+        own_slope_kernel,
+        grid_spec=pltpu.PrefetchScalarGridSpec(
+            num_scalar_prefetch=3,
+            grid=(1,),
+            in_specs=[
+                pl.BlockSpec((2, short, half), lambda i, m, o, b: (m[0], 0, 0)),
+                mine(2, rows, half),
+                mine(16, half),
+                mine(3, half),
+            ],
+            out_specs=[whole(32, half), whole(2, tall, half), whole(2, tall, half)],
+            scratch_shapes=[pltpu.VMEM((2, tall, 256), F32)],
+        ),
+        out_shape=[
+            jax.ShapeDtypeStruct((32, half), BF),
+            jax.ShapeDtypeStruct((2, tall, half), BF),
+            jax.ShapeDtypeStruct((2, tall, half), F32),
+        ],
+        compiler_params=params(),
+        cost_estimate=cost(3 * 10**9, 10**6),
+        name="own_slopes",
+    )(meta, offsets, bins, attention, skip, edge, filt)
+
+
 def own_kernel(
-    slabs, meta, offsets, bins, att, skip, edge, rims, prev, cot, weight,
-    filt, moved, asked, terms, skip_grad, att_grad, ext, pair,
+    slabs, meta, offsets, sums, slopes, rims, prev_far, cot_far, weight_far, filt,
+    moved, terms, skip_grad, att_grad, pair, prev, cot, weight, sems,
 ):
-    rows = skip.shape[1]
-    tall = rows + 2 * PAD
+    copies = [
+        pltpu.make_async_copy(prev_far, prev, sems.at[0]),
+        pltpu.make_async_copy(cot_far, cot, sems.at[1]),
+        pltpu.make_async_copy(weight_far, weight, sems.at[2]),
+    ]
+    for copy in copies:
+        copy.start()
+    half = sums.shape[2]
+    tall = sums.shape[1]
+    rows = tall - 2 * PAD
     wide = cot.shape[2]
     row, col = grid_of(tall, rows)
     last = meta[1] == slabs - 1
+    copies[0].wait()
+    copies[1].wait()
     for s in range(2):
         at = row - PAD
         fits = (at >= -1) & (at < jnp.where(last, rows, rows + 1))
@@ -388,87 +628,80 @@
                 ]
             )
             moved[s, :, cols] = found.astype(BF)
-    width = ext.shape[2]
-    half = skip.shape[2]
+    copies[2].wait()
+    width = 2 * LANES
     first = meta[0] * half
 
     @pl.loop(0, half // width)
     def _(part):
         begin = pl.multiple_of(part * width, width)
         cols = pl.ds(begin, width)
-        slab_sums(att, skip, edge, edge, ext, cols)
         taps = taps_of(filt, cols)
         piece = weight[pl.ds(begin, width), :]
-        sums = [0.0, 0.0, 0.0]
+        total_terms = [0.0, 0.0, 0.0]
         there = pl.ds(pl.multiple_of(first + begin, width), width)
         for s in range(2):
-            field = ext[s]
-            before, after = around(field)
-            slope = slope_of(taps[0] * before + taps[1] * field + taps[2] * after)
-            asked[s * 16 : s * 16 + 16, cols] = asked_rows(
-                meta, offsets, bins, s, field, taps, tall
-            )
-            conv = (dot_rows(moved[s], piece) * slope).astype(BF).astype(F32)
-            sums = [a + b for a, b in zip(sums, tap_sums(conv, field, rows))]
+            conv = (dot_rows(moved[s], piece) * slopes[s, :, cols]).astype(BF).astype(F32)
+            got = tap_sums(conv, sums[s, :, cols].astype(F32), rows)
+            total_terms = [a + b for a, b in zip(total_terms, got)]
             direct = moved[s, :, there].astype(F32)[PAD : PAD + rows]
             total, pairs = grads(conv, direct, taps, rows, pair)
             skip_grad[s, :, cols] = total.astype(BF)
             att_grad[s, :, cols] = pairs.astype(BF)
         for k in range(3):
-            terms[k : k + 1, cols] = sums[k]
-
-
-def own_half(meta, offsets, bins, attention, skip, edge, prev, cot, weight, filt, slabs):
-    seqs, rows, wide = skip.shape
-    _, short, half = attention.shape
-    tall = rows + 2 * PAD
+            terms[k : k + 1, cols] = total_terms[k]
+
+
+def own_half(meta, offsets, sums, slopes, edge, prev, cot, weight, filt, slabs):
+    seqs, rows, wide = cot.shape
+    _, tall, half = sums.shape
+    short = rows // 2
 
     def whole(*shape):
-        return pl.BlockSpec(shape, lambda i, m, o, b: (0,) * len(shape))
+        return pl.BlockSpec(shape, lambda i, m, o: (0,) * len(shape))
 
     def mine(*shape):
-        return pl.BlockSpec(shape, lambda i, m, o, b: (0,) * (len(shape) - 1) + (m[0],))
-
+        return pl.BlockSpec(shape, lambda i, m, o: (0,) * (len(shape) - 1) + (m[0],))
+
+    anywhere = pl.BlockSpec(memory_space=pl.ANY)
     return pl.pallas_call(
         functools.partial(own_kernel, slabs),
         grid_spec=pltpu.PrefetchScalarGridSpec(
-            num_scalar_prefetch=3,
+            num_scalar_prefetch=2,
             grid=(1,),
             in_specs=[
-                pl.BlockSpec((2, short, half), lambda i, m, o, b: (m[0], 0, 0)),
-                mine(2, rows, half),
-                mine(16, half),
+                whole(2, tall, half),
+                whole(2, tall, half),
                 whole(16, wide),
-                whole(2, rows, wide),
-                whole(2, rows, wide),
-                whole(half, wide),
+                anywhere,
+                anywhere,
+                anywhere,
                 mine(3, half),
             ],
             out_specs=[
                 whole(2, tall, wide),
-                whole(32, half),
                 whole(3, half),
                 mine(2, rows, half),
                 mine(2, short, half),
             ],
             scratch_shapes=[
-                pltpu.VMEM((2, tall, 256), F32),
                 pltpu.VMEM((2, rows, LANES), F32),
+                pltpu.VMEM((2, rows, wide), BF),
+                pltpu.VMEM((2, rows, wide), BF),
+                pltpu.VMEM((half, wide), BF),
+                pltpu.SemaphoreType.DMA((3,)),
             ],
         ),
         out_shape=[
             jax.ShapeDtypeStruct((2, tall, wide), BF),
-            jax.ShapeDtypeStruct((32, half), BF),
             jax.ShapeDtypeStruct((3, half), F32),
             jax.ShapeDtypeStruct((2, rows, wide), BF),
             jax.ShapeDtypeStruct((2, short, wide), BF),
         ],
-        compiler_params=params(60),
+        compiler_params=params(),
         cost_estimate=cost(1, 1),
         name="own_half",
-    )(
-        meta, offsets, bins, attention, skip, edge, edge, prev, cot, weight, filt,
-    )
+    )(meta, offsets, sums, slopes, edge, prev, cot, weight, filt)
 
 
 def slope_kernel(
@@ -540,7 +773,7 @@
             jax.ShapeDtypeStruct((16, wide), BF),
         ],
         compiler_params=params(),
-        cost_estimate=cost(10**11, 4 * 1024 * 1024, 2 * tall * half),
+        cost_estimate=cost(3 * 10**9, 10**6),
         name="other_slopes",
     )(meta, offsets, bins, shipped, skip, edge, twin, filt, asked)
 
@@ -752,13 +985,13 @@
     edge_a, edge_b, far, first, last_tile, att_out = packed(
         meta, encoder_skip, attention, cotangent, point_weight, tile
     )
-    prev = passed_along(cotangent, "seq", 1)
     first = paired(first, "head", 1)
     shipped = paired(att_out, "head", 1)
     edge_a = paired(edge_a, "seq", 1)
     edge_b = staggered(edge_b, 1)
     far_a = paired(far, "seq", 2)
     far_b = staggered(far, 2)
+    prev = passed_along(after(cotangent, edge_a, edge_b, far_a, far_b), "seq", 1)
     outer = (slab == 0) | (slab == slabs - 1)
     nothing = jnp.zeros_like(edge_b)
     edge = edge_a + jnp.where(outer, nothing, edge_b)
@@ -767,16 +1000,19 @@
     second = paired(first, "seq", 2)
     third = paired(first, "seq", 4)
     fourth = paired(last_tile, "head", 1)
-    moved, asked, own_terms, skip_grad, att_grad = own_half(
-        meta, crop_offset, target_bins, attention, encoder_skip, edge, prev, cotangent,
-        point_weight, depth_filter, slabs,
+    asked, own_sums, own_slope = own_slopes(
+        meta, crop_offset, target_bins, attention, encoder_skip, edge, depth_filter
+    )
+    sums, slopes, mine, shown = other_slopes(
+        meta, crop_offset, target_bins, shipped, encoder_skip, edge, twin, depth_filter, asked
+    )
+    got = [paired(shown, "seq", 1), staggered(shown, 1)]
+    moved, own_terms, skip_grad, att_grad = own_half(
+        after(meta, shown), crop_offset, own_sums, own_slope, edge, prev, cotangent, point_weight, depth_filter,
+        slabs,
     )
     pieces = [first, second, third, fourth]
     pieces = pieces + [paired(after(piece, own_terms), "seq", 1) for piece in pieces]
-    sums, slopes, mine, shown = other_slopes(
-        meta, crop_offset, target_bins, shipped, encoder_skip, edge, twin, depth_filter, asked
-    )
-    got = [paired(shown, "seq", 1), staggered(shown, 1)]
     convs, terms = other_terms(meta, order, moved, sums, slopes, own_terms, pieces)
     terms, *got = lax.optimization_barrier((terms, *got))
     total = terms + crossed(terms, 1, 0)
@@ -823,3 +1059,15 @@
     )
     out_specs = (P("head", "seq", None), P("head", "seq", None), P("head", "seq", None), P())
     return jax.shard_map(shards, mesh=mesh, in_specs=in_specs, out_specs=out_specs, check_vma=False)
+def solution(mesh):
+    in_specs = (
+        P(None, "seq", "head"),
+        P("head", "seq", None),
+        P(),
+        P("head", None),
+        P("head"),
+        P("head", None),
+        P("head", "seq", None),
+    )
+    out_specs = (P("head", "seq", None), P("head", "seq", None), P("head", "seq", None), P())
+    return jax.shard_map(shards, mesh=mesh, in_specs=in_specs, out_specs=out_specs, check_vma=False)

time: 63.5 us -> 64.6 us (1.017)
  starting transfers between devices: 34.2 us -> 25.5 us
  waiting for transfers between devices: 5.54 us -> 10.4 us
  local copies, waits for them, and re-layouts: 0.92 us -> 4.37 us
  Pallas kernels: 19.8 us -> 21.8 us
    ppermute x3, starting transfers between devices: 13.3 us -> 7.87 us  [staggered(): return lax.ppermute(part, 'seq', pairs)]
    ppermute x13, waiting for transfers between devices: 0.03 us -> 4.59 us  [paired(): return lax.ppermute(part, axis, [(i, i ^ bit) for i in range(count)])]
    unnamed x22 -> x32, local copies, waits for them, and re-layouts: 0.84 us -> 4.29 us
    ppermute x3, waiting for transfers between devices: 0.34 us -> 3.64 us  [staggered(): return lax.ppermute(part, 'seq', pairs)]
    ppermute x7, waiting for transfers between devices: 5.16 us -> 2.21 us  [crossed(): return lax.ppermute(part, ('seq', 'head'), pairs)]
    pallas_call x1, Pallas kernels: 7.61 us -> 4.94 us  [own_half(): pl.pallas_call(functools.partial(own_kernel, slabs), grid_spec=pltpu.Pref...]
    pallas_call x0 -> x1, Pallas kernels: none -> 2.13 us  [own_slopes(): pl.pallas_call(own_slope_kernel, grid_spec=pltpu.PrefetchScalarGridSpec(n...]
    pallas_call x1, Pallas kernels: 1.93 us -> 3.25 us  [targets(): pl.pallas_call(functools.partial(target_kernel, slabs), grid_spec=pltpu.P...]
  transfers between devices with their start and end apart: 24 -> 24, of which waited for: 5 -> 7; matrix products, arithmetic and copies ran while one was open for 2% -> 0% of each run, Pallas kernels for 31% -> 29%
where the time goes in v6:
time: 64.6 us; the launch traced here: 64.3 us
  starting transfers between devices  25.5 us (39%)
  Pallas kernels  21.8 us (34%)
  waiting for transfers between devices  10.4 us (16%)
  local copies, waits for them, and re-layouts  4.37 us (7%)
  other arithmetic  1.27 us (2%)
  between operations  0.88 us (1%)
    ppermute x13, starting transfers between devices, paired(): return lax.ppermute(part, axis, [(i, i ^ bit) for i in range(count)])  9.17 us
    ppermute x3, starting transfers between devices, staggered(): return lax.ppermute(part, 'seq', pairs)  7.87 us
    ppermute x7, starting transfers between devices, crossed(): return lax.ppermute(part, ('seq', 'head'), pairs)  7.17 us
    pallas_call x1, Pallas kernels, own_half(): pl.pallas_call(functools.partial(own_kernel, slabs), grid_spec=pltpu.Pref...  4.94 us
    ppermute x13, waiting for transfers between devices, paired(): return lax.ppermute(part, axis, [(i, i ^ bit) for i in range(count)])  4.59 us
    unnamed x32, local copies, waits for them, and re-layouts  4.29 us
    pallas_call x1, Pallas kernels, other_terms(): pl.pallas_call(terms_kernel, grid_spec=pltpu.PrefetchScalarGridSpec(num_s...  3.77 us
    ppermute x3, waiting for transfers between devices, staggered(): return lax.ppermute(part, 'seq', pairs)  3.64 us
  transfers between devices with their start and end apart: 24, of which 7 were waited for; matrix products, arithmetic and copies ran while one was open for 0% of the time, Pallas kernels for 29%

profile of v6, /device:TPU:0, one launch (start us, length us, event | category | flops | bytes accessed | tf_op | source)
XLA Modules:
  0.0 64.3 jit_solution(15413569858045597334)
XLA Ops:
  1.3 3.2 %pack_edges.1 = (bf16[16,1536]{1,0:T(8,128)(2,1)}, bf16[16,1536]{1,0:T(8,128)(2,1)}, bf16[16,1536]{1,0:T(8,128)(2,1)}, bf16[384,384]{1,0:T(8,128)(2,1)}, bf16[38...) custom-call(s32[2]{0:T(128)} %pad_add_fusion.meta, bf16[2,128,1536]{2,1,0:T(8,128)(2,1)} %skip.3, ...), custom_call_target="tpu_custom_call" | custom-call | tf_op jit(solution)/shard_map/pack_edges/pallas_call | solution.py:425
  4.5 2.9 %collective-permute-start.3 = (bf16[16,1536]{1,0:T(8,128)(2,1)}, bf16[16,1536]{1,0:T(8,128)(2,1)S(1)}, u32[]{:S(2)}, u32[]{:S(2)}) collective-permute-start(bf16[16,1536]{1,0:T(8,128)(2,1)} %get-tuple-element.40), channel_id=1, source_target_pairs={{0,4},{2,6},{4,0},{6,2},{8,12},{10,14},{12,8},{14,10},{16,20},{18,... | collective-permute-start | bytes 147464 | tf_op jit(solution)/shard_map/ppermute | solution.py:941
  7.5 3.6 %collective-permute-start.4 = (bf16[16,1536]{1,0:T(8,128)(2,1)}, bf16[16,1536]{1,0:T(8,128)(2,1)S(1)}, u32[]{:S(2)}, u32[]{:S(2)}) collective-permute-start(bf16[16,1536]{1,0:T(8,128)(2,1)} %get-tuple-element.40), channel_id=1, source_target_pairs={{0,28},{2,30},{4,8},{6,10},{8,4},{10,6},{12,16},{14,18},{16,12},{1... | collective-permute-start | bytes 147464 | tf_op jit(solution)/shard_map/ppermute | solution.py:950
  11.0 1.3 %collective-permute-start.2 = (bf16[16,1536]{1,0:T(8,128)(2,1)}, bf16[16,1536]{1,0:T(8,128)(2,1)S(1)}, u32[]{:S(2)}, u32[]{:S(2)}) collective-permute-start(bf16[16,1536]{1,0:T(8,128)(2,1)} %get-tuple-element.39), channel_id=1, source_target_pairs={{0,30},{2,4},{4,2},{6,8},{8,6},{10,12},{12,10},{14,16},{16,14},{18... | collective-permute-start | bytes 147464 | tf_op jit(solution)/shard_map/ppermute | solution.py:950
  12.3 1.5 %collective-permute-start.7 = (bf16[384,384]{1,0:T(8,128)(2,1)}, bf16[384,384]{1,0:T(8,128)(2,1)S(1)}, u32[]{:S(2)}, u32[]{:S(2)}) collective-permute-start(bf16[384,384]{1,0:T(8,128)(2,1)} %get-tuple-element.52), channel_id=1, source_target_pairs={{0,1},{1,0},{2,3},{3,2},{4,5},{5,4},{6,7},{7,6},{8,9},{9,8},{10,11... | collective-permute-start | bytes 884744 | tf_op jit(solution)/shard_map/ppermute | solution.py:941
  14.5 3.0 %collective-permute-done.2 = bf16[16,1536]{1,0:T(8,128)(2,1)S(1)} collective-permute-done((bf16[16,1536]{1,0:T(8,128)(2,1)}, bf16[16,1536]{1,0:T(8,128)(2,1)S(1)}, u32[]{:S(2)}, u32[]{:S(2)}) %collective-permute-start.2) | collective-permute-done | bytes 49184 | tf_op jit(solution)/shard_map/ppermute | solution.py:950
  17.5 1.3 %collective-permute-start.6 = (bf16[2,128,1536]{2,1,0:T(8,128)(2,1)S(1)}, bf16[2,128,1536]{2,1,0:T(8,128)(2,1)S(1)}, u32[]{:S(2)}, u32[]{:S(2)}) collective-permute-start(bf16[2,128,1536]{2,1,0:T(8,128)(2,1)S(1)} %copy-done.1), channel_id=1, source_target_pairs={{0,2},{2,4},{4,6},{6,8},{8,10},{10,12},{12,14},{14,16},{16,18},{18... | collective-permute-start | bytes 2359304 | tf_op jit(solution)/shard_map/ppermute | solution.py:204
  18.8 1.6 %collective-permute-start.5 = (bf16[16,1536]{1,0:T(8,128)(2,1)S(1)}, bf16[16,1536]{1,0:T(8,128)(2,1)S(1)}, u32[]{:S(2)}, u32[]{:S(2)}) collective-permute-start(bf16[16,1536]{1,0:T(8,128)(2,1)S(1)} %get-tuple-element.71), channel_id=1, source_target_pairs={{0,1},{1,0},{2,3},{3,2},{4,5},{5,4},{6,7},{7,6},{8,9},{9,8},{10,11... | collective-permute-start | bytes 147464 | tf_op jit(solution)/shard_map/ppermute | solution.py:941
  20.9 1.5 %collective-permute-start.10 = (bf16[384,384]{1,0:T(8,128)(2,1)}, bf16[384,384]{1,0:T(8,128)(2,1)}, u32[]{:S(2)}, u32[]{:S(2)}) collective-permute-start(bf16[384,384]{1,0:T(8,128)(2,1)} %get-tuple-element.53), channel_id=1, source_target_pairs={{0,1},{1,0},{2,3},{3,2},{4,5},{5,4},{6,7},{7,6},{8,9},{9,8},{10,11... | collective-permute-start | bytes 884744 | tf_op jit(solution)/shard_map/ppermute | solution.py:941
  23.6 2.1 %own_slopes.1 = (bf16[32,768]{1,0:T(8,128)(2,1)S(1)}, bf16[2,144,768]{2,1,0:T(8,128)(2,1)S(1)}, f32[2,144,768]{2,1,0:T(8,128)S(1)}) custom-call(s32[2]{0:T(128)S(1)} %copy-done.12, s32[2]{0:T(128)S(1)} %copy-done.13, s32[2,32]{1,0:T(2,128)S(1)} %copy-done.15, bf16[4,64,768]{2,1,0:T(8,128)(2,1)S(1)} %copy-done.2, bf16[2,128,1536]{2,1,0:T(8,128)(2,1)S(1)} %copy-done.5, ...), custom_call_target="tpu_custom_call" | custom-call | flops 3000000000 | bytes 1000000 | tf_op jit(solution)/shard_map/own_slopes/pallas_call | solution.py:564
  25.7 2.8 %collective-permute-done.att = bf16[2,64,768]{2,1,0:T(8,128)(2,1)S(1)} collective-permute-done((bf16[2,64,768]{2,1,0:T(8,128)(2,1)}, bf16[2,64,768]{2,1,0:T(8,128)(2,1)S(1)}, u32[]{:S(2)}, u32[]{:S(2)}) %collective-permute-start) | collective-permute-done | bytes 196640 | tf_op jit(solution)/shard_map/ppermute | solution.py:941
  28.5 2.6 %other_slopes.1 = (bf16[2,144,768]{2,1,0:T(8,128)(2,1)S(1)}, f32[2,144,768]{2,1,0:T(8,128)S(1)}, bf16[16,1536]{1,0:T(8,128)(2,1)S(1)}, bf16[16,1536]{1,0:T(8,128)(2,1)S(1)}) custom-call(s32[2]{0:T(128)S(1)} %copy-done.12, s32[2]{0:T(128)S(1)} %copy-done.13, s32[2,32]{1,0:T(2,128)S(1)} %copy-done.15, bf16[2,64,768]{2,1,0:T(8,128)(2,1)S(1)} %collective-permute-done.att, ...), custom_call_target="tpu_custom_call" | custom-call | flops 3000000000 | bytes 1000000 | tf_op jit(solution)/shard_map/other_slopes/pallas_call | solution.py:753
  31.1 4.9 %own_half.1 = (bf16[2,144,1536]{2,1,0:T(8,128)(2,1)S(1)}, f32[3,768]{1,0:T(4,128)S(1)}, bf16[2,128,1536]{2,1,0:T(8,128)(2,1)}, bf16[2,64,1536]{2,1,0:T(8,128)(2,1)}) custom-call(s32[2]{0:T(128)S(1)} %copy-done.12, s32[2]{0:T(128)S(1)} %copy-done.13, bf16[2,144,768]{2,1,0:T(8,128)(2,1)S(1)} %get-tuple-element.45.sums, ...), custom_call_target="tpu_custom_call" | custom-call | flops 1 | bytes 1 | tf_op jit(solution)/shard_map/own_half/pallas_call | solution.py:667
  38.9 3.0 %collective-permute-start.16 = (bf16[16,1536]{1,0:T(8,128)(2,1)}, bf16[16,1536]{1,0:T(8,128)(2,1)S(1)}, u32[]{:S(2)}, u32[]{:S(2)}) collective-permute-start(bf16[16,1536]{1,0:T(8,128)(2,1)} %copy-done.14), channel_id=1, source_target_pairs={{0,30},{2,4},{4,2},{6,8},{8,6},{10,12},{12,10},{14,16},{16,14},{18... | collective-permute-start | bytes 147464 | tf_op jit(solution)/shard_map/ppermute | solution.py:950
  42.0 1.2 %copy-done.4 = bf16[2,144,1536]{2,1,0:T(8,128)(2,1)S(1)} copy-done((bf16[2,144,1536]{2,1,0:T(8,128)(2,1)S(1)}, bf16[2,144,1536]{2,1,0:T(8,128)(2,1)}, u32[]{:S(2)}) %copy-start.4) | copy-done | bytes 884760
  43.1 1.2 %copy-done.8 = f32[2,144,768]{2,1,0:T(8,128)S(1)} copy-done((f32[2,144,768]{2,1,0:T(8,128)S(1)}, f32[2,144,768]{2,1,0:T(8,128)}, u32[]{:S(2)}) %copy-start.8) | copy-done | bytes 884760
  45.3 3.8 %other_terms.1 = (bf16[2,144,768]{2,1,0:T(8,128)(2,1)S(1)}, f32[3,1536]{1,0:T(4,128)S(1)}) custom-call(s32[2]{0:T(128)S(1)} %copy-done.12, s32[6]{0:T(128)S(1)} %stack.39.order, bf16[2,144,1536]{2,1,0:T(8,128)(2,1)S(1)} %copy-done.4, bf16[2,144,768]{2,1,0:T(8,128)(2,1)S(1)} %copy-done.10, f32[2,144,768]{2,1,0:T(8,128)S(1)} %copy-done.8, ...), custom_call_target="tpu_custom_call" | custom-call | flops 679477248 | bytes 6291456 | tf_op jit(solution)/shard_map/other_terms/pallas_call | solution.py:823
  49.2 1.2 %collective-permute-done.17 = f32[3,1536]{1,0:T(4,128)S(1)} collective-permute-done((f32[3,1536]{1,0:T(4,128)S(1)}, f32[3,1536]{1,0:T(4,128)S(1)}, u32[]{:S(2)}, u32[]{:S(2)}) %collective-permute-start.17) | collective-permute-done | bytes 18464 | tf_op jit(solution)/shard_map/ppermute | solution.py:964
  50.4 1.7 %collective-permute-start.19 = (f32[3,1536]{1,0:T(4,128)S(1)}, f32[3,1536]{1,0:T(4,128)S(1)}, u32[]{:S(2)}, u32[]{:S(2)}) collective-permute-start(f32[3,1536]{1,0:T(4,128)S(1)} %add.43), channel_id=1, source_target_pairs={{0,1},{1,0},{2,3},{3,2},{4,5},{5,4},{6,7},{7,6},{8,9},{9,8},{10,11... | collective-permute-start | bytes 55304 | tf_op jit(solution)/shard_map/ppermute | solution.py:964
  52.1 1.9 %collective-permute-start.18 = (f32[3,1536]{1,0:T(4,128)S(1)}, f32[3,1536]{1,0:T(4,128)S(1)}, u32[]{:S(2)}, u32[]{:S(2)}) collective-permute-start(f32[3,1536]{1,0:T(4,128)S(1)} %add.43), channel_id=1, source_target_pairs={{0,4},{1,5},{2,6},{3,7},{4,0},{5,1},{6,2},{7,3},{8,12},{9,13},{10,... | collective-permute-start | bytes 55304 | tf_op jit(solution)/shard_map/ppermute | solution.py:964
  53.9 1.8 %other_grads.1 = (bf16[2,128,1536]{2,1,0:T(8,128)(2,1)}, bf16[2,64,1536]{2,1,0:T(8,128)(2,1)}) custom-call(s32[2]{0:T(128)S(1)} %copy-done.12, bf16[2,144,1536]{2,1,0:T(8,128)(2,1)S(1)} %copy-done.4, bf16[2,144,768]{2,1,0:T(8,128)(2,1)S(1)} %get-tuple-element.62.convs, f32[3,1536]{1,0:T(4,128)S(1)} %copy-done.11, ...), custom_call_target="tpu_custom_call", output_to_operand_aliasing={{0}: (4, {}), {1}: (5, {})} | custom-call | flops 4423680 | bytes 4194304 | tf_op jit(solution)/shard_map/other_grads/pallas_call | solution.py:875
  56.9 1.1 %collective-permute-start.23 = (f32[3,1536]{1,0:T(4,128)S(1)}, f32[3,1536]{1,0:T(4,128)S(1)}, u32[]{:S(2)}, u32[]{:S(2)}) collective-permute-start(f32[3,1536]{1,0:T(4,128)S(1)} %add_add_fusion), channel_id=1, source_target_pairs={{0,24},{1,25},{2,26},{3,27},{4,28},{5,29},{6,30},{7,31},{8,16},{9,... | collective-permute-start | bytes 55304 | tf_op jit(solution)/shard_map/ppermute | solution.py:964
  58.0 2.3 %collective-permute-start.21 = (f32[3,1536]{1,0:T(4,128)S(1)}, f32[3,1536]{1,0:T(4,128)S(1)}, u32[]{:S(2)}, u32[]{:S(2)}) collective-permute-start(f32[3,1536]{1,0:T(4,128)S(1)} %add_add_fusion), channel_id=1, source_target_pairs={{0,8},{1,9},{2,10},{3,11},{4,12},{5,13},{6,14},{7,15},{8,0},{9,1},... | collective-permute-start | bytes 55304 | tf_op jit(solution)/shard_map/ppermute | solution.py:964
  60.4 3.2 %targets.1 = bf16[2,2,1536]{2,1,0:T(2,128)(2,1)} custom-call(s32[2]{0:T(128)S(1)} %copy-done.12, s32[6]{0:T(128)S(1)} %stack.39.order, bf16[16,1536]{1,0:T(8,128)(2,1)S(1)} %get-tuple-element.42.mine, bf16[16,1536]{1,0:T(8,128)(2,1)S(1)} %collective-permute-done.15.got_a, bf16[16,1536]{1,0:T(8,128)(2,1)S(1)} %collective-permute-done.16.got_b, ...), custom_call_target="tpu_custom_call" | custom-call | flops 75497472 | bytes 6291456 | tf_op jit(solution)/shard_map/targets/pallas_call | solution.py:922
  (69 shorter events, 8.6 us)
Async XLA Ops:
  4.5 9.3 %collective-permute-start.3 = (bf16[16,1536]{1,0:T(8,128)(2,1)}, bf16[16,1536]{1,0:T(8,128)(2,1)S(1)}, u32[]{:S(2)}, u32[]{:S(2)}) collective-permute-start(bf16[16,1536]{1,0:T(8,128)(2,1)} %get-tuple-element.40), channel_id=1, source_target_pairs={{0,4},{2,6},{4,0},{6,2},{8,12},{10,14},{12,8},{14,10},{16,20},{18,... | collective-permute-start | bytes 147464 | tf_op jit(solution)/shard_map/ppermute | solution.py:941
  7.5 7.0 %collective-permute-start.4 = (bf16[16,1536]{1,0:T(8,128)(2,1)}, bf16[16,1536]{1,0:T(8,128)(2,1)S(1)}, u32[]{:S(2)}, u32[]{:S(2)}) collective-permute-start(bf16[16,1536]{1,0:T(8,128)(2,1)} %get-tuple-element.40), channel_id=1, source_target_pairs={{0,28},{2,30},{4,8},{6,10},{8,4},{10,6},{12,16},{14,18},{16,12},{1... | collective-permute-start | bytes 147464 | tf_op jit(solution)/shard_map/ppermute | solution.py:950
  11.0 3.4 %collective-permute-start.1 = (bf16[16,1536]{1,0:T(8,128)(2,1)}, bf16[16,1536]{1,0:T(8,128)(2,1)S(1)}, u32[]{:S(2)}, u32[]{:S(2)}) collective-permute-start(bf16[16,1536]{1,0:T(8,128)(2,1)} %get-tuple-element.38), channel_id=1, source_target_pairs={{0,2},{2,0},{4,6},{6,4},{8,10},{10,8},{12,14},{14,12},{16,18},{18,... | collective-permute-start | bytes 147464 | tf_op jit(solution)/shard_map/ppermute | solution.py:941
  11.0 6.4 %collective-permute-start.2 = (bf16[16,1536]{1,0:T(8,128)(2,1)}, bf16[16,1536]{1,0:T(8,128)(2,1)S(1)}, u32[]{:S(2)}, u32[]{:S(2)}) collective-permute-start(bf16[16,1536]{1,0:T(8,128)(2,1)} %get-tuple-element.39), channel_id=1, source_target_pairs={{0,30},{2,4},{4,2},{6,8},{8,6},{10,12},{12,10},{14,16},{16,14},{18... | collective-permute-start | bytes 147464 | tf_op jit(solution)/shard_map/ppermute | solution.py:950
  12.3 10.1 %collective-permute-start.7 = (bf16[384,384]{1,0:T(8,128)(2,1)}, bf16[384,384]{1,0:T(8,128)(2,1)S(1)}, u32[]{:S(2)}, u32[]{:S(2)}) collective-permute-start(bf16[384,384]{1,0:T(8,128)(2,1)} %get-tuple-element.52), channel_id=1, source_target_pairs={{0,1},{1,0},{2,3},{3,2},{4,5},{5,4},{6,7},{7,6},{8,9},{9,8},{10,11... | collective-permute-start | bytes 884744 | tf_op jit(solution)/shard_map/ppermute | solution.py:941
  17.5 13.6 %collective-permute-start.6 = (bf16[2,128,1536]{2,1,0:T(8,128)(2,1)S(1)}, bf16[2,128,1536]{2,1,0:T(8,128)(2,1)S(1)}, u32[]{:S(2)}, u32[]{:S(2)}) collective-permute-start(bf16[2,128,1536]{2,1,0:T(8,128)(2,1)S(1)} %copy-done.1), channel_id=1, source_target_pairs={{0,2},{2,4},{4,6},{6,8},{8,10},{10,12},{12,14},{14,16},{16,18},{18... | collective-permute-start | bytes 2359304 | tf_op jit(solution)/shard_map/ppermute | solution.py:204
  18.8 4.7 %collective-permute-start.5 = (bf16[16,1536]{1,0:T(8,128)(2,1)S(1)}, bf16[16,1536]{1,0:T(8,128)(2,1)S(1)}, u32[]{:S(2)}, u32[]{:S(2)}) collective-permute-start(bf16[16,1536]{1,0:T(8,128)(2,1)S(1)} %get-tuple-element.71), channel_id=1, source_target_pairs={{0,1},{1,0},{2,3},{3,2},{4,5},{5,4},{6,7},{7,6},{8,9},{9,8},{10,11... | collective-permute-start | bytes 147464 | tf_op jit(solution)/shard_map/ppermute | solution.py:941
  20.4 8.1 %collective-permute-start = (bf16[2,64,768]{2,1,0:T(8,128)(2,1)}, bf16[2,64,768]{2,1,0:T(8,128)(2,1)S(1)}, u32[]{:S(2)}, u32[]{:S(2)}) collective-permute-start(bf16[2,64,768]{2,1,0:T(8,128)(2,1)} %get-tuple-element.37), channel_id=1, source_target_pairs={{0,1},{1,0},{2,3},{3,2},{4,5},{5,4},{6,7},{7,6},{8,9},{9,8},{10,11... | collective-permute-start | bytes 589832 | tf_op jit(solution)/shard_map/ppermute | solution.py:941
  20.9 16.7 %collective-permute-start.10 = (bf16[384,384]{1,0:T(8,128)(2,1)}, bf16[384,384]{1,0:T(8,128)(2,1)}, u32[]{:S(2)}, u32[]{:S(2)}) collective-permute-start(bf16[384,384]{1,0:T(8,128)(2,1)} %get-tuple-element.53), channel_id=1, source_target_pairs={{0,1},{1,0},{2,3},{3,2},{4,5},{5,4},{6,7},{7,6},{8,9},{9,8},{10,11... | collective-permute-start | bytes 884744 | tf_op jit(solution)/shard_map/ppermute | solution.py:941
  22.4 14.6 %collective-permute-start.8 = (bf16[384,384]{1,0:T(8,128)(2,1)S(1)}, bf16[384,384]{1,0:T(8,128)(2,1)}, u32[]{:S(2)}, u32[]{:S(2)}) collective-permute-start(bf16[384,384]{1,0:T(8,128)(2,1)S(1)} %collective-permute-done.7.refs_0_), channel_id=1, source_target_pairs={{0,4},{2,6},{4,0},{6,2},{8,12},{10,14},{12,8},{14,10},{16,20},{18,... | collective-permute-start | bytes 884744 | tf_op jit(solution)/shard_map/ppermute | solution.py:941
  23.5 14.0 %collective-permute-start.9 = (bf16[384,384]{1,0:T(8,128)(2,1)S(1)}, bf16[384,384]{1,0:T(8,128)(2,1)}, u32[]{:S(2)}, u32[]{:S(2)}) collective-permute-start(bf16[384,384]{1,0:T(8,128)(2,1)S(1)} %collective-permute-done.7.refs_0_), channel_id=1, source_target_pairs={{0,8},{2,10},{4,12},{6,14},{8,0},{10,2},{12,4},{14,6},{16,24},{18,... | collective-permute-start | bytes 884744 | tf_op jit(solution)/shard_map/ppermute | solution.py:941
  37.0 1.9 %collective-permute-start.11 = (bf16[384,384]{1,0:T(8,128)(2,1)S(1)}, bf16[384,384]{1,0:T(8,128)(2,1)S(1)}, u32[]{:S(2)}, u32[]{:S(2)}) collective-permute-start(bf16[384,384]{1,0:T(8,128)(2,1)S(1)} %collective-permute-done.7.refs_0_), channel_id=1, source_target_pairs={{0,2},{2,0},{4,6},{6,4},{8,10},{10,8},{12,14},{14,12},{16,18},{18,... | collective-permute-start | bytes 884744 | tf_op jit(solution)/shard_map/ppermute | solution.py:941
  37.0 5.0 %collective-permute-start.12 = (bf16[384,384]{1,0:T(8,128)(2,1)}, bf16[384,384]{1,0:T(8,128)(2,1)S(1)}, u32[]{:S(2)}, u32[]{:S(2)}) collective-permute-start(bf16[384,384]{1,0:T(8,128)(2,1)} %collective-permute-done.8.refs_1_), channel_id=1, source_target_pairs={{0,2},{2,0},{4,6},{6,4},{8,10},{10,8},{12,14},{14,12},{16,18},{18,... | collective-permute-start | bytes 884744 | tf_op jit(solution)/shard_map/ppermute | solution.py:941
  37.5 4.5 %collective-permute-start.13 = (bf16[384,384]{1,0:T(8,128)(2,1)}, bf16[384,384]{1,0:T(8,128)(2,1)}, u32[]{:S(2)}, u32[]{:S(2)}) collective-permute-start(bf16[384,384]{1,0:T(8,128)(2,1)} %collective-permute-done.9.refs_2_), channel_id=1, source_target_pairs={{0,2},{2,0},{4,6},{6,4},{8,10},{10,8},{12,14},{14,12},{16,18},{18,... | collective-permute-start | bytes 884744 | tf_op jit(solution)/shard_map/ppermute | solution.py:941
  37.6 4.4 %collective-permute-start.14 = (bf16[384,384]{1,0:T(8,128)(2,1)}, bf16[384,384]{1,0:T(8,128)(2,1)}, u32[]{:S(2)}, u32[]{:S(2)}) collective-permute-start(bf16[384,384]{1,0:T(8,128)(2,1)} %collective-permute-done.10.refs_3_), channel_id=1, source_target_pairs={{0,2},{2,0},{4,6},{6,4},{8,10},{10,8},{12,14},{14,12},{16,18},{18,... | collective-permute-start | bytes 884744 | tf_op jit(solution)/shard_map/ppermute | solution.py:941
  38.1 11.0 %collective-permute-start.15 = (bf16[16,1536]{1,0:T(8,128)(2,1)}, bf16[16,1536]{1,0:T(8,128)(2,1)S(1)}, u32[]{:S(2)}, u32[]{:S(2)}) collective-permute-start(bf16[16,1536]{1,0:T(8,128)(2,1)} %copy-done.14), channel_id=1, source_target_pairs={{0,2},{2,0},{4,6},{6,4},{8,10},{10,8},{12,14},{14,12},{16,18},{18,... | collective-permute-start | bytes 147464 | tf_op jit(solution)/shard_map/ppermute | solution.py:941
  38.9 10.2 %collective-permute-start.16 = (bf16[16,1536]{1,0:T(8,128)(2,1)}, bf16[16,1536]{1,0:T(8,128)(2,1)S(1)}, u32[]{:S(2)}, u32[]{:S(2)}) collective-permute-start(bf16[16,1536]{1,0:T(8,128)(2,1)} %copy-done.14), channel_id=1, source_target_pairs={{0,30},{2,4},{4,2},{6,8},{8,6},{10,12},{12,10},{14,16},{16,14},{18... | collective-permute-start | bytes 147464 | tf_op jit(solution)/shard_map/ppermute | solution.py:950
  49.1 1.3 %collective-permute-start.17 = (f32[3,1536]{1,0:T(4,128)S(1)}, f32[3,1536]{1,0:T(4,128)S(1)}, u32[]{:S(2)}, u32[]{:S(2)}) collective-permute-start(f32[3,1536]{1,0:T(4,128)S(1)} %get-tuple-element.61), channel_id=1, source_target_pairs={{0,2},{1,3},{2,0},{3,1},{4,6},{5,7},{6,4},{7,5},{8,10},{9,11},{10,... | collective-permute-start | bytes 55304 | tf_op jit(solution)/shard_map/ppermute | solution.py:964
  50.4 5.4 %collective-permute-start.19 = (f32[3,1536]{1,0:T(4,128)S(1)}, f32[3,1536]{1,0:T(4,128)S(1)}, u32[]{:S(2)}, u32[]{:S(2)}) collective-permute-start(f32[3,1536]{1,0:T(4,128)S(1)} %add.43), channel_id=1, source_target_pairs={{0,1},{1,0},{2,3},{3,2},{4,5},{5,4},{6,7},{7,6},{8,9},{9,8},{10,11... | collective-permute-start | bytes 55304 | tf_op jit(solution)/shard_map/ppermute | solution.py:964
  52.1 4.7 %collective-permute-start.20 = (f32[3,1536]{1,0:T(4,128)S(1)}, f32[3,1536]{1,0:T(4,128)S(1)}, u32[]{:S(2)}, u32[]{:S(2)}) collective-permute-start(f32[3,1536]{1,0:T(4,128)S(1)} %add.43), channel_id=1, source_target_pairs={{0,5},{1,4},{2,7},{3,6},{4,1},{5,0},{6,3},{7,2},{8,13},{9,12},{10,... | collective-permute-start | bytes 55304 | tf_op jit(solution)/shard_map/ppermute | solution.py:964
  52.1 4.7 %collective-permute-start.18 = (f32[3,1536]{1,0:T(4,128)S(1)}, f32[3,1536]{1,0:T(4,128)S(1)}, u32[]{:S(2)}, u32[]{:S(2)}) collective-permute-start(f32[3,1536]{1,0:T(4,128)S(1)} %add.43), channel_id=1, source_target_pairs={{0,4},{1,5},{2,6},{3,7},{4,0},{5,1},{6,2},{7,3},{8,12},{9,13},{10,... | collective-permute-start | bytes 55304 | tf_op jit(solution)/shard_map/ppermute | solution.py:964
  56.8 6.8 %collective-permute-start.22 = (f32[3,1536]{1,0:T(4,128)S(1)}, f32[3,1536]{1,0:T(4,128)S(1)}, u32[]{:S(2)}, u32[]{:S(2)}) collective-permute-start(f32[3,1536]{1,0:T(4,128)S(1)} %add_add_fusion), channel_id=1, source_target_pairs={{0,16},{1,17},{2,18},{3,19},{4,20},{5,21},{6,22},{7,23},{8,24},{9,... | collective-permute-start | bytes 55304 | tf_op jit(solution)/shard_map/ppermute | solution.py:964
  56.9 6.7 %collective-permute-start.23 = (f32[3,1536]{1,0:T(4,128)S(1)}, f32[3,1536]{1,0:T(4,128)S(1)}, u32[]{:S(2)}, u32[]{:S(2)}) collective-permute-start(f32[3,1536]{1,0:T(4,128)S(1)} %add_add_fusion), channel_id=1, source_target_pairs={{0,24},{1,25},{2,26},{3,27},{4,28},{5,29},{6,30},{7,31},{8,16},{9,... | collective-permute-start | bytes 55304 | tf_op jit(solution)/shard_map/ppermute | solution.py:964
  58.0 5.6 %collective-permute-start.21 = (f32[3,1536]{1,0:T(4,128)S(1)}, f32[3,1536]{1,0:T(4,128)S(1)}, u32[]{:S(2)}, u32[]{:S(2)}) collective-permute-start(f32[3,1536]{1,0:T(4,128)S(1)} %add_add_fusion), channel_id=1, source_target_pairs={{0,8},{1,9},{2,10},{3,11},{4,12},{5,13},{6,14},{7,15},{8,0},{9,1},... | collective-permute-start | bytes 55304 | tf_op jit(solution)/shard_map/ppermute | solution.py:964
  (16 other events, 176.6 us)

commit v7 on v6

--- a/solution.py
+++ b/solution.py
@@ -371,7 +371,7 @@
     return jnp.where(match, 1.0, 0.0).astype(BF)
 
 
-def params(mib=36):
+def params(mib=20):
     return pltpu.CompilerParams(vmem_limit_bytes=mib * 1024 * 1024)
 
 
@@ -384,32 +384,26 @@
     edge_a, edge_b, far, tile_a, tile_b, att_out,
 ):
     att_out[...] = att[...]
-    half = att_lo.shape[2]
     tile_a[...] = near[...]
     tile_b[...] = distant[...]
-    row, col = grid_of(16, 32)
-    at, base = row & 7, (row >> 3) * 16
+    wide = cot_lo.shape[2]
+    at = lax.broadcasted_iota(jnp.int32, (8, wide), 0)
     even = (meta[1] & 1) == 0
-
-    def edges(body, others, edge):
-        parts = []
-        for group in range(2):
-            rows = others[2 * group : 2 * group + 2].reshape(32, half)
-            parts.append(body[:, group * half : (group + 1) * half] + dot(edge, rows))
-        return jnp.concatenate(parts, axis=1)
-
-    skips = skip_hi[...].reshape(32, 2 * half)
-    up = dot(picks((at >= 6) & (col == base + at + 8)), skips)
-    up = edges(up, att_hi, picks((at == 5) & (col == base + 15)))
-    skips = skip_lo[...].reshape(32, 2 * half)
-    cots = cot_lo[...].reshape(32, 2 * half)
-    down = dot(picks((at < 2) & (col == base + at)), skips)
-    down = down + dot(picks((at == 3) & (col == base)), cots)
-    down = edges(down, att_lo, picks((at == 2) & (col == base)))
+    ups, downs, ends = [], [], []
+    for s in range(2):
+        feats = [jnp.concatenate([part[s], part[2 + s]], axis=1) for part in (att_hi, att_lo)]
+        high, low = feats[0].astype(F32)[8:], feats[1].astype(F32)[:8]
+        up = jnp.where(at >= 6, skip_hi[s].astype(F32)[8:], 0.0)
+        ups.append(jnp.where(at == 5, pltpu.roll(high, 6, 0), up))
+        down = jnp.where(at < 2, skip_lo[s].astype(F32)[:8], 0.0)
+        down = jnp.where(at == 2, pltpu.roll(low, 2, 0), down)
+        downs.append(jnp.where(at == 3, pltpu.roll(cot_lo[s].astype(F32)[:8], 3, 0), down))
+        last = pltpu.roll(cot_hi[s].astype(F32)[8:], 5, 0)
+        ends.append(jnp.where(at == 4, last, 0.0))
+    up, down = jnp.concatenate(ups), jnp.concatenate(downs)
     edge_a[...] = jnp.where(even, up, down).astype(BF)
     edge_b[...] = jnp.where(even, down, up).astype(BF)
-    cots = cot_hi[...].reshape(32, 2 * half)
-    far[...] = dot(picks((at == 4) & (col == base + 15)), cots).astype(BF)
+    far[...] = jnp.concatenate(ends).astype(BF)
 
 
 def packed(meta, encoder_skip, attention, cotangent, weight, tile):
@@ -991,7 +985,7 @@
     edge_b = staggered(edge_b, 1)
     far_a = paired(far, "seq", 2)
     far_b = staggered(far, 2)
-    prev = passed_along(after(cotangent, edge_a, edge_b, far_a, far_b), "seq", 1)
+    prev = passed_along(after(cotangent, edge_b), "seq", 1)
     outer = (slab == 0) | (slab == slabs - 1)
     nothing = jnp.zeros_like(edge_b)
     edge = edge_a + jnp.where(outer, nothing, edge_b)

time: 64.6 us -> 62.6 us (0.969)
  waiting for transfers between devices: 10.4 us -> 7.56 us
  starting transfers between devices: 25.5 us -> 26.5 us
    ppermute x3, waiting for transfers between devices: 3.64 us -> 1.38 us  [staggered(): return lax.ppermute(part, 'seq', pairs)]
    ppermute x3, starting transfers between devices: 7.87 us -> 9.63 us  [staggered(): return lax.ppermute(part, 'seq', pairs)]
    ppermute x13, starting transfers between devices: 9.17 us -> 7.78 us  [paired(): return lax.ppermute(part, axis, [(i, i ^ bit) for i in range(count)])]
  transfers between devices with their start and end apart: 24 -> 24, of which waited for: 7 -> 7; matrix products, arithmetic and copies ran while one was open for 0% -> 0% of each run, Pallas kernels for 29% -> 30%
where the time goes in v7:
time: 62.6 us; the launch traced here: 62.3 us
  starting transfers between devices  26.5 us (42%)
  Pallas kernels  21.7 us (35%)
  waiting for transfers between devices  7.56 us (12%)
  local copies, waits for them, and re-layouts  4.37 us (7%)
  other arithmetic  1.27 us (2%)
  between operations  0.87 us (1%)
    ppermute x3, starting transfers between devices, staggered(): return lax.ppermute(part, 'seq', pairs)  9.63 us
    ppermute x13, starting transfers between devices, paired(): return lax.ppermute(part, axis, [(i, i ^ bit) for i in range(count)])  7.78 us
    ppermute x7, starting transfers between devices, crossed(): return lax.ppermute(part, ('seq', 'head'), pairs)  7.17 us
    pallas_call x1, Pallas kernels, own_half(): pl.pallas_call(functools.partial(own_kernel, slabs), grid_spec=pltpu.Pref...  4.93 us
    unnamed x32, local copies, waits for them, and re-layouts  4.29 us
    ppermute x13, waiting for transfers between devices, paired(): return lax.ppermute(part, axis, [(i, i ^ bit) for i in range(count)])  4.08 us
    pallas_call x1, Pallas kernels, other_terms(): pl.pallas_call(terms_kernel, grid_spec=pltpu.PrefetchScalarGridSpec(num_s...  3.77 us
    pallas_call x1, Pallas kernels, targets(): pl.pallas_call(functools.partial(target_kernel, slabs), grid_spec=pltpu.P...  3.25 us
  transfers between devices with their start and end apart: 24, of which 7 were waited for; matrix products, arithmetic and copies ran while one was open for 0% of the time, Pallas kernels for 30%

profile of v7, /device:TPU:0, one launch (start us, length us, event | category | flops | bytes accessed | tf_op | source)
XLA Modules:
  0.0 62.3 jit_solution(13482635751716327225)
XLA Ops:
  1.3 3.2 %pack_edges.1 = (bf16[16,1536]{1,0:T(8,128)(2,1)}, bf16[16,1536]{1,0:T(8,128)(2,1)}, bf16[16,1536]{1,0:T(8,128)(2,1)}, bf16[384,384]{1,0:T(8,128)(2,1)}, bf16[38...) custom-call(s32[2]{0:T(128)} %pad_add_fusion.meta, bf16[2,128,1536]{2,1,0:T(8,128)(2,1)} %skip.3, ...), custom_call_target="tpu_custom_call" | custom-call | tf_op jit(solution)/shard_map/pack_edges/pallas_call | solution.py:419
  4.4 5.4 %collective-permute-start.2 = (bf16[16,1536]{1,0:T(8,128)(2,1)}, bf16[16,1536]{1,0:T(8,128)(2,1)S(1)}, u32[]{:S(2)}, u32[]{:S(2)}) collective-permute-start(bf16[16,1536]{1,0:T(8,128)(2,1)} %get-tuple-element.39), channel_id=1, source_target_pairs={{0,30},{2,4},{4,2},{6,8},{8,6},{10,12},{12,10},{14,16},{16,14},{18... | collective-permute-start | bytes 147464 | tf_op jit(solution)/shard_map/ppermute | solution.py:944
  9.9 1.9 %collective-permute-start.4 = (bf16[16,1536]{1,0:T(8,128)(2,1)}, bf16[16,1536]{1,0:T(8,128)(2,1)S(1)}, u32[]{:S(2)}, u32[]{:S(2)}) collective-permute-start(bf16[16,1536]{1,0:T(8,128)(2,1)} %get-tuple-element.40), channel_id=1, source_target_pairs={{0,28},{2,30},{4,8},{6,10},{8,4},{10,6},{12,16},{14,18},{16,12},{1... | collective-permute-start | bytes 147464 | tf_op jit(solution)/shard_map/ppermute | solution.py:944
  12.0 1.5 %collective-permute-start.7 = (bf16[384,384]{1,0:T(8,128)(2,1)}, bf16[384,384]{1,0:T(8,128)(2,1)S(1)}, u32[]{:S(2)}, u32[]{:S(2)}) collective-permute-start(bf16[384,384]{1,0:T(8,128)(2,1)} %get-tuple-element.52), channel_id=1, source_target_pairs={{0,1},{1,0},{2,3},{3,2},{4,5},{5,4},{6,7},{7,6},{8,9},{9,8},{10,11... | collective-permute-start | bytes 884744 | tf_op jit(solution)/shard_map/ppermute | solution.py:935
  13.5 1.9 %collective-permute-start.6 = (bf16[2,128,1536]{2,1,0:T(8,128)(2,1)S(1)}, bf16[2,128,1536]{2,1,0:T(8,128)(2,1)S(1)}, u32[]{:S(2)}, u32[]{:S(2)}) collective-permute-start(bf16[2,128,1536]{2,1,0:T(8,128)(2,1)S(1)} %copy-done.1), channel_id=1, source_target_pairs={{0,2},{2,4},{4,6},{6,8},{8,10},{10,12},{12,14},{14,16},{16,18},{18... | collective-permute-start | bytes 2359304 | tf_op jit(solution)/shard_map/ppermute | solution.py:204
  15.5 1.4 %collective-permute-done.4 = bf16[16,1536]{1,0:T(8,128)(2,1)S(1)} collective-permute-done((bf16[16,1536]{1,0:T(8,128)(2,1)}, bf16[16,1536]{1,0:T(8,128)(2,1)S(1)}, u32[]{:S(2)}, u32[]{:S(2)}) %collective-permute-start.4) | collective-permute-done | bytes 49184 | tf_op jit(solution)/shard_map/ppermute | solution.py:944
  16.9 1.6 %collective-permute-start.5 = (bf16[16,1536]{1,0:T(8,128)(2,1)S(1)}, bf16[16,1536]{1,0:T(8,128)(2,1)S(1)}, u32[]{:S(2)}, u32[]{:S(2)}) collective-permute-start(bf16[16,1536]{1,0:T(8,128)(2,1)S(1)} %get-tuple-element.71), channel_id=1, source_target_pairs={{0,1},{1,0},{2,3},{3,2},{4,5},{5,4},{6,7},{7,6},{8,9},{9,8},{10,11... | collective-permute-start | bytes 147464 | tf_op jit(solution)/shard_map/ppermute | solution.py:935
  19.0 1.5 %collective-permute-start.10 = (bf16[384,384]{1,0:T(8,128)(2,1)}, bf16[384,384]{1,0:T(8,128)(2,1)}, u32[]{:S(2)}, u32[]{:S(2)}) collective-permute-start(bf16[384,384]{1,0:T(8,128)(2,1)} %get-tuple-element.53), channel_id=1, source_target_pairs={{0,1},{1,0},{2,3},{3,2},{4,5},{5,4},{6,7},{7,6},{8,9},{9,8},{10,11... | collective-permute-start | bytes 884744 | tf_op jit(solution)/shard_map/ppermute | solution.py:935
  20.5 1.6 %collective-permute-done.7.refs_0_ = bf16[384,384]{1,0:T(8,128)(2,1)S(1)} collective-permute-done((bf16[384,384]{1,0:T(8,128)(2,1)}, bf16[384,384]{1,0:T(8,128)(2,1)S(1)}, u32[]{:S(2)}, u32[]{:S(2)}) %collective-permute-start.7) | collective-permute-done | bytes 294944 | tf_op jit(solution)/shard_map/ppermute | solution.py:935
  22.1 1.0 %collective-permute-done.5.twin = bf16[16,1536]{1,0:T(8,128)(2,1)S(1)} collective-permute-done((bf16[16,1536]{1,0:T(8,128)(2,1)S(1)}, bf16[16,1536]{1,0:T(8,128)(2,1)S(1)}, u32[]{:S(2)}, u32[]{:S(2)}) %collective-permute-start.5) | collective-permute-done | bytes 49184 | tf_op jit(solution)/shard_map/ppermute | solution.py:935
  23.1 1.3 %collective-permute-start.9 = (bf16[384,384]{1,0:T(8,128)(2,1)S(1)}, bf16[384,384]{1,0:T(8,128)(2,1)}, u32[]{:S(2)}, u32[]{:S(2)}) collective-permute-start(bf16[384,384]{1,0:T(8,128)(2,1)S(1)} %collective-permute-done.7.refs_0_), channel_id=1, source_target_pairs={{0,8},{2,10},{4,12},{6,14},{8,0},{10,2},{12,4},{14,6},{16,24},{18,... | collective-permute-start | bytes 884744 | tf_op jit(solution)/shard_map/ppermute | solution.py:935
  24.5 2.1 %own_slopes.1 = (bf16[32,768]{1,0:T(8,128)(2,1)S(1)}, bf16[2,144,768]{2,1,0:T(8,128)(2,1)S(1)}, f32[2,144,768]{2,1,0:T(8,128)S(1)}) custom-call(s32[2]{0:T(128)S(1)} %copy-done.12, s32[2]{0:T(128)S(1)} %copy-done.13, s32[2,32]{1,0:T(2,128)S(1)} %copy-done.15, bf16[4,64,768]{2,1,0:T(8,128)(2,1)S(1)} %copy-done.2, bf16[2,128,1536]{2,1,0:T(8,128)(2,1)S(1)} %copy-done.5, ...), custom_call_target="tpu_custom_call" | custom-call | flops 3000000000 | bytes 1000000 | tf_op jit(solution)/shard_map/own_slopes/pallas_call | solution.py:558
  27.3 2.6 %other_slopes.1 = (bf16[2,144,768]{2,1,0:T(8,128)(2,1)S(1)}, f32[2,144,768]{2,1,0:T(8,128)S(1)}, bf16[16,1536]{1,0:T(8,128)(2,1)S(1)}, bf16[16,1536]{1,0:T(8,128)(2,1)S(1)}) custom-call(s32[2]{0:T(128)S(1)} %copy-done.12, s32[2]{0:T(128)S(1)} %copy-done.13, s32[2,32]{1,0:T(2,128)S(1)} %copy-done.15, bf16[2,64,768]{2,1,0:T(8,128)(2,1)S(1)} %collective-permute-done.att, ...), custom_call_target="tpu_custom_call" | custom-call | flops 3000000000 | bytes 1000000 | tf_op jit(solution)/shard_map/other_slopes/pallas_call | solution.py:747
  30.0 4.9 %own_half.1 = (bf16[2,144,1536]{2,1,0:T(8,128)(2,1)S(1)}, f32[3,768]{1,0:T(4,128)S(1)}, bf16[2,128,1536]{2,1,0:T(8,128)(2,1)}, bf16[2,64,1536]{2,1,0:T(8,128)(2,1)}) custom-call(s32[2]{0:T(128)S(1)} %copy-done.12, s32[2]{0:T(128)S(1)} %copy-done.13, bf16[2,144,768]{2,1,0:T(8,128)(2,1)S(1)} %get-tuple-element.45.sums, ...), custom_call_target="tpu_custom_call" | custom-call | flops 1 | bytes 1 | tf_op jit(solution)/shard_map/own_half/pallas_call | solution.py:661
  37.8 2.3 %collective-permute-start.16 = (bf16[16,1536]{1,0:T(8,128)(2,1)}, bf16[16,1536]{1,0:T(8,128)(2,1)S(1)}, u32[]{:S(2)}, u32[]{:S(2)}) collective-permute-start(bf16[16,1536]{1,0:T(8,128)(2,1)} %copy-done.14), channel_id=1, source_target_pairs={{0,30},{2,4},{4,2},{6,8},{8,6},{10,12},{12,10},{14,16},{16,14},{18... | collective-permute-start | bytes 147464 | tf_op jit(solution)/shard_map/ppermute | solution.py:944
  40.1 1.2 %copy-done.4 = bf16[2,144,1536]{2,1,0:T(8,128)(2,1)S(1)} copy-done((bf16[2,144,1536]{2,1,0:T(8,128)(2,1)S(1)}, bf16[2,144,1536]{2,1,0:T(8,128)(2,1)}, u32[]{:S(2)}) %copy-start.4) | copy-done | bytes 884760
  41.2 1.2 %copy-done.8 = f32[2,144,768]{2,1,0:T(8,128)S(1)} copy-done((f32[2,144,768]{2,1,0:T(8,128)S(1)}, f32[2,144,768]{2,1,0:T(8,128)}, u32[]{:S(2)}) %copy-start.8) | copy-done | bytes 884760
  43.4 3.8 %other_terms.1 = (bf16[2,144,768]{2,1,0:T(8,128)(2,1)S(1)}, f32[3,1536]{1,0:T(4,128)S(1)}) custom-call(s32[2]{0:T(128)S(1)} %copy-done.12, s32[6]{0:T(128)S(1)} %stack.39.order, bf16[2,144,1536]{2,1,0:T(8,128)(2,1)S(1)} %copy-done.4, bf16[2,144,768]{2,1,0:T(8,128)(2,1)S(1)} %copy-done.10, f32[2,144,768]{2,1,0:T(8,128)S(1)} %copy-done.8, ...), custom_call_target="tpu_custom_call" | custom-call | flops 679477248 | bytes 6291456 | tf_op jit(solution)/shard_map/other_terms/pallas_call | solution.py:817
  47.3 1.2 %collective-permute-done.17 = f32[3,1536]{1,0:T(4,128)S(1)} collective-permute-done((f32[3,1536]{1,0:T(4,128)S(1)}, f32[3,1536]{1,0:T(4,128)S(1)}, u32[]{:S(2)}, u32[]{:S(2)}) %collective-permute-start.17) | collective-permute-done | bytes 18464 | tf_op jit(solution)/shard_map/ppermute | solution.py:958
  48.5 1.6 %collective-permute-start.19 = (f32[3,1536]{1,0:T(4,128)S(1)}, f32[3,1536]{1,0:T(4,128)S(1)}, u32[]{:S(2)}, u32[]{:S(2)}) collective-permute-start(f32[3,1536]{1,0:T(4,128)S(1)} %add.43), channel_id=1, source_target_pairs={{0,1},{1,0},{2,3},{3,2},{4,5},{5,4},{6,7},{7,6},{8,9},{9,8},{10,11... | collective-permute-start | bytes 55304 | tf_op jit(solution)/shard_map/ppermute | solution.py:958
  50.3 1.8 %collective-permute-start.18 = (f32[3,1536]{1,0:T(4,128)S(1)}, f32[3,1536]{1,0:T(4,128)S(1)}, u32[]{:S(2)}, u32[]{:S(2)}) collective-permute-start(f32[3,1536]{1,0:T(4,128)S(1)} %add.43), channel_id=1, source_target_pairs={{0,4},{1,5},{2,6},{3,7},{4,0},{5,1},{6,2},{7,3},{8,12},{9,13},{10,... | collective-permute-start | bytes 55304 | tf_op jit(solution)/shard_map/ppermute | solution.py:958
  52.0 1.8 %other_grads.1 = (bf16[2,128,1536]{2,1,0:T(8,128)(2,1)}, bf16[2,64,1536]{2,1,0:T(8,128)(2,1)}) custom-call(s32[2]{0:T(128)S(1)} %copy-done.12, bf16[2,144,1536]{2,1,0:T(8,128)(2,1)S(1)} %copy-done.4, bf16[2,144,768]{2,1,0:T(8,128)(2,1)S(1)} %get-tuple-element.62.convs, f32[3,1536]{1,0:T(4,128)S(1)} %copy-done.11, ...), custom_call_target="tpu_custom_call", output_to_operand_aliasing={{0}: (4, {}), {1}: (5, {})} | custom-call | flops 4423680 | bytes 4194304 | tf_op jit(solution)/shard_map/other_grads/pallas_call | solution.py:869
  54.9 2.7 %collective-permute-start.23 = (f32[3,1536]{1,0:T(4,128)S(1)}, f32[3,1536]{1,0:T(4,128)S(1)}, u32[]{:S(2)}, u32[]{:S(2)}) collective-permute-start(f32[3,1536]{1,0:T(4,128)S(1)} %add_add_fusion), channel_id=1, source_target_pairs={{0,24},{1,25},{2,26},{3,27},{4,28},{5,29},{6,30},{7,31},{8,16},{9,... | collective-permute-start | bytes 55304 | tf_op jit(solution)/shard_map/ppermute | solution.py:958
  58.4 3.2 %targets.1 = bf16[2,2,1536]{2,1,0:T(2,128)(2,1)} custom-call(s32[2]{0:T(128)S(1)} %copy-done.12, s32[6]{0:T(128)S(1)} %stack.39.order, bf16[16,1536]{1,0:T(8,128)(2,1)S(1)} %get-tuple-element.42.mine, bf16[16,1536]{1,0:T(8,128)(2,1)S(1)} %collective-permute-done.15.got_a, bf16[16,1536]{1,0:T(8,128)(2,1)S(1)} %collective-permute-done.16.got_b, ...), custom_call_target="tpu_custom_call" | custom-call | flops 75497472 | bytes 6291456 | tf_op jit(solution)/shard_map/targets/pallas_call | solution.py:916
  (69 shorter events, 8.7 us)
Async XLA Ops:
  4.4 9.1 %collective-permute-start.2 = (bf16[16,1536]{1,0:T(8,128)(2,1)}, bf16[16,1536]{1,0:T(8,128)(2,1)S(1)}, u32[]{:S(2)}, u32[]{:S(2)}) collective-permute-start(bf16[16,1536]{1,0:T(8,128)(2,1)} %get-tuple-element.39), channel_id=1, source_target_pairs={{0,30},{2,4},{4,2},{6,8},{8,6},{10,12},{12,10},{14,16},{16,14},{18... | collective-permute-start | bytes 147464 | tf_op jit(solution)/shard_map/ppermute | solution.py:944
  9.9 5.6 %collective-permute-start.3 = (bf16[16,1536]{1,0:T(8,128)(2,1)}, bf16[16,1536]{1,0:T(8,128)(2,1)S(1)}, u32[]{:S(2)}, u32[]{:S(2)}) collective-permute-start(bf16[16,1536]{1,0:T(8,128)(2,1)} %get-tuple-element.40), channel_id=1, source_target_pairs={{0,4},{2,6},{4,0},{6,2},{8,12},{10,14},{12,8},{14,10},{16,20},{18,... | collective-permute-start | bytes 147464 | tf_op jit(solution)/shard_map/ppermute | solution.py:935
  9.9 7.0 %collective-permute-start.4 = (bf16[16,1536]{1,0:T(8,128)(2,1)}, bf16[16,1536]{1,0:T(8,128)(2,1)S(1)}, u32[]{:S(2)}, u32[]{:S(2)}) collective-permute-start(bf16[16,1536]{1,0:T(8,128)(2,1)} %get-tuple-element.40), channel_id=1, source_target_pairs={{0,28},{2,30},{4,8},{6,10},{8,4},{10,6},{12,16},{14,18},{16,12},{1... | collective-permute-start | bytes 147464 | tf_op jit(solution)/shard_map/ppermute | solution.py:944
  11.8 5.1 %collective-permute-start.1 = (bf16[16,1536]{1,0:T(8,128)(2,1)}, bf16[16,1536]{1,0:T(8,128)(2,1)S(1)}, u32[]{:S(2)}, u32[]{:S(2)}) collective-permute-start(bf16[16,1536]{1,0:T(8,128)(2,1)} %get-tuple-element.38), channel_id=1, source_target_pairs={{0,2},{2,0},{4,6},{6,4},{8,10},{10,8},{12,14},{14,12},{16,18},{18,... | collective-permute-start | bytes 147464 | tf_op jit(solution)/shard_map/ppermute | solution.py:935
  12.0 10.0 %collective-permute-start.7 = (bf16[384,384]{1,0:T(8,128)(2,1)}, bf16[384,384]{1,0:T(8,128)(2,1)S(1)}, u32[]{:S(2)}, u32[]{:S(2)}) collective-permute-start(bf16[384,384]{1,0:T(8,128)(2,1)} %get-tuple-element.52), channel_id=1, source_target_pairs={{0,1},{1,0},{2,3},{3,2},{4,5},{5,4},{6,7},{7,6},{8,9},{9,8},{10,11... | collective-permute-start | bytes 884744 | tf_op jit(solution)/shard_map/ppermute | solution.py:935
  13.5 16.4 %collective-permute-start.6 = (bf16[2,128,1536]{2,1,0:T(8,128)(2,1)S(1)}, bf16[2,128,1536]{2,1,0:T(8,128)(2,1)S(1)}, u32[]{:S(2)}, u32[]{:S(2)}) collective-permute-start(bf16[2,128,1536]{2,1,0:T(8,128)(2,1)S(1)} %copy-done.1), channel_id=1, source_target_pairs={{0,2},{2,4},{4,6},{6,8},{8,10},{10,12},{12,14},{14,16},{16,18},{18... | collective-permute-start | bytes 2359304 | tf_op jit(solution)/shard_map/ppermute | solution.py:204
  16.9 6.2 %collective-permute-start.5 = (bf16[16,1536]{1,0:T(8,128)(2,1)S(1)}, bf16[16,1536]{1,0:T(8,128)(2,1)S(1)}, u32[]{:S(2)}, u32[]{:S(2)}) collective-permute-start(bf16[16,1536]{1,0:T(8,128)(2,1)S(1)} %get-tuple-element.71), channel_id=1, source_target_pairs={{0,1},{1,0},{2,3},{3,2},{4,5},{5,4},{6,7},{7,6},{8,9},{9,8},{10,11... | collective-permute-start | bytes 147464 | tf_op jit(solution)/shard_map/ppermute | solution.py:935
  18.5 8.8 %collective-permute-start = (bf16[2,64,768]{2,1,0:T(8,128)(2,1)}, bf16[2,64,768]{2,1,0:T(8,128)(2,1)S(1)}, u32[]{:S(2)}, u32[]{:S(2)}) collective-permute-start(bf16[2,64,768]{2,1,0:T(8,128)(2,1)} %get-tuple-element.37), channel_id=1, source_target_pairs={{0,1},{1,0},{2,3},{3,2},{4,5},{5,4},{6,7},{7,6},{8,9},{9,8},{10,11... | collective-permute-start | bytes 589832 | tf_op jit(solution)/shard_map/ppermute | solution.py:935
  19.0 17.4 %collective-permute-start.10 = (bf16[384,384]{1,0:T(8,128)(2,1)}, bf16[384,384]{1,0:T(8,128)(2,1)}, u32[]{:S(2)}, u32[]{:S(2)}) collective-permute-start(bf16[384,384]{1,0:T(8,128)(2,1)} %get-tuple-element.53), channel_id=1, source_target_pairs={{0,1},{1,0},{2,3},{3,2},{4,5},{5,4},{6,7},{7,6},{8,9},{9,8},{10,11... | collective-permute-start | bytes 884744 | tf_op jit(solution)/shard_map/ppermute | solution.py:935
  22.0 13.8 %collective-permute-start.8 = (bf16[384,384]{1,0:T(8,128)(2,1)S(1)}, bf16[384,384]{1,0:T(8,128)(2,1)}, u32[]{:S(2)}, u32[]{:S(2)}) collective-permute-start(bf16[384,384]{1,0:T(8,128)(2,1)S(1)} %collective-permute-done.7.refs_0_), channel_id=1, source_target_pairs={{0,4},{2,6},{4,0},{6,2},{8,12},{10,14},{12,8},{14,10},{16,20},{18,... | collective-permute-start | bytes 884744 | tf_op jit(solution)/shard_map/ppermute | solution.py:935
  23.1 13.2 %collective-permute-start.9 = (bf16[384,384]{1,0:T(8,128)(2,1)S(1)}, bf16[384,384]{1,0:T(8,128)(2,1)}, u32[]{:S(2)}, u32[]{:S(2)}) collective-permute-start(bf16[384,384]{1,0:T(8,128)(2,1)S(1)} %collective-permute-done.7.refs_0_), channel_id=1, source_target_pairs={{0,8},{2,10},{4,12},{6,14},{8,0},{10,2},{12,4},{14,6},{16,24},{18,... | collective-permute-start | bytes 884744 | tf_op jit(solution)/shard_map/ppermute | solution.py:935
  35.8 1.9 %collective-permute-start.11 = (bf16[384,384]{1,0:T(8,128)(2,1)S(1)}, bf16[384,384]{1,0:T(8,128)(2,1)S(1)}, u32[]{:S(2)}, u32[]{:S(2)}) collective-permute-start(bf16[384,384]{1,0:T(8,128)(2,1)S(1)} %collective-permute-done.7.refs_0_), channel_id=1, source_target_pairs={{0,2},{2,0},{4,6},{6,4},{8,10},{10,8},{12,14},{14,12},{16,18},{18,... | collective-permute-start | bytes 884744 | tf_op jit(solution)/shard_map/ppermute | solution.py:935
  35.8 4.2 %collective-permute-start.12 = (bf16[384,384]{1,0:T(8,128)(2,1)}, bf16[384,384]{1,0:T(8,128)(2,1)S(1)}, u32[]{:S(2)}, u32[]{:S(2)}) collective-permute-start(bf16[384,384]{1,0:T(8,128)(2,1)} %collective-permute-done.8.refs_1_), channel_id=1, source_target_pairs={{0,2},{2,0},{4,6},{6,4},{8,10},{10,8},{12,14},{14,12},{16,18},{18,... | collective-permute-start | bytes 884744 | tf_op jit(solution)/shard_map/ppermute | solution.py:935
  36.4 3.7 %collective-permute-start.13 = (bf16[384,384]{1,0:T(8,128)(2,1)}, bf16[384,384]{1,0:T(8,128)(2,1)}, u32[]{:S(2)}, u32[]{:S(2)}) collective-permute-start(bf16[384,384]{1,0:T(8,128)(2,1)} %collective-permute-done.9.refs_2_), channel_id=1, source_target_pairs={{0,2},{2,0},{4,6},{6,4},{8,10},{10,8},{12,14},{14,12},{16,18},{18,... | collective-permute-start | bytes 884744 | tf_op jit(solution)/shard_map/ppermute | solution.py:935
  36.4 3.6 %collective-permute-start.14 = (bf16[384,384]{1,0:T(8,128)(2,1)}, bf16[384,384]{1,0:T(8,128)(2,1)}, u32[]{:S(2)}, u32[]{:S(2)}) collective-permute-start(bf16[384,384]{1,0:T(8,128)(2,1)} %collective-permute-done.10.refs_3_), channel_id=1, source_target_pairs={{0,2},{2,0},{4,6},{6,4},{8,10},{10,8},{12,14},{14,12},{16,18},{18,... | collective-permute-start | bytes 884744 | tf_op jit(solution)/shard_map/ppermute | solution.py:935
  36.9 10.3 %collective-permute-start.15 = (bf16[16,1536]{1,0:T(8,128)(2,1)}, bf16[16,1536]{1,0:T(8,128)(2,1)S(1)}, u32[]{:S(2)}, u32[]{:S(2)}) collective-permute-start(bf16[16,1536]{1,0:T(8,128)(2,1)} %copy-done.14), channel_id=1, source_target_pairs={{0,2},{2,0},{4,6},{6,4},{8,10},{10,8},{12,14},{14,12},{16,18},{18,... | collective-permute-start | bytes 147464 | tf_op jit(solution)/shard_map/ppermute | solution.py:935
  37.8 9.5 %collective-permute-start.16 = (bf16[16,1536]{1,0:T(8,128)(2,1)}, bf16[16,1536]{1,0:T(8,128)(2,1)S(1)}, u32[]{:S(2)}, u32[]{:S(2)}) collective-permute-start(bf16[16,1536]{1,0:T(8,128)(2,1)} %copy-done.14), channel_id=1, source_target_pairs={{0,30},{2,4},{4,2},{6,8},{8,6},{10,12},{12,10},{14,16},{16,14},{18... | collective-permute-start | bytes 147464 | tf_op jit(solution)/shard_map/ppermute | solution.py:944
  47.2 1.3 %collective-permute-start.17 = (f32[3,1536]{1,0:T(4,128)S(1)}, f32[3,1536]{1,0:T(4,128)S(1)}, u32[]{:S(2)}, u32[]{:S(2)}) collective-permute-start(f32[3,1536]{1,0:T(4,128)S(1)} %get-tuple-element.61), channel_id=1, source_target_pairs={{0,2},{1,3},{2,0},{3,1},{4,6},{5,7},{6,4},{7,5},{8,10},{9,11},{10,... | collective-permute-start | bytes 55304 | tf_op jit(solution)/shard_map/ppermute | solution.py:958
  48.5 5.4 %collective-permute-start.19 = (f32[3,1536]{1,0:T(4,128)S(1)}, f32[3,1536]{1,0:T(4,128)S(1)}, u32[]{:S(2)}, u32[]{:S(2)}) collective-permute-start(f32[3,1536]{1,0:T(4,128)S(1)} %add.43), channel_id=1, source_target_pairs={{0,1},{1,0},{2,3},{3,2},{4,5},{5,4},{6,7},{7,6},{8,9},{9,8},{10,11... | collective-permute-start | bytes 55304 | tf_op jit(solution)/shard_map/ppermute | solution.py:958
  50.1 4.7 %collective-permute-start.20 = (f32[3,1536]{1,0:T(4,128)S(1)}, f32[3,1536]{1,0:T(4,128)S(1)}, u32[]{:S(2)}, u32[]{:S(2)}) collective-permute-start(f32[3,1536]{1,0:T(4,128)S(1)} %add.43), channel_id=1, source_target_pairs={{0,5},{1,4},{2,7},{3,6},{4,1},{5,0},{6,3},{7,2},{8,13},{9,12},{10,... | collective-permute-start | bytes 55304 | tf_op jit(solution)/shard_map/ppermute | solution.py:958
  50.3 4.5 %collective-permute-start.18 = (f32[3,1536]{1,0:T(4,128)S(1)}, f32[3,1536]{1,0:T(4,128)S(1)}, u32[]{:S(2)}, u32[]{:S(2)}) collective-permute-start(f32[3,1536]{1,0:T(4,128)S(1)} %add.43), channel_id=1, source_target_pairs={{0,4},{1,5},{2,6},{3,7},{4,0},{5,1},{6,2},{7,3},{8,12},{9,13},{10,... | collective-permute-start | bytes 55304 | tf_op jit(solution)/shard_map/ppermute | solution.py:958
  54.8 6.8 %collective-permute-start.22 = (f32[3,1536]{1,0:T(4,128)S(1)}, f32[3,1536]{1,0:T(4,128)S(1)}, u32[]{:S(2)}, u32[]{:S(2)}) collective-permute-start(f32[3,1536]{1,0:T(4,128)S(1)} %add_add_fusion), channel_id=1, source_target_pairs={{0,16},{1,17},{2,18},{3,19},{4,20},{5,21},{6,22},{7,23},{8,24},{9,... | collective-permute-start | bytes 55304 | tf_op jit(solution)/shard_map/ppermute | solution.py:958
  54.9 6.7 %collective-permute-start.23 = (f32[3,1536]{1,0:T(4,128)S(1)}, f32[3,1536]{1,0:T(4,128)S(1)}, u32[]{:S(2)}, u32[]{:S(2)}) collective-permute-start(f32[3,1536]{1,0:T(4,128)S(1)} %add_add_fusion), channel_id=1, source_target_pairs={{0,24},{1,25},{2,26},{3,27},{4,28},{5,29},{6,30},{7,31},{8,16},{9,... | collective-permute-start | bytes 55304 | tf_op jit(solution)/shard_map/ppermute | solution.py:958
  57.6 4.0 %collective-permute-start.21 = (f32[3,1536]{1,0:T(4,128)S(1)}, f32[3,1536]{1,0:T(4,128)S(1)}, u32[]{:S(2)}, u32[]{:S(2)}) collective-permute-start(f32[3,1536]{1,0:T(4,128)S(1)} %add_add_fusion), channel_id=1, source_target_pairs={{0,8},{1,9},{2,10},{3,11},{4,12},{5,13},{6,14},{7,15},{8,0},{9,1},... | collective-permute-start | bytes 55304 | tf_op jit(solution)/shard_map/ppermute | solution.py:958
  (16 other events, 176.0 us)

commit v8 on v7

--- a/solution.py
+++ b/solution.py
@@ -772,7 +772,16 @@
     )(meta, offsets, bins, shipped, skip, edge, twin, filt, asked)
 
 
-def terms_kernel(meta, order, moved, sums, slopes, own_terms, *refs):
+def spots(meta, tile):
+    core, block = meta[1] & 1, (meta[1] >> 1) & 3
+    return [
+        (pl.multiple_of(row * tile, tile), pl.multiple_of((block ^ k) * tile, tile))
+        for row in (core, 1 - core)
+        for k in range(4)
+    ]
+
+
+def terms_kernel(meta, moved, sums, slopes, own_terms, *refs):
     pieces, (convs, terms, full, sems) = refs[:8], refs[8:]
     half = sums.shape[2]
     tall = sums.shape[1]
@@ -780,12 +789,10 @@
     there = (1 - meta[0]) * half
     tile = pieces[0].shape[0]
     copies = []
-    for k, piece in enumerate(pieces):
-        down = pl.multiple_of(order[4 + k // 4] * tile, tile)
-        over = pl.multiple_of(order[k % 4] * tile, tile)
+    for k, (down, over) in enumerate(spots(meta, tile)):
         copies.append(
             pltpu.make_async_copy(
-                piece, full.at[pl.ds(down, tile), pl.ds(over, tile)], sems.at[k]
+                pieces[k], full.at[pl.ds(down, tile), pl.ds(over, tile)], sems.at[k]
             )
         )
         copies[-1].start()
@@ -807,17 +814,17 @@
             terms[k : k + 1, place] = total[k]
 
 
-def other_terms(meta, order, moved, sums, slopes, own_terms, pieces):
+def other_terms(meta, moved, sums, slopes, own_terms, pieces):
     _, tall, wide = moved.shape
     half = sums.shape[2]
 
     def whole(*shape):
-        return pl.BlockSpec(shape, lambda i, m, o: (0,) * len(shape))
+        return pl.BlockSpec(shape, lambda i, m: (0,) * len(shape))
 
     return pl.pallas_call(
         terms_kernel,
         grid_spec=pltpu.PrefetchScalarGridSpec(
-            num_scalar_prefetch=2,
+            num_scalar_prefetch=1,
             grid=(1,),
             in_specs=[
                 whole(2, tall, wide),
@@ -836,7 +843,7 @@
         compiler_params=params(),
         cost_estimate=cost(2 * 2 * tall * half * wide, 6 * 1024 * 1024),
         name="other_terms",
-    )(meta, order, moved, sums, slopes, own_terms, *pieces)
+    )(meta, moved, sums, slopes, own_terms, *pieces)
 
 
 def grads_kernel(meta, moved, convs, filt, old_skip, old_att, skip_grad, att_grad, pair):
@@ -887,7 +894,7 @@
     )(meta, moved, convs, filt, skip_grad, att_grad)
 
 
-def target_kernel(slabs, meta, order, mine, got_a, got_b, weight, *refs):
+def target_kernel(slabs, meta, mine, got_a, got_b, weight, *refs):
     pieces, (target, total) = refs[:8], refs[8:]
     half = weight.shape[0]
     there = (1 - meta[0]) * half
@@ -898,25 +905,24 @@
     mine[...] = (mine[...].astype(F32) + got).astype(BF)
     here = pl.ds(pl.multiple_of(meta[0] * half, half), half)
     total[...] = dot(mine[:, here], weight[...]) + pltpu.roll(mine[...].astype(F32), 12 + 2, 0)
-    for k, piece in enumerate(pieces):
-        place = pl.ds(pl.multiple_of(there + order[4 + k // 4] * tile, tile), tile)
-        over = pl.ds(pl.multiple_of(order[k % 4] * tile, tile), tile)
-        total[:, over] += dot(mine[:, place], piece[...])
+    for k, (down, over) in enumerate(spots(meta, tile)):
+        place = pl.ds(pl.multiple_of(there + down, tile), tile)
+        total[:, pl.ds(over, tile)] += dot(mine[:, place], pieces[k][...])
     for s in range(2):
         target[s] = total[s * 8 : s * 8 + 2].astype(BF)
 
 
-def targets(meta, order, mine, got, weight, pieces, slabs):
+def targets(meta, mine, got, weight, pieces, slabs):
     half, wide = weight.shape
     tile = pieces[0].shape[0]
 
     def whole(*shape):
-        return pl.BlockSpec(shape, lambda i, m, o: (0,) * len(shape))
+        return pl.BlockSpec(shape, lambda i, m: (0,) * len(shape))
 
     return pl.pallas_call(
         functools.partial(target_kernel, slabs),
         grid_spec=pltpu.PrefetchScalarGridSpec(
-            num_scalar_prefetch=2,
+            num_scalar_prefetch=1,
             grid=(1,),
             in_specs=[whole(16, wide)] * 3 + [whole(half, wide)]
             + [whole(tile, tile)] * 8,
@@ -927,7 +933,7 @@
         compiler_params=params(),
         cost_estimate=cost(2 * 16 * wide * wide, 6 * 1024 * 1024),
         name="targets",
-    )(meta, order, mine, *got, weight, *pieces)
+    )(meta, mine, *got, weight, *pieces)
 
 
 def paired(part, axis, bit):
@@ -971,10 +977,7 @@
     slab = lax.axis_index("seq")
     slabs = lax.axis_size("seq")
     meta = jnp.stack([head, slab]).astype(jnp.int32)
-    core = slab % 2
-    block = slab // 2 % 4
     tile = 3 * LANES
-    order = jnp.stack([block, block ^ 1, block ^ 2, block ^ 3, core, 1 - core]).astype(jnp.int32)
 
     edge_a, edge_b, far, first, last_tile, att_out = packed(
         meta, encoder_skip, attention, cotangent, point_weight, tile
@@ -1007,14 +1010,14 @@
     )
     pieces = [first, second, third, fourth]
     pieces = pieces + [paired(after(piece, own_terms), "seq", 1) for piece in pieces]
-    convs, terms = other_terms(meta, order, moved, sums, slopes, own_terms, pieces)
+    convs, terms = other_terms(meta, moved, sums, slopes, own_terms, pieces)
     terms, *got = lax.optimization_barrier((terms, *got))
     total = terms + crossed(terms, 1, 0)
     total = joined(total, (2, 0), (0, 1))
     skip_grad, attention_grad = other_grads(
         meta, moved, convs, depth_filter, skip_grad, att_grad
     )
-    target_rows = targets(meta, order, mine, got, point_weight, pieces, slabs)
+    target_rows = targets(meta, mine, got, point_weight, pieces, slabs)
     total, skip_grad, attention_grad = lax.optimization_barrier(
         (total, skip_grad, attention_grad)
     )

time: 62.6 us -> 57.1 us (0.912)
  local copies, waits for them, and re-layouts: 4.37 us -> 0.04 us
  Pallas kernels: 21.7 us -> 19.3 us
  waiting for transfers between devices: 7.56 us -> 9.06 us
    unnamed x32 -> x16, local copies, waits for them, and re-layouts: 4.29 us -> 0.04 us
    pallas_call x1, Pallas kernels: 3.25 us -> 1.93 us  [targets(): pl.pallas_call(functools.partial(target_kernel, slabs), grid_spec=pltpu.P...]
    ppermute x3, waiting for transfers between devices: 1.38 us -> 2.58 us  [staggered(): return lax.ppermute(part, 'seq', pairs)]
    pallas_call x1, Pallas kernels: 3.77 us -> 2.67 us  [other_terms(): pl.pallas_call(terms_kernel, grid_spec=pltpu.PrefetchScalarGridSpec(num_s...]
  transfers between devices with their start and end apart: 24 -> 24, of which waited for: 7 -> 10; matrix products, arithmetic and copies ran while one was open for 0% -> 0% of each run, Pallas kernels for 30% -> 28%
where the time goes in v8:
time: 57.1 us; the launch traced here: 56.9 us
  starting transfers between devices  26.5 us (46%)
  Pallas kernels  19.3 us (34%)
  waiting for transfers between devices  9.06 us (16%)
  other arithmetic  1.27 us (2%)
  between operations  0.8 us (1%)
    ppermute x3, starting transfers between devices, staggered(): return lax.ppermute(part, 'seq', pairs)  9.63 us
    ppermute x13, starting transfers between devices, paired(): return lax.ppermute(part, axis, [(i, i ^ bit) for i in range(count)])  7.84 us
    ppermute x7, starting transfers between devices, crossed(): return lax.ppermute(part, ('seq', 'head'), pairs)  7.1 us
    pallas_call x1, Pallas kernels, own_half(): pl.pallas_call(functools.partial(own_kernel, slabs), grid_spec=pltpu.Pref...  4.94 us
    ppermute x13, waiting for transfers between devices, paired(): return lax.ppermute(part, axis, [(i, i ^ bit) for i in range(count)])  3.82 us
    pallas_call x1, Pallas kernels, packed(): pl.pallas_call(pack_kernel, grid_spec=pltpu.PrefetchScalarGridSpec(num_sc...  3.15 us
    pallas_call x1, Pallas kernels, other_terms(): pl.pallas_call(terms_kernel, grid_spec=pltpu.PrefetchScalarGridSpec(num_s...  2.67 us
    ppermute x7, waiting for transfers between devices, crossed(): return lax.ppermute(part, ('seq', 'head'), pairs)  2.66 us
  transfers between devices with their start and end apart: 24, of which 10 were waited for; matrix products, arithmetic and copies ran while one was open for 0% of the time, Pallas kernels for 28%

profile of v8, /device:TPU:0, one launch (start us, length us, event | category | flops | bytes accessed | tf_op | source)
XLA Modules:
  0.0 56.9 jit_solution(2960909129831610902)
XLA Ops:
  1.3 3.1 %pack_edges.1 = (bf16[16,1536]{1,0:T(8,128)(2,1)}, bf16[16,1536]{1,0:T(8,128)(2,1)}, bf16[16,1536]{1,0:T(8,128)(2,1)}, bf16[384,384]{1,0:T(8,128)(2,1)}, bf16[38...) custom-call(s32[2]{0:T(128)} %pad_add_fusion.meta, bf16[2,128,1536]{2,1,0:T(8,128)(2,1)} %skip.3, ...), custom_call_target="tpu_custom_call" | custom-call | tf_op jit(solution)/shard_map/pack_edges/pallas_call | solution.py:419
  4.4 5.4 %collective-permute-start.2 = (bf16[16,1536]{1,0:T(8,128)(2,1)}, bf16[16,1536]{1,0:T(8,128)(2,1)S(1)}, u32[]{:S(2)}, u32[]{:S(2)}) collective-permute-start(bf16[16,1536]{1,0:T(8,128)(2,1)} %get-tuple-element.39), channel_id=1, source_target_pairs={{0,30},{2,4},{4,2},{6,8},{8,6},{10,12},{12,10},{14,16},{16,14},{18... | collective-permute-start | bytes 147464 | tf_op jit(solution)/shard_map/ppermute | solution.py:950
  9.9 1.9 %collective-permute-start.4 = (bf16[16,1536]{1,0:T(8,128)(2,1)}, bf16[16,1536]{1,0:T(8,128)(2,1)S(1)}, u32[]{:S(2)}, u32[]{:S(2)}) collective-permute-start(bf16[16,1536]{1,0:T(8,128)(2,1)} %get-tuple-element.40), channel_id=1, source_target_pairs={{0,28},{2,30},{4,8},{6,10},{8,4},{10,6},{12,16},{14,18},{16,12},{1... | collective-permute-start | bytes 147464 | tf_op jit(solution)/shard_map/ppermute | solution.py:950
  12.0 1.5 %collective-permute-start.7 = (bf16[384,384]{1,0:T(8,128)(2,1)}, bf16[384,384]{1,0:T(8,128)(2,1)S(1)}, u32[]{:S(2)}, u32[]{:S(2)}) collective-permute-start(bf16[384,384]{1,0:T(8,128)(2,1)} %get-tuple-element.52), channel_id=1, source_target_pairs={{0,1},{1,0},{2,3},{3,2},{4,5},{5,4},{6,7},{7,6},{8,9},{9,8},{10,11... | collective-permute-start | bytes 884744 | tf_op jit(solution)/shard_map/ppermute | solution.py:941
  13.5 1.9 %collective-permute-start.6 = (bf16[2,128,1536]{2,1,0:T(8,128)(2,1)S(1)}, bf16[2,128,1536]{2,1,0:T(8,128)(2,1)S(1)}, u32[]{:S(2)}, u32[]{:S(2)}) collective-permute-start(bf16[2,128,1536]{2,1,0:T(8,128)(2,1)S(1)} %copy-done.1), channel_id=1, source_target_pairs={{0,2},{2,4},{4,6},{6,8},{8,10},{10,12},{12,14},{14,16},{16,18},{18... | collective-permute-start | bytes 2359304 | tf_op jit(solution)/shard_map/ppermute | solution.py:204
  15.5 1.4 %collective-permute-done.4 = bf16[16,1536]{1,0:T(8,128)(2,1)S(1)} collective-permute-done((bf16[16,1536]{1,0:T(8,128)(2,1)}, bf16[16,1536]{1,0:T(8,128)(2,1)S(1)}, u32[]{:S(2)}, u32[]{:S(2)}) %collective-permute-start.4) | collective-permute-done | bytes 49184 | tf_op jit(solution)/shard_map/ppermute | solution.py:950
  16.9 1.6 %collective-permute-start.5 = (bf16[16,1536]{1,0:T(8,128)(2,1)S(1)}, bf16[16,1536]{1,0:T(8,128)(2,1)S(1)}, u32[]{:S(2)}, u32[]{:S(2)}) collective-permute-start(bf16[16,1536]{1,0:T(8,128)(2,1)S(1)} %get-tuple-element.71), channel_id=1, source_target_pairs={{0,1},{1,0},{2,3},{3,2},{4,5},{5,4},{6,7},{7,6},{8,9},{9,8},{10,11... | collective-permute-start | bytes 147464 | tf_op jit(solution)/shard_map/ppermute | solution.py:941
  19.0 1.5 %collective-permute-start.10 = (bf16[384,384]{1,0:T(8,128)(2,1)}, bf16[384,384]{1,0:T(8,128)(2,1)S(1)}, u32[]{:S(2)}, u32[]{:S(2)}) collective-permute-start(bf16[384,384]{1,0:T(8,128)(2,1)} %get-tuple-element.53), channel_id=1, source_target_pairs={{0,1},{1,0},{2,3},{3,2},{4,5},{5,4},{6,7},{7,6},{8,9},{9,8},{10,11... | collective-permute-start | bytes 884744 | tf_op jit(solution)/shard_map/ppermute | solution.py:941
  20.5 1.6 %collective-permute-done.7.refs_0_ = bf16[384,384]{1,0:T(8,128)(2,1)S(1)} collective-permute-done((bf16[384,384]{1,0:T(8,128)(2,1)}, bf16[384,384]{1,0:T(8,128)(2,1)S(1)}, u32[]{:S(2)}, u32[]{:S(2)}) %collective-permute-start.7) | collective-permute-done | bytes 294944 | tf_op jit(solution)/shard_map/ppermute | solution.py:941
  22.0 1.0 %collective-permute-done.5.twin = bf16[16,1536]{1,0:T(8,128)(2,1)S(1)} collective-permute-done((bf16[16,1536]{1,0:T(8,128)(2,1)S(1)}, bf16[16,1536]{1,0:T(8,128)(2,1)S(1)}, u32[]{:S(2)}, u32[]{:S(2)}) %collective-permute-start.5) | collective-permute-done | bytes 49184 | tf_op jit(solution)/shard_map/ppermute | solution.py:941
  23.1 1.3 %collective-permute-start.9 = (bf16[384,384]{1,0:T(8,128)(2,1)S(1)}, bf16[384,384]{1,0:T(8,128)(2,1)S(1)}, u32[]{:S(2)}, u32[]{:S(2)}) collective-permute-start(bf16[384,384]{1,0:T(8,128)(2,1)S(1)} %collective-permute-done.7.refs_0_), channel_id=1, source_target_pairs={{0,8},{2,10},{4,12},{6,14},{8,0},{10,2},{12,4},{14,6},{16,24},{18,... | collective-permute-start | bytes 884744 | tf_op jit(solution)/shard_map/ppermute | solution.py:941
  24.4 2.1 %own_slopes.1 = (bf16[32,768]{1,0:T(8,128)(2,1)S(1)}, bf16[2,144,768]{2,1,0:T(8,128)(2,1)S(1)}, f32[2,144,768]{2,1,0:T(8,128)S(1)}) custom-call(s32[2]{0:T(128)S(1)} %copy-done.5, s32[2]{0:T(128)S(1)} %copy-done.6, s32[2,32]{1,0:T(2,128)S(1)} %copy-done.7, bf16[4,64,768]{2,1,0:T(8,128)(2,1)S(1)} %copy-done.2, bf16[2,128,1536]{2,1,0:T(8,128)(2,1)S(1)} %copy-done.3, ...), custom_call_target="tpu_custom_call" | custom-call | flops 3000000000 | bytes 1000000 | tf_op jit(solution)/shard_map/own_slopes/pallas_call | solution.py:558
  27.3 2.6 %other_slopes.1 = (bf16[2,144,768]{2,1,0:T(8,128)(2,1)S(1)}, f32[2,144,768]{2,1,0:T(8,128)S(1)}, bf16[16,1536]{1,0:T(8,128)(2,1)S(1)}, bf16[16,1536]{1,0:T(8,128)(2,1)S(1)}) custom-call(s32[2]{0:T(128)S(1)} %copy-done.5, s32[2]{0:T(128)S(1)} %copy-done.6, s32[2,32]{1,0:T(2,128)S(1)} %copy-done.7, bf16[2,64,768]{2,1,0:T(8,128)(2,1)S(1)} %collective-permute-done.att, ...), custom_call_target="tpu_custom_call" | custom-call | flops 3000000000 | bytes 1000000 | tf_op jit(solution)/shard_map/other_slopes/pallas_call | solution.py:747
  29.9 4.9 %own_half.1 = (bf16[2,144,1536]{2,1,0:T(8,128)(2,1)S(1)}, f32[3,768]{1,0:T(4,128)S(1)}, bf16[2,128,1536]{2,1,0:T(8,128)(2,1)}, bf16[2,64,1536]{2,1,0:T(8,128)(2,1)}) custom-call(s32[2]{0:T(128)S(1)} %copy-done.5, s32[2]{0:T(128)S(1)} %copy-done.6, bf16[2,144,768]{2,1,0:T(8,128)(2,1)S(1)} %get-tuple-element.45.sums, ...), custom_call_target="tpu_custom_call" | custom-call | flops 1 | bytes 1 | tf_op jit(solution)/shard_map/own_half/pallas_call | solution.py:661
  36.5 2.3 %collective-permute-start.16 = (bf16[16,1536]{1,0:T(8,128)(2,1)S(1)}, bf16[16,1536]{1,0:T(8,128)(2,1)S(1)}, u32[]{:S(2)}, u32[]{:S(2)}) collective-permute-start(bf16[16,1536]{1,0:T(8,128)(2,1)S(1)} %get-tuple-element.43), channel_id=1, source_target_pairs={{0,30},{2,4},{4,2},{6,8},{8,6},{10,12},{12,10},{14,16},{16,14},{18... | collective-permute-start | bytes 147464 | tf_op jit(solution)/shard_map/ppermute | solution.py:950
  38.8 2.7 %other_terms.1 = (bf16[2,144,768]{2,1,0:T(8,128)(2,1)S(1)}, f32[3,1536]{1,0:T(4,128)S(1)}) custom-call(s32[2]{0:T(128)S(1)} %copy-done.5, bf16[2,144,1536]{2,1,0:T(8,128)(2,1)S(1)} %get-tuple-element.48.moved, bf16[2,144,768]{2,1,0:T(8,128)(2,1)S(1)} %get-tuple-element.49.sums, f32[2,144,768]{2,1,0:T(8,128)S(1)} %get-tuple-element.50.slopes, ...), custom_call_target="tpu_custom_call" | custom-call | flops 679477248 | bytes 6291456 | tf_op jit(solution)/shard_map/other_terms/pallas_call | solution.py:824
  41.5 1.2 %collective-permute-done.16.got_b = bf16[16,1536]{1,0:T(8,128)(2,1)S(1)} collective-permute-done((bf16[16,1536]{1,0:T(8,128)(2,1)S(1)}, bf16[16,1536]{1,0:T(8,128)(2,1)S(1)}, u32[]{:S(2)}, u32[]{:S(2)}) %collective-permute-start.16) | collective-permute-done | bytes 49184 | tf_op jit(solution)/shard_map/ppermute | solution.py:950
  42.7 1.2 %collective-permute-done.17 = f32[3,1536]{1,0:T(4,128)S(1)} collective-permute-done((f32[3,1536]{1,0:T(4,128)S(1)}, f32[3,1536]{1,0:T(4,128)S(1)}, u32[]{:S(2)}, u32[]{:S(2)}) %collective-permute-start.17) | collective-permute-done | bytes 18464 | tf_op jit(solution)/shard_map/ppermute | solution.py:964
  43.9 1.6 %collective-permute-start.19 = (f32[3,1536]{1,0:T(4,128)S(1)}, f32[3,1536]{1,0:T(4,128)S(1)}, u32[]{:S(2)}, u32[]{:S(2)}) collective-permute-start(f32[3,1536]{1,0:T(4,128)S(1)} %add.34), channel_id=1, source_target_pairs={{0,1},{1,0},{2,3},{3,2},{4,5},{5,4},{6,7},{7,6},{8,9},{9,8},{10,11... | collective-permute-start | bytes 55304 | tf_op jit(solution)/shard_map/ppermute | solution.py:964
  45.5 2.0 %collective-permute-start.18 = (f32[3,1536]{1,0:T(4,128)S(1)}, f32[3,1536]{1,0:T(4,128)S(1)}, u32[]{:S(2)}, u32[]{:S(2)}) collective-permute-start(f32[3,1536]{1,0:T(4,128)S(1)} %add.34), channel_id=1, source_target_pairs={{0,4},{1,5},{2,6},{3,7},{4,0},{5,1},{6,2},{7,3},{8,12},{9,13},{10,... | collective-permute-start | bytes 55304 | tf_op jit(solution)/shard_map/ppermute | solution.py:964
  47.5 1.8 %other_grads.1 = (bf16[2,128,1536]{2,1,0:T(8,128)(2,1)}, bf16[2,64,1536]{2,1,0:T(8,128)(2,1)}) custom-call(s32[2]{0:T(128)S(1)} %copy-done.5, bf16[2,144,1536]{2,1,0:T(8,128)(2,1)S(1)} %get-tuple-element.48.moved, bf16[2,144,768]{2,1,0:T(8,128)(2,1)S(1)} %get-tuple-element.62.convs, ...), custom_call_target="tpu_custom_call", output_to_operand_aliasing={{0}: (4, {}), {1}: (5, {})} | custom-call | flops 4423680 | bytes 4194304 | tf_op jit(solution)/shard_map/other_grads/pallas_call | solution.py:876
  50.4 2.0 %collective-permute-start.23 = (f32[3,1536]{1,0:T(4,128)S(1)}, f32[3,1536]{1,0:T(4,128)S(1)}, u32[]{:S(2)}, u32[]{:S(2)}) collective-permute-start(f32[3,1536]{1,0:T(4,128)S(1)} %add_add_fusion), channel_id=1, source_target_pairs={{0,24},{1,25},{2,26},{3,27},{4,28},{5,29},{6,30},{7,31},{8,16},{9,... | collective-permute-start | bytes 55304 | tf_op jit(solution)/shard_map/ppermute | solution.py:964
  52.4 1.5 %collective-permute-start.21 = (f32[3,1536]{1,0:T(4,128)S(1)}, f32[3,1536]{1,0:T(4,128)S(1)}, u32[]{:S(2)}, u32[]{:S(2)}) collective-permute-start(f32[3,1536]{1,0:T(4,128)S(1)} %add_add_fusion), channel_id=1, source_target_pairs={{0,8},{1,9},{2,10},{3,11},{4,12},{5,13},{6,14},{7,15},{8,0},{9,1},... | collective-permute-start | bytes 55304 | tf_op jit(solution)/shard_map/ppermute | solution.py:964
  53.8 1.9 %targets.1 = bf16[2,2,1536]{2,1,0:T(2,128)(2,1)} custom-call(s32[2]{0:T(128)S(1)} %copy-done.5, bf16[16,1536]{1,0:T(8,128)(2,1)S(1)} %get-tuple-element.42.mine, bf16[16,1536]{1,0:T(8,128)(2,1)S(1)} %collective-permute-done.15.got_a, bf16[16,1536]{1,0:T(8,128)(2,1)S(1)} %collective-permute-done.16.got_b, bf16[768,1536]{1,0:T(8,128)(2,1)S(1)} %copy-done, ...), custom_call_target="tpu_custom_call" | custom-call | flops 75497472 | bytes 6291456 | tf_op jit(solution)/shard_map/targets/pallas_call | solution.py:922
  (52 shorter events, 6.0 us)
Async XLA Ops:
  4.4 9.1 %collective-permute-start.2 = (bf16[16,1536]{1,0:T(8,128)(2,1)}, bf16[16,1536]{1,0:T(8,128)(2,1)S(1)}, u32[]{:S(2)}, u32[]{:S(2)}) collective-permute-start(bf16[16,1536]{1,0:T(8,128)(2,1)} %get-tuple-element.39), channel_id=1, source_target_pairs={{0,30},{2,4},{4,2},{6,8},{8,6},{10,12},{12,10},{14,16},{16,14},{18... | collective-permute-start | bytes 147464 | tf_op jit(solution)/shard_map/ppermute | solution.py:950
  9.9 5.6 %collective-permute-start.3 = (bf16[16,1536]{1,0:T(8,128)(2,1)}, bf16[16,1536]{1,0:T(8,128)(2,1)S(1)}, u32[]{:S(2)}, u32[]{:S(2)}) collective-permute-start(bf16[16,1536]{1,0:T(8,128)(2,1)} %get-tuple-element.40), channel_id=1, source_target_pairs={{0,4},{2,6},{4,0},{6,2},{8,12},{10,14},{12,8},{14,10},{16,20},{18,... | collective-permute-start | bytes 147464 | tf_op jit(solution)/shard_map/ppermute | solution.py:941
  9.9 7.0 %collective-permute-start.4 = (bf16[16,1536]{1,0:T(8,128)(2,1)}, bf16[16,1536]{1,0:T(8,128)(2,1)S(1)}, u32[]{:S(2)}, u32[]{:S(2)}) collective-permute-start(bf16[16,1536]{1,0:T(8,128)(2,1)} %get-tuple-element.40), channel_id=1, source_target_pairs={{0,28},{2,30},{4,8},{6,10},{8,4},{10,6},{12,16},{14,18},{16,12},{1... | collective-permute-start | bytes 147464 | tf_op jit(solution)/shard_map/ppermute | solution.py:950
  11.8 5.1 %collective-permute-start.1 = (bf16[16,1536]{1,0:T(8,128)(2,1)}, bf16[16,1536]{1,0:T(8,128)(2,1)S(1)}, u32[]{:S(2)}, u32[]{:S(2)}) collective-permute-start(bf16[16,1536]{1,0:T(8,128)(2,1)} %get-tuple-element.38), channel_id=1, source_target_pairs={{0,2},{2,0},{4,6},{6,4},{8,10},{10,8},{12,14},{14,12},{16,18},{18,... | collective-permute-start | bytes 147464 | tf_op jit(solution)/shard_map/ppermute | solution.py:941
  12.0 10.0 %collective-permute-start.7 = (bf16[384,384]{1,0:T(8,128)(2,1)}, bf16[384,384]{1,0:T(8,128)(2,1)S(1)}, u32[]{:S(2)}, u32[]{:S(2)}) collective-permute-start(bf16[384,384]{1,0:T(8,128)(2,1)} %get-tuple-element.52), channel_id=1, source_target_pairs={{0,1},{1,0},{2,3},{3,2},{4,5},{5,4},{6,7},{7,6},{8,9},{9,8},{10,11... | collective-permute-start | bytes 884744 | tf_op jit(solution)/shard_map/ppermute | solution.py:941
  13.5 16.4 %collective-permute-start.6 = (bf16[2,128,1536]{2,1,0:T(8,128)(2,1)S(1)}, bf16[2,128,1536]{2,1,0:T(8,128)(2,1)S(1)}, u32[]{:S(2)}, u32[]{:S(2)}) collective-permute-start(bf16[2,128,1536]{2,1,0:T(8,128)(2,1)S(1)} %copy-done.1), channel_id=1, source_target_pairs={{0,2},{2,4},{4,6},{6,8},{8,10},{10,12},{12,14},{14,16},{16,18},{18... | collective-permute-start | bytes 2359304 | tf_op jit(solution)/shard_map/ppermute | solution.py:204
  16.9 6.2 %collective-permute-start.5 = (bf16[16,1536]{1,0:T(8,128)(2,1)S(1)}, bf16[16,1536]{1,0:T(8,128)(2,1)S(1)}, u32[]{:S(2)}, u32[]{:S(2)}) collective-permute-start(bf16[16,1536]{1,0:T(8,128)(2,1)S(1)} %get-tuple-element.71), channel_id=1, source_target_pairs={{0,1},{1,0},{2,3},{3,2},{4,5},{5,4},{6,7},{7,6},{8,9},{9,8},{10,11... | collective-permute-start | bytes 147464 | tf_op jit(solution)/shard_map/ppermute | solution.py:941
  18.5 8.8 %collective-permute-start = (bf16[2,64,768]{2,1,0:T(8,128)(2,1)}, bf16[2,64,768]{2,1,0:T(8,128)(2,1)S(1)}, u32[]{:S(2)}, u32[]{:S(2)}) collective-permute-start(bf16[2,64,768]{2,1,0:T(8,128)(2,1)} %get-tuple-element.37), channel_id=1, source_target_pairs={{0,1},{1,0},{2,3},{3,2},{4,5},{5,4},{6,7},{7,6},{8,9},{9,8},{10,11... | collective-permute-start | bytes 589832 | tf_op jit(solution)/shard_map/ppermute | solution.py:941
  19.0 16.6 %collective-permute-start.10 = (bf16[384,384]{1,0:T(8,128)(2,1)}, bf16[384,384]{1,0:T(8,128)(2,1)S(1)}, u32[]{:S(2)}, u32[]{:S(2)}) collective-permute-start(bf16[384,384]{1,0:T(8,128)(2,1)} %get-tuple-element.53), channel_id=1, source_target_pairs={{0,1},{1,0},{2,3},{3,2},{4,5},{5,4},{6,7},{7,6},{8,9},{9,8},{10,11... | collective-permute-start | bytes 884744 | tf_op jit(solution)/shard_map/ppermute | solution.py:941
  22.0 12.9 %collective-permute-start.8 = (bf16[384,384]{1,0:T(8,128)(2,1)S(1)}, bf16[384,384]{1,0:T(8,128)(2,1)S(1)}, u32[]{:S(2)}, u32[]{:S(2)}) collective-permute-start(bf16[384,384]{1,0:T(8,128)(2,1)S(1)} %collective-permute-done.7.refs_0_), channel_id=1, source_target_pairs={{0,4},{2,6},{4,0},{6,2},{8,12},{10,14},{12,8},{14,10},{16,20},{18,... | collective-permute-start | bytes 884744 | tf_op jit(solution)/shard_map/ppermute | solution.py:941
  23.1 12.4 %collective-permute-start.9 = (bf16[384,384]{1,0:T(8,128)(2,1)S(1)}, bf16[384,384]{1,0:T(8,128)(2,1)S(1)}, u32[]{:S(2)}, u32[]{:S(2)}) collective-permute-start(bf16[384,384]{1,0:T(8,128)(2,1)S(1)} %collective-permute-done.7.refs_0_), channel_id=1, source_target_pairs={{0,8},{2,10},{4,12},{6,14},{8,0},{10,2},{12,4},{14,6},{16,24},{18,... | collective-permute-start | bytes 884744 | tf_op jit(solution)/shard_map/ppermute | solution.py:941
  34.9 1.6 %collective-permute-start.11 = (bf16[384,384]{1,0:T(8,128)(2,1)S(1)}, bf16[384,384]{1,0:T(8,128)(2,1)S(1)}, u32[]{:S(2)}, u32[]{:S(2)}) collective-permute-start(bf16[384,384]{1,0:T(8,128)(2,1)S(1)} %collective-permute-done.7.refs_0_), channel_id=1, source_target_pairs={{0,2},{2,0},{4,6},{6,4},{8,10},{10,8},{12,14},{14,12},{16,18},{18,... | collective-permute-start | bytes 884744 | tf_op jit(solution)/shard_map/ppermute | solution.py:941
  35.0 3.9 %collective-permute-start.12 = (bf16[384,384]{1,0:T(8,128)(2,1)S(1)}, bf16[384,384]{1,0:T(8,128)(2,1)S(1)}, u32[]{:S(2)}, u32[]{:S(2)}) collective-permute-start(bf16[384,384]{1,0:T(8,128)(2,1)S(1)} %collective-permute-done.8.refs_1_), channel_id=1, source_target_pairs={{0,2},{2,0},{4,6},{6,4},{8,10},{10,8},{12,14},{14,12},{16,18},{18,... | collective-permute-start | bytes 884744 | tf_op jit(solution)/shard_map/ppermute | solution.py:941
  35.5 3.4 %collective-permute-start.13 = (bf16[384,384]{1,0:T(8,128)(2,1)S(1)}, bf16[384,384]{1,0:T(8,128)(2,1)S(1)}, u32[]{:S(2)}, u32[]{:S(2)}) collective-permute-start(bf16[384,384]{1,0:T(8,128)(2,1)S(1)} %collective-permute-done.9.refs_2_), channel_id=1, source_target_pairs={{0,2},{2,0},{4,6},{6,4},{8,10},{10,8},{12,14},{14,12},{16,18},{18,... | collective-permute-start | bytes 884744 | tf_op jit(solution)/shard_map/ppermute | solution.py:941
  35.5 3.3 %collective-permute-start.14 = (bf16[384,384]{1,0:T(8,128)(2,1)S(1)}, bf16[384,384]{1,0:T(8,128)(2,1)S(1)}, u32[]{:S(2)}, u32[]{:S(2)}) collective-permute-start(bf16[384,384]{1,0:T(8,128)(2,1)S(1)} %collective-permute-done.10.refs_3_), channel_id=1, source_target_pairs={{0,2},{2,0},{4,6},{6,4},{8,10},{10,8},{12,14},{14,12},{16,18},{18,... | collective-permute-start | bytes 884744 | tf_op jit(solution)/shard_map/ppermute | solution.py:941
  36.0 5.5 %collective-permute-start.15 = (bf16[16,1536]{1,0:T(8,128)(2,1)S(1)}, bf16[16,1536]{1,0:T(8,128)(2,1)S(1)}, u32[]{:S(2)}, u32[]{:S(2)}) collective-permute-start(bf16[16,1536]{1,0:T(8,128)(2,1)S(1)} %get-tuple-element.43), channel_id=1, source_target_pairs={{0,2},{2,0},{4,6},{6,4},{8,10},{10,8},{12,14},{14,12},{16,18},{18,... | collective-permute-start | bytes 147464 | tf_op jit(solution)/shard_map/ppermute | solution.py:941
  36.5 6.2 %collective-permute-start.16 = (bf16[16,1536]{1,0:T(8,128)(2,1)S(1)}, bf16[16,1536]{1,0:T(8,128)(2,1)S(1)}, u32[]{:S(2)}, u32[]{:S(2)}) collective-permute-start(bf16[16,1536]{1,0:T(8,128)(2,1)S(1)} %get-tuple-element.43), channel_id=1, source_target_pairs={{0,30},{2,4},{4,2},{6,8},{8,6},{10,12},{12,10},{14,16},{16,14},{18... | collective-permute-start | bytes 147464 | tf_op jit(solution)/shard_map/ppermute | solution.py:950
  42.7 1.2 %collective-permute-start.17 = (f32[3,1536]{1,0:T(4,128)S(1)}, f32[3,1536]{1,0:T(4,128)S(1)}, u32[]{:S(2)}, u32[]{:S(2)}) collective-permute-start(f32[3,1536]{1,0:T(4,128)S(1)} %get-tuple-element.61), channel_id=1, source_target_pairs={{0,2},{1,3},{2,0},{3,1},{4,6},{5,7},{6,4},{7,5},{8,10},{9,11},{10,... | collective-permute-start | bytes 55304 | tf_op jit(solution)/shard_map/ppermute | solution.py:964
  43.9 5.4 %collective-permute-start.19 = (f32[3,1536]{1,0:T(4,128)S(1)}, f32[3,1536]{1,0:T(4,128)S(1)}, u32[]{:S(2)}, u32[]{:S(2)}) collective-permute-start(f32[3,1536]{1,0:T(4,128)S(1)} %add.34), channel_id=1, source_target_pairs={{0,1},{1,0},{2,3},{3,2},{4,5},{5,4},{6,7},{7,6},{8,9},{9,8},{10,11... | collective-permute-start | bytes 55304 | tf_op jit(solution)/shard_map/ppermute | solution.py:964
  45.5 4.7 %collective-permute-start.20 = (f32[3,1536]{1,0:T(4,128)S(1)}, f32[3,1536]{1,0:T(4,128)S(1)}, u32[]{:S(2)}, u32[]{:S(2)}) collective-permute-start(f32[3,1536]{1,0:T(4,128)S(1)} %add.34), channel_id=1, source_target_pairs={{0,5},{1,4},{2,7},{3,6},{4,1},{5,0},{6,3},{7,2},{8,13},{9,12},{10,... | collective-permute-start | bytes 55304 | tf_op jit(solution)/shard_map/ppermute | solution.py:964
  45.5 4.7 %collective-permute-start.18 = (f32[3,1536]{1,0:T(4,128)S(1)}, f32[3,1536]{1,0:T(4,128)S(1)}, u32[]{:S(2)}, u32[]{:S(2)}) collective-permute-start(f32[3,1536]{1,0:T(4,128)S(1)} %add.34), channel_id=1, source_target_pairs={{0,4},{1,5},{2,6},{3,7},{4,0},{5,1},{6,2},{7,3},{8,12},{9,13},{10,... | collective-permute-start | bytes 55304 | tf_op jit(solution)/shard_map/ppermute | solution.py:964
  50.3 5.5 %collective-permute-start.22 = (f32[3,1536]{1,0:T(4,128)S(1)}, f32[3,1536]{1,0:T(4,128)S(1)}, u32[]{:S(2)}, u32[]{:S(2)}) collective-permute-start(f32[3,1536]{1,0:T(4,128)S(1)} %add_add_fusion), channel_id=1, source_target_pairs={{0,16},{1,17},{2,18},{3,19},{4,20},{5,21},{6,22},{7,23},{8,24},{9,... | collective-permute-start | bytes 55304 | tf_op jit(solution)/shard_map/ppermute | solution.py:964
  50.4 5.7 %collective-permute-start.23 = (f32[3,1536]{1,0:T(4,128)S(1)}, f32[3,1536]{1,0:T(4,128)S(1)}, u32[]{:S(2)}, u32[]{:S(2)}) collective-permute-start(f32[3,1536]{1,0:T(4,128)S(1)} %add_add_fusion), channel_id=1, source_target_pairs={{0,24},{1,25},{2,26},{3,27},{4,28},{5,29},{6,30},{7,31},{8,16},{9,... | collective-permute-start | bytes 55304 | tf_op jit(solution)/shard_map/ppermute | solution.py:964
  52.4 3.9 %collective-permute-start.21 = (f32[3,1536]{1,0:T(4,128)S(1)}, f32[3,1536]{1,0:T(4,128)S(1)}, u32[]{:S(2)}, u32[]{:S(2)}) collective-permute-start(f32[3,1536]{1,0:T(4,128)S(1)} %add_add_fusion), channel_id=1, source_target_pairs={{0,8},{1,9},{2,10},{3,11},{4,12},{5,13},{6,14},{7,15},{8,0},{9,1},... | collective-permute-start | bytes 55304 | tf_op jit(solution)/shard_map/ppermute | solution.py:964
  (8 other events, 153.9 us)

commit v9 on v8

--- a/solution.py
+++ b/solution.py
@@ -994,22 +994,23 @@
     edge = edge_a + jnp.where(outer, nothing, edge_b)
     twin = paired(edge, "head", 1)
     edge = edge + jnp.where(slab % 4 >= 2, far_a, jnp.where(slab < 2, nothing, far_b))
+    asked, own_sums, own_slope = own_slopes(
+        meta, crop_offset, target_bins, attention, encoder_skip, edge, depth_filter
+    )
     second = paired(first, "seq", 2)
     third = paired(first, "seq", 4)
     fourth = paired(last_tile, "head", 1)
-    asked, own_sums, own_slope = own_slopes(
-        meta, crop_offset, target_bins, attention, encoder_skip, edge, depth_filter
+    moved, own_terms, skip_grad, att_grad = own_half(
+        meta, crop_offset, own_sums, own_slope, edge, prev, cotangent, point_weight, depth_filter,
+        slabs,
     )
     sums, slopes, mine, shown = other_slopes(
-        meta, crop_offset, target_bins, shipped, encoder_skip, edge, twin, depth_filter, asked
+        after(meta, own_terms), crop_offset, target_bins, shipped, encoder_skip, edge, twin, depth_filter, asked
     )
     got = [paired(shown, "seq", 1), staggered(shown, 1)]
-    moved, own_terms, skip_grad, att_grad = own_half(
-        after(meta, shown), crop_offset, own_sums, own_slope, edge, prev, cotangent, point_weight, depth_filter,
-        slabs,
-    )
     pieces = [first, second, third, fourth]
-    pieces = pieces + [paired(after(piece, own_terms), "seq", 1) for piece in pieces]
+    ties = [own_terms] * 3 + [shown]
+    pieces = pieces + [paired(after(*both), "seq", 1) for both in zip(pieces, ties)]
     convs, terms = other_terms(meta, moved, sums, slopes, own_terms, pieces)
     terms, *got = lax.optimization_barrier((terms, *got))
     total = terms + crossed(terms, 1, 0)

time: 57.1 us -> 65.7 us (1.15)
  starting transfers between devices: 26.5 us -> 36 us
  waiting for transfers between devices: 9.06 us -> 8.14 us
    ppermute x13, starting transfers between devices: 7.84 us -> 13 us  [paired(): return lax.ppermute(part, axis, [(i, i ^ bit) for i in range(count)])]
    ppermute x3, starting transfers between devices: 9.63 us -> 14.4 us  [staggered(): return lax.ppermute(part, 'seq', pairs)]
    ppermute x13, waiting for transfers between devices: 3.82 us -> 0.03 us  [paired(): return lax.ppermute(part, axis, [(i, i ^ bit) for i in range(count)])]
    ppermute x3, waiting for transfers between devices: 2.58 us -> 4.24 us  [staggered(): return lax.ppermute(part, 'seq', pairs)]
    ppermute x7, waiting for transfers between devices: 2.66 us -> 3.86 us  [crossed(): return lax.ppermute(part, ('seq', 'head'), pairs)]
  transfers between devices with their start and end apart: 24 -> 24, of which waited for: 10 -> 5; matrix products, arithmetic and copies ran while one was open for 0% -> 0% of each run, Pallas kernels for 28% -> 25%
where the time goes in v9:
time: 65.7 us; the launch traced here: 65.5 us
  starting transfers between devices  36 us (55%)
  Pallas kernels  19.3 us (29%)
  waiting for transfers between devices  8.14 us (12%)
  other arithmetic  1.27 us (2%)
  between operations  0.83 us (1%)
    ppermute x3, starting transfers between devices, staggered(): return lax.ppermute(part, 'seq', pairs)  14.4 us
    ppermute x13, starting transfers between devices, paired(): return lax.ppermute(part, axis, [(i, i ^ bit) for i in range(count)])  13 us
    ppermute x7, starting transfers between devices, crossed(): return lax.ppermute(part, ('seq', 'head'), pairs)  7.34 us
    pallas_call x1, Pallas kernels, own_half(): pl.pallas_call(functools.partial(own_kernel, slabs), grid_spec=pltpu.Pref...  4.93 us
    ppermute x3, waiting for transfers between devices, staggered(): return lax.ppermute(part, 'seq', pairs)  4.24 us
    ppermute x7, waiting for transfers between devices, crossed(): return lax.ppermute(part, ('seq', 'head'), pairs)  3.86 us
    pallas_call x1, Pallas kernels, packed(): pl.pallas_call(pack_kernel, grid_spec=pltpu.PrefetchScalarGridSpec(num_sc...  3.16 us
    pallas_call x1, Pallas kernels, other_terms(): pl.pallas_call(terms_kernel, grid_spec=pltpu.PrefetchScalarGridSpec(num_s...  2.68 us
  transfers between devices with their start and end apart: 24, of which 5 were waited for; matrix products, arithmetic and copies ran while one was open for 0% of the time, Pallas kernels for 25%

profile of v9, /device:TPU:0, one launch (start us, length us, event | category | flops | bytes accessed | tf_op | source)
XLA Modules:
  0.0 65.5 jit_solution(12828948614583235923)
XLA Ops:
  1.3 3.2 %pack_edges.1 = (bf16[16,1536]{1,0:T(8,128)(2,1)}, bf16[16,1536]{1,0:T(8,128)(2,1)}, bf16[16,1536]{1,0:T(8,128)(2,1)}, bf16[384,384]{1,0:T(8,128)(2,1)}, bf16[38...) custom-call(s32[2]{0:T(128)} %pad_add_fusion.meta, bf16[2,128,1536]{2,1,0:T(8,128)(2,1)} %skip.3, ...), custom_call_target="tpu_custom_call" | custom-call | tf_op jit(solution)/shard_map/pack_edges/pallas_call | solution.py:419
  4.4 5.4 %collective-permute-start.1 = (bf16[16,1536]{1,0:T(8,128)(2,1)}, bf16[16,1536]{1,0:T(8,128)(2,1)S(1)}, u32[]{:S(2)}, u32[]{:S(2)}) collective-permute-start(bf16[16,1536]{1,0:T(8,128)(2,1)} %get-tuple-element.38), channel_id=1, source_target_pairs={{0,30},{2,4},{4,2},{6,8},{8,6},{10,12},{12,10},{14,16},{16,14},{18... | collective-permute-start | bytes 147464 | tf_op jit(solution)/shard_map/ppermute | solution.py:950
  9.9 2.1 %collective-permute-done.1 = bf16[16,1536]{1,0:T(8,128)(2,1)S(1)} collective-permute-done((bf16[16,1536]{1,0:T(8,128)(2,1)}, bf16[16,1536]{1,0:T(8,128)(2,1)S(1)}, u32[]{:S(2)}, u32[]{:S(2)}) %collective-permute-start.1) | collective-permute-done | bytes 49184 | tf_op jit(solution)/shard_map/ppermute | solution.py:950
  11.9 1.3 %collective-permute-start.4 = (bf16[2,128,1536]{2,1,0:T(8,128)(2,1)S(1)}, bf16[2,128,1536]{2,1,0:T(8,128)(2,1)S(1)}, u32[]{:S(2)}, u32[]{:S(2)}) collective-permute-start(bf16[2,128,1536]{2,1,0:T(8,128)(2,1)S(1)} %copy-done.1), channel_id=1, source_target_pairs={{0,2},{2,4},{4,6},{6,8},{8,10},{10,12},{12,14},{14,16},{16,18},{18... | collective-permute-start | bytes 2359304 | tf_op jit(solution)/shard_map/ppermute | solution.py:204
  13.3 2.0 %collective-permute-start.7 = (bf16[384,384]{1,0:T(8,128)(2,1)}, bf16[384,384]{1,0:T(8,128)(2,1)S(1)}, u32[]{:S(2)}, u32[]{:S(2)}) collective-permute-start(bf16[384,384]{1,0:T(8,128)(2,1)} %get-tuple-element.51), channel_id=1, source_target_pairs={{0,1},{1,0},{2,3},{3,2},{4,5},{5,4},{6,7},{7,6},{8,9},{9,8},{10,11... | collective-permute-start | bytes 884744 | tf_op jit(solution)/shard_map/ppermute | solution.py:941
  15.3 4.8 %collective-permute-start.3 = (bf16[16,1536]{1,0:T(8,128)(2,1)}, bf16[16,1536]{1,0:T(8,128)(2,1)S(1)}, u32[]{:S(2)}, u32[]{:S(2)}) collective-permute-start(bf16[16,1536]{1,0:T(8,128)(2,1)} %get-tuple-element.39), channel_id=1, source_target_pairs={{0,28},{2,30},{4,8},{6,10},{8,4},{10,6},{12,16},{14,18},{16,12},{1... | collective-permute-start | bytes 147464 | tf_op jit(solution)/shard_map/ppermute | solution.py:950
  20.7 2.2 %collective-permute-done.3 = bf16[16,1536]{1,0:T(8,128)(2,1)S(1)} collective-permute-done((bf16[16,1536]{1,0:T(8,128)(2,1)}, bf16[16,1536]{1,0:T(8,128)(2,1)S(1)}, u32[]{:S(2)}, u32[]{:S(2)}) %collective-permute-start.3) | collective-permute-done | bytes 49184 | tf_op jit(solution)/shard_map/ppermute | solution.py:950
  23.4 7.1 %collective-permute-start.9 = (bf16[384,384]{1,0:T(8,128)(2,1)S(1)}, bf16[384,384]{1,0:T(8,128)(2,1)S(1)}, u32[]{:S(2)}, u32[]{:S(2)}) collective-permute-start(bf16[384,384]{1,0:T(8,128)(2,1)S(1)} %collective-permute-done.7.refs_0_), channel_id=1, source_target_pairs={{0,8},{2,10},{4,12},{6,14},{8,0},{10,2},{12,4},{14,6},{16,24},{18,... | collective-permute-start | bytes 884744 | tf_op jit(solution)/shard_map/ppermute | solution.py:941
  30.5 1.6 %collective-permute-start.6 = (bf16[16,1536]{1,0:T(8,128)(2,1)S(1)}, bf16[16,1536]{1,0:T(8,128)(2,1)S(1)}, u32[]{:S(2)}, u32[]{:S(2)}) collective-permute-start(bf16[16,1536]{1,0:T(8,128)(2,1)S(1)} %get-tuple-element.71), channel_id=1, source_target_pairs={{0,1},{1,0},{2,3},{3,2},{4,5},{5,4},{6,7},{7,6},{8,9},{9,8},{10,11... | collective-permute-start | bytes 147464 | tf_op jit(solution)/shard_map/ppermute | solution.py:941
  32.2 2.1 %own_slopes.1 = (bf16[32,768]{1,0:T(8,128)(2,1)S(1)}, bf16[2,144,768]{2,1,0:T(8,128)(2,1)S(1)}, f32[2,144,768]{2,1,0:T(8,128)S(1)}) custom-call(s32[2]{0:T(128)S(1)} %copy-done.5, s32[2]{0:T(128)S(1)} %copy-done.6, s32[2,32]{1,0:T(2,128)S(1)} %copy-done.7, bf16[4,64,768]{2,1,0:T(8,128)(2,1)S(1)} %copy-done.2, bf16[2,128,1536]{2,1,0:T(8,128)(2,1)S(1)} %copy-done.3, ...), custom_call_target="tpu_custom_call" | custom-call | flops 3000000000 | bytes 1000000 | tf_op jit(solution)/shard_map/own_slopes/pallas_call | solution.py:558
  34.3 4.9 %own_half.1 = (bf16[2,144,1536]{2,1,0:T(8,128)(2,1)S(1)}, f32[3,768]{1,0:T(4,128)S(1)}, bf16[2,128,1536]{2,1,0:T(8,128)(2,1)}, bf16[2,64,1536]{2,1,0:T(8,128)(2,1)}) custom-call(s32[2]{0:T(128)S(1)} %copy-done.5, s32[2]{0:T(128)S(1)} %copy-done.6, bf16[2,144,768]{2,1,0:T(8,128)(2,1)S(1)} %get-tuple-element.40.sums, ...), custom_call_target="tpu_custom_call" | custom-call | flops 1 | bytes 1 | tf_op jit(solution)/shard_map/own_half/pallas_call | solution.py:661
  39.9 2.6 %other_slopes.1 = (bf16[2,144,768]{2,1,0:T(8,128)(2,1)S(1)}, f32[2,144,768]{2,1,0:T(8,128)S(1)}, bf16[16,1536]{1,0:T(8,128)(2,1)S(1)}, bf16[16,1536]{1,0:T(8,128)(2,1)S(1)}) custom-call(s32[2]{0:T(128)S(1)} %copy-done.5, s32[2]{0:T(128)S(1)} %copy-done.6, s32[2,32]{1,0:T(2,128)S(1)} %copy-done.7, bf16[2,64,768]{2,1,0:T(8,128)(2,1)S(1)} %collective-permute-done.5.att, ...), custom_call_target="tpu_custom_call" | custom-call | flops 3000000000 | bytes 1000000 | tf_op jit(solution)/shard_map/other_slopes/pallas_call | solution.py:747
  43.1 4.1 %collective-permute-start.16 = (bf16[16,1536]{1,0:T(8,128)(2,1)S(1)}, bf16[16,1536]{1,0:T(8,128)(2,1)S(1)}, u32[]{:S(2)}, u32[]{:S(2)}) collective-permute-start(bf16[16,1536]{1,0:T(8,128)(2,1)S(1)} %get-tuple-element.56), channel_id=1, source_target_pairs={{0,30},{2,4},{4,2},{6,8},{8,6},{10,12},{12,10},{14,16},{16,14},{18... | collective-permute-start | bytes 147464 | tf_op jit(solution)/shard_map/ppermute | solution.py:950
  47.2 2.7 %other_terms.1 = (bf16[2,144,768]{2,1,0:T(8,128)(2,1)S(1)}, f32[3,1536]{1,0:T(4,128)S(1)}) custom-call(s32[2]{0:T(128)S(1)} %copy-done.5, bf16[2,144,1536]{2,1,0:T(8,128)(2,1)S(1)} %get-tuple-element.48.moved, bf16[2,144,768]{2,1,0:T(8,128)(2,1)S(1)} %get-tuple-element.49.sums, f32[2,144,768]{2,1,0:T(8,128)S(1)} %get-tuple-element.50.slopes, ...), custom_call_target="tpu_custom_call" | custom-call | flops 679477248 | bytes 6291456 | tf_op jit(solution)/shard_map/other_terms/pallas_call | solution.py:824
  50.0 1.2 %collective-permute-done.17 = f32[3,1536]{1,0:T(4,128)S(1)} collective-permute-done((f32[3,1536]{1,0:T(4,128)S(1)}, f32[3,1536]{1,0:T(4,128)S(1)}, u32[]{:S(2)}, u32[]{:S(2)}) %collective-permute-start.17) | collective-permute-done | bytes 18464 | tf_op jit(solution)/shard_map/ppermute | solution.py:964
  51.2 1.6 %collective-permute-start.19 = (f32[3,1536]{1,0:T(4,128)S(1)}, f32[3,1536]{1,0:T(4,128)S(1)}, u32[]{:S(2)}, u32[]{:S(2)}) collective-permute-start(f32[3,1536]{1,0:T(4,128)S(1)} %add.34), channel_id=1, source_target_pairs={{0,1},{1,0},{2,3},{3,2},{4,5},{5,4},{6,7},{7,6},{8,9},{9,8},{10,11... | collective-permute-start | bytes 55304 | tf_op jit(solution)/shard_map/ppermute | solution.py:964
  52.8 1.9 %collective-permute-start.18 = (f32[3,1536]{1,0:T(4,128)S(1)}, f32[3,1536]{1,0:T(4,128)S(1)}, u32[]{:S(2)}, u32[]{:S(2)}) collective-permute-start(f32[3,1536]{1,0:T(4,128)S(1)} %add.34), channel_id=1, source_target_pairs={{0,4},{1,5},{2,6},{3,7},{4,0},{5,1},{6,2},{7,3},{8,12},{9,13},{10,... | collective-permute-start | bytes 55304 | tf_op jit(solution)/shard_map/ppermute | solution.py:964
  54.7 1.8 %other_grads.1 = (bf16[2,128,1536]{2,1,0:T(8,128)(2,1)}, bf16[2,64,1536]{2,1,0:T(8,128)(2,1)}) custom-call(s32[2]{0:T(128)S(1)} %copy-done.5, bf16[2,144,1536]{2,1,0:T(8,128)(2,1)S(1)} %get-tuple-element.48.moved, bf16[2,144,768]{2,1,0:T(8,128)(2,1)S(1)} %get-tuple-element.62.convs, ...), custom_call_target="tpu_custom_call", output_to_operand_aliasing={{0}: (4, {}), {1}: (5, {})} | custom-call | flops 4423680 | bytes 4194304 | tf_op jit(solution)/shard_map/other_grads/pallas_call | solution.py:876
  56.6 0.9 %collective-permute-done.20 = f32[3,1536]{1,0:T(4,128)S(1)} collective-permute-done((f32[3,1536]{1,0:T(4,128)S(1)}, f32[3,1536]{1,0:T(4,128)S(1)}, u32[]{:S(2)}, u32[]{:S(2)}) %collective-permute-start.20) | collective-permute-done | bytes 18464 | tf_op jit(solution)/shard_map/ppermute | solution.py:964
  57.5 1.8 %collective-permute-start.22 = (f32[3,1536]{1,0:T(4,128)S(1)}, f32[3,1536]{1,0:T(4,128)S(1)}, u32[]{:S(2)}, u32[]{:S(2)}) collective-permute-start(f32[3,1536]{1,0:T(4,128)S(1)} %add_add_fusion), channel_id=1, source_target_pairs={{0,16},{1,17},{2,18},{3,19},{4,20},{5,21},{6,22},{7,23},{8,24},{9,... | collective-permute-start | bytes 55304 | tf_op jit(solution)/shard_map/ppermute | solution.py:964
  59.3 1.4 %collective-permute-start.23 = (f32[3,1536]{1,0:T(4,128)S(1)}, f32[3,1536]{1,0:T(4,128)S(1)}, u32[]{:S(2)}, u32[]{:S(2)}) collective-permute-start(f32[3,1536]{1,0:T(4,128)S(1)} %add_add_fusion), channel_id=1, source_target_pairs={{0,24},{1,25},{2,26},{3,27},{4,28},{5,29},{6,30},{7,31},{8,16},{9,... | collective-permute-start | bytes 55304 | tf_op jit(solution)/shard_map/ppermute | solution.py:964
  61.2 1.9 %targets.1 = bf16[2,2,1536]{2,1,0:T(2,128)(2,1)} custom-call(s32[2]{0:T(128)S(1)} %copy-done.5, bf16[16,1536]{1,0:T(8,128)(2,1)S(1)} %get-tuple-element.47.mine, bf16[16,1536]{1,0:T(8,128)(2,1)S(1)} %collective-permute-done.15.got_a, bf16[16,1536]{1,0:T(8,128)(2,1)S(1)} %collective-permute-done.16.got_b, bf16[768,1536]{1,0:T(8,128)(2,1)S(1)} %copy-done, ...), custom_call_target="tpu_custom_call" | custom-call | flops 75497472 | bytes 6291456 | tf_op jit(solution)/shard_map/targets/pallas_call | solution.py:922
  63.1 1.8 %collective-permute-done.23 = f32[3,1536]{1,0:T(4,128)S(1)} collective-permute-done((f32[3,1536]{1,0:T(4,128)S(1)}, f32[3,1536]{1,0:T(4,128)S(1)}, u32[]{:S(2)}, u32[]{:S(2)}) %collective-permute-start.23) | collective-permute-done | bytes 18464 | tf_op jit(solution)/shard_map/ppermute | solution.py:964
  64.9 0.6 add_multiply_fusion
  (52 shorter events, 3.7 us)
Async XLA Ops:
  4.4 7.5 %collective-permute-start.1 = (bf16[16,1536]{1,0:T(8,128)(2,1)}, bf16[16,1536]{1,0:T(8,128)(2,1)S(1)}, u32[]{:S(2)}, u32[]{:S(2)}) collective-permute-start(bf16[16,1536]{1,0:T(8,128)(2,1)} %get-tuple-element.38), channel_id=1, source_target_pairs={{0,30},{2,4},{4,2},{6,8},{8,6},{10,12},{12,10},{14,16},{16,14},{18... | collective-permute-start | bytes 147464 | tf_op jit(solution)/shard_map/ppermute | solution.py:950
  11.9 18.6 %collective-permute-start.4 = (bf16[2,128,1536]{2,1,0:T(8,128)(2,1)S(1)}, bf16[2,128,1536]{2,1,0:T(8,128)(2,1)S(1)}, u32[]{:S(2)}, u32[]{:S(2)}) collective-permute-start(bf16[2,128,1536]{2,1,0:T(8,128)(2,1)S(1)} %copy-done.1), channel_id=1, source_target_pairs={{0,2},{2,4},{4,6},{6,8},{8,10},{10,12},{12,14},{14,16},{16,18},{18... | collective-permute-start | bytes 2359304 | tf_op jit(solution)/shard_map/ppermute | solution.py:204
  13.3 10.1 %collective-permute-start.7 = (bf16[384,384]{1,0:T(8,128)(2,1)}, bf16[384,384]{1,0:T(8,128)(2,1)S(1)}, u32[]{:S(2)}, u32[]{:S(2)}) collective-permute-start(bf16[384,384]{1,0:T(8,128)(2,1)} %get-tuple-element.51), channel_id=1, source_target_pairs={{0,1},{1,0},{2,3},{3,2},{4,5},{5,4},{6,7},{7,6},{8,9},{9,8},{10,11... | collective-permute-start | bytes 884744 | tf_op jit(solution)/shard_map/ppermute | solution.py:941
  15.2 4.9 %collective-permute-start.2 = (bf16[16,1536]{1,0:T(8,128)(2,1)}, bf16[16,1536]{1,0:T(8,128)(2,1)S(1)}, u32[]{:S(2)}, u32[]{:S(2)}) collective-permute-start(bf16[16,1536]{1,0:T(8,128)(2,1)} %get-tuple-element.39), channel_id=1, source_target_pairs={{0,4},{2,6},{4,0},{6,2},{8,12},{10,14},{12,8},{14,10},{16,20},{18,... | collective-permute-start | bytes 147464 | tf_op jit(solution)/shard_map/ppermute | solution.py:941
  15.3 7.5 %collective-permute-start.3 = (bf16[16,1536]{1,0:T(8,128)(2,1)}, bf16[16,1536]{1,0:T(8,128)(2,1)S(1)}, u32[]{:S(2)}, u32[]{:S(2)}) collective-permute-start(bf16[16,1536]{1,0:T(8,128)(2,1)} %get-tuple-element.39), channel_id=1, source_target_pairs={{0,28},{2,30},{4,8},{6,10},{8,4},{10,6},{12,16},{14,18},{16,12},{1... | collective-permute-start | bytes 147464 | tf_op jit(solution)/shard_map/ppermute | solution.py:950
  20.2 3.2 %collective-permute-start = (bf16[16,1536]{1,0:T(8,128)(2,1)}, bf16[16,1536]{1,0:T(8,128)(2,1)S(1)}, u32[]{:S(2)}, u32[]{:S(2)}) collective-permute-start(bf16[16,1536]{1,0:T(8,128)(2,1)} %get-tuple-element.37), channel_id=1, source_target_pairs={{0,2},{2,0},{4,6},{6,4},{8,10},{10,8},{12,14},{14,12},{16,18},{18,... | collective-permute-start | bytes 147464 | tf_op jit(solution)/shard_map/ppermute | solution.py:941
  20.2 19.7 %collective-permute-start.5 = (bf16[2,64,768]{2,1,0:T(8,128)(2,1)}, bf16[2,64,768]{2,1,0:T(8,128)(2,1)S(1)}, u32[]{:S(2)}, u32[]{:S(2)}) collective-permute-start(bf16[2,64,768]{2,1,0:T(8,128)(2,1)} %get-tuple-element.45), channel_id=1, source_target_pairs={{0,1},{1,0},{2,3},{3,2},{4,5},{5,4},{6,7},{7,6},{8,9},{9,8},{10,11... | collective-permute-start | bytes 589832 | tf_op jit(solution)/shard_map/ppermute | solution.py:941
  22.9 19.7 %collective-permute-start.10 = (bf16[384,384]{1,0:T(8,128)(2,1)}, bf16[384,384]{1,0:T(8,128)(2,1)S(1)}, u32[]{:S(2)}, u32[]{:S(2)}) collective-permute-start(bf16[384,384]{1,0:T(8,128)(2,1)} %get-tuple-element.52), channel_id=1, source_target_pairs={{0,1},{1,0},{2,3},{3,2},{4,5},{5,4},{6,7},{7,6},{8,9},{9,8},{10,11... | collective-permute-start | bytes 884744 | tf_op jit(solution)/shard_map/ppermute | solution.py:941
  23.4 15.9 %collective-permute-start.8 = (bf16[384,384]{1,0:T(8,128)(2,1)S(1)}, bf16[384,384]{1,0:T(8,128)(2,1)S(1)}, u32[]{:S(2)}, u32[]{:S(2)}) collective-permute-start(bf16[384,384]{1,0:T(8,128)(2,1)S(1)} %collective-permute-done.7.refs_0_), channel_id=1, source_target_pairs={{0,4},{2,6},{4,0},{6,2},{8,12},{10,14},{12,8},{14,10},{16,20},{18,... | collective-permute-start | bytes 884744 | tf_op jit(solution)/shard_map/ppermute | solution.py:941
  23.4 16.0 %collective-permute-start.9 = (bf16[384,384]{1,0:T(8,128)(2,1)S(1)}, bf16[384,384]{1,0:T(8,128)(2,1)S(1)}, u32[]{:S(2)}, u32[]{:S(2)}) collective-permute-start(bf16[384,384]{1,0:T(8,128)(2,1)S(1)} %collective-permute-done.7.refs_0_), channel_id=1, source_target_pairs={{0,8},{2,10},{4,12},{6,14},{8,0},{10,2},{12,4},{14,6},{16,24},{18,... | collective-permute-start | bytes 884744 | tf_op jit(solution)/shard_map/ppermute | solution.py:941
  30.5 9.3 %collective-permute-start.6 = (bf16[16,1536]{1,0:T(8,128)(2,1)S(1)}, bf16[16,1536]{1,0:T(8,128)(2,1)S(1)}, u32[]{:S(2)}, u32[]{:S(2)}) collective-permute-start(bf16[16,1536]{1,0:T(8,128)(2,1)S(1)} %get-tuple-element.71), channel_id=1, source_target_pairs={{0,1},{1,0},{2,3},{3,2},{4,5},{5,4},{6,7},{7,6},{8,9},{9,8},{10,11... | collective-permute-start | bytes 147464 | tf_op jit(solution)/shard_map/ppermute | solution.py:941
  39.3 3.8 %collective-permute-start.11 = (bf16[384,384]{1,0:T(8,128)(2,1)S(1)}, bf16[384,384]{1,0:T(8,128)(2,1)S(1)}, u32[]{:S(2)}, u32[]{:S(2)}) collective-permute-start(bf16[384,384]{1,0:T(8,128)(2,1)S(1)} %collective-permute-done.7.refs_0_), channel_id=1, source_target_pairs={{0,2},{2,0},{4,6},{6,4},{8,10},{10,8},{12,14},{14,12},{16,18},{18,... | collective-permute-start | bytes 884744 | tf_op jit(solution)/shard_map/ppermute | solution.py:941
  39.3 7.8 %collective-permute-start.12 = (bf16[384,384]{1,0:T(8,128)(2,1)S(1)}, bf16[384,384]{1,0:T(8,128)(2,1)S(1)}, u32[]{:S(2)}, u32[]{:S(2)}) collective-permute-start(bf16[384,384]{1,0:T(8,128)(2,1)S(1)} %collective-permute-done.8.refs_1_), channel_id=1, source_target_pairs={{0,2},{2,0},{4,6},{6,4},{8,10},{10,8},{12,14},{14,12},{16,18},{18,... | collective-permute-start | bytes 884744 | tf_op jit(solution)/shard_map/ppermute | solution.py:941
  39.8 7.3 %collective-permute-start.13 = (bf16[384,384]{1,0:T(8,128)(2,1)S(1)}, bf16[384,384]{1,0:T(8,128)(2,1)S(1)}, u32[]{:S(2)}, u32[]{:S(2)}) collective-permute-start(bf16[384,384]{1,0:T(8,128)(2,1)S(1)} %collective-permute-done.9.refs_2_), channel_id=1, source_target_pairs={{0,2},{2,0},{4,6},{6,4},{8,10},{10,8},{12,14},{14,12},{16,18},{18,... | collective-permute-start | bytes 884744 | tf_op jit(solution)/shard_map/ppermute | solution.py:941
  42.5 4.6 %collective-permute-start.14 = (bf16[384,384]{1,0:T(8,128)(2,1)S(1)}, bf16[384,384]{1,0:T(8,128)(2,1)S(1)}, u32[]{:S(2)}, u32[]{:S(2)}) collective-permute-start(bf16[384,384]{1,0:T(8,128)(2,1)S(1)} %collective-permute-done.10.refs_3_), channel_id=1, source_target_pairs={{0,2},{2,0},{4,6},{6,4},{8,10},{10,8},{12,14},{14,12},{16,18},{18,... | collective-permute-start | bytes 884744 | tf_op jit(solution)/shard_map/ppermute | solution.py:941
  43.0 6.9 %collective-permute-start.15 = (bf16[16,1536]{1,0:T(8,128)(2,1)S(1)}, bf16[16,1536]{1,0:T(8,128)(2,1)S(1)}, u32[]{:S(2)}, u32[]{:S(2)}) collective-permute-start(bf16[16,1536]{1,0:T(8,128)(2,1)S(1)} %get-tuple-element.56), channel_id=1, source_target_pairs={{0,2},{2,0},{4,6},{6,4},{8,10},{10,8},{12,14},{14,12},{16,18},{18,... | collective-permute-start | bytes 147464 | tf_op jit(solution)/shard_map/ppermute | solution.py:941
  43.1 6.8 %collective-permute-start.16 = (bf16[16,1536]{1,0:T(8,128)(2,1)S(1)}, bf16[16,1536]{1,0:T(8,128)(2,1)S(1)}, u32[]{:S(2)}, u32[]{:S(2)}) collective-permute-start(bf16[16,1536]{1,0:T(8,128)(2,1)S(1)} %get-tuple-element.56), channel_id=1, source_target_pairs={{0,30},{2,4},{4,2},{6,8},{8,6},{10,12},{12,10},{14,16},{16,14},{18... | collective-permute-start | bytes 147464 | tf_op jit(solution)/shard_map/ppermute | solution.py:950
  49.9 1.3 %collective-permute-start.17 = (f32[3,1536]{1,0:T(4,128)S(1)}, f32[3,1536]{1,0:T(4,128)S(1)}, u32[]{:S(2)}, u32[]{:S(2)}) collective-permute-start(f32[3,1536]{1,0:T(4,128)S(1)} %get-tuple-element.61), channel_id=1, source_target_pairs={{0,2},{1,3},{2,0},{3,1},{4,6},{5,7},{6,4},{7,5},{8,10},{9,11},{10,... | collective-permute-start | bytes 55304 | tf_op jit(solution)/shard_map/ppermute | solution.py:964
  51.2 5.4 %collective-permute-start.19 = (f32[3,1536]{1,0:T(4,128)S(1)}, f32[3,1536]{1,0:T(4,128)S(1)}, u32[]{:S(2)}, u32[]{:S(2)}) collective-permute-start(f32[3,1536]{1,0:T(4,128)S(1)} %add.34), channel_id=1, source_target_pairs={{0,1},{1,0},{2,3},{3,2},{4,5},{5,4},{6,7},{7,6},{8,9},{9,8},{10,11... | collective-permute-start | bytes 55304 | tf_op jit(solution)/shard_map/ppermute | solution.py:964
  52.7 4.7 %collective-permute-start.20 = (f32[3,1536]{1,0:T(4,128)S(1)}, f32[3,1536]{1,0:T(4,128)S(1)}, u32[]{:S(2)}, u32[]{:S(2)}) collective-permute-start(f32[3,1536]{1,0:T(4,128)S(1)} %add.34), channel_id=1, source_target_pairs={{0,5},{1,4},{2,7},{3,6},{4,1},{5,0},{6,3},{7,2},{8,13},{9,12},{10,... | collective-permute-start | bytes 55304 | tf_op jit(solution)/shard_map/ppermute | solution.py:964
  52.8 4.6 %collective-permute-start.18 = (f32[3,1536]{1,0:T(4,128)S(1)}, f32[3,1536]{1,0:T(4,128)S(1)}, u32[]{:S(2)}, u32[]{:S(2)}) collective-permute-start(f32[3,1536]{1,0:T(4,128)S(1)} %add.34), channel_id=1, source_target_pairs={{0,4},{1,5},{2,6},{3,7},{4,0},{5,1},{6,2},{7,3},{8,12},{9,13},{10,... | collective-permute-start | bytes 55304 | tf_op jit(solution)/shard_map/ppermute | solution.py:964
  57.5 5.6 %collective-permute-start.22 = (f32[3,1536]{1,0:T(4,128)S(1)}, f32[3,1536]{1,0:T(4,128)S(1)}, u32[]{:S(2)}, u32[]{:S(2)}) collective-permute-start(f32[3,1536]{1,0:T(4,128)S(1)} %add_add_fusion), channel_id=1, source_target_pairs={{0,16},{1,17},{2,18},{3,19},{4,20},{5,21},{6,22},{7,23},{8,24},{9,... | collective-permute-start | bytes 55304 | tf_op jit(solution)/shard_map/ppermute | solution.py:964
  59.3 5.6 %collective-permute-start.23 = (f32[3,1536]{1,0:T(4,128)S(1)}, f32[3,1536]{1,0:T(4,128)S(1)}, u32[]{:S(2)}, u32[]{:S(2)}) collective-permute-start(f32[3,1536]{1,0:T(4,128)S(1)} %add_add_fusion), channel_id=1, source_target_pairs={{0,24},{1,25},{2,26},{3,27},{4,28},{5,29},{6,30},{7,31},{8,16},{9,... | collective-permute-start | bytes 55304 | tf_op jit(solution)/shard_map/ppermute | solution.py:964
  60.7 4.2 %collective-permute-start.21 = (f32[3,1536]{1,0:T(4,128)S(1)}, f32[3,1536]{1,0:T(4,128)S(1)}, u32[]{:S(2)}, u32[]{:S(2)}) collective-permute-start(f32[3,1536]{1,0:T(4,128)S(1)} %add_add_fusion), channel_id=1, source_target_pairs={{0,8},{1,9},{2,10},{3,11},{4,12},{5,13},{6,14},{7,15},{8,0},{9,1},... | collective-permute-start | bytes 55304 | tf_op jit(solution)/shard_map/ppermute | solution.py:964
  (8 other events, 198.0 us)

commit v10 on v8

--- a/solution.py
+++ b/solution.py
@@ -380,15 +380,38 @@
 
 
 def pack_kernel(
-    meta, skip_lo, skip_hi, att_lo, att_hi, cot_lo, cot_hi, near, distant, att,
-    edge_a, edge_b, far, tile_a, tile_b, att_out,
+    skip, attention, cotangent, weight, edge_a, edge_b, far, tile_a, tile_b, att_out,
+    skip_lo, skip_hi, att_lo, att_hi, cot_lo, cot_hi, sems,
 ):
-    att_out[...] = att[...]
-    tile_a[...] = near[...]
-    tile_b[...] = distant[...]
+    head, slab = lax.axis_index("head"), lax.axis_index("seq")
+    tile = tile_a.shape[0]
+    core, block = slab & 1, (slab >> 1) & 3
+    down = pl.ds(pl.multiple_of(core * tile, tile), tile)
+
+    def piece(which):
+        return weight.at[down, pl.ds(pl.multiple_of(which * tile, tile), tile)]
+
+    edges = []
+    for source, lo, hi in (
+        (skip, skip_lo, skip_hi), (attention, att_lo, att_hi), (cotangent, cot_lo, cot_hi)
+    ):
+        rows = source.shape[1]
+        for part, begin in ((lo, 0), (hi, rows - 16)):
+            edges.append(
+                pltpu.make_async_copy(source.at[:, pl.ds(begin, 16)], part, sems.at[len(edges)])
+            )
+    whole = [
+        pltpu.make_async_copy(piece(block), tile_a, sems.at[6]),
+        pltpu.make_async_copy(piece(3 - block), tile_b, sems.at[7]),
+        pltpu.make_async_copy(attention.at[pl.ds(2 - 2 * head, 2)], att_out, sems.at[8]),
+    ]
+    for copy in edges + whole:
+        copy.start()
+    for copy in edges:
+        copy.wait()
     wide = cot_lo.shape[2]
     at = lax.broadcasted_iota(jnp.int32, (8, wide), 0)
-    even = (meta[1] & 1) == 0
+    even = core == 0
     ups, downs, ends = [], [], []
     for s in range(2):
         feats = [jnp.concatenate([part[s], part[2 + s]], axis=1) for part in (att_hi, att_lo)]
@@ -404,45 +427,33 @@
     edge_a[...] = jnp.where(even, up, down).astype(BF)
     edge_b[...] = jnp.where(even, down, up).astype(BF)
     far[...] = jnp.concatenate(ends).astype(BF)
-
-
-def packed(meta, encoder_skip, attention, cotangent, weight, tile):
+    for copy in whole:
+        copy.wait()
+
+
+def packed(encoder_skip, attention, cotangent, weight, tile):
     seqs, rows, wide = encoder_skip.shape
-    half = attention.shape[2]
-    short = attention.shape[1]
-
-    def block(count, width, place):
-        return pl.BlockSpec((count, 16, width), lambda i, m: (0, place, 0))
-
+    count, short, half = attention.shape
     out = jax.ShapeDtypeStruct((16, wide), BF)
     square = jax.ShapeDtypeStruct((tile, tile), BF)
+    anywhere = pl.BlockSpec(memory_space=pl.ANY)
     return pl.pallas_call(
         pack_kernel,
-        grid_spec=pltpu.PrefetchScalarGridSpec(
-            num_scalar_prefetch=1,
-            grid=(1,),
-            in_specs=[
-                block(seqs, wide, 0),
-                block(seqs, wide, rows // 16 - 1),
-                block(2 * seqs, half, 0),
-                block(2 * seqs, half, short // 16 - 1),
-                block(seqs, wide, 0),
-                block(seqs, wide, rows // 16 - 1),
-                pl.BlockSpec((tile, tile), lambda i, m: (m[1] & 1, (m[1] >> 1) & 3)),
-                pl.BlockSpec((tile, tile), lambda i, m: (m[1] & 1, 3 - ((m[1] >> 1) & 3))),
-                pl.BlockSpec((2, short, half), lambda i, m: (1 - m[0], 0, 0)),
-            ],
-            out_specs=[pl.BlockSpec((16, wide), lambda i, m: (0, 0))] * 3
-            + [pl.BlockSpec((tile, tile), lambda i, m: (0, 0))] * 2
-            + [pl.BlockSpec((2, short, half), lambda i, m: (0, 0, 0))],
-        ),
+        in_specs=[anywhere] * 4,
+        out_specs=[pl.BlockSpec(memory_space=pltpu.VMEM)] * 3 + [anywhere] * 3,
         out_shape=[out, out, out, square, square, jax.ShapeDtypeStruct((2, short, half), BF)],
+        scratch_shapes=[
+            pltpu.VMEM((seqs, 16, wide), BF),
+            pltpu.VMEM((seqs, 16, wide), BF),
+            pltpu.VMEM((count, 16, half), BF),
+            pltpu.VMEM((count, 16, half), BF),
+            pltpu.VMEM((seqs, 16, wide), BF),
+            pltpu.VMEM((seqs, 16, wide), BF),
+            pltpu.SemaphoreType.DMA((9,)),
+        ],
         compiler_params=params(60),
         name="pack_edges",
-    )(
-        meta, encoder_skip, encoder_skip, attention, attention, cotangent, cotangent, weight,
-        weight, attention,
-    )
+    )(encoder_skip, attention, cotangent, weight)
 
 
 def slab_sums(att, skip, edge, twin, ext, cols):
@@ -980,10 +991,9 @@
     tile = 3 * LANES
 
     edge_a, edge_b, far, first, last_tile, att_out = packed(
-        meta, encoder_skip, attention, cotangent, point_weight, tile
+        encoder_skip, attention, cotangent, point_weight, tile
     )
     first = paired(first, "head", 1)
-    shipped = paired(att_out, "head", 1)
     edge_a = paired(edge_a, "seq", 1)
     edge_b = staggered(edge_b, 1)
     far_a = paired(far, "seq", 2)
@@ -993,13 +1003,15 @@
     nothing = jnp.zeros_like(edge_b)
     edge = edge_a + jnp.where(outer, nothing, edge_b)
     twin = paired(edge, "head", 1)
+    shipped = paired(after(att_out, edge), "head", 1)
     edge = edge + jnp.where(slab % 4 >= 2, far_a, jnp.where(slab < 2, nothing, far_b))
-    second = paired(first, "seq", 2)
-    third = paired(first, "seq", 4)
-    fourth = paired(last_tile, "head", 1)
     asked, own_sums, own_slope = own_slopes(
         meta, crop_offset, target_bins, attention, encoder_skip, edge, depth_filter
     )
+    ready = after(first, asked)
+    second = paired(ready, "seq", 2)
+    third = paired(ready, "seq", 4)
+    fourth = paired(last_tile, "head", 1)
     sums, slopes, mine, shown = other_slopes(
         meta, crop_offset, target_bins, shipped, encoder_skip, edge, twin, depth_filter, asked
     )

time: 57.1 us -> 79.8 us (1.40)
  Pallas kernels: 19.3 us -> 41.8 us
    pallas_call x1, Pallas kernels: 3.15 us -> 25.7 us  [packed(): pl.pallas_call(pack_kernel, in_specs=[anywhere] * 4, out_specs=[pl.BlockS...]
    ppermute x13, starting transfers between devices: 7.84 us -> 9.74 us  [paired(): return lax.ppermute(part, axis, [(i, i ^ bit) for i in range(count)])]
    ppermute x3, starting transfers between devices: 9.63 us -> 8.22 us  [staggered(): return lax.ppermute(part, 'seq', pairs)]
    ppermute x13, waiting for transfers between devices: 3.82 us -> 2.45 us  [paired(): return lax.ppermute(part, axis, [(i, i ^ bit) for i in range(count)])]
    ppermute x3, waiting for transfers between devices: 2.58 us -> 3.69 us  [staggered(): return lax.ppermute(part, 'seq', pairs)]
    ppermute x7, starting transfers between devices: 7.1 us -> 7.92 us  [crossed(): return lax.ppermute(part, ('seq', 'head'), pairs)]
  transfers between devices with their start and end apart: 24 -> 24, of which waited for: 10 -> 9; matrix products, arithmetic and copies ran while one was open for 0% -> 0% of each run, Pallas kernels for 28% -> 20%
where the time goes in v10:
time: 79.8 us; the launch traced here: 79.6 us
  Pallas kernels  41.8 us (52%)
  starting transfers between devices  27.2 us (34%)
  waiting for transfers between devices  8.96 us (11%)
  between operations  0.84 us (1%)
    pallas_call x1, Pallas kernels, packed(): pl.pallas_call(pack_kernel, in_specs=[anywhere] * 4, out_specs=[pl.BlockS...  25.7 us
    ppermute x13, starting transfers between devices, paired(): return lax.ppermute(part, axis, [(i, i ^ bit) for i in range(count)])  9.74 us
    ppermute x3, starting transfers between devices, staggered(): return lax.ppermute(part, 'seq', pairs)  8.22 us
    ppermute x7, starting transfers between devices, crossed(): return lax.ppermute(part, ('seq', 'head'), pairs)  7.92 us
    pallas_call x1, Pallas kernels, own_half(): pl.pallas_call(functools.partial(own_kernel, slabs), grid_spec=pltpu.Pref...  4.94 us
    ppermute x3, waiting for transfers between devices, staggered(): return lax.ppermute(part, 'seq', pairs)  3.69 us
    ppermute x7, waiting for transfers between devices, crossed(): return lax.ppermute(part, ('seq', 'head'), pairs)  2.82 us
    pallas_call x1, Pallas kernels, other_terms(): pl.pallas_call(terms_kernel, grid_spec=pltpu.PrefetchScalarGridSpec(num_s...  2.67 us
  transfers between devices with their start and end apart: 24, of which 9 were waited for; matrix products, arithmetic and copies ran while one was open for 0% of the time, Pallas kernels for 20%

profile of v10, /device:TPU:0, one launch (start us, length us, event | category | flops | bytes accessed | tf_op | source)
XLA Modules:
  0.0 79.6 jit_solution(10766088327747151701)
XLA Ops:
  0.7 25.7 %pack_edges.1 = (bf16[16,1536]{1,0:T(8,128)(2,1)}, bf16[16,1536]{1,0:T(8,128)(2,1)}, bf16[16,1536]{1,0:T(8,128)(2,1)}, bf16[384,384]{1,0:T(8,128)(2,1)}, bf16[38...) custom-call(bf16[2,128,1536]{2,1,0:T(8,128)(2,1)} %skip.5, bf16[4,64,768]{2,1,0:T(8,128)(2,1)} %att.1, ...), custom_call_target="tpu_custom_call" | custom-call | tf_op jit(solution)/shard_map/pack_edges/pallas_call | solution.py:440
  26.4 3.0 %collective-permute-start.3 = (bf16[16,1536]{1,0:T(8,128)(2,1)}, bf16[16,1536]{1,0:T(8,128)(2,1)S(1)}, u32[]{:S(2)}, u32[]{:S(2)}) collective-permute-start(bf16[16,1536]{1,0:T(8,128)(2,1)} %get-tuple-element.43), channel_id=1, source_target_pairs={{0,4},{2,6},{4,0},{6,2},{8,12},{10,14},{12,8},{14,10},{16,20},{18,... | collective-permute-start | bytes 147464 | tf_op jit(solution)/shard_map/ppermute | solution.py:952
  29.4 3.6 %collective-permute-start.4 = (bf16[16,1536]{1,0:T(8,128)(2,1)}, bf16[16,1536]{1,0:T(8,128)(2,1)S(1)}, u32[]{:S(2)}, u32[]{:S(2)}) collective-permute-start(bf16[16,1536]{1,0:T(8,128)(2,1)} %get-tuple-element.43), channel_id=1, source_target_pairs={{0,28},{2,30},{4,8},{6,10},{8,4},{10,6},{12,16},{14,18},{16,12},{1... | collective-permute-start | bytes 147464 | tf_op jit(solution)/shard_map/ppermute | solution.py:961
  33.0 1.3 %collective-permute-start.1 = (bf16[16,1536]{1,0:T(8,128)(2,1)}, bf16[16,1536]{1,0:T(8,128)(2,1)S(1)}, u32[]{:S(2)}, u32[]{:S(2)}) collective-permute-start(bf16[16,1536]{1,0:T(8,128)(2,1)} %get-tuple-element.41), channel_id=1, source_target_pairs={{0,30},{2,4},{4,2},{6,8},{8,6},{10,12},{12,10},{14,16},{16,14},{18... | collective-permute-start | bytes 147464 | tf_op jit(solution)/shard_map/ppermute | solution.py:961
  34.2 1.5 %collective-permute-start.7 = (bf16[384,384]{1,0:T(8,128)(2,1)}, bf16[384,384]{1,0:T(8,128)(2,1)S(1)}, u32[]{:S(2)}, u32[]{:S(2)}) collective-permute-start(bf16[384,384]{1,0:T(8,128)(2,1)} %get-tuple-element.55), channel_id=1, source_target_pairs={{0,1},{1,0},{2,3},{3,2},{4,5},{5,4},{6,7},{7,6},{8,9},{9,8},{10,11... | collective-permute-start | bytes 884744 | tf_op jit(solution)/shard_map/ppermute | solution.py:952
  35.8 3.6 %collective-permute-done.1 = bf16[16,1536]{1,0:T(8,128)(2,1)S(1)} collective-permute-done((bf16[16,1536]{1,0:T(8,128)(2,1)}, bf16[16,1536]{1,0:T(8,128)(2,1)S(1)}, u32[]{:S(2)}, u32[]{:S(2)}) %collective-permute-start.1) | collective-permute-done | bytes 49184 | tf_op jit(solution)/shard_map/ppermute | solution.py:961
  39.4 1.3 %collective-permute-start.6 = (bf16[2,128,1536]{2,1,0:T(8,128)(2,1)S(1)}, bf16[2,128,1536]{2,1,0:T(8,128)(2,1)S(1)}, u32[]{:S(2)}, u32[]{:S(2)}) collective-permute-start(bf16[2,128,1536]{2,1,0:T(8,128)(2,1)S(1)} %copy-done.1), channel_id=1, source_target_pairs={{0,2},{2,4},{4,6},{6,8},{8,10},{10,12},{12,14},{14,16},{16,18},{18... | collective-permute-start | bytes 2359304 | tf_op jit(solution)/shard_map/ppermute | solution.py:204
  40.8 1.6 %collective-permute-start.5 = (bf16[16,1536]{1,0:T(8,128)(2,1)S(1)}, bf16[16,1536]{1,0:T(8,128)(2,1)S(1)}, u32[]{:S(2)}, u32[]{:S(2)}) collective-permute-start(bf16[16,1536]{1,0:T(8,128)(2,1)S(1)} %get-tuple-element.75), channel_id=1, source_target_pairs={{0,1},{1,0},{2,3},{3,2},{4,5},{5,4},{6,7},{7,6},{8,9},{9,8},{10,11... | collective-permute-start | bytes 147464 | tf_op jit(solution)/shard_map/ppermute | solution.py:952
  42.9 2.1 %own_slopes.1 = (bf16[32,768]{1,0:T(8,128)(2,1)S(1)}, bf16[2,144,768]{2,1,0:T(8,128)(2,1)S(1)}, f32[2,144,768]{2,1,0:T(8,128)S(1)}) custom-call(s32[2]{0:T(128)S(1)} %pad_add_fusion.meta, s32[2]{0:T(128)S(1)} %copy-done.5, s32[2,32]{1,0:T(2,128)S(1)} %copy-done.6, bf16[4,64,768]{2,1,0:T(8,128)(2,1)S(1)} %copy-done.3, bf16[2,128,1536]{2,1,0:T(8,128)(2,1)S(1)} %copy-done.2, ...), custom_call_target="tpu_custom_call" | custom-call | flops 3000000000 | bytes 1000000 | tf_op jit(solution)/shard_map/own_slopes/pallas_call | solution.py:569
  45.5 1.6 %collective-permute-start.10 = (bf16[384,384]{1,0:T(8,128)(2,1)S(1)}, bf16[384,384]{1,0:T(8,128)(2,1)S(1)}, u32[]{:S(2)}, u32[]{:S(2)}) collective-permute-start(bf16[384,384]{1,0:T(8,128)(2,1)S(1)} %copy-done.7), channel_id=1, source_target_pairs={{0,1},{1,0},{2,3},{3,2},{4,5},{5,4},{6,7},{7,6},{8,9},{9,8},{10,11... | collective-permute-start | bytes 884744 | tf_op jit(solution)/shard_map/ppermute | solution.py:952
  47.1 1.9 %collective-permute-done.2.att = bf16[2,64,768]{2,1,0:T(8,128)(2,1)S(1)} collective-permute-done((bf16[2,64,768]{2,1,0:T(8,128)(2,1)}, bf16[2,64,768]{2,1,0:T(8,128)(2,1)S(1)}, u32[]{:S(2)}, u32[]{:S(2)}) %collective-permute-start.2) | collective-permute-done | bytes 196640 | tf_op jit(solution)/shard_map/ppermute | solution.py:952
  49.0 2.6 %other_slopes.1 = (bf16[2,144,768]{2,1,0:T(8,128)(2,1)S(1)}, f32[2,144,768]{2,1,0:T(8,128)S(1)}, bf16[16,1536]{1,0:T(8,128)(2,1)S(1)}, bf16[16,1536]{1,0:T(8,128)(2,1)S(1)}) custom-call(s32[2]{0:T(128)S(1)} %pad_add_fusion.meta, s32[2]{0:T(128)S(1)} %copy-done.5, s32[2,32]{1,0:T(2,128)S(1)} %copy-done.6, bf16[2,64,768]{2,1,0:T(8,128)(2,1)S(1)} %collective-permute-done.2.att, ...), custom_call_target="tpu_custom_call" | custom-call | flops 3000000000 | bytes 1000000 | tf_op jit(solution)/shard_map/other_slopes/pallas_call | solution.py:758
  51.6 4.9 %own_half.1 = (bf16[2,144,1536]{2,1,0:T(8,128)(2,1)S(1)}, f32[3,768]{1,0:T(4,128)S(1)}, bf16[2,128,1536]{2,1,0:T(8,128)(2,1)}, bf16[2,64,1536]{2,1,0:T(8,128)(2,1)}) custom-call(s32[2]{0:T(128)S(1)} %pad_add_fusion.meta, s32[2]{0:T(128)S(1)} %copy-done.5, bf16[2,144,768]{2,1,0:T(8,128)(2,1)S(1)} %get-tuple-element.48.sums, ...), custom_call_target="tpu_custom_call" | custom-call | flops 1 | bytes 1 | tf_op jit(solution)/shard_map/own_half/pallas_call | solution.py:672
  58.2 3.4 %collective-permute-start.16 = (bf16[16,1536]{1,0:T(8,128)(2,1)S(1)}, bf16[16,1536]{1,0:T(8,128)(2,1)S(1)}, u32[]{:S(2)}, u32[]{:S(2)}) collective-permute-start(bf16[16,1536]{1,0:T(8,128)(2,1)S(1)} %get-tuple-element.46), channel_id=1, source_target_pairs={{0,30},{2,4},{4,2},{6,8},{8,6},{10,12},{12,10},{14,16},{16,14},{18... | collective-permute-start | bytes 147464 | tf_op jit(solution)/shard_map/ppermute | solution.py:961
  61.6 2.7 %other_terms.1 = (bf16[2,144,768]{2,1,0:T(8,128)(2,1)S(1)}, f32[3,1536]{1,0:T(4,128)S(1)}) custom-call(s32[2]{0:T(128)S(1)} %pad_add_fusion.meta, bf16[2,144,1536]{2,1,0:T(8,128)(2,1)S(1)} %get-tuple-element.51.moved, bf16[2,144,768]{2,1,0:T(8,128)(2,1)S(1)} %get-tuple-element.52.sums, f32[2,144,768]{2,1,0:T(8,128)S(1)} %get-tuple-element.53.slopes, ...), custom_call_target="tpu_custom_call" | custom-call | flops 679477248 | bytes 6291456 | tf_op jit(solution)/shard_map/other_terms/pallas_call | solution.py:835
  64.4 1.2 %collective-permute-done.17 = f32[3,1536]{1,0:T(4,128)S(1)} collective-permute-done((f32[3,1536]{1,0:T(4,128)S(1)}, f32[3,1536]{1,0:T(4,128)S(1)}, u32[]{:S(2)}, u32[]{:S(2)}) %collective-permute-start.17) | collective-permute-done | bytes 18464 | tf_op jit(solution)/shard_map/ppermute | solution.py:975
  65.6 0.8 collective-permute-start.19
  66.4 2.8 %collective-permute-start.18 = (f32[3,1536]{1,0:T(4,128)S(1)}, f32[3,1536]{1,0:T(4,128)S(1)}, u32[]{:S(2)}, u32[]{:S(2)}) collective-permute-start(f32[3,1536]{1,0:T(4,128)S(1)} %add.34), channel_id=1, source_target_pairs={{0,4},{1,5},{2,6},{3,7},{4,0},{5,1},{6,2},{7,3},{8,12},{9,13},{10,... | collective-permute-start | bytes 55304 | tf_op jit(solution)/shard_map/ppermute | solution.py:975
  69.2 1.8 %other_grads.1 = (bf16[2,128,1536]{2,1,0:T(8,128)(2,1)}, bf16[2,64,1536]{2,1,0:T(8,128)(2,1)}) custom-call(s32[2]{0:T(128)S(1)} %pad_add_fusion.meta, bf16[2,144,1536]{2,1,0:T(8,128)(2,1)S(1)} %get-tuple-element.51.moved, bf16[2,144,768]{2,1,0:T(8,128)(2,1)S(1)} %get-tuple-element.66.convs, ...), custom_call_target="tpu_custom_call", output_to_operand_aliasing={{0}: (4, {}), {1}: (5, {})} | custom-call | flops 4423680 | bytes 4194304 | tf_op jit(solution)/shard_map/other_grads/pallas_call | solution.py:887
  71.3 1.0 %collective-permute-start.22 = (f32[3,1536]{1,0:T(4,128)S(1)}, f32[3,1536]{1,0:T(4,128)S(1)}, u32[]{:S(2)}, u32[]{:S(2)}) collective-permute-start(f32[3,1536]{1,0:T(4,128)S(1)} %add_add_fusion), channel_id=1, source_target_pairs={{0,16},{1,17},{2,18},{3,19},{4,20},{5,21},{6,22},{7,23},{8,24},{9,... | collective-permute-start | bytes 55304 | tf_op jit(solution)/shard_map/ppermute | solution.py:975
  72.3 2.9 %collective-permute-start.23 = (f32[3,1536]{1,0:T(4,128)S(1)}, f32[3,1536]{1,0:T(4,128)S(1)}, u32[]{:S(2)}, u32[]{:S(2)}) collective-permute-start(f32[3,1536]{1,0:T(4,128)S(1)} %add_add_fusion), channel_id=1, source_target_pairs={{0,24},{1,25},{2,26},{3,27},{4,28},{5,29},{6,30},{7,31},{8,16},{9,... | collective-permute-start | bytes 55304 | tf_op jit(solution)/shard_map/ppermute | solution.py:975
  75.6 1.9 %targets.1 = bf16[2,2,1536]{2,1,0:T(2,128)(2,1)} custom-call(s32[2]{0:T(128)S(1)} %pad_add_fusion.meta, bf16[16,1536]{1,0:T(8,128)(2,1)S(1)} %get-tuple-element.45.mine, bf16[16,1536]{1,0:T(8,128)(2,1)S(1)} %collective-permute-done.15.got_a, bf16[16,1536]{1,0:T(8,128)(2,1)S(1)} %collective-permute-done.16.got_b, bf16[768,1536]{1,0:T(8,128)(2,1)S(1)} %copy-done, ...), custom_call_target="tpu_custom_call" | custom-call | flops 75497472 | bytes 6291456 | tf_op jit(solution)/shard_map/targets/pallas_call | solution.py:933
  77.9 1.1 %collective-permute-done.21 = f32[3,1536]{1,0:T(4,128)S(1)} collective-permute-done((f32[3,1536]{1,0:T(4,128)S(1)}, f32[3,1536]{1,0:T(4,128)S(1)}, u32[]{:S(2)}, u32[]{:S(2)}) %collective-permute-start.21) | collective-permute-done | bytes 18464 | tf_op jit(solution)/shard_map/ppermute | solution.py:975
  79.0 0.6 add_multiply_fusion
  (52 shorter events, 3.9 us)
Async XLA Ops:
  26.4 14.3 %collective-permute-start.3 = (bf16[16,1536]{1,0:T(8,128)(2,1)}, bf16[16,1536]{1,0:T(8,128)(2,1)S(1)}, u32[]{:S(2)}, u32[]{:S(2)}) collective-permute-start(bf16[16,1536]{1,0:T(8,128)(2,1)} %get-tuple-element.43), channel_id=1, source_target_pairs={{0,4},{2,6},{4,0},{6,2},{8,12},{10,14},{12,8},{14,10},{16,20},{18,... | collective-permute-start | bytes 147464 | tf_op jit(solution)/shard_map/ppermute | solution.py:952
  29.4 11.4 %collective-permute-start.4 = (bf16[16,1536]{1,0:T(8,128)(2,1)}, bf16[16,1536]{1,0:T(8,128)(2,1)S(1)}, u32[]{:S(2)}, u32[]{:S(2)}) collective-permute-start(bf16[16,1536]{1,0:T(8,128)(2,1)} %get-tuple-element.43), channel_id=1, source_target_pairs={{0,28},{2,30},{4,8},{6,10},{8,4},{10,6},{12,16},{14,18},{16,12},{1... | collective-permute-start | bytes 147464 | tf_op jit(solution)/shard_map/ppermute | solution.py:961
  33.0 7.8 %collective-permute-start = (bf16[16,1536]{1,0:T(8,128)(2,1)}, bf16[16,1536]{1,0:T(8,128)(2,1)S(1)}, u32[]{:S(2)}, u32[]{:S(2)}) collective-permute-start(bf16[16,1536]{1,0:T(8,128)(2,1)} %get-tuple-element.40), channel_id=1, source_target_pairs={{0,2},{2,0},{4,6},{6,4},{8,10},{10,8},{12,14},{14,12},{16,18},{18,... | collective-permute-start | bytes 147464 | tf_op jit(solution)/shard_map/ppermute | solution.py:952
  33.0 6.4 %collective-permute-start.1 = (bf16[16,1536]{1,0:T(8,128)(2,1)}, bf16[16,1536]{1,0:T(8,128)(2,1)S(1)}, u32[]{:S(2)}, u32[]{:S(2)}) collective-permute-start(bf16[16,1536]{1,0:T(8,128)(2,1)} %get-tuple-element.41), channel_id=1, source_target_pairs={{0,30},{2,4},{4,2},{6,8},{8,6},{10,12},{12,10},{14,16},{16,14},{18... | collective-permute-start | bytes 147464 | tf_op jit(solution)/shard_map/ppermute | solution.py:961
  34.2 10.8 %collective-permute-start.7 = (bf16[384,384]{1,0:T(8,128)(2,1)}, bf16[384,384]{1,0:T(8,128)(2,1)S(1)}, u32[]{:S(2)}, u32[]{:S(2)}) collective-permute-start(bf16[384,384]{1,0:T(8,128)(2,1)} %get-tuple-element.55), channel_id=1, source_target_pairs={{0,1},{1,0},{2,3},{3,2},{4,5},{5,4},{6,7},{7,6},{8,9},{9,8},{10,11... | collective-permute-start | bytes 884744 | tf_op jit(solution)/shard_map/ppermute | solution.py:952
  39.4 12.2 %collective-permute-start.6 = (bf16[2,128,1536]{2,1,0:T(8,128)(2,1)S(1)}, bf16[2,128,1536]{2,1,0:T(8,128)(2,1)S(1)}, u32[]{:S(2)}, u32[]{:S(2)}) collective-permute-start(bf16[2,128,1536]{2,1,0:T(8,128)(2,1)S(1)} %copy-done.1), channel_id=1, source_target_pairs={{0,2},{2,4},{4,6},{6,8},{8,10},{10,12},{12,14},{14,16},{16,18},{18... | collective-permute-start | bytes 2359304 | tf_op jit(solution)/shard_map/ppermute | solution.py:204
  40.8 4.7 %collective-permute-start.5 = (bf16[16,1536]{1,0:T(8,128)(2,1)S(1)}, bf16[16,1536]{1,0:T(8,128)(2,1)S(1)}, u32[]{:S(2)}, u32[]{:S(2)}) collective-permute-start(bf16[16,1536]{1,0:T(8,128)(2,1)S(1)} %get-tuple-element.75), channel_id=1, source_target_pairs={{0,1},{1,0},{2,3},{3,2},{4,5},{5,4},{6,7},{7,6},{8,9},{9,8},{10,11... | collective-permute-start | bytes 147464 | tf_op jit(solution)/shard_map/ppermute | solution.py:952
  42.4 6.6 %collective-permute-start.2 = (bf16[2,64,768]{2,1,0:T(8,128)(2,1)}, bf16[2,64,768]{2,1,0:T(8,128)(2,1)S(1)}, u32[]{:S(2)}, u32[]{:S(2)}) collective-permute-start(bf16[2,64,768]{2,1,0:T(8,128)(2,1)} %get-tuple-element.42), channel_id=1, source_target_pairs={{0,1},{1,0},{2,3},{3,2},{4,5},{5,4},{6,7},{7,6},{8,9},{9,8},{10,11... | collective-permute-start | bytes 589832 | tf_op jit(solution)/shard_map/ppermute | solution.py:952
  45.1 11.6 %collective-permute-start.8 = (bf16[384,384]{1,0:T(8,128)(2,1)S(1)}, bf16[384,384]{1,0:T(8,128)(2,1)S(1)}, u32[]{:S(2)}, u32[]{:S(2)}) collective-permute-start(bf16[384,384]{1,0:T(8,128)(2,1)S(1)} %collective-permute-done.7.refs_0_), channel_id=1, source_target_pairs={{0,4},{2,6},{4,0},{6,2},{8,12},{10,14},{12,8},{14,10},{16,20},{18,... | collective-permute-start | bytes 884744 | tf_op jit(solution)/shard_map/ppermute | solution.py:952
  45.1 12.0 %collective-permute-start.9 = (bf16[384,384]{1,0:T(8,128)(2,1)S(1)}, bf16[384,384]{1,0:T(8,128)(2,1)S(1)}, u32[]{:S(2)}, u32[]{:S(2)}) collective-permute-start(bf16[384,384]{1,0:T(8,128)(2,1)S(1)} %collective-permute-done.7.refs_0_), channel_id=1, source_target_pairs={{0,8},{2,10},{4,12},{6,14},{8,0},{10,2},{12,4},{14,6},{16,24},{18,... | collective-permute-start | bytes 884744 | tf_op jit(solution)/shard_map/ppermute | solution.py:952
  45.5 11.8 %collective-permute-start.10 = (bf16[384,384]{1,0:T(8,128)(2,1)S(1)}, bf16[384,384]{1,0:T(8,128)(2,1)S(1)}, u32[]{:S(2)}, u32[]{:S(2)}) collective-permute-start(bf16[384,384]{1,0:T(8,128)(2,1)S(1)} %copy-done.7), channel_id=1, source_target_pairs={{0,1},{1,0},{2,3},{3,2},{4,5},{5,4},{6,7},{7,6},{8,9},{9,8},{10,11... | collective-permute-start | bytes 884744 | tf_op jit(solution)/shard_map/ppermute | solution.py:952
  56.6 1.6 %collective-permute-start.11 = (bf16[384,384]{1,0:T(8,128)(2,1)S(1)}, bf16[384,384]{1,0:T(8,128)(2,1)S(1)}, u32[]{:S(2)}, u32[]{:S(2)}) collective-permute-start(bf16[384,384]{1,0:T(8,128)(2,1)S(1)} %collective-permute-done.7.refs_0_), channel_id=1, source_target_pairs={{0,2},{2,0},{4,6},{6,4},{8,10},{10,8},{12,14},{14,12},{16,18},{18,... | collective-permute-start | bytes 884744 | tf_op jit(solution)/shard_map/ppermute | solution.py:952
  56.7 4.9 %collective-permute-start.12 = (bf16[384,384]{1,0:T(8,128)(2,1)S(1)}, bf16[384,384]{1,0:T(8,128)(2,1)S(1)}, u32[]{:S(2)}, u32[]{:S(2)}) collective-permute-start(bf16[384,384]{1,0:T(8,128)(2,1)S(1)} %collective-permute-done.8.refs_1_), channel_id=1, source_target_pairs={{0,2},{2,0},{4,6},{6,4},{8,10},{10,8},{12,14},{14,12},{16,18},{18,... | collective-permute-start | bytes 884744 | tf_op jit(solution)/shard_map/ppermute | solution.py:952
  57.2 4.5 %collective-permute-start.13 = (bf16[384,384]{1,0:T(8,128)(2,1)S(1)}, bf16[384,384]{1,0:T(8,128)(2,1)S(1)}, u32[]{:S(2)}, u32[]{:S(2)}) collective-permute-start(bf16[384,384]{1,0:T(8,128)(2,1)S(1)} %collective-permute-done.9.refs_2_), channel_id=1, source_target_pairs={{0,2},{2,0},{4,6},{6,4},{8,10},{10,8},{12,14},{14,12},{16,18},{18,... | collective-permute-start | bytes 884744 | tf_op jit(solution)/shard_map/ppermute | solution.py:952
  57.2 4.4 %collective-permute-start.14 = (bf16[384,384]{1,0:T(8,128)(2,1)S(1)}, bf16[384,384]{1,0:T(8,128)(2,1)S(1)}, u32[]{:S(2)}, u32[]{:S(2)}) collective-permute-start(bf16[384,384]{1,0:T(8,128)(2,1)S(1)} %collective-permute-done.10.refs_3_), channel_id=1, source_target_pairs={{0,2},{2,0},{4,6},{6,4},{8,10},{10,8},{12,14},{14,12},{16,18},{18,... | collective-permute-start | bytes 884744 | tf_op jit(solution)/shard_map/ppermute | solution.py:952
  57.7 6.6 %collective-permute-start.15 = (bf16[16,1536]{1,0:T(8,128)(2,1)S(1)}, bf16[16,1536]{1,0:T(8,128)(2,1)S(1)}, u32[]{:S(2)}, u32[]{:S(2)}) collective-permute-start(bf16[16,1536]{1,0:T(8,128)(2,1)S(1)} %get-tuple-element.46), channel_id=1, source_target_pairs={{0,2},{2,0},{4,6},{6,4},{8,10},{10,8},{12,14},{14,12},{16,18},{18,... | collective-permute-start | bytes 147464 | tf_op jit(solution)/shard_map/ppermute | solution.py:952
  58.2 6.2 %collective-permute-start.16 = (bf16[16,1536]{1,0:T(8,128)(2,1)S(1)}, bf16[16,1536]{1,0:T(8,128)(2,1)S(1)}, u32[]{:S(2)}, u32[]{:S(2)}) collective-permute-start(bf16[16,1536]{1,0:T(8,128)(2,1)S(1)} %get-tuple-element.46), channel_id=1, source_target_pairs={{0,30},{2,4},{4,2},{6,8},{8,6},{10,12},{12,10},{14,16},{16,14},{18... | collective-permute-start | bytes 147464 | tf_op jit(solution)/shard_map/ppermute | solution.py:961
  64.4 1.2 %collective-permute-start.17 = (f32[3,1536]{1,0:T(4,128)S(1)}, f32[3,1536]{1,0:T(4,128)S(1)}, u32[]{:S(2)}, u32[]{:S(2)}) collective-permute-start(f32[3,1536]{1,0:T(4,128)S(1)} %get-tuple-element.65), channel_id=1, source_target_pairs={{0,2},{1,3},{2,0},{3,1},{4,6},{5,7},{6,4},{7,5},{8,10},{9,11},{10,... | collective-permute-start | bytes 55304 | tf_op jit(solution)/shard_map/ppermute | solution.py:975
  65.6 5.4 %collective-permute-start.19 = (f32[3,1536]{1,0:T(4,128)S(1)}, f32[3,1536]{1,0:T(4,128)S(1)}, u32[]{:S(2)}, u32[]{:S(2)}) collective-permute-start(f32[3,1536]{1,0:T(4,128)S(1)} %add.34), channel_id=1, source_target_pairs={{0,1},{1,0},{2,3},{3,2},{4,5},{5,4},{6,7},{7,6},{8,9},{9,8},{10,11... | collective-permute-start | bytes 55304 | tf_op jit(solution)/shard_map/ppermute | solution.py:975
  66.4 4.7 %collective-permute-start.20 = (f32[3,1536]{1,0:T(4,128)S(1)}, f32[3,1536]{1,0:T(4,128)S(1)}, u32[]{:S(2)}, u32[]{:S(2)}) collective-permute-start(f32[3,1536]{1,0:T(4,128)S(1)} %add.34), channel_id=1, source_target_pairs={{0,5},{1,4},{2,7},{3,6},{4,1},{5,0},{6,3},{7,2},{8,13},{9,12},{10,... | collective-permute-start | bytes 55304 | tf_op jit(solution)/shard_map/ppermute | solution.py:975
  66.4 4.8 %collective-permute-start.18 = (f32[3,1536]{1,0:T(4,128)S(1)}, f32[3,1536]{1,0:T(4,128)S(1)}, u32[]{:S(2)}, u32[]{:S(2)}) collective-permute-start(f32[3,1536]{1,0:T(4,128)S(1)} %add.34), channel_id=1, source_target_pairs={{0,4},{1,5},{2,6},{3,7},{4,0},{5,1},{6,2},{7,3},{8,12},{9,13},{10,... | collective-permute-start | bytes 55304 | tf_op jit(solution)/shard_map/ppermute | solution.py:975
  71.3 6.3 %collective-permute-start.22 = (f32[3,1536]{1,0:T(4,128)S(1)}, f32[3,1536]{1,0:T(4,128)S(1)}, u32[]{:S(2)}, u32[]{:S(2)}) collective-permute-start(f32[3,1536]{1,0:T(4,128)S(1)} %add_add_fusion), channel_id=1, source_target_pairs={{0,16},{1,17},{2,18},{3,19},{4,20},{5,21},{6,22},{7,23},{8,24},{9,... | collective-permute-start | bytes 55304 | tf_op jit(solution)/shard_map/ppermute | solution.py:975
  72.3 5.6 %collective-permute-start.23 = (f32[3,1536]{1,0:T(4,128)S(1)}, f32[3,1536]{1,0:T(4,128)S(1)}, u32[]{:S(2)}, u32[]{:S(2)}) collective-permute-start(f32[3,1536]{1,0:T(4,128)S(1)} %add_add_fusion), channel_id=1, source_target_pairs={{0,24},{1,25},{2,26},{3,27},{4,28},{5,29},{6,30},{7,31},{8,16},{9,... | collective-permute-start | bytes 55304 | tf_op jit(solution)/shard_map/ppermute | solution.py:975
  75.1 3.8 %collective-permute-start.21 = (f32[3,1536]{1,0:T(4,128)S(1)}, f32[3,1536]{1,0:T(4,128)S(1)}, u32[]{:S(2)}, u32[]{:S(2)}) collective-permute-start(f32[3,1536]{1,0:T(4,128)S(1)} %add_add_fusion), channel_id=1, source_target_pairs={{0,8},{1,9},{2,10},{3,11},{4,12},{5,13},{6,14},{7,15},{8,0},{9,1},... | collective-permute-start | bytes 55304 | tf_op jit(solution)/shard_map/ppermute | solution.py:975
  (8 other events, 258.6 us)

commit v11 on v10

--- a/solution.py
+++ b/solution.py
@@ -437,10 +437,13 @@
     out = jax.ShapeDtypeStruct((16, wide), BF)
     square = jax.ShapeDtypeStruct((tile, tile), BF)
     anywhere = pl.BlockSpec(memory_space=pl.ANY)
+    flat = pl.BlockSpec((16, wide), lambda i: (0, 0))
+    cut = pl.BlockSpec((tile, tile), lambda i: (0, 0))
     return pl.pallas_call(
         pack_kernel,
+        grid=(1,),
         in_specs=[anywhere] * 4,
-        out_specs=[pl.BlockSpec(memory_space=pltpu.VMEM)] * 3 + [anywhere] * 3,
+        out_specs=[flat] * 3 + [cut] * 2 + [pl.BlockSpec((2, short, half), lambda i: (0, 0, 0))],
         out_shape=[out, out, out, square, square, jax.ShapeDtypeStruct((2, short, half), BF)],
         scratch_shapes=[
             pltpu.VMEM((seqs, 16, wide), BF),
@@ -998,7 +1001,7 @@
     edge_b = staggered(edge_b, 1)
     far_a = paired(far, "seq", 2)
     far_b = staggered(far, 2)
-    prev = passed_along(after(cotangent, edge_b), "seq", 1)
+    prev = passed_along(after(cotangent, edge_a), "seq", 1)
     outer = (slab == 0) | (slab == slabs - 1)
     nothing = jnp.zeros_like(edge_b)
     edge = edge_a + jnp.where(outer, nothing, edge_b)

time: 79.8 us -> 55.9 us (0.70)
  Pallas kernels: 41.8 us -> 18.6 us
  starting transfers between devices: 27.2 us -> 24.7 us
  waiting for transfers between devices: 8.96 us -> 10.8 us
    pallas_call x1, Pallas kernels: 25.7 us -> 2.52 us  [packed(): pl.pallas_call(pack_kernel, grid=(1,), in_specs=[anywhere] * 4, out_specs...]
    ppermute x3, starting transfers between devices: 8.22 us -> 5.87 us  [staggered(): return lax.ppermute(part, 'seq', pairs)]
    ppermute x13, waiting for transfers between devices: 2.45 us -> 3.55 us  [paired(): return lax.ppermute(part, axis, [(i, i ^ bit) for i in range(count)])]
  transfers between devices with their start and end apart: 24 -> 24, of which waited for: 9 -> 9; matrix products, arithmetic and copies ran while one was open for 0% -> 0% of each run, Pallas kernels for 20% -> 29%
where the time goes in v11:
time: 55.9 us; the launch traced here: 55.8 us
  starting transfers between devices  24.7 us (44%)
  Pallas kernels  18.6 us (33%)
  waiting for transfers between devices  10.8 us (19%)
  between operations  0.83 us (1%)
  other arithmetic  0.74 us (1%)
    ppermute x13, starting transfers between devices, paired(): return lax.ppermute(part, axis, [(i, i ^ bit) for i in range(count)])  10.3 us
    ppermute x7, starting transfers between devices, crossed(): return lax.ppermute(part, ('seq', 'head'), pairs)  7.2 us
    ppermute x3, starting transfers between devices, staggered(): return lax.ppermute(part, 'seq', pairs)  5.87 us
    pallas_call x1, Pallas kernels, own_half(): pl.pallas_call(functools.partial(own_kernel, slabs), grid_spec=pltpu.Pref...  4.94 us
    ppermute x3, waiting for transfers between devices, staggered(): return lax.ppermute(part, 'seq', pairs)  4.46 us
    ppermute x13, waiting for transfers between devices, paired(): return lax.ppermute(part, axis, [(i, i ^ bit) for i in range(count)])  3.55 us
    ppermute x7, waiting for transfers between devices, crossed(): return lax.ppermute(part, ('seq', 'head'), pairs)  2.82 us
    pallas_call x1, Pallas kernels, other_terms(): pl.pallas_call(terms_kernel, grid_spec=pltpu.PrefetchScalarGridSpec(num_s...  2.67 us
  transfers between devices with their start and end apart: 24, of which 9 were waited for; matrix products, arithmetic and copies ran while one was open for 0% of the time, Pallas kernels for 29%

profile of v11, /device:TPU:0, one launch (start us, length us, event | category | flops | bytes accessed | tf_op | source)
XLA Modules:
  0.0 55.8 jit_solution(13474625544546655255)
XLA Ops:
  0.7 2.5 %pack_edges.1 = (bf16[16,1536]{1,0:T(8,128)(2,1)}, bf16[16,1536]{1,0:T(8,128)(2,1)}, bf16[16,1536]{1,0:T(8,128)(2,1)}, bf16[384,384]{1,0:T(8,128)(2,1)}, bf16[38...) custom-call(bf16[2,128,1536]{2,1,0:T(8,128)(2,1)} %skip.5, bf16[4,64,768]{2,1,0:T(8,128)(2,1)} %att.1, ...), custom_call_target="tpu_custom_call" | custom-call | tf_op jit(solution)/shard_map/pack_edges/pallas_call | solution.py:442
  3.2 3.0 %collective-permute-start.3 = (bf16[16,1536]{1,0:T(8,128)(2,1)}, bf16[16,1536]{1,0:T(8,128)(2,1)S(1)}, u32[]{:S(2)}, u32[]{:S(2)}) collective-permute-start(bf16[16,1536]{1,0:T(8,128)(2,1)} %get-tuple-element.43), channel_id=1, source_target_pairs={{0,4},{2,6},{4,0},{6,2},{8,12},{10,14},{12,8},{14,10},{16,20},{18,... | collective-permute-start | bytes 147464 | tf_op jit(solution)/shard_map/ppermute | solution.py:955
  6.2 3.6 %collective-permute-start.4 = (bf16[16,1536]{1,0:T(8,128)(2,1)}, bf16[16,1536]{1,0:T(8,128)(2,1)S(1)}, u32[]{:S(2)}, u32[]{:S(2)}) collective-permute-start(bf16[16,1536]{1,0:T(8,128)(2,1)} %get-tuple-element.43), channel_id=1, source_target_pairs={{0,28},{2,30},{4,8},{6,10},{8,4},{10,6},{12,16},{14,18},{16,12},{1... | collective-permute-start | bytes 147464 | tf_op jit(solution)/shard_map/ppermute | solution.py:964
  9.8 1.3 %collective-permute-start.1 = (bf16[16,1536]{1,0:T(8,128)(2,1)}, bf16[16,1536]{1,0:T(8,128)(2,1)S(1)}, u32[]{:S(2)}, u32[]{:S(2)}) collective-permute-start(bf16[16,1536]{1,0:T(8,128)(2,1)} %get-tuple-element.41), channel_id=1, source_target_pairs={{0,30},{2,4},{4,2},{6,8},{8,6},{10,12},{12,10},{14,16},{16,14},{18... | collective-permute-start | bytes 147464 | tf_op jit(solution)/shard_map/ppermute | solution.py:964
  11.1 1.5 %collective-permute-start.7 = (bf16[384,384]{1,0:T(8,128)(2,1)}, bf16[384,384]{1,0:T(8,128)(2,1)S(1)}, u32[]{:S(2)}, u32[]{:S(2)}) collective-permute-start(bf16[384,384]{1,0:T(8,128)(2,1)} %get-tuple-element.55), channel_id=1, source_target_pairs={{0,1},{1,0},{2,3},{3,2},{4,5},{5,4},{6,7},{7,6},{8,9},{9,8},{10,11... | collective-permute-start | bytes 884744 | tf_op jit(solution)/shard_map/ppermute | solution.py:955
  12.7 1.3 %collective-permute-start.6 = (bf16[2,128,1536]{2,1,0:T(8,128)(2,1)S(1)}, bf16[2,128,1536]{2,1,0:T(8,128)(2,1)S(1)}, u32[]{:S(2)}, u32[]{:S(2)}) collective-permute-start(bf16[2,128,1536]{2,1,0:T(8,128)(2,1)S(1)} %copy-done.1), channel_id=1, source_target_pairs={{0,2},{2,4},{4,6},{6,8},{8,10},{10,12},{12,14},{14,16},{16,18},{18... | collective-permute-start | bytes 2359304 | tf_op jit(solution)/shard_map/ppermute | solution.py:204
  14.0 2.2 %collective-permute-done.1 = bf16[16,1536]{1,0:T(8,128)(2,1)S(1)} collective-permute-done((bf16[16,1536]{1,0:T(8,128)(2,1)}, bf16[16,1536]{1,0:T(8,128)(2,1)S(1)}, u32[]{:S(2)}, u32[]{:S(2)}) %collective-permute-start.1) | collective-permute-done | bytes 49184 | tf_op jit(solution)/shard_map/ppermute | solution.py:964
  16.2 1.6 %collective-permute-start.5 = (bf16[16,1536]{1,0:T(8,128)(2,1)S(1)}, bf16[16,1536]{1,0:T(8,128)(2,1)S(1)}, u32[]{:S(2)}, u32[]{:S(2)}) collective-permute-start(bf16[16,1536]{1,0:T(8,128)(2,1)S(1)} %get-tuple-element.75), channel_id=1, source_target_pairs={{0,1},{1,0},{2,3},{3,2},{4,5},{5,4},{6,7},{7,6},{8,9},{9,8},{10,11... | collective-permute-start | bytes 147464 | tf_op jit(solution)/shard_map/ppermute | solution.py:955
  18.4 2.1 %own_slopes.1 = (bf16[32,768]{1,0:T(8,128)(2,1)S(1)}, bf16[2,144,768]{2,1,0:T(8,128)(2,1)S(1)}, f32[2,144,768]{2,1,0:T(8,128)S(1)}) custom-call(s32[2]{0:T(128)S(1)} %pad_add_fusion.meta, s32[2]{0:T(128)S(1)} %copy-done.5, s32[2,32]{1,0:T(2,128)S(1)} %copy-done.6, bf16[4,64,768]{2,1,0:T(8,128)(2,1)S(1)} %copy-done.3, bf16[2,128,1536]{2,1,0:T(8,128)(2,1)S(1)} %copy-done.2, ...), custom_call_target="tpu_custom_call" | custom-call | flops 3000000000 | bytes 1000000 | tf_op jit(solution)/shard_map/own_slopes/pallas_call | solution.py:572
  20.9 0.7 %collective-permute-done.5.twin = bf16[16,1536]{1,0:T(8,128)(2,1)S(1)} collective-permute-done((bf16[16,1536]{1,0:T(8,128)(2,1)S(1)}, bf16[16,1536]{1,0:T(8,128)(2,1)S(1)}, u32[]{:S(2)}, u32[]{:S(2)}) %collective-permute-start.5) | collective-permute-done | bytes 49184 | tf_op jit(solution)/shard_map/ppermute | solution.py:955
  21.6 2.1 %collective-permute-start.10 = (bf16[384,384]{1,0:T(8,128)(2,1)S(1)}, bf16[384,384]{1,0:T(8,128)(2,1)S(1)}, u32[]{:S(2)}, u32[]{:S(2)}) collective-permute-start(bf16[384,384]{1,0:T(8,128)(2,1)S(1)} %copy-done.7), channel_id=1, source_target_pairs={{0,1},{1,0},{2,3},{3,2},{4,5},{5,4},{6,7},{7,6},{8,9},{9,8},{10,11... | collective-permute-start | bytes 884744 | tf_op jit(solution)/shard_map/ppermute | solution.py:955
  23.7 2.2 %collective-permute-done.2.att = bf16[2,64,768]{2,1,0:T(8,128)(2,1)S(1)} collective-permute-done((bf16[2,64,768]{2,1,0:T(8,128)(2,1)}, bf16[2,64,768]{2,1,0:T(8,128)(2,1)S(1)}, u32[]{:S(2)}, u32[]{:S(2)}) %collective-permute-start.2) | collective-permute-done | bytes 196640 | tf_op jit(solution)/shard_map/ppermute | solution.py:955
  25.9 2.6 %other_slopes.1 = (bf16[2,144,768]{2,1,0:T(8,128)(2,1)S(1)}, f32[2,144,768]{2,1,0:T(8,128)S(1)}, bf16[16,1536]{1,0:T(8,128)(2,1)S(1)}, bf16[16,1536]{1,0:T(8,128)(2,1)S(1)}) custom-call(s32[2]{0:T(128)S(1)} %pad_add_fusion.meta, s32[2]{0:T(128)S(1)} %copy-done.5, s32[2,32]{1,0:T(2,128)S(1)} %copy-done.6, bf16[2,64,768]{2,1,0:T(8,128)(2,1)S(1)} %collective-permute-done.2.att, ...), custom_call_target="tpu_custom_call" | custom-call | flops 3000000000 | bytes 1000000 | tf_op jit(solution)/shard_map/other_slopes/pallas_call | solution.py:761
  28.5 4.9 %own_half.1 = (bf16[2,144,1536]{2,1,0:T(8,128)(2,1)S(1)}, f32[3,768]{1,0:T(4,128)S(1)}, bf16[2,128,1536]{2,1,0:T(8,128)(2,1)}, bf16[2,64,1536]{2,1,0:T(8,128)(2,1)}) custom-call(s32[2]{0:T(128)S(1)} %pad_add_fusion.meta, s32[2]{0:T(128)S(1)} %copy-done.5, bf16[2,144,768]{2,1,0:T(8,128)(2,1)S(1)} %get-tuple-element.48.sums, ...), custom_call_target="tpu_custom_call" | custom-call | flops 1 | bytes 1 | tf_op jit(solution)/shard_map/own_half/pallas_call | solution.py:675
  35.1 1.0 %collective-permute-start.16 = (bf16[16,1536]{1,0:T(8,128)(2,1)S(1)}, bf16[16,1536]{1,0:T(8,128)(2,1)S(1)}, u32[]{:S(2)}, u32[]{:S(2)}) collective-permute-start(bf16[16,1536]{1,0:T(8,128)(2,1)S(1)} %get-tuple-element.46), channel_id=1, source_target_pairs={{0,30},{2,4},{4,2},{6,8},{8,6},{10,12},{12,10},{14,16},{16,14},{18... | collective-permute-start | bytes 147464 | tf_op jit(solution)/shard_map/ppermute | solution.py:964
  36.3 2.7 %other_terms.1 = (bf16[2,144,768]{2,1,0:T(8,128)(2,1)S(1)}, f32[3,1536]{1,0:T(4,128)S(1)}) custom-call(s32[2]{0:T(128)S(1)} %pad_add_fusion.meta, bf16[2,144,1536]{2,1,0:T(8,128)(2,1)S(1)} %get-tuple-element.51.moved, bf16[2,144,768]{2,1,0:T(8,128)(2,1)S(1)} %get-tuple-element.52.sums, f32[2,144,768]{2,1,0:T(8,128)S(1)} %get-tuple-element.53.slopes, ...), custom_call_target="tpu_custom_call" | custom-call | flops 679477248 | bytes 6291456 | tf_op jit(solution)/shard_map/other_terms/pallas_call | solution.py:838
  39.0 2.3 %collective-permute-done.16.got_b = bf16[16,1536]{1,0:T(8,128)(2,1)S(1)} collective-permute-done((bf16[16,1536]{1,0:T(8,128)(2,1)S(1)}, bf16[16,1536]{1,0:T(8,128)(2,1)S(1)}, u32[]{:S(2)}, u32[]{:S(2)}) %collective-permute-start.16) | collective-permute-done | bytes 49184 | tf_op jit(solution)/shard_map/ppermute | solution.py:964
  41.3 1.2 %collective-permute-done.17 = f32[3,1536]{1,0:T(4,128)S(1)} collective-permute-done((f32[3,1536]{1,0:T(4,128)S(1)}, f32[3,1536]{1,0:T(4,128)S(1)}, u32[]{:S(2)}, u32[]{:S(2)}) %collective-permute-start.17) | collective-permute-done | bytes 18464 | tf_op jit(solution)/shard_map/ppermute | solution.py:978
  42.5 2.1 %collective-permute-start.19 = (f32[3,1536]{1,0:T(4,128)S(1)}, f32[3,1536]{1,0:T(4,128)S(1)}, u32[]{:S(2)}, u32[]{:S(2)}) collective-permute-start(f32[3,1536]{1,0:T(4,128)S(1)} %add.34), channel_id=1, source_target_pairs={{0,1},{1,0},{2,3},{3,2},{4,5},{5,4},{6,7},{7,6},{8,9},{9,8},{10,11... | collective-permute-start | bytes 55304 | tf_op jit(solution)/shard_map/ppermute | solution.py:978
  44.6 1.5 %collective-permute-start.18 = (f32[3,1536]{1,0:T(4,128)S(1)}, f32[3,1536]{1,0:T(4,128)S(1)}, u32[]{:S(2)}, u32[]{:S(2)}) collective-permute-start(f32[3,1536]{1,0:T(4,128)S(1)} %add.34), channel_id=1, source_target_pairs={{0,4},{1,5},{2,6},{3,7},{4,0},{5,1},{6,2},{7,3},{8,12},{9,13},{10,... | collective-permute-start | bytes 55304 | tf_op jit(solution)/shard_map/ppermute | solution.py:978
  46.2 1.8 %other_grads.1 = (bf16[2,128,1536]{2,1,0:T(8,128)(2,1)}, bf16[2,64,1536]{2,1,0:T(8,128)(2,1)}) custom-call(s32[2]{0:T(128)S(1)} %pad_add_fusion.meta, bf16[2,144,1536]{2,1,0:T(8,128)(2,1)S(1)} %get-tuple-element.51.moved, bf16[2,144,768]{2,1,0:T(8,128)(2,1)S(1)} %get-tuple-element.66.convs, ...), custom_call_target="tpu_custom_call", output_to_operand_aliasing={{0}: (4, {}), {1}: (5, {})} | custom-call | flops 4423680 | bytes 4194304 | tf_op jit(solution)/shard_map/other_grads/pallas_call | solution.py:890
  48.0 1.3 %collective-permute-done.20 = f32[3,1536]{1,0:T(4,128)S(1)} collective-permute-done((f32[3,1536]{1,0:T(4,128)S(1)}, f32[3,1536]{1,0:T(4,128)S(1)}, u32[]{:S(2)}, u32[]{:S(2)}) %collective-permute-start.20) | collective-permute-done | bytes 18464 | tf_op jit(solution)/shard_map/ppermute | solution.py:978
  49.8 3.1 %collective-permute-start.21 = (f32[3,1536]{1,0:T(4,128)S(1)}, f32[3,1536]{1,0:T(4,128)S(1)}, u32[]{:S(2)}, u32[]{:S(2)}) collective-permute-start(f32[3,1536]{1,0:T(4,128)S(1)} %add_add_fusion), channel_id=1, source_target_pairs={{0,8},{1,9},{2,10},{3,11},{4,12},{5,13},{6,14},{7,15},{8,0},{9,1},... | collective-permute-start | bytes 55304 | tf_op jit(solution)/shard_map/ppermute | solution.py:978
  52.9 1.9 %targets.1 = bf16[2,2,1536]{2,1,0:T(2,128)(2,1)} custom-call(s32[2]{0:T(128)S(1)} %pad_add_fusion.meta, bf16[16,1536]{1,0:T(8,128)(2,1)S(1)} %get-tuple-element.45.mine, bf16[16,1536]{1,0:T(8,128)(2,1)S(1)} %collective-permute-done.15.got_a, bf16[16,1536]{1,0:T(8,128)(2,1)S(1)} %collective-permute-done.16.got_b, bf16[768,1536]{1,0:T(8,128)(2,1)S(1)} %copy-done, ...), custom_call_target="tpu_custom_call" | custom-call | flops 75497472 | bytes 6291456 | tf_op jit(solution)/shard_map/targets/pallas_call | solution.py:936
  (52 shorter events, 4.2 us)
Async XLA Ops:
  3.2 10.8 %collective-permute-start.3 = (bf16[16,1536]{1,0:T(8,128)(2,1)}, bf16[16,1536]{1,0:T(8,128)(2,1)S(1)}, u32[]{:S(2)}, u32[]{:S(2)}) collective-permute-start(bf16[16,1536]{1,0:T(8,128)(2,1)} %get-tuple-element.43), channel_id=1, source_target_pairs={{0,4},{2,6},{4,0},{6,2},{8,12},{10,14},{12,8},{14,10},{16,20},{18,... | collective-permute-start | bytes 147464 | tf_op jit(solution)/shard_map/ppermute | solution.py:955
  6.2 7.8 %collective-permute-start.4 = (bf16[16,1536]{1,0:T(8,128)(2,1)}, bf16[16,1536]{1,0:T(8,128)(2,1)S(1)}, u32[]{:S(2)}, u32[]{:S(2)}) collective-permute-start(bf16[16,1536]{1,0:T(8,128)(2,1)} %get-tuple-element.43), channel_id=1, source_target_pairs={{0,28},{2,30},{4,8},{6,10},{8,4},{10,6},{12,16},{14,18},{16,12},{1... | collective-permute-start | bytes 147464 | tf_op jit(solution)/shard_map/ppermute | solution.py:964
  9.8 2.9 %collective-permute-start = (bf16[16,1536]{1,0:T(8,128)(2,1)}, bf16[16,1536]{1,0:T(8,128)(2,1)S(1)}, u32[]{:S(2)}, u32[]{:S(2)}) collective-permute-start(bf16[16,1536]{1,0:T(8,128)(2,1)} %get-tuple-element.40), channel_id=1, source_target_pairs={{0,2},{2,0},{4,6},{6,4},{8,10},{10,8},{12,14},{14,12},{16,18},{18,... | collective-permute-start | bytes 147464 | tf_op jit(solution)/shard_map/ppermute | solution.py:955
  9.8 6.4 %collective-permute-start.1 = (bf16[16,1536]{1,0:T(8,128)(2,1)}, bf16[16,1536]{1,0:T(8,128)(2,1)S(1)}, u32[]{:S(2)}, u32[]{:S(2)}) collective-permute-start(bf16[16,1536]{1,0:T(8,128)(2,1)} %get-tuple-element.41), channel_id=1, source_target_pairs={{0,30},{2,4},{4,2},{6,8},{8,6},{10,12},{12,10},{14,16},{16,14},{18... | collective-permute-start | bytes 147464 | tf_op jit(solution)/shard_map/ppermute | solution.py:964
  11.1 9.5 %collective-permute-start.7 = (bf16[384,384]{1,0:T(8,128)(2,1)}, bf16[384,384]{1,0:T(8,128)(2,1)S(1)}, u32[]{:S(2)}, u32[]{:S(2)}) collective-permute-start(bf16[384,384]{1,0:T(8,128)(2,1)} %get-tuple-element.55), channel_id=1, source_target_pairs={{0,1},{1,0},{2,3},{3,2},{4,5},{5,4},{6,7},{7,6},{8,9},{9,8},{10,11... | collective-permute-start | bytes 884744 | tf_op jit(solution)/shard_map/ppermute | solution.py:955
  12.7 15.8 %collective-permute-start.6 = (bf16[2,128,1536]{2,1,0:T(8,128)(2,1)S(1)}, bf16[2,128,1536]{2,1,0:T(8,128)(2,1)S(1)}, u32[]{:S(2)}, u32[]{:S(2)}) collective-permute-start(bf16[2,128,1536]{2,1,0:T(8,128)(2,1)S(1)} %copy-done.1), channel_id=1, source_target_pairs={{0,2},{2,4},{4,6},{6,8},{8,10},{10,12},{12,14},{14,16},{16,18},{18... | collective-permute-start | bytes 2359304 | tf_op jit(solution)/shard_map/ppermute | solution.py:204
  16.2 5.3 %collective-permute-start.5 = (bf16[16,1536]{1,0:T(8,128)(2,1)S(1)}, bf16[16,1536]{1,0:T(8,128)(2,1)S(1)}, u32[]{:S(2)}, u32[]{:S(2)}) collective-permute-start(bf16[16,1536]{1,0:T(8,128)(2,1)S(1)} %get-tuple-element.75), channel_id=1, source_target_pairs={{0,1},{1,0},{2,3},{3,2},{4,5},{5,4},{6,7},{7,6},{8,9},{9,8},{10,11... | collective-permute-start | bytes 147464 | tf_op jit(solution)/shard_map/ppermute | solution.py:955
  17.8 8.0 %collective-permute-start.2 = (bf16[2,64,768]{2,1,0:T(8,128)(2,1)}, bf16[2,64,768]{2,1,0:T(8,128)(2,1)S(1)}, u32[]{:S(2)}, u32[]{:S(2)}) collective-permute-start(bf16[2,64,768]{2,1,0:T(8,128)(2,1)} %get-tuple-element.42), channel_id=1, source_target_pairs={{0,1},{1,0},{2,3},{3,2},{4,5},{5,4},{6,7},{7,6},{8,9},{9,8},{10,11... | collective-permute-start | bytes 589832 | tf_op jit(solution)/shard_map/ppermute | solution.py:955
  20.5 13.0 %collective-permute-start.8 = (bf16[384,384]{1,0:T(8,128)(2,1)S(1)}, bf16[384,384]{1,0:T(8,128)(2,1)S(1)}, u32[]{:S(2)}, u32[]{:S(2)}) collective-permute-start(bf16[384,384]{1,0:T(8,128)(2,1)S(1)} %collective-permute-done.7.refs_0_), channel_id=1, source_target_pairs={{0,4},{2,6},{4,0},{6,2},{8,12},{10,14},{12,8},{14,10},{16,20},{18,... | collective-permute-start | bytes 884744 | tf_op jit(solution)/shard_map/ppermute | solution.py:955
  20.6 13.4 %collective-permute-start.9 = (bf16[384,384]{1,0:T(8,128)(2,1)S(1)}, bf16[384,384]{1,0:T(8,128)(2,1)S(1)}, u32[]{:S(2)}, u32[]{:S(2)}) collective-permute-start(bf16[384,384]{1,0:T(8,128)(2,1)S(1)} %collective-permute-done.7.refs_0_), channel_id=1, source_target_pairs={{0,8},{2,10},{4,12},{6,14},{8,0},{10,2},{12,4},{14,6},{16,24},{18,... | collective-permute-start | bytes 884744 | tf_op jit(solution)/shard_map/ppermute | solution.py:955
  21.6 12.5 %collective-permute-start.10 = (bf16[384,384]{1,0:T(8,128)(2,1)S(1)}, bf16[384,384]{1,0:T(8,128)(2,1)S(1)}, u32[]{:S(2)}, u32[]{:S(2)}) collective-permute-start(bf16[384,384]{1,0:T(8,128)(2,1)S(1)} %copy-done.7), channel_id=1, source_target_pairs={{0,1},{1,0},{2,3},{3,2},{4,5},{5,4},{6,7},{7,6},{8,9},{9,8},{10,11... | collective-permute-start | bytes 884744 | tf_op jit(solution)/shard_map/ppermute | solution.py:955
  33.4 1.6 %collective-permute-start.11 = (bf16[384,384]{1,0:T(8,128)(2,1)S(1)}, bf16[384,384]{1,0:T(8,128)(2,1)S(1)}, u32[]{:S(2)}, u32[]{:S(2)}) collective-permute-start(bf16[384,384]{1,0:T(8,128)(2,1)S(1)} %collective-permute-done.7.refs_0_), channel_id=1, source_target_pairs={{0,2},{2,0},{4,6},{6,4},{8,10},{10,8},{12,14},{14,12},{16,18},{18,... | collective-permute-start | bytes 884744 | tf_op jit(solution)/shard_map/ppermute | solution.py:955
  33.5 2.6 %collective-permute-start.12 = (bf16[384,384]{1,0:T(8,128)(2,1)S(1)}, bf16[384,384]{1,0:T(8,128)(2,1)S(1)}, u32[]{:S(2)}, u32[]{:S(2)}) collective-permute-start(bf16[384,384]{1,0:T(8,128)(2,1)S(1)} %collective-permute-done.8.refs_1_), channel_id=1, source_target_pairs={{0,2},{2,0},{4,6},{6,4},{8,10},{10,8},{12,14},{14,12},{16,18},{18,... | collective-permute-start | bytes 884744 | tf_op jit(solution)/shard_map/ppermute | solution.py:955
  34.0 2.1 %collective-permute-start.13 = (bf16[384,384]{1,0:T(8,128)(2,1)S(1)}, bf16[384,384]{1,0:T(8,128)(2,1)S(1)}, u32[]{:S(2)}, u32[]{:S(2)}) collective-permute-start(bf16[384,384]{1,0:T(8,128)(2,1)S(1)} %collective-permute-done.9.refs_2_), channel_id=1, source_target_pairs={{0,2},{2,0},{4,6},{6,4},{8,10},{10,8},{12,14},{14,12},{16,18},{18,... | collective-permute-start | bytes 884744 | tf_op jit(solution)/shard_map/ppermute | solution.py:955
  34.1 2.2 %collective-permute-start.14 = (bf16[384,384]{1,0:T(8,128)(2,1)S(1)}, bf16[384,384]{1,0:T(8,128)(2,1)S(1)}, u32[]{:S(2)}, u32[]{:S(2)}) collective-permute-start(bf16[384,384]{1,0:T(8,128)(2,1)S(1)} %collective-permute-done.10.refs_3_), channel_id=1, source_target_pairs={{0,2},{2,0},{4,6},{6,4},{8,10},{10,8},{12,14},{14,12},{16,18},{18,... | collective-permute-start | bytes 884744 | tf_op jit(solution)/shard_map/ppermute | solution.py:955
  34.5 4.5 %collective-permute-start.15 = (bf16[16,1536]{1,0:T(8,128)(2,1)S(1)}, bf16[16,1536]{1,0:T(8,128)(2,1)S(1)}, u32[]{:S(2)}, u32[]{:S(2)}) collective-permute-start(bf16[16,1536]{1,0:T(8,128)(2,1)S(1)} %get-tuple-element.46), channel_id=1, source_target_pairs={{0,2},{2,0},{4,6},{6,4},{8,10},{10,8},{12,14},{14,12},{16,18},{18,... | collective-permute-start | bytes 147464 | tf_op jit(solution)/shard_map/ppermute | solution.py:955
  35.1 6.2 %collective-permute-start.16 = (bf16[16,1536]{1,0:T(8,128)(2,1)S(1)}, bf16[16,1536]{1,0:T(8,128)(2,1)S(1)}, u32[]{:S(2)}, u32[]{:S(2)}) collective-permute-start(bf16[16,1536]{1,0:T(8,128)(2,1)S(1)} %get-tuple-element.46), channel_id=1, source_target_pairs={{0,30},{2,4},{4,2},{6,8},{8,6},{10,12},{12,10},{14,16},{16,14},{18... | collective-permute-start | bytes 147464 | tf_op jit(solution)/shard_map/ppermute | solution.py:964
  41.3 1.2 %collective-permute-start.17 = (f32[3,1536]{1,0:T(4,128)S(1)}, f32[3,1536]{1,0:T(4,128)S(1)}, u32[]{:S(2)}, u32[]{:S(2)}) collective-permute-start(f32[3,1536]{1,0:T(4,128)S(1)} %get-tuple-element.65), channel_id=1, source_target_pairs={{0,2},{1,3},{2,0},{3,1},{4,6},{5,7},{6,4},{7,5},{8,10},{9,11},{10,... | collective-permute-start | bytes 55304 | tf_op jit(solution)/shard_map/ppermute | solution.py:978
  42.5 5.5 %collective-permute-start.19 = (f32[3,1536]{1,0:T(4,128)S(1)}, f32[3,1536]{1,0:T(4,128)S(1)}, u32[]{:S(2)}, u32[]{:S(2)}) collective-permute-start(f32[3,1536]{1,0:T(4,128)S(1)} %add.34), channel_id=1, source_target_pairs={{0,1},{1,0},{2,3},{3,2},{4,5},{5,4},{6,7},{7,6},{8,9},{9,8},{10,11... | collective-permute-start | bytes 55304 | tf_op jit(solution)/shard_map/ppermute | solution.py:978
  44.6 4.7 %collective-permute-start.20 = (f32[3,1536]{1,0:T(4,128)S(1)}, f32[3,1536]{1,0:T(4,128)S(1)}, u32[]{:S(2)}, u32[]{:S(2)}) collective-permute-start(f32[3,1536]{1,0:T(4,128)S(1)} %add.34), channel_id=1, source_target_pairs={{0,5},{1,4},{2,7},{3,6},{4,1},{5,0},{6,3},{7,2},{8,13},{9,12},{10,... | collective-permute-start | bytes 55304 | tf_op jit(solution)/shard_map/ppermute | solution.py:978
  44.6 4.7 %collective-permute-start.18 = (f32[3,1536]{1,0:T(4,128)S(1)}, f32[3,1536]{1,0:T(4,128)S(1)}, u32[]{:S(2)}, u32[]{:S(2)}) collective-permute-start(f32[3,1536]{1,0:T(4,128)S(1)} %add.34), channel_id=1, source_target_pairs={{0,4},{1,5},{2,6},{3,7},{4,0},{5,1},{6,2},{7,3},{8,12},{9,13},{10,... | collective-permute-start | bytes 55304 | tf_op jit(solution)/shard_map/ppermute | solution.py:978
  49.4 5.5 %collective-permute-start.22 = (f32[3,1536]{1,0:T(4,128)S(1)}, f32[3,1536]{1,0:T(4,128)S(1)}, u32[]{:S(2)}, u32[]{:S(2)}) collective-permute-start(f32[3,1536]{1,0:T(4,128)S(1)} %add_add_fusion), channel_id=1, source_target_pairs={{0,16},{1,17},{2,18},{3,19},{4,20},{5,21},{6,22},{7,23},{8,24},{9,... | collective-permute-start | bytes 55304 | tf_op jit(solution)/shard_map/ppermute | solution.py:978
  49.4 5.7 %collective-permute-start.23 = (f32[3,1536]{1,0:T(4,128)S(1)}, f32[3,1536]{1,0:T(4,128)S(1)}, u32[]{:S(2)}, u32[]{:S(2)}) collective-permute-start(f32[3,1536]{1,0:T(4,128)S(1)} %add_add_fusion), channel_id=1, source_target_pairs={{0,24},{1,25},{2,26},{3,27},{4,28},{5,29},{6,30},{7,31},{8,16},{9,... | collective-permute-start | bytes 55304 | tf_op jit(solution)/shard_map/ppermute | solution.py:978
  49.8 5.4 %collective-permute-start.21 = (f32[3,1536]{1,0:T(4,128)S(1)}, f32[3,1536]{1,0:T(4,128)S(1)}, u32[]{:S(2)}, u32[]{:S(2)}) collective-permute-start(f32[3,1536]{1,0:T(4,128)S(1)} %add_add_fusion), channel_id=1, source_target_pairs={{0,8},{1,9},{2,10},{3,11},{4,12},{5,13},{6,14},{7,15},{8,0},{9,1},... | collective-permute-start | bytes 55304 | tf_op jit(solution)/shard_map/ppermute | solution.py:978
  (8 other events, 110.5 us)

commit v12 on v11

--- a/solution.py
+++ b/solution.py
@@ -1,3 +1,177 @@
+import functools
+import math
+
+import jax
+import jax.numpy as jnp
+from jax import lax
+from jax.experimental import pallas as pl
+from jax.experimental.pallas import tpu as pltpu
+from jax.sharding import PartitionSpec as P
+
+NTD = 2
+
+
+def extended(shard, sides, width):
+    for axis, dim in sides:
+        count, length = (lax.axis_size(axis), shard.shape[dim])
+        up = [(i, (i + 1) % count) for i in range(count - 1)]
+        down = [(j, i) for i, j in up]
+        last = lax.slice_in_dim(shard, length - width, length, axis=dim)
+        initial = lax.slice_in_dim(shard, 0, width, axis=dim)
+        before = lax.ppermute(last, axis, up)
+        after = lax.ppermute(initial, axis, down)
+        shard = jnp.concatenate([before, shard, after], axis=dim)
+    return shard
+
+
+def passed_along(shard, axis, by):
+    count = lax.axis_size(axis)
+    pairs = [(i, i + by) for i in range(count) if 0 <= i + by < count]
+    return lax.ppermute(shard, axis, pairs)
+
+
+def gelu_slope(values):
+    return (
+        0.5 * (1.0 + lax.erf(values * 0.7071067811865476))
+        + values * jnp.exp(-0.5 * values * values) * 0.3989422804014327
+    )
+
+
+def with_rims(field):
+    return extended(field, (("seq", 1),), 1)
+
+
+def one_hot(places, length):
+    return (places[:, :, None] == jnp.arange(length, dtype=jnp.int32)[None, None, :]).astype(
+        jnp.bfloat16
+    )
+
+
+def core_swap(part):
+    count = lax.axis_size("seq")
+    return lax.ppermute(part, "seq", [(i, i ^ 1) for i in range(count)])
+
+
+def gathered_weight(rows):
+    heads = lax.axis_size("head")
+    here = lax.axis_index("head")
+    core = lax.axis_index("seq") % 2
+    half = rows.shape[0] // 2
+    mine = lax.dynamic_slice_in_dim(rows, core * half, half, 0)
+    blocks = [(0, rows)]
+    for step in range(1, heads):
+        pairs = [(i, (i + step) % heads) for i in range(heads)]
+        got = lax.ppermute(mine, "head", pairs)
+        twin = core_swap(got)
+        low = jnp.where(core == 0, got, twin)
+        high = jnp.where(core == 0, twin, got)
+        blocks.append((step, jnp.concatenate([low, high], axis=0)))
+    full = jnp.zeros((heads * rows.shape[0], rows.shape[1]), rows.dtype)
+    for step, block in blocks:
+        place = (here - step) % heads
+        full = lax.dynamic_update_slice_in_dim(full, block, place * rows.shape[0], 0)
+    return full
+
+
+def butterfly(total, axis):
+    count = lax.axis_size(axis)
+    if count & (count - 1):
+        return lax.psum(total, axis)
+    step = 1
+    while step < count:
+        total = total + lax.ppermute(total, axis, [(i, i ^ step) for i in range(count)])
+        step *= 2
+    return total
+
+
+def plain_shards(
+    attention, encoder_skip, depth_filter, point_weight, crop_offset, target_bins, cotangent
+):
+    slab_input = lax.all_to_all(attention, "head", split_axis=0, concat_axis=2, tiled=True)
+    local_seqs = encoder_skip.shape[0]
+    slab_rows = encoder_skip.shape[1]
+    channels = encoder_skip.shape[2]
+    summed = (
+        jnp.repeat(slab_input, 2, axis=1).astype(jnp.float32) + encoder_skip.astype(jnp.float32)
+    ).astype(jnp.bfloat16)
+    padded = with_rims(summed)
+    filtered = (
+        depth_filter[0] * padded[:, :-2]
+        + depth_filter[1] * padded[:, 1:-1]
+        + depth_filter[2] * padded[:, 2:]
+    )
+    activated = jax.nn.gelu(filtered, approximate=False).astype(jnp.bfloat16)
+    flat_act = activated.reshape(local_seqs * slab_rows, channels)
+    full_weight = gathered_weight(point_weight)
+    mixed_rows = jnp.dot(flat_act, full_weight, preferred_element_type=jnp.float32)
+    block_out = (
+        summed.astype(jnp.float32) + mixed_rows.reshape(local_seqs, slab_rows, channels)
+    ).astype(jnp.bfloat16)
+    slab_index = lax.axis_index("seq")
+    bins = jnp.concatenate(
+        [jnp.zeros_like(target_bins[:, :NTD]), target_bins], axis=1
+    )
+    asked = lax.dynamic_slice_in_dim(bins, slab_index * NTD, 2 * NTD, 1) + crop_offset[:, None]
+    back = jnp.where(jnp.arange(2 * NTD, dtype=jnp.int32) < NTD, slab_rows, 0)
+    asked = asked - back[None, :]
+    picked = jnp.einsum(
+        "sjr,srd->sjd",
+        one_hot(asked, slab_rows),
+        block_out,
+        preferred_element_type=jnp.float32,
+    ).astype(jnp.bfloat16)
+    from_next = passed_along(picked[:, :NTD], "seq", -1)
+    target_rows = picked[:, NTD:] + from_next
+    prev_cot = passed_along(cotangent, "seq", 1)
+    cot_pair = jnp.concatenate([prev_cot, cotangent], axis=1)
+
+    def crop_back(cot_block, shift_by):
+        return lax.dynamic_slice_in_dim(cot_block, slab_rows - shift_by, slab_rows, 0)
+
+    grad_out = jax.vmap(crop_back)(cot_pair, crop_offset)
+    flat_grad = grad_out.reshape(local_seqs * slab_rows, channels)
+    grad_act = lax.dot_general(
+        flat_grad, full_weight, (((1,), (1,)), ((), ())), preferred_element_type=jnp.float32
+    )
+    grad_conv = (grad_act.reshape(local_seqs, slab_rows, channels) * gelu_slope(filtered)).astype(
+        jnp.bfloat16
+    )
+    grad_padded = with_rims(grad_conv)
+    grad_sum = (
+        grad_out.astype(jnp.float32)
+        + depth_filter[0] * grad_padded[:, 2:]
+        + depth_filter[1] * grad_padded[:, 1:-1]
+        + depth_filter[2] * grad_padded[:, :-2]
+    )
+    skip_grad = grad_sum.astype(jnp.bfloat16)
+    attention_grad = (
+        grad_sum.reshape(local_seqs, slab_rows // 2, 2, channels).sum(axis=2).astype(jnp.bfloat16)
+    )
+    filter_terms = jnp.stack(
+        [
+            jnp.einsum(
+                "srd,srd->d", grad_conv, padded[:, 0:slab_rows], preferred_element_type=jnp.float32
+            ),
+            jnp.einsum(
+                "srd,srd->d",
+                grad_conv,
+                padded[:, 1 : slab_rows + 1],
+                preferred_element_type=jnp.float32,
+            ),
+            jnp.einsum(
+                "srd,srd->d",
+                grad_conv,
+                padded[:, 2 : slab_rows + 2],
+                preferred_element_type=jnp.float32,
+            ),
+        ]
+    )
+    filter_sum = butterfly(butterfly(filter_terms, "seq"), "head")
+    row_count = local_seqs * lax.axis_size("head") * slab_rows * lax.axis_size("seq")
+    filter_grad = filter_sum * (1.0 / math.sqrt(row_count))
+    return (target_rows, attention_grad, skip_grad, filter_grad)
+
+
 import functools
 import math
 
@@ -1014,7 +1188,7 @@
     ready = after(first, asked)
     second = paired(ready, "seq", 2)
     third = paired(ready, "seq", 4)
-    fourth = paired(last_tile, "head", 1)
+    fourth = paired(after(last_tile, asked), "head", 1)
     sums, slopes, mine, shown = other_slopes(
         meta, crop_offset, target_bins, shipped, encoder_skip, edge, twin, depth_filter, asked
     )
@@ -1024,9 +1198,9 @@
         slabs,
     )
     pieces = [first, second, third, fourth]
-    pieces = pieces + [paired(after(piece, own_terms), "seq", 1) for piece in pieces]
+    ties = [own_terms, own_terms, own_terms, own_terms]
+    pieces = pieces + [paired(after(*both), "seq", 1) for both in zip(pieces, ties)]
     convs, terms = other_terms(meta, moved, sums, slopes, own_terms, pieces)
-    terms, *got = lax.optimization_barrier((terms, *got))
     total = terms + crossed(terms, 1, 0)
     total = joined(total, (2, 0), (0, 1))
     skip_grad, attention_grad = other_grads(
@@ -1083,3 +1257,15 @@
     )
     out_specs = (P("head", "seq", None), P("head", "seq", None), P("head", "seq", None), P())
     return jax.shard_map(shards, mesh=mesh, in_specs=in_specs, out_specs=out_specs, check_vma=False)
+def solution(mesh):
+    in_specs = (
+        P(None, "seq", "head"),
+        P("head", "seq", None),
+        P(),
+        P("head", None),
+        P("head"),
+        P("head", None),
+        P("head", "seq", None),
+    )
+    out_specs = (P("head", "seq", None), P("head", "seq", None), P("head", "seq", None), P())
+    return jax.shard_map(shards, mesh=mesh, in_specs=in_specs, out_specs=out_specs, check_vma=False)

time: 55.9 us -> 56.2 us (level)
  starting transfers between devices: 24.7 us -> 25.8 us
  waiting for transfers between devices: 10.8 us -> 9.97 us
    ppermute x3, waiting for transfers between devices: 4.46 us -> 2.21 us  [staggered(): return lax.ppermute(part, 'seq', pairs)]
    ppermute x13, waiting for transfers between devices: 3.55 us -> 5.51 us  [paired(): return lax.ppermute(part, axis, [(i, i ^ bit) for i in range(count)])]
    ppermute x7, starting transfers between devices: 7.2 us -> 8.23 us  [crossed(): return lax.ppermute(part, ('seq', 'head'), pairs)]
    ppermute x3, starting transfers between devices: 5.87 us -> 6.87 us  [staggered(): return lax.ppermute(part, 'seq', pairs)]
    ppermute x13, starting transfers between devices: 10.3 us -> 9.35 us  [paired(): return lax.ppermute(part, axis, [(i, i ^ bit) for i in range(count)])]
    ppermute x7, waiting for transfers between devices: 2.82 us -> 2.25 us  [crossed(): return lax.ppermute(part, ('seq', 'head'), pairs)]
  transfers between devices with their start and end apart: 24 -> 24, of which waited for: 9 -> 8; matrix products, arithmetic and copies ran while one was open for 0% -> 0% of each run, Pallas kernels for 29% -> 24%
where the time goes in v12:
time: 56.2 us; the launch traced here: 56 us
  starting transfers between devices  25.8 us (46%)
  Pallas kernels  18.6 us (33%)
  waiting for transfers between devices  9.97 us (18%)
  between operations  0.85 us (2%)
  other arithmetic  0.74 us (1%)
    ppermute x13, starting transfers between devices, paired(): return lax.ppermute(part, axis, [(i, i ^ bit) for i in range(count)])  9.35 us
    ppermute x7, starting transfers between devices, crossed(): return lax.ppermute(part, ('seq', 'head'), pairs)  8.23 us
    ppermute x3, starting transfers between devices, staggered(): return lax.ppermute(part, 'seq', pairs)  6.87 us
    ppermute x13, waiting for transfers between devices, paired(): return lax.ppermute(part, axis, [(i, i ^ bit) for i in range(count)])  5.51 us
    pallas_call x1, Pallas kernels, own_half(): pl.pallas_call(functools.partial(own_kernel, slabs), grid_spec=pltpu.Pref...  4.94 us
    pallas_call x1, Pallas kernels, other_terms(): pl.pallas_call(terms_kernel, grid_spec=pltpu.PrefetchScalarGridSpec(num_s...  2.67 us
    pallas_call x1, Pallas kernels, other_slopes(): pl.pallas_call(slope_kernel, grid_spec=pltpu.PrefetchScalarGridSpec(num_s...  2.61 us
    pallas_call x1, Pallas kernels, packed(): pl.pallas_call(pack_kernel, grid=(1,), in_specs=[anywhere] * 4, out_specs...  2.52 us
  transfers between devices with their start and end apart: 24, of which 8 were waited for; matrix products, arithmetic and copies ran while one was open for 0% of the time, Pallas kernels for 24%

profile of v12, /device:TPU:0, one launch (start us, length us, event | category | flops | bytes accessed | tf_op | source)
XLA Modules:
  0.0 56.0 jit_solution(2156687471276280420)
XLA Ops:
  0.7 2.5 %pack_edges.1 = (bf16[16,1536]{1,0:T(8,128)(2,1)}, bf16[16,1536]{1,0:T(8,128)(2,1)}, bf16[16,1536]{1,0:T(8,128)(2,1)}, bf16[384,384]{1,0:T(8,128)(2,1)}, bf16[38...) custom-call(bf16[2,128,1536]{2,1,0:T(8,128)(2,1)} %skip.5, bf16[4,64,768]{2,1,0:T(8,128)(2,1)} %att.1, ...), custom_call_target="tpu_custom_call" | custom-call | tf_op jit(solution)/shard_map/pack_edges/pallas_call | solution.py:616
  3.2 3.0 %collective-permute-start.3 = (bf16[16,1536]{1,0:T(8,128)(2,1)}, bf16[16,1536]{1,0:T(8,128)(2,1)S(1)}, u32[]{:S(2)}, u32[]{:S(2)}) collective-permute-start(bf16[16,1536]{1,0:T(8,128)(2,1)} %get-tuple-element.41), channel_id=1, source_target_pairs={{0,4},{2,6},{4,0},{6,2},{8,12},{10,14},{12,8},{14,10},{16,20},{18,... | collective-permute-start | bytes 147464 | tf_op jit(solution)/shard_map/ppermute | solution.py:1129
  6.2 3.6 %collective-permute-start.4 = (bf16[16,1536]{1,0:T(8,128)(2,1)}, bf16[16,1536]{1,0:T(8,128)(2,1)S(1)}, u32[]{:S(2)}, u32[]{:S(2)}) collective-permute-start(bf16[16,1536]{1,0:T(8,128)(2,1)} %get-tuple-element.41), channel_id=1, source_target_pairs={{0,28},{2,30},{4,8},{6,10},{8,4},{10,6},{12,16},{14,18},{16,12},{1... | collective-permute-start | bytes 147464 | tf_op jit(solution)/shard_map/ppermute | solution.py:1138
  9.8 1.3 %collective-permute-start.1 = (bf16[16,1536]{1,0:T(8,128)(2,1)}, bf16[16,1536]{1,0:T(8,128)(2,1)S(1)}, u32[]{:S(2)}, u32[]{:S(2)}) collective-permute-start(bf16[16,1536]{1,0:T(8,128)(2,1)} %get-tuple-element.39), channel_id=1, source_target_pairs={{0,30},{2,4},{4,2},{6,8},{8,6},{10,12},{12,10},{14,16},{16,14},{18... | collective-permute-start | bytes 147464 | tf_op jit(solution)/shard_map/ppermute | solution.py:1138
  11.1 1.5 %collective-permute-start.8 = (bf16[384,384]{1,0:T(8,128)(2,1)}, bf16[384,384]{1,0:T(8,128)(2,1)S(1)}, u32[]{:S(2)}, u32[]{:S(2)}) collective-permute-start(bf16[384,384]{1,0:T(8,128)(2,1)} %get-tuple-element.45), channel_id=1, source_target_pairs={{0,1},{1,0},{2,3},{3,2},{4,5},{5,4},{6,7},{7,6},{8,9},{9,8},{10,11... | collective-permute-start | bytes 884744 | tf_op jit(solution)/shard_map/ppermute | solution.py:1129
  12.7 1.3 %collective-permute-start.12 = (bf16[2,128,1536]{2,1,0:T(8,128)(2,1)S(1)}, bf16[2,128,1536]{2,1,0:T(8,128)(2,1)S(1)}, u32[]{:S(2)}, u32[]{:S(2)}) collective-permute-start(bf16[2,128,1536]{2,1,0:T(8,128)(2,1)S(1)} %copy-done.1), channel_id=1, source_target_pairs={{0,2},{2,4},{4,6},{6,8},{8,10},{10,12},{12,14},{14,16},{16,18},{18... | collective-permute-start | bytes 2359304 | tf_op jit(solution)/shard_map/ppermute | solution.py:378
  14.0 2.2 %collective-permute-done.1 = bf16[16,1536]{1,0:T(8,128)(2,1)S(1)} collective-permute-done((bf16[16,1536]{1,0:T(8,128)(2,1)}, bf16[16,1536]{1,0:T(8,128)(2,1)S(1)}, u32[]{:S(2)}, u32[]{:S(2)}) %collective-permute-start.1) | collective-permute-done | bytes 49184 | tf_op jit(solution)/shard_map/ppermute | solution.py:1138
  16.2 1.6 %collective-permute-start.5 = (bf16[16,1536]{1,0:T(8,128)(2,1)S(1)}, bf16[16,1536]{1,0:T(8,128)(2,1)S(1)}, u32[]{:S(2)}, u32[]{:S(2)}) collective-permute-start(bf16[16,1536]{1,0:T(8,128)(2,1)S(1)} %get-tuple-element.71), channel_id=1, source_target_pairs={{0,1},{1,0},{2,3},{3,2},{4,5},{5,4},{6,7},{7,6},{8,9},{9,8},{10,11... | collective-permute-start | bytes 147464 | tf_op jit(solution)/shard_map/ppermute | solution.py:1129
  18.4 2.1 %own_slopes.1 = (bf16[32,768]{1,0:T(8,128)(2,1)S(1)}, bf16[2,144,768]{2,1,0:T(8,128)(2,1)S(1)}, f32[2,144,768]{2,1,0:T(8,128)S(1)}) custom-call(s32[2]{0:T(128)S(1)} %pad_add_fusion.meta, s32[2]{0:T(128)S(1)} %copy-done.5, s32[2,32]{1,0:T(2,128)S(1)} %copy-done.6, bf16[4,64,768]{2,1,0:T(8,128)(2,1)S(1)} %copy-done.3, bf16[2,128,1536]{2,1,0:T(8,128)(2,1)S(1)} %copy-done.2, ...), custom_call_target="tpu_custom_call" | custom-call | flops 3000000000 | bytes 1000000 | tf_op jit(solution)/shard_map/own_slopes/pallas_call | solution.py:746
  20.5 1.6 %collective-permute-start.11 = (bf16[384,384]{1,0:T(8,128)(2,1)S(1)}, bf16[384,384]{1,0:T(8,128)(2,1)S(1)}, u32[]{:S(2)}, u32[]{:S(2)}) collective-permute-start(bf16[384,384]{1,0:T(8,128)(2,1)S(1)} %copy-done.7), channel_id=1, source_target_pairs={{0,1},{1,0},{2,3},{3,2},{4,5},{5,4},{6,7},{7,6},{8,9},{9,8},{10,11... | collective-permute-start | bytes 884744 | tf_op jit(solution)/shard_map/ppermute | solution.py:1129
  22.2 3.7 %collective-permute-done.2.att = bf16[2,64,768]{2,1,0:T(8,128)(2,1)S(1)} collective-permute-done((bf16[2,64,768]{2,1,0:T(8,128)(2,1)}, bf16[2,64,768]{2,1,0:T(8,128)(2,1)S(1)}, u32[]{:S(2)}, u32[]{:S(2)}) %collective-permute-start.2) | collective-permute-done | bytes 196640 | tf_op jit(solution)/shard_map/ppermute | solution.py:1129
  25.9 2.6 %other_slopes.1 = (bf16[2,144,768]{2,1,0:T(8,128)(2,1)S(1)}, f32[2,144,768]{2,1,0:T(8,128)S(1)}, bf16[16,1536]{1,0:T(8,128)(2,1)S(1)}, bf16[16,1536]{1,0:T(8,128)(2,1)S(1)}) custom-call(s32[2]{0:T(128)S(1)} %pad_add_fusion.meta, s32[2]{0:T(128)S(1)} %copy-done.5, s32[2,32]{1,0:T(2,128)S(1)} %copy-done.6, bf16[2,64,768]{2,1,0:T(8,128)(2,1)S(1)} %collective-permute-done.2.att, ...), custom_call_target="tpu_custom_call" | custom-call | flops 3000000000 | bytes 1000000 | tf_op jit(solution)/shard_map/other_slopes/pallas_call | solution.py:935
  28.5 4.9 %own_half.1 = (bf16[2,144,1536]{2,1,0:T(8,128)(2,1)S(1)}, f32[3,768]{1,0:T(4,128)S(1)}, bf16[2,128,1536]{2,1,0:T(8,128)(2,1)}, bf16[2,64,1536]{2,1,0:T(8,128)(2,1)}) custom-call(s32[2]{0:T(128)S(1)} %pad_add_fusion.meta, s32[2]{0:T(128)S(1)} %copy-done.5, bf16[2,144,768]{2,1,0:T(8,128)(2,1)S(1)} %get-tuple-element.50.sums, ...), custom_call_target="tpu_custom_call" | custom-call | flops 1 | bytes 1 | tf_op jit(solution)/shard_map/own_half/pallas_call | solution.py:849
  36.4 2.7 %other_terms.1 = (bf16[2,144,768]{2,1,0:T(8,128)(2,1)S(1)}, f32[3,1536]{1,0:T(4,128)S(1)}) custom-call(s32[2]{0:T(128)S(1)} %pad_add_fusion.meta, bf16[2,144,1536]{2,1,0:T(8,128)(2,1)S(1)} %get-tuple-element.58.moved, bf16[2,144,768]{2,1,0:T(8,128)(2,1)S(1)} %get-tuple-element.59.sums, f32[2,144,768]{2,1,0:T(8,128)S(1)} %get-tuple-element.60.slopes, ...), custom_call_target="tpu_custom_call" | custom-call | flops 679477248 | bytes 6291456 | tf_op jit(solution)/shard_map/other_terms/pallas_call | solution.py:1012
  39.2 1.1 %collective-permute-done.17 = f32[3,1536]{1,0:T(4,128)S(1)} collective-permute-done((f32[3,1536]{1,0:T(4,128)S(1)}, f32[3,1536]{1,0:T(4,128)S(1)}, u32[]{:S(2)}, u32[]{:S(2)}) %collective-permute-start.17) | collective-permute-done | bytes 18464 | tf_op jit(solution)/shard_map/ppermute | solution.py:1152
  40.4 2.1 %collective-permute-start.19 = (f32[3,1536]{1,0:T(4,128)S(1)}, f32[3,1536]{1,0:T(4,128)S(1)}, u32[]{:S(2)}, u32[]{:S(2)}) collective-permute-start(f32[3,1536]{1,0:T(4,128)S(1)} %add.34), channel_id=1, source_target_pairs={{0,1},{1,0},{2,3},{3,2},{4,5},{5,4},{6,7},{7,6},{8,9},{9,8},{10,11... | collective-permute-start | bytes 55304 | tf_op jit(solution)/shard_map/ppermute | solution.py:1152
  42.5 1.4 %collective-permute-start.20 = (f32[3,1536]{1,0:T(4,128)S(1)}, f32[3,1536]{1,0:T(4,128)S(1)}, u32[]{:S(2)}, u32[]{:S(2)}) collective-permute-start(f32[3,1536]{1,0:T(4,128)S(1)} %add.34), channel_id=1, source_target_pairs={{0,5},{1,4},{2,7},{3,6},{4,1},{5,0},{6,3},{7,2},{8,13},{9,12},{10,... | collective-permute-start | bytes 55304 | tf_op jit(solution)/shard_map/ppermute | solution.py:1152
  43.9 2.0 %collective-permute-start.7 = (bf16[16,1536]{1,0:T(8,128)(2,1)S(1)}, bf16[16,1536]{1,0:T(8,128)(2,1)S(1)}, u32[]{:S(2)}, u32[]{:S(2)}) collective-permute-start(bf16[16,1536]{1,0:T(8,128)(2,1)S(1)} %get-tuple-element.44), channel_id=1, source_target_pairs={{0,30},{2,4},{4,2},{6,8},{8,6},{10,12},{12,10},{14,16},{16,14},{18... | collective-permute-start | bytes 147464 | tf_op jit(solution)/shard_map/ppermute | solution.py:1138
  45.9 1.8 %other_grads.1 = (bf16[2,128,1536]{2,1,0:T(8,128)(2,1)}, bf16[2,64,1536]{2,1,0:T(8,128)(2,1)}) custom-call(s32[2]{0:T(128)S(1)} %pad_add_fusion.meta, bf16[2,144,1536]{2,1,0:T(8,128)(2,1)S(1)} %get-tuple-element.58.moved, bf16[2,144,768]{2,1,0:T(8,128)(2,1)S(1)} %get-tuple-element.62.convs, ...), custom_call_target="tpu_custom_call", output_to_operand_aliasing={{0}: (4, {}), {1}: (5, {})} | custom-call | flops 4423680 | bytes 4194304 | tf_op jit(solution)/shard_map/other_grads/pallas_call | solution.py:1064
  48.0 1.8 %collective-permute-start.22 = (f32[3,1536]{1,0:T(4,128)S(1)}, f32[3,1536]{1,0:T(4,128)S(1)}, u32[]{:S(2)}, u32[]{:S(2)}) collective-permute-start(f32[3,1536]{1,0:T(4,128)S(1)} %add_add_fusion), channel_id=1, source_target_pairs={{0,16},{1,17},{2,18},{3,19},{4,20},{5,21},{6,22},{7,23},{8,24},{9,... | collective-permute-start | bytes 55304 | tf_op jit(solution)/shard_map/ppermute | solution.py:1152
  49.8 2.5 %collective-permute-start.23 = (f32[3,1536]{1,0:T(4,128)S(1)}, f32[3,1536]{1,0:T(4,128)S(1)}, u32[]{:S(2)}, u32[]{:S(2)}) collective-permute-start(f32[3,1536]{1,0:T(4,128)S(1)} %add_add_fusion), channel_id=1, source_target_pairs={{0,24},{1,25},{2,26},{3,27},{4,28},{5,29},{6,30},{7,31},{8,16},{9,... | collective-permute-start | bytes 55304 | tf_op jit(solution)/shard_map/ppermute | solution.py:1152
  52.3 1.9 %targets.1 = bf16[2,2,1536]{2,1,0:T(2,128)(2,1)} custom-call(s32[2]{0:T(128)S(1)} %pad_add_fusion.meta, bf16[16,1536]{1,0:T(8,128)(2,1)S(1)} %get-tuple-element.43.mine, bf16[16,1536]{1,0:T(8,128)(2,1)S(1)} %collective-permute-done.6.got_a, bf16[16,1536]{1,0:T(8,128)(2,1)S(1)} %collective-permute-done.7.got_b, bf16[768,1536]{1,0:T(8,128)(2,1)S(1)} %copy-done, ...), custom_call_target="tpu_custom_call" | custom-call | flops 75497472 | bytes 6291456 | tf_op jit(solution)/shard_map/targets/pallas_call | solution.py:1110
  54.2 1.2 %collective-permute-done.23 = f32[3,1536]{1,0:T(4,128)S(1)} collective-permute-done((f32[3,1536]{1,0:T(4,128)S(1)}, f32[3,1536]{1,0:T(4,128)S(1)}, u32[]{:S(2)}, u32[]{:S(2)}) %collective-permute-start.23) | collective-permute-done | bytes 18464 | tf_op jit(solution)/shard_map/ppermute | solution.py:1152
  55.4 0.6 %add_multiply_fusion = f32[3,1536]{1,0:T(4,128)} fusion(f32[3,1536]{1,0:T(4,128)S(1)} %collective-permute-done.22, f32[3,1536]{1,0:T(4,128)S(1)} %collective-permute-done.23, f32[3,1536]{1,0:T(4,128)S(1)} %add_add_fusion, f32[3,1536]{1,0:T(4,128)S(1)} %collective-permute-done.21), kind=kLoop, calls=%fused_computation.2 | loop fusion | flops 18432 | bytes 92160 | tf_op jit(solution)/shard_map/mul | solution.py:1221
  (52 shorter events, 4.1 us)
Async XLA Ops:
  3.2 10.8 %collective-permute-start.3 = (bf16[16,1536]{1,0:T(8,128)(2,1)}, bf16[16,1536]{1,0:T(8,128)(2,1)S(1)}, u32[]{:S(2)}, u32[]{:S(2)}) collective-permute-start(bf16[16,1536]{1,0:T(8,128)(2,1)} %get-tuple-element.41), channel_id=1, source_target_pairs={{0,4},{2,6},{4,0},{6,2},{8,12},{10,14},{12,8},{14,10},{16,20},{18,... | collective-permute-start | bytes 147464 | tf_op jit(solution)/shard_map/ppermute | solution.py:1129
  6.2 7.8 %collective-permute-start.4 = (bf16[16,1536]{1,0:T(8,128)(2,1)}, bf16[16,1536]{1,0:T(8,128)(2,1)S(1)}, u32[]{:S(2)}, u32[]{:S(2)}) collective-permute-start(bf16[16,1536]{1,0:T(8,128)(2,1)} %get-tuple-element.41), channel_id=1, source_target_pairs={{0,28},{2,30},{4,8},{6,10},{8,4},{10,6},{12,16},{14,18},{16,12},{1... | collective-permute-start | bytes 147464 | tf_op jit(solution)/shard_map/ppermute | solution.py:1138
  9.8 2.9 %collective-permute-start = (bf16[16,1536]{1,0:T(8,128)(2,1)}, bf16[16,1536]{1,0:T(8,128)(2,1)S(1)}, u32[]{:S(2)}, u32[]{:S(2)}) collective-permute-start(bf16[16,1536]{1,0:T(8,128)(2,1)} %get-tuple-element.38), channel_id=1, source_target_pairs={{0,2},{2,0},{4,6},{6,4},{8,10},{10,8},{12,14},{14,12},{16,18},{18,... | collective-permute-start | bytes 147464 | tf_op jit(solution)/shard_map/ppermute | solution.py:1129
  9.8 6.4 %collective-permute-start.1 = (bf16[16,1536]{1,0:T(8,128)(2,1)}, bf16[16,1536]{1,0:T(8,128)(2,1)S(1)}, u32[]{:S(2)}, u32[]{:S(2)}) collective-permute-start(bf16[16,1536]{1,0:T(8,128)(2,1)} %get-tuple-element.39), channel_id=1, source_target_pairs={{0,30},{2,4},{4,2},{6,8},{8,6},{10,12},{12,10},{14,16},{16,14},{18... | collective-permute-start | bytes 147464 | tf_op jit(solution)/shard_map/ppermute | solution.py:1138
  11.1 11.1 %collective-permute-start.8 = (bf16[384,384]{1,0:T(8,128)(2,1)}, bf16[384,384]{1,0:T(8,128)(2,1)S(1)}, u32[]{:S(2)}, u32[]{:S(2)}) collective-permute-start(bf16[384,384]{1,0:T(8,128)(2,1)} %get-tuple-element.45), channel_id=1, source_target_pairs={{0,1},{1,0},{2,3},{3,2},{4,5},{5,4},{6,7},{7,6},{8,9},{9,8},{10,11... | collective-permute-start | bytes 884744 | tf_op jit(solution)/shard_map/ppermute | solution.py:1129
  12.7 15.8 %collective-permute-start.12 = (bf16[2,128,1536]{2,1,0:T(8,128)(2,1)S(1)}, bf16[2,128,1536]{2,1,0:T(8,128)(2,1)S(1)}, u32[]{:S(2)}, u32[]{:S(2)}) collective-permute-start(bf16[2,128,1536]{2,1,0:T(8,128)(2,1)S(1)} %copy-done.1), channel_id=1, source_target_pairs={{0,2},{2,4},{4,6},{6,8},{8,10},{10,12},{12,14},{14,16},{16,18},{18... | collective-permute-start | bytes 2359304 | tf_op jit(solution)/shard_map/ppermute | solution.py:378
  16.2 5.9 %collective-permute-start.5 = (bf16[16,1536]{1,0:T(8,128)(2,1)S(1)}, bf16[16,1536]{1,0:T(8,128)(2,1)S(1)}, u32[]{:S(2)}, u32[]{:S(2)}) collective-permute-start(bf16[16,1536]{1,0:T(8,128)(2,1)S(1)} %get-tuple-element.71), channel_id=1, source_target_pairs={{0,1},{1,0},{2,3},{3,2},{4,5},{5,4},{6,7},{7,6},{8,9},{9,8},{10,11... | collective-permute-start | bytes 147464 | tf_op jit(solution)/shard_map/ppermute | solution.py:1129
  17.8 8.0 %collective-permute-start.2 = (bf16[2,64,768]{2,1,0:T(8,128)(2,1)}, bf16[2,64,768]{2,1,0:T(8,128)(2,1)S(1)}, u32[]{:S(2)}, u32[]{:S(2)}) collective-permute-start(bf16[2,64,768]{2,1,0:T(8,128)(2,1)} %get-tuple-element.40), channel_id=1, source_target_pairs={{0,1},{1,0},{2,3},{3,2},{4,5},{5,4},{6,7},{7,6},{8,9},{9,8},{10,11... | collective-permute-start | bytes 589832 | tf_op jit(solution)/shard_map/ppermute | solution.py:1129
  20.5 12.9 %collective-permute-start.11 = (bf16[384,384]{1,0:T(8,128)(2,1)S(1)}, bf16[384,384]{1,0:T(8,128)(2,1)S(1)}, u32[]{:S(2)}, u32[]{:S(2)}) collective-permute-start(bf16[384,384]{1,0:T(8,128)(2,1)S(1)} %copy-done.7), channel_id=1, source_target_pairs={{0,1},{1,0},{2,3},{3,2},{4,5},{5,4},{6,7},{7,6},{8,9},{9,8},{10,11... | collective-permute-start | bytes 884744 | tf_op jit(solution)/shard_map/ppermute | solution.py:1129
  22.1 11.4 %collective-permute-start.10 = (bf16[384,384]{1,0:T(8,128)(2,1)S(1)}, bf16[384,384]{1,0:T(8,128)(2,1)S(1)}, u32[]{:S(2)}, u32[]{:S(2)}) collective-permute-start(bf16[384,384]{1,0:T(8,128)(2,1)S(1)} %collective-permute-done.8.refs_0_), channel_id=1, source_target_pairs={{0,8},{2,10},{4,12},{6,14},{8,0},{10,2},{12,4},{14,6},{16,24},{18,... | collective-permute-start | bytes 884744 | tf_op jit(solution)/shard_map/ppermute | solution.py:1129
  22.1 11.9 %collective-permute-start.9 = (bf16[384,384]{1,0:T(8,128)(2,1)S(1)}, bf16[384,384]{1,0:T(8,128)(2,1)S(1)}, u32[]{:S(2)}, u32[]{:S(2)}) collective-permute-start(bf16[384,384]{1,0:T(8,128)(2,1)S(1)} %collective-permute-done.8.refs_0_), channel_id=1, source_target_pairs={{0,4},{2,6},{4,0},{6,2},{8,12},{10,14},{12,8},{14,10},{16,20},{18,... | collective-permute-start | bytes 884744 | tf_op jit(solution)/shard_map/ppermute | solution.py:1129
  33.4 1.6 %collective-permute-start.16 = (bf16[384,384]{1,0:T(8,128)(2,1)S(1)}, bf16[384,384]{1,0:T(8,128)(2,1)S(1)}, u32[]{:S(2)}, u32[]{:S(2)}) collective-permute-start(bf16[384,384]{1,0:T(8,128)(2,1)S(1)} %collective-permute-done.11.refs_3_), channel_id=1, source_target_pairs={{0,2},{2,0},{4,6},{6,4},{8,10},{10,8},{12,14},{14,12},{16,18},{18,... | collective-permute-start | bytes 884744 | tf_op jit(solution)/shard_map/ppermute | solution.py:1129
  33.5 2.0 %collective-permute-start.15 = (bf16[384,384]{1,0:T(8,128)(2,1)S(1)}, bf16[384,384]{1,0:T(8,128)(2,1)S(1)}, u32[]{:S(2)}, u32[]{:S(2)}) collective-permute-start(bf16[384,384]{1,0:T(8,128)(2,1)S(1)} %collective-permute-done.10.refs_2_), channel_id=1, source_target_pairs={{0,2},{2,0},{4,6},{6,4},{8,10},{10,8},{12,14},{14,12},{16,18},{18,... | collective-permute-start | bytes 884744 | tf_op jit(solution)/shard_map/ppermute | solution.py:1129
  34.0 1.9 %collective-permute-start.14 = (bf16[384,384]{1,0:T(8,128)(2,1)S(1)}, bf16[384,384]{1,0:T(8,128)(2,1)S(1)}, u32[]{:S(2)}, u32[]{:S(2)}) collective-permute-start(bf16[384,384]{1,0:T(8,128)(2,1)S(1)} %collective-permute-done.9.refs_1_), channel_id=1, source_target_pairs={{0,2},{2,0},{4,6},{6,4},{8,10},{10,8},{12,14},{14,12},{16,18},{18,... | collective-permute-start | bytes 884744 | tf_op jit(solution)/shard_map/ppermute | solution.py:1129
  34.1 2.2 %collective-permute-start.13 = (bf16[384,384]{1,0:T(8,128)(2,1)S(1)}, bf16[384,384]{1,0:T(8,128)(2,1)S(1)}, u32[]{:S(2)}, u32[]{:S(2)}) collective-permute-start(bf16[384,384]{1,0:T(8,128)(2,1)S(1)} %collective-permute-done.8.refs_0_), channel_id=1, source_target_pairs={{0,2},{2,0},{4,6},{6,4},{8,10},{10,8},{12,14},{14,12},{16,18},{18,... | collective-permute-start | bytes 884744 | tf_op jit(solution)/shard_map/ppermute | solution.py:1129
  39.0 1.3 %collective-permute-start.17 = (f32[3,1536]{1,0:T(4,128)S(1)}, f32[3,1536]{1,0:T(4,128)S(1)}, u32[]{:S(2)}, u32[]{:S(2)}) collective-permute-start(f32[3,1536]{1,0:T(4,128)S(1)} %get-tuple-element.61), channel_id=1, source_target_pairs={{0,2},{1,3},{2,0},{3,1},{4,6},{5,7},{6,4},{7,5},{8,10},{9,11},{10,... | collective-permute-start | bytes 55304 | tf_op jit(solution)/shard_map/ppermute | solution.py:1152
  40.3 7.5 %collective-permute-start.18 = (f32[3,1536]{1,0:T(4,128)S(1)}, f32[3,1536]{1,0:T(4,128)S(1)}, u32[]{:S(2)}, u32[]{:S(2)}) collective-permute-start(f32[3,1536]{1,0:T(4,128)S(1)} %add.34), channel_id=1, source_target_pairs={{0,4},{1,5},{2,6},{3,7},{4,0},{5,1},{6,2},{7,3},{8,12},{9,13},{10,... | collective-permute-start | bytes 55304 | tf_op jit(solution)/shard_map/ppermute | solution.py:1152
  40.4 7.4 %collective-permute-start.19 = (f32[3,1536]{1,0:T(4,128)S(1)}, f32[3,1536]{1,0:T(4,128)S(1)}, u32[]{:S(2)}, u32[]{:S(2)}) collective-permute-start(f32[3,1536]{1,0:T(4,128)S(1)} %add.34), channel_id=1, source_target_pairs={{0,1},{1,0},{2,3},{3,2},{4,5},{5,4},{6,7},{7,6},{8,9},{9,8},{10,11... | collective-permute-start | bytes 55304 | tf_op jit(solution)/shard_map/ppermute | solution.py:1152
  42.5 5.3 %collective-permute-start.20 = (f32[3,1536]{1,0:T(4,128)S(1)}, f32[3,1536]{1,0:T(4,128)S(1)}, u32[]{:S(2)}, u32[]{:S(2)}) collective-permute-start(f32[3,1536]{1,0:T(4,128)S(1)} %add.34), channel_id=1, source_target_pairs={{0,5},{1,4},{2,7},{3,6},{4,1},{5,0},{6,3},{7,2},{8,13},{9,12},{10,... | collective-permute-start | bytes 55304 | tf_op jit(solution)/shard_map/ppermute | solution.py:1152
  43.9 8.4 %collective-permute-start.6 = (bf16[16,1536]{1,0:T(8,128)(2,1)S(1)}, bf16[16,1536]{1,0:T(8,128)(2,1)S(1)}, u32[]{:S(2)}, u32[]{:S(2)}) collective-permute-start(bf16[16,1536]{1,0:T(8,128)(2,1)S(1)} %get-tuple-element.44), channel_id=1, source_target_pairs={{0,2},{2,0},{4,6},{6,4},{8,10},{10,8},{12,14},{14,12},{16,18},{18,... | collective-permute-start | bytes 147464 | tf_op jit(solution)/shard_map/ppermute | solution.py:1129
  43.9 8.4 %collective-permute-start.7 = (bf16[16,1536]{1,0:T(8,128)(2,1)S(1)}, bf16[16,1536]{1,0:T(8,128)(2,1)S(1)}, u32[]{:S(2)}, u32[]{:S(2)}) collective-permute-start(bf16[16,1536]{1,0:T(8,128)(2,1)S(1)} %get-tuple-element.44), channel_id=1, source_target_pairs={{0,30},{2,4},{4,2},{6,8},{8,6},{10,12},{12,10},{14,16},{16,14},{18... | collective-permute-start | bytes 147464 | tf_op jit(solution)/shard_map/ppermute | solution.py:1138
  47.8 6.4 %collective-permute-start.21 = (f32[3,1536]{1,0:T(4,128)S(1)}, f32[3,1536]{1,0:T(4,128)S(1)}, u32[]{:S(2)}, u32[]{:S(2)}) collective-permute-start(f32[3,1536]{1,0:T(4,128)S(1)} %add_add_fusion), channel_id=1, source_target_pairs={{0,8},{1,9},{2,10},{3,11},{4,12},{5,13},{6,14},{7,15},{8,0},{9,1},... | collective-permute-start | bytes 55304 | tf_op jit(solution)/shard_map/ppermute | solution.py:1152
  48.0 6.2 %collective-permute-start.22 = (f32[3,1536]{1,0:T(4,128)S(1)}, f32[3,1536]{1,0:T(4,128)S(1)}, u32[]{:S(2)}, u32[]{:S(2)}) collective-permute-start(f32[3,1536]{1,0:T(4,128)S(1)} %add_add_fusion), channel_id=1, source_target_pairs={{0,16},{1,17},{2,18},{3,19},{4,20},{5,21},{6,22},{7,23},{8,24},{9,... | collective-permute-start | bytes 55304 | tf_op jit(solution)/shard_map/ppermute | solution.py:1152
  49.8 5.6 %collective-permute-start.23 = (f32[3,1536]{1,0:T(4,128)S(1)}, f32[3,1536]{1,0:T(4,128)S(1)}, u32[]{:S(2)}, u32[]{:S(2)}) collective-permute-start(f32[3,1536]{1,0:T(4,128)S(1)} %add_add_fusion), channel_id=1, source_target_pairs={{0,24},{1,25},{2,26},{3,27},{4,28},{5,29},{6,30},{7,31},{8,16},{9,... | collective-permute-start | bytes 55304 | tf_op jit(solution)/shard_map/ppermute | solution.py:1152
  (8 other events, 110.5 us)
